TPU v7x, 32 devices: a whole 2x2x4 slice. The times are simulated.
32 devices in a mesh: heads: 2 (over x), pages: 16 (over z, y, core).
Axes of the slice: x: 2, y: 2, z: 4, core: 2. Of those that a mesh axis runs over, the one named last changes fastest.
Arguments:
- queries: bfloat16 [4608, 16, 128], P('pages', 'heads'), may hold values from -60 to 60
- keys: bfloat16 [4608, 16, 128], P('pages', 'heads'), may hold values from -6 to 6
- values: bfloat16 [4608, 16, 128], P('pages', 'heads'), may hold values from -6 to 6
- key_cache: bfloat16 [192, 128, 16, 128], P('pages', None, 'heads'), may hold values from -6 to 6
- value_cache: bfloat16 [192, 128, 16, 128], P('pages', None, 'heads'), may hold values from -6 to 6
- cache_len: int32 [6], replicated, may hold values from 0 to 3328, as said below
- page_table: int32 [6, 26], replicated, may hold values from 0 to 191, as said below
- append_slots: int32 [6, 6], replicated, may hold values from 0 to 191
- out_weight: bfloat16 [2048, 4096], P('heads', 'pages'), may hold values from -0.125 to 0.125
- out_bias: float32 [4096], P('heads'), may hold values from -3 to 3
Outputs:
- hidden: bfloat16 [4608, 4096], P('pages', 'heads')
- key_cache_out: bfloat16 [192, 128, 16, 128], P('pages', None, 'heads')
- value_cache_out: bfloat16 [192, 128, 16, 128], P('pages', None, 'heads')
Inputs may be any that keep to these rules, and one draw needn't show every extreme that they name: Every entry of page_table and append_slots together is a different slot. `cache_len`: A multiple of 128; some request has exactly 3328.
All inputs are finite; a program needn't handle non-finite values.
Results may differ from a plain program's by a relative error of at most 0.018.
Values may be sent and summed in bfloat16 or wider, within the bound.
No kernel may reach another device: no remote copies, remote signals or barrier semaphores. Data moves between devices by JAX's collectives and lax.ppermute only.
A program may use at most 128 MiB of HBM per device.

v0:
```python
import functools
import math

import jax
import jax.numpy as jnp
from jax import lax
from jax.experimental import pallas as pl
from jax.experimental.layout import Layout, with_layout_constraint
from jax.experimental.pallas import tpu as pltpu
from jax.sharding import PartitionSpec as P

ROT = 32
PAGE = 128
QTILE = 256

low_score = -(2.0**99)


def rotate(vectors, positions):
    half_rot = ROT // 2
    inv_freq = 10000.0 ** (-2.0 * jnp.arange(half_rot, dtype=jnp.float32) / ROT)
    angles = positions[:, None] * inv_freq[None, :]
    cosine = jnp.cos(angles)[:, None, :]
    sine = jnp.sin(angles)[:, None, :]
    first_half = vectors[..., :half_rot]
    second_half = vectors[..., half_rot:ROT]
    return jnp.concatenate(
        [
            first_half * cosine - second_half * sine,
            second_half * cosine + first_half * sine,
            vectors[..., ROT:],
        ],
        axis=-1,
    )


def stat_rows_of(part_len, unit):
    per_unit = -(-unit // 128)
    units = part_len // unit
    return per_unit, units, -(-3 * units * per_unit // 16) * 16


def stat_rows(row):
    unit = row.shape[1]
    full = -(-unit // 128) * 128
    if full > unit:
        row = jnp.concatenate([row, jnp.zeros((1, full - unit), row.dtype)], axis=1)
    return [row[:, at : at + 128] for at in range(0, full, 128)]


def stat_block(kinds, pad_to):
    rows = [piece for kind in kinds for row in kind for piece in stat_rows(row)]
    rows.append(jnp.zeros((pad_to - len(rows), 128), jnp.float32))
    return jnp.concatenate(rows, axis=0).astype(jnp.bfloat16)


def cached_kernel(unit, stat_unit, span, scale2, places, at_ref, ok_ref, order_ref, start_ref, count_ref,
                  *refs):
    q_refs, (k_ref, v_ref), refs = refs[:places], refs[places : places + 2], refs[places + 2 :]
    o_refs, (q_all, o_all, s_all, q_scr, m_scr, l_scr, acc_scr) = refs[:-7], refs[-7:]
    requests = count_ref.shape[0]
    chips, part_len, _ = q_all.shape
    per_part = part_len // unit
    per_request = span // unit
    per_unit, units, pad_to = stat_rows_of(part_len, stat_unit)

    for index in range(places):

        @pl.when(ok_ref[index] > 0)
        def _(index=index):
            q_all[at_ref[index]] = q_refs[index][0]

    def place(at, per_part):
        return at // per_part, at % per_part

    def one_request(request, _):
        for index in range(per_request):
            part, piece = place(request * per_request + index, per_part)
            row = pl.ds(pl.multiple_of(piece * unit, unit), unit)
            q_scr[index * unit : (index + 1) * unit, :] = q_all[part, row, :]
        first = start_ref[request]
        count = count_ref[request]
        m_scr[...] = jnp.full((1, span), low_score, jnp.float32)
        l_scr[...] = jnp.zeros((1, span), jnp.float32)
        acc_scr[...] = jnp.zeros(acc_scr.shape, jnp.float32)

        def pages(slots):
            k = jnp.concatenate([k_ref[0, s] for s in slots], axis=0)
            v = jnp.concatenate([v_ref[0, s] for s in slots], axis=1)
            for c in range(0, span, QTILE):
                cols = slice(c, c + QTILE)
                scores = lax.dot_general(
                    k, q_scr[cols, :], (((1,), (1,)), ((), ())),
                    preferred_element_type=jnp.float32,
                )
                before = m_scr[:, cols]
                peak = jnp.maximum(before, jnp.max(scores, axis=0, keepdims=True))
                weights = jnp.exp2((scores - peak) * scale2)
                fade = jnp.exp2((before - peak) * scale2)
                m_scr[:, cols] = peak
                l_scr[:, cols] = l_scr[:, cols] * fade + jnp.sum(weights, axis=0, keepdims=True)
                acc_scr[:, cols] = acc_scr[:, cols] * fade + jnp.dot(
                    v, weights.astype(jnp.bfloat16), preferred_element_type=jnp.float32
                )

        def pair(index, _):
            at = first + 2 * index
            pages([order_ref[at], order_ref[at + 1]])
            return 0

        lax.fori_loop(0, count // 2, pair, 0)

        @pl.when(count % 2 == 1)
        def _():
            pages([order_ref[first + count - 1]])

        totals = l_scr[...]
        peaks = m_scr[...]
        out = (acc_scr[...] / jnp.maximum(totals, 1e-30)).T.astype(jnp.bfloat16)
        sent = peaks.astype(jnp.bfloat16).astype(jnp.float32)
        totals = totals * jnp.exp2((peaks - sent) * scale2)
        high = totals.astype(jnp.bfloat16).astype(jnp.float32)
        kinds = [sent, high, totals - high]
        for index in range(per_request):
            part, piece = place(request * per_request + index, per_part)
            row = pl.ds(pl.multiple_of(piece * unit, unit), unit)
            o_all[part, row, :] = out[index * unit : (index + 1) * unit, :]
        for index in range(span // stat_unit):
            part, piece = place(request * (span // stat_unit) + index, units)
            cols = slice(index * stat_unit, (index + 1) * stat_unit)
            for kind, values in enumerate(kinds):
                for r, line in enumerate(stat_rows(values[:, cols])):
                    at = (kind * units + piece) * per_unit + r
                    s_all[part, pl.ds(at, 1), :] = line
        return 0

    lax.fori_loop(0, requests, one_request, 0)
    for index in range(chips):
        part = at_ref[places + index]
        o_refs[index][0, :part_len, :] = o_all[part]
        o_refs[index][0, part_len:, :] = s_all[part].astype(jnp.bfloat16)


def cached_attention(q_places, at, ok, out_at, k_heads, v_heads, order, starts, counts, span,
                     stat_unit, scale2):
    places = len(q_places)
    chips = len(out_at)
    heads, part_len, head_dim = q_places[0].shape
    slots = k_heads.shape[1]
    unit = math.gcd(span, part_len)
    _, _, pad_to = stat_rows_of(part_len, stat_unit)
    own_block = lambda *dims: pl.BlockSpec(
        (1,) + dims, lambda h, *_: (h,) + (0,) * len(dims)
    )
    return pl.pallas_call(
        lambda *refs: cached_kernel(unit, stat_unit, span, scale2, places, *refs),
        grid_spec=pltpu.PrefetchScalarGridSpec(
            num_scalar_prefetch=5,
            grid=(heads,),
            in_specs=[own_block(part_len, head_dim)] * places
            + [own_block(slots, PAGE, head_dim), own_block(slots, head_dim, PAGE)],
            out_specs=[own_block(part_len + pad_to, head_dim)] * chips,
            scratch_shapes=[
                pltpu.VMEM((chips, part_len, head_dim), jnp.bfloat16),
                pltpu.VMEM((chips, part_len, head_dim), jnp.bfloat16),
                pltpu.VMEM((chips, pad_to, 128), jnp.float32),
                pltpu.VMEM((span, head_dim), jnp.bfloat16),
                pltpu.VMEM((1, span), jnp.float32),
                pltpu.VMEM((1, span), jnp.float32),
                pltpu.VMEM((head_dim, span), jnp.float32),
            ],
        ),
        out_shape=[
            jax.ShapeDtypeStruct((heads, part_len + pad_to, head_dim), jnp.bfloat16)
        ] * chips,
        compiler_params=pltpu.CompilerParams(vmem_limit_bytes=40 * 2**20),
        cost_estimate=pl.CostEstimate(
            flops=40 * 10**9, bytes_accessed=20 * 2**20, transcendentals=10**7
        ),
        name="cached_attention",
    )(jnp.stack(at + out_at), jnp.stack(ok), order, starts, counts, *q_places, k_heads, v_heads)


def spread(row, width, unit):
    return jnp.broadcast_to(row, (width, row.shape[1])).T[:unit]


def merge_kernel(unit, part_len, scale2, ok_ref, *refs):
    in_refs, out_ref = refs[:-1], refs[-1]
    head_dim = out_ref.shape[2]
    per_unit, units, pad_to = stat_rows_of(part_len, unit)
    stats = [ref[0, part_len:, :].astype(jnp.float32) for ref in in_refs]
    rows = [ref[0, :part_len, :].astype(jnp.float32) for ref in in_refs]
    outs = []
    kinds = [[], [], []]
    for u in range(units):

        def line(stat, kind):
            at = (kind * units + u) * per_unit
            pieces = [stat[at + r : at + r + 1, :] for r in range(per_unit)]
            return jnp.concatenate(pieces, axis=1)

        peaks, totals = [], []
        for index, stat in enumerate(stats):
            ok = ok_ref[index] > 0
            peaks.append(jnp.where(ok, line(stat, 0), low_score))
            totals.append(jnp.where(ok, line(stat, 1) + line(stat, 2), 0.0))
        top = functools.reduce(jnp.maximum, peaks)
        shares = [t * jnp.exp2((p - top) * scale2) for t, p in zip(totals, peaks)]
        total = functools.reduce(jnp.add, shares)
        inverse = 1.0 / jnp.maximum(total, 1e-30)
        merged = None
        for values, share in zip(rows, shares):
            part = spread(share * inverse, head_dim, unit) * values[u * unit : (u + 1) * unit]
            merged = part if merged is None else merged + part
        outs.append(merged)
        high = total.astype(jnp.bfloat16).astype(jnp.float32)
        for kind, value in zip(kinds, (top, high, total - high)):
            kind.append(value)
    out_ref[0, :part_len, :] = jnp.concatenate(outs, axis=0).astype(jnp.bfloat16)
    out_ref[0, part_len:, :] = stat_block(kinds, pad_to)


def merge(parts, ok, part_len, unit, scale2):
    block = pl.BlockSpec((1,) + parts[0].shape[1:], lambda h, *_: (h, 0, 0))
    return pl.pallas_call(
        lambda *refs: merge_kernel(unit, part_len, scale2, *refs),
        grid_spec=pltpu.PrefetchScalarGridSpec(
            num_scalar_prefetch=1,
            grid=(parts[0].shape[0],),
            in_specs=[block] * len(parts),
            out_specs=block,
        ),
        out_shape=jax.ShapeDtypeStruct(parts[0].shape, jnp.bfloat16),
        name="merge",
    )(jnp.stack(ok).astype(jnp.int32), *parts)


def page_kernel(fresh_ref, index_ref, kc_ref, vc_ref, kn_ref, vn_ref, ko_ref, vo_ref):
    fresh = fresh_ref[pl.program_id(0)] > 0

    @pl.when(fresh)
    def _():
        ko_ref[...] = kn_ref[...]
        vo_ref[...] = vn_ref[...]

    @pl.when(jnp.logical_not(fresh))
    def _():
        ko_ref[...] = kc_ref[...]
        vo_ref[...] = vc_ref[...]


def write_pages(key_cache, value_cache, new_keys, new_values, is_fresh, fresh_index):
    block = (1,) + key_cache.shape[1:]
    own = pl.BlockSpec(block, lambda s, fresh, index: (s, 0, 0, 0))
    new = pl.BlockSpec(block, lambda s, fresh, index: (index[s], 0, 0, 0))
    return pl.pallas_call(
        page_kernel,
        grid_spec=pltpu.PrefetchScalarGridSpec(
            num_scalar_prefetch=2,
            grid=(key_cache.shape[0],),
            in_specs=[own, own, new, new],
            out_specs=[own, own],
        ),
        out_shape=[jax.ShapeDtypeStruct(key_cache.shape, key_cache.dtype)] * 2,
        compiler_params=pltpu.CompilerParams(vmem_limit_bytes=40 * 2**20),
        name="write_pages",
    )(is_fresh.astype(jnp.int32), fresh_index, key_cache, value_cache, new_keys, new_values)


def swap(x, bit):
    devs = lax.axis_size("pages")
    return lax.ppermute(x, "pages", [(p, p ^ bit) for p in range(devs)])


def shift(x, hop, senders):
    devs = lax.axis_size("pages")
    moves = [(p, p + 4 * hop) for p in range(devs) if p // 4 in senders]
    return lax.ppermute(x, "pages", moves)


def gather_lines(x):
    line = lax.axis_size("pages") // 4
    device_at = lax.axis_index("pages")
    at, across = device_at // 4, (device_at // 2) % 2
    always = jnp.int32(1)
    held = [(x, at, across, always), (swap(x, 2), at, 1 - across, always)]
    up = down = x
    for t in range(1, line):
        up = shift(up, 1, range(t - 1, line - 1))
        down = shift(down, -1, range(1, line - t + 1))
        has_up = (at >= t).astype(jnp.int32)
        has_down = (at + t < line).astype(jnp.int32)
        devs = lax.axis_size("pages")
        cross_up = [(p, p ^ 2) for p in range(devs) if p // 4 >= t]
        cross_down = [(p, p ^ 2) for p in range(devs) if p // 4 + t < line]
        held += [
            (up, at - t, across, has_up),
            (lax.ppermute(up, "pages", cross_up), at - t, 1 - across, has_up),
            (down, at + t, across, has_down),
            (lax.ppermute(down, "pages", cross_down), at + t, 1 - across, has_down),
        ]
    return held


def merge_lines(parts, merged, last):
    line = lax.axis_size("pages") // 4
    at = lax.axis_index("pages") // 4
    turns = []
    for t in range(1, line):
        turns += [k for k in (line - t, t) if k not in turns]
    yes = jnp.int32(1)
    crossed = {k: swap(parts[k][1], 2) for k in turns + [0]}
    shares = {}

    def share(k):
        if k not in shares:
            shares[k] = merged([parts[k][0], crossed[k]], [yes, yes])
        return shares[k]

    up = down = None
    for t in range(1, line):
        up_out, down_out = share(line - t), share(t)
        if up is not None:
            up_out = merged([up_out, up], [yes, (at >= 1) & (at <= t - 1)])
            down_out = merged([down_out, down], [yes, (at <= line - 2) & (at >= line - t)])
        up = shift(up_out, 1, range(0, t))
        down = shift(down_out, -1, range(line - t, line))
    return merged([share(0), up, down, last()], [yes, at >= 1, at <= line - 2, yes])


def fresh_kernel(unit, scale2, q_ref, k_ref, v_ref, tok_ref, key_ref, o_ref):
    token, first, key = tok_ref[0:1, :], tok_ref[1:2, :], key_ref[:, 0:1]
    scores = lax.dot_general(
        k_ref[0], q_ref[0], (((1,), (1,)), ((), ())), preferred_element_type=jnp.float32
    )
    visible = (key <= token) & (key >= first)
    scores = jnp.where(visible, scores, low_score)
    peak = jnp.max(scores, axis=0, keepdims=True)
    weights = jnp.where(visible, jnp.exp2((scores - peak) * scale2), 0.0)
    totals = jnp.sum(weights, axis=0, keepdims=True)
    out = lax.dot_general(
        v_ref[0], weights.astype(jnp.bfloat16), (((0,), (0,)), ((), ())),
        preferred_element_type=jnp.float32,
    )
    out = out / totals
    part_len = out.shape[1]
    pad = -part_len % 128
    out = jnp.concatenate([out, jnp.zeros((out.shape[0], pad), jnp.float32)], axis=1)
    o_ref[0, :part_len, :] = out.T[:part_len].astype(jnp.bfloat16)
    sent = peak.astype(jnp.bfloat16).astype(jnp.float32)
    totals = totals * jnp.exp2((peak - sent) * scale2)
    high = totals.astype(jnp.bfloat16).astype(jnp.float32)
    kinds = [
        [values[:, at : at + unit] for at in range(0, part_len, unit)]
        for values in (sent, high, totals - high)
    ]
    o_ref[0, part_len:, :] = stat_block(kinds, o_ref.shape[1] - part_len)


def fresh_attention(q_chip, k_window, v_window, token_rows, key_cols, unit, scale2):
    heads, part_len, head_dim = q_chip.shape
    _, _, pad_to = stat_rows_of(part_len, unit)
    own = lambda x: pl.BlockSpec((1,) + x.shape[1:], lambda h: (h, 0, 0))
    fixed = lambda x: pl.BlockSpec(x.shape, lambda h: (0, 0))
    return pl.pallas_call(
        lambda *refs: fresh_kernel(unit, scale2, *refs),
        grid=(heads,),
        in_specs=[own(q_chip), own(k_window), own(v_window), fixed(token_rows), fixed(key_cols)],
        out_specs=pl.BlockSpec((1, part_len + pad_to, head_dim), lambda h: (h, 0, 0)),
        out_shape=jax.ShapeDtypeStruct((heads, part_len + pad_to, head_dim), jnp.bfloat16),
        compiler_params=pltpu.CompilerParams(vmem_limit_bytes=40 * 2**20),
        name="fresh_attention",
    )(q_chip, k_window, v_window, token_rows, key_cols)


def project_kernel(groups, at_ref, *refs):
    att_refs, w_refs = refs[: 2 * groups], refs[2 * groups : -3]
    bias_ref, out_ref, rows_ref = refs[-3:]
    core = at_ref[0]
    wide = rows_ref.shape[2]

    @pl.when(pl.program_id(0) == 0)
    def _():
        for index, ref in enumerate(att_refs):
            rows_ref[index] = jnp.concatenate([ref[h] for h in range(ref.shape[0])], axis=1)

    total = bias_ref[...].reshape(1, -1)
    for s in range(groups):
        for d in range(2):
            feats = pl.ds(pl.multiple_of((core ^ d) * wide, wide), wide)
            total = total + jnp.dot(
                rows_ref[2 * s + d], w_refs[s][0, feats, :], preferred_element_type=jnp.float32
            )
    out_ref[...] = total.astype(jnp.bfloat16).reshape(out_ref.shape)


def project(pieces, weights, bias, core, group_at):
    groups = len(pieces) // 2
    half, tok_dev, head_dim = pieces[0].shape
    blocks, feats, cols = weights.shape
    blocks //= groups
    wide = cols % 128 == 0

    def weight_spec(s):
        return pl.BlockSpec(
            (1, feats, cols),
            lambda j, at: (lax.rem(at[1] + groups - s, groups) * blocks + j, 0, 0),
        )

    if wide:
        out_spec = pl.BlockSpec((tok_dev, cols), lambda j, at: (0, j))
        out_shape = (tok_dev, blocks * cols)
    else:
        out_spec = pl.BlockSpec((1, tok_dev, cols), lambda j, at: (j, 0, 0))
        out_shape = (blocks, tok_dev, cols)
    out = pl.pallas_call(
        lambda *refs: project_kernel(groups, *refs),
        grid_spec=pltpu.PrefetchScalarGridSpec(
            num_scalar_prefetch=1,
            grid=(blocks,),
            in_specs=[pl.BlockSpec(x.shape, lambda j, at: (0, 0, 0)) for x in pieces]
            + [weight_spec(s) for s in range(groups)]
            + [pl.BlockSpec((1, 1, cols), lambda j, at: (j, 0, 0))],
            out_specs=out_spec,
            scratch_shapes=[pltpu.VMEM((2 * groups, tok_dev, half * head_dim), jnp.bfloat16)],
        ),
        out_shape=jax.ShapeDtypeStruct(out_shape, jnp.bfloat16),
        compiler_params=pltpu.CompilerParams(vmem_limit_bytes=40 * 2**20),
        name="project",
    )(
        jnp.stack([core, group_at]),
        *pieces,
        *[weights] * groups,
        bias.reshape(blocks, 1, cols),
    )
    return out if wide else jnp.transpose(out, (1, 0, 2)).reshape(tok_dev, blocks * cols)


def per_device(
    queries,
    keys,
    values,
    key_cache,
    value_cache,
    cache_len,
    page_table,
    append_slots,
    out_weight,
    out_bias,
):
    tok_dev, head_count, head_dim = queries.shape
    requests = cache_len.shape[0]
    max_pages = page_table.shape[1]
    new_pages = append_slots.shape[1]
    span_len = new_pages * PAGE
    slot_count = key_cache.shape[0]
    tokens = requests * span_len
    page_devs = tokens // tok_dev
    scale2 = math.log2(math.e) / math.sqrt(head_dim)
    device_at = lax.axis_index("pages")
    token_ids = device_at * tok_dev + jnp.arange(tok_dev, dtype=jnp.int32)
    request_ids = token_ids // span_len
    request_grid = jnp.arange(requests, dtype=jnp.int32)
    starts = jnp.sum(
        jnp.where(request_ids[:, None] == request_grid[None, :], cache_len[None, :], 0), axis=1
    )
    positions = (starts + token_ids % span_len).astype(jnp.float32)
    rotated_q = rotate(queries.astype(jnp.float32), positions).astype(jnp.bfloat16)
    rotated_k = rotate(keys.astype(jnp.float32), positions).astype(jnp.bfloat16)
    core = device_at % 2
    half = head_count // 2
    chip_len = 2 * tok_dev

    def halves(x):
        return (
            lax.dynamic_slice_in_dim(x, core * half, half, 0),
            lax.dynamic_slice_in_dim(x, (1 - core) * half, half, 0),
        )

    def in_order(mine, got, axis):
        return jnp.where(
            core == 0,
            jnp.concatenate([mine, got], axis=axis),
            jnp.concatenate([got, mine], axis=axis),
        )

    q_own = jnp.transpose(rotated_q, (1, 0, 2))
    q_mine, q_other = halves(q_own)
    q_chip = in_order(q_mine, swap(q_other, 1), 1)
    q_places = gather_lines(q_chip)
    groups = lax.axis_size("heads")
    group_at = lax.axis_index("heads")
    share = page_devs // groups
    moves = [
        (i * page_devs + h * share + j, h * page_devs + i * share + j)
        for i in range(groups)
        for h in range(groups)
        for j in range(share)
    ]
    weight_block = lax.ppermute(out_weight, ("heads", "pages"), moves)
    natural = Layout((0, 1, 2))
    all_k = lax.all_gather(rotated_k, "pages", axis=0, tiled=True)
    all_v = lax.all_gather(values, "pages", axis=0, tiled=True)
    all_k = with_layout_constraint(all_k, natural)
    all_v = with_layout_constraint(all_v, natural)
    weights = lax.all_gather(weight_block, "pages", axis=0, tiled=False)

    my_slots = device_at * slot_count + jnp.arange(slot_count, dtype=jnp.int32)
    chip_slots = jnp.concatenate(
        [my_slots, (device_at ^ 1) * slot_count + jnp.arange(slot_count, dtype=jnp.int32)]
    )
    cached_hit = page_table.reshape(-1)[None, :] == chip_slots[:, None]
    fresh_hit = append_slots.reshape(-1)[None, :] == my_slots[:, None]
    table_at = jnp.arange(requests * max_pages, dtype=jnp.int32)
    shown = (table_at % max_pages) * PAGE < jnp.repeat(cache_len, max_pages)
    is_fresh = jnp.any(fresh_hit, axis=1)
    fresh_index = jnp.sum(
        jnp.where(fresh_hit, jnp.arange(requests * new_pages, dtype=jnp.int32)[None, :], 0), axis=1
    )
    slot_key = requests - jnp.sum(
        jnp.where(cached_hit & shown[None, :], requests - (table_at // max_pages)[None, :], 0),
        axis=1,
    )
    slot_at = jnp.arange(2 * slot_count, dtype=jnp.int32)
    earlier = (slot_key[None, :] < slot_key[:, None]) | (
        (slot_key[None, :] == slot_key[:, None]) & (slot_at[None, :] < slot_at[:, None])
    )
    rank = jnp.sum(earlier.astype(jnp.int32), axis=1)
    order = jnp.sum(jnp.where(rank[None, :] == slot_at[:, None], slot_at[None, :], 0), axis=1)
    slot_starts = jnp.sum((slot_key[None, :] < request_grid[:, None]).astype(jnp.int32), axis=1)
    slot_counts = jnp.sum((slot_key[None, :] == request_grid[:, None]).astype(jnp.int32), axis=1)

    k_mine, k_other = halves(jnp.transpose(key_cache, (2, 0, 1, 3)))
    v_mine, v_other = halves(jnp.transpose(value_cache, (2, 0, 3, 1)))
    k_heads = jnp.concatenate([k_mine, swap(k_other, 1)], axis=1)
    v_heads = jnp.concatenate([v_mine, swap(v_other, 1)], axis=1)

    unit = math.gcd(span_len, tok_dev)
    line = page_devs // 4
    line_at, across = device_at // 4, (device_at // 2) % 2
    outs = cached_attention(
        [q for q, _, _, _ in q_places],
        [jnp.clip(at, 0, line - 1) * 2 + side for _, at, side, _ in q_places],
        [ok for _, _, _, ok in q_places],
        [((line_at + k) % line) * 2 + (across ^ d) for k in range(line) for d in range(2)],
        k_heads,
        v_heads,
        order,
        slot_starts,
        slot_counts,
        span_len,
        unit,
        scale2,
    )
    merged = lambda parts, ok: merge(parts, ok, chip_len, unit, scale2)

    def fresh_part():
        chip_at = device_at // 2
        back = -(-(span_len - math.gcd(span_len, chip_len)) // chip_len)
        window = (back + 1) * chip_len
        window_at = jnp.maximum(chip_at - back, 0) * chip_len

        def by_head(rows):
            rows = lax.dynamic_slice(
                rows, (window_at, core * half, 0), (window, half, head_dim)
            )
            return jnp.transpose(rows, (1, 0, 2))

        chip_tokens = chip_at * chip_len + jnp.arange(chip_len, dtype=jnp.int32)
        token_rows = jnp.stack([chip_tokens, chip_tokens // span_len * span_len])
        key_cols = (window_at + jnp.arange(window, dtype=jnp.int32))[:, None]
        return fresh_attention(
            q_chip, by_head(all_k), by_head(all_v), token_rows, key_cols, unit, scale2
        )

    chip_part = merge_lines(
        [outs[2 * k : 2 * k + 2] for k in range(line)], merged, fresh_part
    )
    rows_of = lambda c: lax.dynamic_slice_in_dim(chip_part[:, :chip_len], c * tok_dev, tok_dev, 1)
    own_rows, other_rows = rows_of(core), rows_of(1 - core)
    pieces = []
    for s in range(groups):
        for d, rows in ((0, own_rows), (1, other_rows)):
            if s or d:
                rows = lax.ppermute(
                    rows,
                    ("heads", "pages"),
                    [
                        (h * page_devs + p, (h + s) % groups * page_devs + (p ^ d))
                        for h in range(groups)
                        for p in range(page_devs)
                    ],
                )
            pieces.append(rows)
    hidden = project(pieces, weights, out_bias, core, group_at)
    page_shape = (requests * new_pages, PAGE, head_count, head_dim)
    key_out, value_out = write_pages(
        key_cache,
        value_cache,
        all_k.reshape(page_shape),
        all_v.reshape(page_shape),
        is_fresh,
        fresh_index,
    )
    return (hidden, key_out, value_out)


def solution(mesh):
    placed = (
        P("pages", "heads", None),
        P("pages", "heads", None),
        P("pages", "heads", None),
        P("pages", None, "heads", None),
        P("pages", None, "heads", None),
        P(),
        P(),
        P(),
        P("heads", "pages"),
        P("heads"),
    )
    return jax.shard_map(
        per_device,
        mesh=mesh,
        in_specs=placed,
        out_specs=(
            P("pages", "heads"),
            P("pages", None, "heads", None),
            P("pages", None, "heads", None),
        ),
        check_vma=False,
    )
```

profile of v0, /device:TPU:12, one launch (start us, length us, event | category | flops | bytes accessed | tf_op | source)
XLA Modules:
  0.0 403.3 jit_solution(11271593332753455875)
XLA Ops:
  24.4 47.2 %collective-permute-start.2 = (bf16[4,576,128]{2,1,0:T(8,128)(2,1)}, bf16[4,576,128]{2,1,0:T(8,128)(2,1)}, u32[]{:S(2)}, u32[]{:S(2)}) collective-permute-start(bf16[4,576,128]{2,1,0:T(8,128)(2,1)} %maximum_select_fusion.refs_5_.refs_0_), channel_id=1, source_target_pairs={{0,4},{1,5},{2,6},{3,7},{4,8},{5,9},{6,10},{7,11},{8,12},{9,13},{1... | collective-permute-start | bytes 1769480 | tf_op jit(solution)/shard_map/ppermute | solution.py:279
  73.6 7.3 %constant_dynamic-slice_fusion.5 = (bf16[12,128,4,128]{3,2,1,0:T(4,128)(2,1)}, bf16[12,128,4,128]{3,2,1,0:T(4,128)(2,1)}, bf16[12,128,4,128]{3,2,1,0:T(4,128)(2,1)S(1)}, bf16[12,128,4,128]{3,2,1,0:T(4,128)(2,1)}) fusion(bf16[12,128,8,128]{3,2,1,0:T(8,128)(2,1)S(1)} %copy-done.1, s32[]{:T(128)S(6)} %select_n.160, s32[]{:T(128)S(6)} %select_n.161, ...), kind=kLoop, calls=%fused_computation.46 | loop fusion | bytes 12582920 | tf_op jit(solution)/shard_map/dynamic-slice.4
  87.2 28.1 %collective-permute-done.2.refs_7_ = bf16[4,576,128]{2,1,0:T(8,128)(2,1)} collective-permute-done((bf16[4,576,128]{2,1,0:T(8,128)(2,1)}, bf16[4,576,128]{2,1,0:T(8,128)(2,1)}, u32[]{:S(2)}, u32[]{:S(2)}) %collective-permute-start.2) | collective-permute-done | bytes 589856 | tf_op jit(solution)/shard_map/ppermute | solution.py:279
  115.3 5.2 %collective-permute-start.6 = (bf16[4,576,128]{2,1,0:T(8,128)(2,1)}, bf16[4,576,128]{2,1,0:T(8,128)(2,1)}, u32[]{:S(2)}, u32[]{:S(2)}) collective-permute-start(bf16[4,576,128]{2,1,0:T(8,128)(2,1)} %collective-permute-done.2.refs_7_), channel_id=1, source_target_pairs={{4,8},{5,9},{6,10},{7,11},{8,12},{9,13},{10,14},{11,15},{20,24},{2... | collective-permute-start | bytes 1769480 | tf_op jit(solution)/shard_map/ppermute | solution.py:279
  125.1 8.5 %collective-permute-done.6.refs_11_ = bf16[4,576,128]{2,1,0:T(8,128)(2,1)} collective-permute-done((bf16[4,576,128]{2,1,0:T(8,128)(2,1)}, bf16[4,576,128]{2,1,0:T(8,128)(2,1)}, u32[]{:S(2)}, u32[]{:S(2)}) %collective-permute-start.6) | collective-permute-done | bytes 589856 | tf_op jit(solution)/shard_map/ppermute | solution.py:279
  154.9 14.5 %collective-permute-done.12.refs_17_ = bf16[4,576,128]{2,1,0:T(8,128)(2,1)} collective-permute-done((bf16[4,576,128]{2,1,0:T(8,128)(2,1)}, bf16[4,576,128]{2,1,0:T(8,128)(2,1)}, u32[]{:S(2)}, u32[]{:S(2)}) %collective-permute-start.12) | collective-permute-done | bytes 589856 | tf_op jit(solution)/shard_map/ppermute | solution.py:279
  177.7 22.6 %cached_attention.1 = (bf16[4,608,128]{2,1,0:T(8,128)(2,1)S(1)}, bf16[4,608,128]{2,1,0:T(8,128)(2,1)S(1)}, bf16[4,608,128]{2,1,0:T(8,128)(2,1)S(1)}, bf16[4,608,...) custom-call(s32[22]{0:T(128)S(1)} %stack.197.refs_0_, ...), custom_call_target="tpu_custom_call" | custom-call | flops 40000000000 | bytes 20971520 | tf_op jit(solution)/shard_map/cached_attention/pallas_call | solution.py:155
  204.5 12.4 %collective-permute-start.17 = (bf16[4,608,128]{2,1,0:T(8,128)(2,1)S(1)}, bf16[4,608,128]{2,1,0:T(8,128)(2,1)S(1)}, u32[]{:S(2)}, u32[]{:S(2)}) collective-permute-start(bf16[4,608,128]{2,1,0:T(8,128)(2,1)S(1)} %get-tuple-element.16), channel_id=1, source_target_pairs={{0,2},{1,3},{2,0},{3,1},{4,6},{5,7},{6,4},{7,5},{8,10},{9,11},{10,... | collective-permute-start | bytes 1867784 | tf_op jit(solution)/shard_map/ppermute | solution.py:273
  218.9 12.9 %collective-permute-done.17.refs_2_ = bf16[4,608,128]{2,1,0:T(8,128)(2,1)S(1)} collective-permute-done((bf16[4,608,128]{2,1,0:T(8,128)(2,1)S(1)}, bf16[4,608,128]{2,1,0:T(8,128)(2,1)S(1)}, u32[]{:S(2)}, u32[]{:S(2)}) %collective-permute-start.17) | collective-permute-done | bytes 622624 | tf_op jit(solution)/shard_map/ppermute | solution.py:273
  238.7 10.1 %collective-permute-done.19.refs_2_ = bf16[4,608,128]{2,1,0:T(8,128)(2,1)} collective-permute-done((bf16[4,608,128]{2,1,0:T(8,128)(2,1)}, bf16[4,608,128]{2,1,0:T(8,128)(2,1)}, u32[]{:S(2)}, u32[]{:S(2)}) %collective-permute-start.19) | collective-permute-done | bytes 622624 | tf_op jit(solution)/shard_map/ppermute | solution.py:273
  248.8 4.6 %merge.12.refs_1_ = bf16[4,608,128]{2,1,0:T(8,128)(2,1)} custom-call(s32[2]{0:T(128)} %copy-done.18, bf16[4,608,128]{2,1,0:T(8,128)(2,1)} %copy-done.8, bf16[4,608,128]{2,1,0:T(8,128)(2,1)} %collective-permute-done.19.refs_2_), custom_call_target="tpu_custom_call" | custom-call | tf_op jit(solution)/shard_map/merge/pallas_call | solution.py:226
  258.8 4.6 %merge.11.refs_1_ = bf16[4,608,128]{2,1,0:T(8,128)(2,1)} custom-call(s32[2]{0:T(128)} %copy-done.18, bf16[4,608,128]{2,1,0:T(8,128)(2,1)} %copy-done.7, bf16[4,608,128]{2,1,0:T(8,128)(2,1)} %collective-permute-done.18.refs_2_), custom_call_target="tpu_custom_call" | custom-call | tf_op jit(solution)/shard_map/merge/pallas_call | solution.py:226
  263.4 4.6 %merge.15 = bf16[4,608,128]{2,1,0:T(8,128)(2,1)} custom-call(s32[2]{0:T(128)} %fusion.13.refs_0_, bf16[4,608,128]{2,1,0:T(8,128)(2,1)} %merge.11.refs_1_, bf16[4,608,128]{2,1,0:T(8,128)(2,1)} %collective-permute-done.23.refs_2_), custom_call_target="tpu_custom_call" | custom-call | tf_op jit(solution)/shard_map/merge/pallas_call | solution.py:226
  269.4 40.2 %collective-permute-done.20.refs_2_ = bf16[4,608,128]{2,1,0:T(8,128)(2,1)} collective-permute-done((bf16[4,608,128]{2,1,0:T(8,128)(2,1)}, bf16[4,608,128]{2,1,0:T(8,128)(2,1)}, u32[]{:S(2)}, u32[]{:S(2)}) %collective-permute-start.20) | collective-permute-done | bytes 622624 | tf_op jit(solution)/shard_map/ppermute | solution.py:279
  309.6 4.6 %merge.13 = bf16[4,608,128]{2,1,0:T(8,128)(2,1)} custom-call(s32[2]{0:T(128)} %fusion.12.refs_0_, bf16[4,608,128]{2,1,0:T(8,128)(2,1)} %merge.11.refs_1_, bf16[4,608,128]{2,1,0:T(8,128)(2,1)} %collective-permute-done.20.refs_2_), custom_call_target="tpu_custom_call" | custom-call | tf_op jit(solution)/shard_map/merge/pallas_call | solution.py:226
  317.5 4.6 %merge.16 = bf16[4,608,128]{2,1,0:T(8,128)(2,1)} custom-call(s32[2]{0:T(128)} %fusion.11.refs_0_, bf16[4,608,128]{2,1,0:T(8,128)(2,1)} %merge.12.refs_1_, bf16[4,608,128]{2,1,0:T(8,128)(2,1)} %collective-permute-done.24.refs_2_), custom_call_target="tpu_custom_call" | custom-call | tf_op jit(solution)/shard_map/merge/pallas_call | solution.py:226
  322.1 4.8 %collective-permute-start.25 = (bf16[4,608,128]{2,1,0:T(8,128)(2,1)}, bf16[4,608,128]{2,1,0:T(8,128)(2,1)}, u32[]{:S(2)}, u32[]{:S(2)}) collective-permute-start(bf16[4,608,128]{2,1,0:T(8,128)(2,1)} %merge.16), channel_id=1, source_target_pairs={{4,0},{5,1},{6,2},{7,3},{8,4},{9,5},{10,6},{11,7},{12,8},{13,9},{1... | collective-permute-start | bytes 1867784 | tf_op jit(solution)/shard_map/ppermute | solution.py:279
  327.0 6.3 %collective-permute-done.21.refs_2_ = bf16[4,608,128]{2,1,0:T(8,128)(2,1)} collective-permute-done((bf16[4,608,128]{2,1,0:T(8,128)(2,1)}, bf16[4,608,128]{2,1,0:T(8,128)(2,1)}, u32[]{:S(2)}, u32[]{:S(2)}) %collective-permute-start.21) | collective-permute-done | bytes 622624 | tf_op jit(solution)/shard_map/ppermute | solution.py:279
  333.3 4.6 %merge.14 = bf16[4,608,128]{2,1,0:T(8,128)(2,1)} custom-call(s32[2]{0:T(128)} %fusion.11.refs_0_, bf16[4,608,128]{2,1,0:T(8,128)(2,1)} %merge.10.refs_1_, bf16[4,608,128]{2,1,0:T(8,128)(2,1)} %collective-permute-done.21.refs_2_), custom_call_target="tpu_custom_call" | custom-call | tf_op jit(solution)/shard_map/merge/pallas_call | solution.py:226
  341.3 4.6 %merge.9.refs_1_ = bf16[4,608,128]{2,1,0:T(8,128)(2,1)} custom-call(s32[2]{0:T(128)} %copy-done.18, bf16[4,608,128]{2,1,0:T(8,128)(2,1)} %copy-done.6, bf16[4,608,128]{2,1,0:T(8,128)(2,1)} %collective-permute-done.16.refs_2_), custom_call_target="tpu_custom_call" | custom-call | tf_op jit(solution)/shard_map/merge/pallas_call | solution.py:226
  352.4 9.4 %fresh_attention.1.refs_4_ = bf16[4,608,128]{2,1,0:T(8,128)(2,1)S(1)} custom-call(bf16[4,576,128]{2,1,0:T(8,128)(2,1)} %maximum_select_fusion.refs_5_.refs_0_, bf16[4,1152,128]{2,1,0:T(8,128)(2,1)S(1)} %bitcast.58, bf16[4,1152,128]{2,1,0:T(8,128)(2,1)S(1)} %bitcast.59, s32[2,576]{1,0:T(2,128)S(1)} %pad_add_fusion.refs_3_, s32[1152,1]{1,0:T(8,128)S(1)} %copy-done.5), custom_call_target="tpu_custom_call" | custom-call | tf_op jit(solution)/shard_map/fresh_attention/pallas_call | solution.py:366
  362.7 5.3 %merge.17 = bf16[4,608,128]{2,1,0:T(8,128)(2,1)} custom-call(s32[4]{0:T(128)} %pad_add_fusion.5.refs_0_, bf16[4,608,128]{2,1,0:T(8,128)(2,1)} %merge.9.refs_1_, bf16[4,608,128]{2,1,0:T(8,128)(2,1)} %collective-permute-done.22.refs_2_, bf16[4,608,128]{2,1,0:T(8,128)(2,1)} %collective-permute-done.25.refs_3_, bf16[4,608,128]{2,1,0:T(8,128)(2,1)} %copy-done.4), custom_call_target="tpu_custom_call" | custom-call | tf_op jit(solution)/shard_map/merge/pallas_call | solution.py:226
  374.7 7.8 %write_pages.1 = (bf16[12,128,8,128]{3,2,1,0:T(8,128)(2,1)}, bf16[12,128,8,128]{3,2,1,0:T(8,128)(2,1)}) custom-call(s32[12]{0:T(128)S(1)} %convert_element_type.45.fresh_ref, s32[12]{0:T(128)S(1)} %fusion.2.index_ref, bf16[12,128,8,128]{3,2,1,0:T(8,128)(2,1)S(1)} %copy-done.2, bf16[12,128,8,128]{3,2,1,0:T(8,128)(2,1)S(1)} %copy-done.1, ...), custom_call_target="tpu_custom_call" | custom-call | tf_op jit(solution)/shard_map/write_pages/pallas_call | solution.py:257
  390.0 6.8 %project.1 = bf16[288,2048]{1,0:T(8,128)(2,1)} custom-call(s32[2]{0:T(128)S(1)} %pad_add_fusion.4.refs_0_, bf16[4,288,128]{2,1,0:T(8,128)(2,1)S(1)} %get-tuple-element.34.refs_1_, bf16[4,288,128]{2,1,0:T(8,128)(2,1)} %collective-permute-done.26.refs_2_, bf16[4,288,128]{2,1,0:T(8,128)(2,1)} %collective-permute-done.27.refs_3_, ...), custom_call_target="tpu_custom_call" | custom-call | tf_op jit(solution)/shard_map/project/pallas_call | solution.py:417
  (164 shorter events, 107.3 us)
Async XLA Ops:
  7.2 338.8 %all-gather.5.cloned.1.call-start = ((), (), s32[]{:S(2)}) async-start(), calls=%async_computation | async-start | bytes 10027008 | tf_op jit(solution)/shard_map/all_gather | solution.py:503
  13.8 335.3 %all-gather.7.cloned.1.call-start = ((), (), s32[]{:S(2)}) async-start(), calls=%async_computation.1 | async-start | bytes 10027008 | tf_op jit(solution)/shard_map/all_gather | solution.py:504
  14.5 367.9 %all-gather.9.cloned.1.call-start = ((), (), s32[]{:S(2)}) async-start(), calls=%async_computation.2 | async-start | bytes 8912896 | tf_op jit(solution)/shard_map/all_gather | solution.py:507
  24.4 90.9 %collective-permute-start.2 = (bf16[4,576,128]{2,1,0:T(8,128)(2,1)}, bf16[4,576,128]{2,1,0:T(8,128)(2,1)}, u32[]{:S(2)}, u32[]{:S(2)}) collective-permute-start(bf16[4,576,128]{2,1,0:T(8,128)(2,1)} %maximum_select_fusion.refs_5_.refs_0_), channel_id=1, source_target_pairs={{0,4},{1,5},{2,6},{3,7},{4,8},{5,9},{6,10},{7,11},{8,12},{9,13},{1... | collective-permute-start | bytes 1769480 | tf_op jit(solution)/shard_map/ppermute | solution.py:279
  71.6 48.9 %collective-permute-start.4 = (bf16[4,576,128]{2,1,0:T(8,128)(2,1)}, bf16[4,576,128]{2,1,0:T(8,128)(2,1)}, u32[]{:S(2)}, u32[]{:S(2)}) collective-permute-start(bf16[4,576,128]{2,1,0:T(8,128)(2,1)} %maximum_select_fusion.refs_5_.refs_0_), channel_id=1, source_target_pairs={{4,0},{5,1},{6,2},{7,3},{8,4},{9,5},{10,6},{11,7},{12,8},{13,9},{1... | collective-permute-start | bytes 1769480 | tf_op jit(solution)/shard_map/ppermute | solution.py:279
  82.4 67.6 %collective-permute-start.14 = (bf16[4,12,128,128]{3,2,1,0:T(8,128)(2,1)}, bf16[4,12,128,128]{3,2,1,0:T(8,128)(2,1)}, u32[]{:S(2)}, u32[]{:S(2)}) collective-permute-start(bf16[4,12,128,128]{3,2,1,0:T(8,128)(2,1)} %bitcast.52), channel_id=1, source_target_pairs={{0,1},{1,0},{2,3},{3,2},{4,5},{5,4},{6,7},{7,6},{8,9},{9,8},{10,11... | collective-permute-start | bytes 4718600 | tf_op jit(solution)/shard_map/ppermute | solution.py:273
  86.2 64.5 %collective-permute-start.15 = (bf16[4,12,128,128]{3,2,1,0:T(8,128)(2,1)}, bf16[4,12,128,128]{3,2,1,0:T(8,128)(2,1)}, u32[]{:S(2)}, u32[]{:S(2)}) collective-permute-start(bf16[4,12,128,128]{3,2,1,0:T(8,128)(2,1)} %bitcast.65), channel_id=1, source_target_pairs={{0,1},{1,0},{2,3},{3,2},{4,5},{5,4},{6,7},{7,6},{8,9},{9,8},{10,11... | collective-permute-start | bytes 4718600 | tf_op jit(solution)/shard_map/ppermute | solution.py:273
  86.7 35.9 %collective-permute-start.1 = (bf16[4,576,128]{2,1,0:T(8,128)(2,1)}, bf16[4,576,128]{2,1,0:T(8,128)(2,1)}, u32[]{:S(2)}, u32[]{:S(2)}) collective-permute-start(bf16[4,576,128]{2,1,0:T(8,128)(2,1)} %maximum_select_fusion.refs_5_.refs_0_), channel_id=1, source_target_pairs={{0,2},{1,3},{2,0},{3,1},{4,6},{5,7},{6,4},{7,5},{8,10},{9,11},{10,... | collective-permute-start | bytes 1769480 | tf_op jit(solution)/shard_map/ppermute | solution.py:273
  122.7 24.9 %collective-permute-start.3 = (bf16[4,576,128]{2,1,0:T(8,128)(2,1)}, bf16[4,576,128]{2,1,0:T(8,128)(2,1)}, u32[]{:S(2)}, u32[]{:S(2)}) collective-permute-start(bf16[4,576,128]{2,1,0:T(8,128)(2,1)} %collective-permute-done.2.refs_7_), channel_id=1, source_target_pairs={{4,6},{5,7},{6,4},{7,5},{8,10},{9,11},{10,8},{11,9},{12,14},{13,15... | collective-permute-start | bytes 1769480 | tf_op jit(solution)/shard_map/ppermute | solution.py:299
  133.6 20.6 %collective-permute-start.10 = (bf16[4,576,128]{2,1,0:T(8,128)(2,1)}, bf16[4,576,128]{2,1,0:T(8,128)(2,1)}, u32[]{:S(2)}, u32[]{:S(2)}) collective-permute-start(bf16[4,576,128]{2,1,0:T(8,128)(2,1)} %collective-permute-done.6.refs_11_), channel_id=1, source_target_pairs={{8,12},{9,13},{10,14},{11,15},{24,28},{25,29},{26,30},{27,31}} | collective-permute-start | bytes 1769480 | tf_op jit(solution)/shard_map/ppermute | solution.py:279
  136.9 32.5 %collective-permute-start.12 = (bf16[4,576,128]{2,1,0:T(8,128)(2,1)}, bf16[4,576,128]{2,1,0:T(8,128)(2,1)}, u32[]{:S(2)}, u32[]{:S(2)}) collective-permute-start(bf16[4,576,128]{2,1,0:T(8,128)(2,1)} %collective-permute-done.8.refs_13_), channel_id=1, source_target_pairs={{4,0},{5,1},{6,2},{7,3},{20,16},{21,17},{22,18},{23,19}} | collective-permute-start | bytes 1769480 | tf_op jit(solution)/shard_map/ppermute | solution.py:279
  147.5 30.1 %collective-permute-start.5 = (bf16[4,576,128]{2,1,0:T(8,128)(2,1)}, bf16[4,576,128]{2,1,0:T(8,128)(2,1)S(1)}, u32[]{:S(2)}, u32[]{:S(2)}) collective-permute-start(bf16[4,576,128]{2,1,0:T(8,128)(2,1)} %collective-permute-done.4.refs_9_), channel_id=1, source_target_pairs={{0,2},{1,3},{2,0},{3,1},{4,6},{5,7},{6,4},{7,5},{8,10},{9,11},{10,... | collective-permute-start | bytes 1769480 | tf_op jit(solution)/shard_map/ppermute | solution.py:301
  150.0 27.7 %collective-permute-start.7 = (bf16[4,576,128]{2,1,0:T(8,128)(2,1)}, bf16[4,576,128]{2,1,0:T(8,128)(2,1)S(1)}, u32[]{:S(2)}, u32[]{:S(2)}) collective-permute-start(bf16[4,576,128]{2,1,0:T(8,128)(2,1)} %collective-permute-done.6.refs_11_), channel_id=1, source_target_pairs={{8,10},{9,11},{10,8},{11,9},{12,14},{13,15},{14,12},{15,13},{24,26... | collective-permute-start | bytes 1769480 | tf_op jit(solution)/shard_map/ppermute | solution.py:299
  150.7 26.9 %collective-permute-start.9 = (bf16[4,576,128]{2,1,0:T(8,128)(2,1)}, bf16[4,576,128]{2,1,0:T(8,128)(2,1)S(1)}, u32[]{:S(2)}, u32[]{:S(2)}) collective-permute-start(bf16[4,576,128]{2,1,0:T(8,128)(2,1)} %collective-permute-done.8.refs_13_), channel_id=1, source_target_pairs={{0,2},{1,3},{2,0},{3,1},{4,6},{5,7},{6,4},{7,5},{16,18},{17,19},{1... | collective-permute-start | bytes 1769480 | tf_op jit(solution)/shard_map/ppermute | solution.py:301
  154.1 23.5 %collective-permute-start.11 = (bf16[4,576,128]{2,1,0:T(8,128)(2,1)}, bf16[4,576,128]{2,1,0:T(8,128)(2,1)S(1)}, u32[]{:S(2)}, u32[]{:S(2)}) collective-permute-start(bf16[4,576,128]{2,1,0:T(8,128)(2,1)} %collective-permute-done.10.refs_15_), channel_id=1, source_target_pairs={{12,14},{13,15},{14,12},{15,13},{28,30},{29,31},{30,28},{31,29}} | collective-permute-start | bytes 1769480 | tf_op jit(solution)/shard_map/ppermute | solution.py:299
  204.5 27.4 %collective-permute-start.17 = (bf16[4,608,128]{2,1,0:T(8,128)(2,1)S(1)}, bf16[4,608,128]{2,1,0:T(8,128)(2,1)S(1)}, u32[]{:S(2)}, u32[]{:S(2)}) collective-permute-start(bf16[4,608,128]{2,1,0:T(8,128)(2,1)S(1)} %get-tuple-element.16), channel_id=1, source_target_pairs={{0,2},{1,3},{2,0},{3,1},{4,6},{5,7},{6,4},{7,5},{8,10},{9,11},{10,... | collective-permute-start | bytes 1867784 | tf_op jit(solution)/shard_map/ppermute | solution.py:273
  216.9 32.0 %collective-permute-start.19 = (bf16[4,608,128]{2,1,0:T(8,128)(2,1)}, bf16[4,608,128]{2,1,0:T(8,128)(2,1)}, u32[]{:S(2)}, u32[]{:S(2)}) collective-permute-start(bf16[4,608,128]{2,1,0:T(8,128)(2,1)} %get-tuple-element.20), channel_id=1, source_target_pairs={{0,2},{1,3},{2,0},{3,1},{4,6},{5,7},{6,4},{7,5},{8,10},{9,11},{10,... | collective-permute-start | bytes 1867784 | tf_op jit(solution)/shard_map/ppermute | solution.py:273
  216.9 41.9 %collective-permute-start.18 = (bf16[4,608,128]{2,1,0:T(8,128)(2,1)}, bf16[4,608,128]{2,1,0:T(8,128)(2,1)}, u32[]{:S(2)}, u32[]{:S(2)}) collective-permute-start(bf16[4,608,128]{2,1,0:T(8,128)(2,1)} %get-tuple-element.18), channel_id=1, source_target_pairs={{0,2},{1,3},{2,0},{3,1},{4,6},{5,7},{6,4},{7,5},{8,10},{9,11},{10,... | collective-permute-start | bytes 1867784 | tf_op jit(solution)/shard_map/ppermute | solution.py:273
  237.2 26.1 %collective-permute-start.23 = (bf16[4,608,128]{2,1,0:T(8,128)(2,1)}, bf16[4,608,128]{2,1,0:T(8,128)(2,1)}, u32[]{:S(2)}, u32[]{:S(2)}) collective-permute-start(bf16[4,608,128]{2,1,0:T(8,128)(2,1)} %merge.10.refs_1_), channel_id=1, source_target_pairs={{12,8},{13,9},{14,10},{15,11},{28,24},{29,25},{30,26},{31,27}} | collective-permute-start | bytes 1867784 | tf_op jit(solution)/shard_map/ppermute | solution.py:279
  253.4 56.1 %collective-permute-start.20 = (bf16[4,608,128]{2,1,0:T(8,128)(2,1)}, bf16[4,608,128]{2,1,0:T(8,128)(2,1)}, u32[]{:S(2)}, u32[]{:S(2)}) collective-permute-start(bf16[4,608,128]{2,1,0:T(8,128)(2,1)} %merge.12.refs_1_), channel_id=1, source_target_pairs={{0,4},{1,5},{2,6},{3,7},{16,20},{17,21},{18,22},{19,23}} | collective-permute-start | bytes 1867784 | tf_op jit(solution)/shard_map/ppermute | solution.py:279
  268.0 49.6 %collective-permute-start.24 = (bf16[4,608,128]{2,1,0:T(8,128)(2,1)}, bf16[4,608,128]{2,1,0:T(8,128)(2,1)}, u32[]{:S(2)}, u32[]{:S(2)}) collective-permute-start(bf16[4,608,128]{2,1,0:T(8,128)(2,1)} %merge.15), channel_id=1, source_target_pairs={{8,4},{9,5},{10,6},{11,7},{12,8},{13,9},{14,10},{15,11},{24,20},{2... | collective-permute-start | bytes 1867784 | tf_op jit(solution)/shard_map/ppermute | solution.py:279
  316.1 25.2 %collective-permute-start.16 = (bf16[4,608,128]{2,1,0:T(8,128)(2,1)}, bf16[4,608,128]{2,1,0:T(8,128)(2,1)}, u32[]{:S(2)}, u32[]{:S(2)}) collective-permute-start(bf16[4,608,128]{2,1,0:T(8,128)(2,1)} %copy-done.11), channel_id=1, source_target_pairs={{0,2},{1,3},{2,0},{3,1},{4,6},{5,7},{6,4},{7,5},{8,10},{9,11},{10,... | collective-permute-start | bytes 1867784 | tf_op jit(solution)/shard_map/ppermute | solution.py:273
  322.1 40.5 %collective-permute-start.25 = (bf16[4,608,128]{2,1,0:T(8,128)(2,1)}, bf16[4,608,128]{2,1,0:T(8,128)(2,1)}, u32[]{:S(2)}, u32[]{:S(2)}) collective-permute-start(bf16[4,608,128]{2,1,0:T(8,128)(2,1)} %merge.16), channel_id=1, source_target_pairs={{4,0},{5,1},{6,2},{7,3},{8,4},{9,5},{10,6},{11,7},{12,8},{13,9},{1... | collective-permute-start | bytes 1867784 | tf_op jit(solution)/shard_map/ppermute | solution.py:279
  337.9 24.8 %collective-permute-start.22 = (bf16[4,608,128]{2,1,0:T(8,128)(2,1)}, bf16[4,608,128]{2,1,0:T(8,128)(2,1)}, u32[]{:S(2)}, u32[]{:S(2)}) collective-permute-start(bf16[4,608,128]{2,1,0:T(8,128)(2,1)} %merge.14), channel_id=1, source_target_pairs={{0,4},{1,5},{2,6},{3,7},{4,8},{5,9},{6,10},{7,11},{8,12},{9,13},{1... | collective-permute-start | bytes 1867784 | tf_op jit(solution)/shard_map/ppermute | solution.py:279
  (33 other events, 324.3 us)
Sparse Core Ops, SparseCore 0:
  13.9 110.8 all-gather.4
  127.1 103.1 all-gather.6
  232.4 97.8 all-gather.8
where the time goes:
time: 410 us; the launch traced here: 403 us
  waiting for transfers between devices  132 us (32%)
  starting transfers between devices  103 us (25%)
  Pallas kernels  88.7 us (22%)
  local copies, waits for them, and re-layouts  44.3 us (11%)
  other arithmetic  20.4 us (5%)
  between operations  14.3 us (3%)
    ppermute x12, waiting for transfers between devices, shift(): return lax.ppermute(x, 'pages', moves)  99.6 us
    ppermute x12, starting transfers between devices, shift(): return lax.ppermute(x, 'pages', moves)  73.6 us
    pallas_call x9, Pallas kernels, merge(): pl.pallas_call(lambda *refs: merge_kernel(unit, part_len, scale2, *refs),...  42 us
    unnamed x53, local copies, waits for them, and re-layouts  27.8 us
    ppermute x8, waiting for transfers between devices, swap(): return lax.ppermute(x, 'pages', [(p, p ^ bit) for p in range(devs)])  27.8 us
    pallas_call x1, Pallas kernels, cached_attention(): pl.pallas_call(lambda *refs: cached_kernel(unit, stat_unit, span, scale2,...  22.6 us
    ppermute x8, starting transfers between devices, swap(): return lax.ppermute(x, 'pages', [(p, p ^ bit) for p in range(devs)])  16.1 us
    pallas_call x1, Pallas kernels, fresh_attention(): pl.pallas_call(lambda *refs: fresh_kernel(unit, scale2, *refs), grid=(hea...  9.37 us
  transfers between devices with their start and end apart: 33, of which 11 were waited for; matrix products, arithmetic and copies ran while one was open for 11% of the time, Pallas kernels for 20%

commit v1 on v0

--- a/solution.py
+++ b/solution.py
@@ -173,7 +173,7 @@
         out_shape=[
             jax.ShapeDtypeStruct((heads, part_len + pad_to, head_dim), jnp.bfloat16)
         ] * chips,
-        compiler_params=pltpu.CompilerParams(vmem_limit_bytes=40 * 2**20),
+        compiler_params=pltpu.CompilerParams(vmem_limit_bytes=60 * 2**20),
         cost_estimate=pl.CostEstimate(
             flops=40 * 10**9, bytes_accessed=20 * 2**20, transcendentals=10**7
         ),
@@ -181,53 +181,45 @@
     )(jnp.stack(at + out_at), jnp.stack(ok), order, starts, counts, *q_places, k_heads, v_heads)
 
 
-def spread(row, width, unit):
-    return jnp.broadcast_to(row, (width, row.shape[1])).T[:unit]
-
-
 def merge_kernel(unit, part_len, scale2, ok_ref, *refs):
     in_refs, out_ref = refs[:-1], refs[-1]
-    head_dim = out_ref.shape[2]
-    per_unit, units, pad_to = stat_rows_of(part_len, unit)
-    stats = [ref[0, part_len:, :].astype(jnp.float32) for ref in in_refs]
-    rows = [ref[0, :part_len, :].astype(jnp.float32) for ref in in_refs]
-    outs = []
-    kinds = [[], [], []]
-    for u in range(units):
-
-        def line(stat, kind):
-            at = (kind * units + u) * per_unit
-            pieces = [stat[at + r : at + r + 1, :] for r in range(per_unit)]
-            return jnp.concatenate(pieces, axis=1)
-
+    heads, _, width = out_ref.shape
+    _, units, pad_to = stat_rows_of(part_len, unit)
+    oks = [ok_ref[index] > 0 for index in range(len(in_refs))]
+    for h in range(heads):
         peaks, totals = [], []
-        for index, stat in enumerate(stats):
-            ok = ok_ref[index] > 0
-            peaks.append(jnp.where(ok, line(stat, 0), low_score))
-            totals.append(jnp.where(ok, line(stat, 1) + line(stat, 2), 0.0))
+        for ok, ref in zip(oks, in_refs):
+            stat = ref[h, part_len:, :].astype(jnp.float32)
+            peaks.append(jnp.where(ok, stat[:units], low_score))
+            total = stat[units : 2 * units] + stat[2 * units : 3 * units]
+            totals.append(jnp.where(ok, total, 0.0))
         top = functools.reduce(jnp.maximum, peaks)
         shares = [t * jnp.exp2((p - top) * scale2) for t, p in zip(totals, peaks)]
         total = functools.reduce(jnp.add, shares)
         inverse = 1.0 / jnp.maximum(total, 1e-30)
-        merged = None
-        for values, share in zip(rows, shares):
-            part = spread(share * inverse, head_dim, unit) * values[u * unit : (u + 1) * unit]
-            merged = part if merged is None else merged + part
-        outs.append(merged)
+        merged = [0.0] * units
+        for ref, share in zip(in_refs, shares):
+            weight = jnp.concatenate(
+                [share * inverse, jnp.zeros((-units % 8, 128), jnp.float32)], axis=0
+            ).T
+            rows = ref[h, :part_len, :].astype(jnp.float32)
+            for u in range(units):
+                merged[u] = merged[u] + weight[:unit, u : u + 1] * rows[u * unit : (u + 1) * unit]
         high = total.astype(jnp.bfloat16).astype(jnp.float32)
-        for kind, value in zip(kinds, (top, high, total - high)):
-            kind.append(value)
-    out_ref[0, :part_len, :] = jnp.concatenate(outs, axis=0).astype(jnp.bfloat16)
-    out_ref[0, part_len:, :] = stat_block(kinds, pad_to)
+        stats = [top, high, total - high, jnp.zeros((pad_to - 3 * units, width), jnp.float32)]
+        out_ref[h, :part_len, :] = jnp.concatenate(merged, axis=0).astype(jnp.bfloat16)
+        out_ref[h, part_len:, :] = jnp.concatenate(stats, axis=0).astype(jnp.bfloat16)
 
 
 def merge(parts, ok, part_len, unit, scale2):
-    block = pl.BlockSpec((1,) + parts[0].shape[1:], lambda h, *_: (h, 0, 0))
+    heads = parts[0].shape[0]
+    step = max(1, heads // 2)
+    block = pl.BlockSpec((step,) + parts[0].shape[1:], lambda h, *_: (h, 0, 0))
     return pl.pallas_call(
         lambda *refs: merge_kernel(unit, part_len, scale2, *refs),
         grid_spec=pltpu.PrefetchScalarGridSpec(
             num_scalar_prefetch=1,
-            grid=(parts[0].shape[0],),
+            grid=(heads // step,),
             in_specs=[block] * len(parts),
             out_specs=block,
         ),
@@ -498,6 +490,9 @@
         for h in range(groups)
         for j in range(share)
     ]
+    q_blocks, out_weight = lax.optimization_barrier(
+        ([q for q, _, _, _ in q_places], out_weight)
+    )
     weight_block = lax.ppermute(out_weight, ("heads", "pages"), moves)
     natural = Layout((0, 1, 2))
     all_k = lax.all_gather(rotated_k, "pages", axis=0, tiled=True)
@@ -540,7 +535,7 @@
     line = page_devs // 4
     line_at, across = device_at // 4, (device_at // 2) % 2
     outs = cached_attention(
-        [q for q, _, _, _ in q_places],
+        q_blocks,
         [jnp.clip(at, 0, line - 1) * 2 + side for _, at, side, _ in q_places],
         [ok for _, _, _, ok in q_places],
         [((line_at + k) % line) * 2 + (across ^ d) for k in range(line) for d in range(2)],

time: 410 us -> 430 us (1.049)
  waiting for transfers between devices: 132 us -> 153 us
    ppermute x3, waiting for transfers between devices: 0.01 us -> 20.2 us  [gather_lines(): lax.ppermute(down, 'pages', cross_down)]
    ppermute x12, waiting for transfers between devices: 99.6 us -> 83.6 us  [shift(): return lax.ppermute(x, 'pages', moves)]
    ppermute x3, waiting for transfers between devices: 0.01 us -> 11.9 us  [gather_lines(): lax.ppermute(up, 'pages', cross_up)]
    pallas_call x1, Pallas kernels: 22.6 us -> 31 us  [cached_attention(): pl.pallas_call(lambda *refs: cached_kernel(unit, stat_unit, span, scale2,...]
    pallas_call x9, Pallas kernels: 42 us -> 34.2 us  [merge(): pl.pallas_call(lambda *refs: merge_kernel(unit, part_len, scale2, *refs),...]
    ppermute x8, waiting for transfers between devices: 27.8 us -> 34.2 us  [swap(): return lax.ppermute(x, 'pages', [(p, p ^ bit) for p in range(devs)])]
    unnamed x53 -> x81, local copies, waits for them, and re-layouts: 27.8 us -> 27.1 us
  transfers between devices with their start and end apart: 33 -> 33, of which waited for: 11 -> 13; matrix products, arithmetic and copies ran while one was open for 11% -> 10% of each run, Pallas kernels for 20% -> 19%
where the time goes in v1:
time: 430 us; the launch traced here: 423 us
  waiting for transfers between devices  153 us (36%)
  starting transfers between devices  103 us (24%)
  Pallas kernels  87.7 us (20%)
  local copies, waits for them, and re-layouts  44 us (10%)
  other arithmetic  20.7 us (5%)
  between operations  14.4 us (3%)
    ppermute x12, waiting for transfers between devices, shift(): return lax.ppermute(x, 'pages', moves)  83.6 us
    ppermute x12, starting transfers between devices, shift(): return lax.ppermute(x, 'pages', moves)  74.1 us
    ppermute x8, waiting for transfers between devices, swap(): return lax.ppermute(x, 'pages', [(p, p ^ bit) for p in range(devs)])  34.2 us
    pallas_call x9, Pallas kernels, merge(): pl.pallas_call(lambda *refs: merge_kernel(unit, part_len, scale2, *refs),...  34.2 us
    pallas_call x1, Pallas kernels, cached_attention(): pl.pallas_call(lambda *refs: cached_kernel(unit, stat_unit, span, scale2,...  31 us
    unnamed x81, local copies, waits for them, and re-layouts  27.1 us
    ppermute x3, waiting for transfers between devices, gather_lines(): lax.ppermute(down, 'pages', cross_down)  20.2 us
    ppermute x8, starting transfers between devices, swap(): return lax.ppermute(x, 'pages', [(p, p ^ bit) for p in range(devs)])  14.1 us
  transfers between devices with their start and end apart: 33, of which 13 were waited for; matrix products, arithmetic and copies ran while one was open for 10% of the time, Pallas kernels for 19%

profile of v1, /device:TPU:12, one launch (start us, length us, event | category | flops | bytes accessed | tf_op | source)
XLA Modules:
  0.0 423.1 jit_solution(11933550060252032509)
XLA Ops:
  27.8 28.0 %collective-permute-done.2.refs_7_ = bf16[4,576,128]{2,1,0:T(8,128)(2,1)S(1)} collective-permute-done((bf16[4,576,128]{2,1,0:T(8,128)(2,1)S(1)}, bf16[4,576,128]{2,1,0:T(8,128)(2,1)S(1)}, u32[]{:S(2)}, u32[]{:S(2)}) %collective-permute-start.2) | collective-permute-done | bytes 589856 | tf_op jit(solution)/shard_map/ppermute | solution.py:271
  55.8 4.4 %collective-permute-start.6 = (bf16[4,576,128]{2,1,0:T(8,128)(2,1)S(1)}, bf16[4,576,128]{2,1,0:T(8,128)(2,1)S(1)}, u32[]{:S(2)}, u32[]{:S(2)}) collective-permute-start(bf16[4,576,128]{2,1,0:T(8,128)(2,1)S(1)} %collective-permute-done.2.refs_7_), channel_id=1, source_target_pairs={{4,8},{5,9},{6,10},{7,11},{8,12},{9,13},{10,14},{11,15},{20,24},{2... | collective-permute-start | bytes 1769480 | tf_op jit(solution)/shard_map/ppermute | solution.py:271
  66.2 27.9 %collective-permute-done.6.refs_11_ = bf16[4,576,128]{2,1,0:T(8,128)(2,1)S(1)} collective-permute-done((bf16[4,576,128]{2,1,0:T(8,128)(2,1)S(1)}, bf16[4,576,128]{2,1,0:T(8,128)(2,1)S(1)}, u32[]{:S(2)}, u32[]{:S(2)}) %collective-permute-start.6) | collective-permute-done | bytes 589856 | tf_op jit(solution)/shard_map/ppermute | solution.py:271
  94.7 4.4 %collective-permute-done.8.refs_13_ = bf16[4,576,128]{2,1,0:T(8,128)(2,1)S(1)} collective-permute-done((bf16[4,576,128]{2,1,0:T(8,128)(2,1)S(1)}, bf16[4,576,128]{2,1,0:T(8,128)(2,1)S(1)}, u32[]{:S(2)}, u32[]{:S(2)}) %collective-permute-start.8) | collective-permute-done | bytes 589856 | tf_op jit(solution)/shard_map/ppermute | solution.py:271
  103.5 11.9 %collective-permute-done.3.refs_8_ = bf16[4,576,128]{2,1,0:T(8,128)(2,1)S(1)} collective-permute-done((bf16[4,576,128]{2,1,0:T(8,128)(2,1)S(1)}, bf16[4,576,128]{2,1,0:T(8,128)(2,1)S(1)}, u32[]{:S(2)}, u32[]{:S(2)}) %collective-permute-start.3) | collective-permute-done | bytes 589856 | tf_op jit(solution)/shard_map/ppermute | solution.py:291
  120.1 8.1 %collective-permute-done.5.refs_10_ = bf16[4,576,128]{2,1,0:T(8,128)(2,1)S(1)} collective-permute-done((bf16[4,576,128]{2,1,0:T(8,128)(2,1)S(1)}, bf16[4,576,128]{2,1,0:T(8,128)(2,1)S(1)}, u32[]{:S(2)}, u32[]{:S(2)}) %collective-permute-start.5) | collective-permute-done | bytes 589856 | tf_op jit(solution)/shard_map/ppermute | solution.py:293
  128.1 12.2 %collective-permute-done.9.refs_14_ = bf16[4,576,128]{2,1,0:T(8,128)(2,1)S(1)} collective-permute-done((bf16[4,576,128]{2,1,0:T(8,128)(2,1)S(1)}, bf16[4,576,128]{2,1,0:T(8,128)(2,1)S(1)}, u32[]{:S(2)}, u32[]{:S(2)}) %collective-permute-start.9) | collective-permute-done | bytes 589856 | tf_op jit(solution)/shard_map/ppermute | solution.py:293
  141.9 7.3 %constant_dynamic-slice_fusion.5 = (bf16[12,128,4,128]{3,2,1,0:T(4,128)(2,1)}, bf16[12,128,4,128]{3,2,1,0:T(4,128)(2,1)}, bf16[12,128,4,128]{3,2,1,0:T(4,128)(2,1)S(1)}, bf16[12,128,4,128]{3,2,1,0:T(4,128)(2,1)}) fusion(bf16[12,128,8,128]{3,2,1,0:T(8,128)(2,1)S(1)} %copy-done.1, s32[]{:T(128)S(6)} %select_n.160, s32[]{:T(128)S(6)} %select_n.161, ...), kind=kLoop, calls=%fused_computation.46 | loop fusion | bytes 12582920 | tf_op jit(solution)/shard_map/dynamic-slice.4
  150.8 3.7 copy.62
  158.0 3.8 copy.61
  165.1 4.0 pad_maximum_fusion.refs_19_
  172.4 31.0 %cached_attention.1 = (bf16[4,608,128]{2,1,0:T(8,128)(2,1)}, bf16[4,608,128]{2,1,0:T(8,128)(2,1)}, bf16[4,608,128]{2,1,0:T(8,128)(2,1)}, bf16[4,608,128]{2,1,0:T...) custom-call(s32[22]{0:T(128)} %stack.197.refs_0_, ...), custom_call_target="tpu_custom_call" | custom-call | flops 40000000000 | bytes 20971520 | tf_op jit(solution)/shard_map/cached_attention/pallas_call | solution.py:155
  203.4 8.7 %collective-permute-start.17 = (bf16[4,608,128]{2,1,0:T(8,128)(2,1)}, bf16[4,608,128]{2,1,0:T(8,128)(2,1)}, u32[]{:S(2)}, u32[]{:S(2)}) collective-permute-start(bf16[4,608,128]{2,1,0:T(8,128)(2,1)} %get-tuple-element.45), channel_id=1, source_target_pairs={{0,2},{1,3},{2,0},{3,1},{4,6},{5,7},{6,4},{7,5},{8,10},{9,11},{10,... | collective-permute-start | bytes 1867784 | tf_op jit(solution)/shard_map/ppermute | solution.py:265
  214.1 17.2 %collective-permute-done.17.refs_2_ = bf16[4,608,128]{2,1,0:T(8,128)(2,1)} collective-permute-done((bf16[4,608,128]{2,1,0:T(8,128)(2,1)}, bf16[4,608,128]{2,1,0:T(8,128)(2,1)}, u32[]{:S(2)}, u32[]{:S(2)}) %collective-permute-start.17) | collective-permute-done | bytes 622624 | tf_op jit(solution)/shard_map/ppermute | solution.py:265
  236.5 8.2 %collective-permute-done.19.refs_2_ = bf16[4,608,128]{2,1,0:T(8,128)(2,1)} collective-permute-done((bf16[4,608,128]{2,1,0:T(8,128)(2,1)}, bf16[4,608,128]{2,1,0:T(8,128)(2,1)}, u32[]{:S(2)}, u32[]{:S(2)}) %collective-permute-start.19) | collective-permute-done | bytes 622624 | tf_op jit(solution)/shard_map/ppermute | solution.py:265
  250.9 6.9 %collective-permute-done.18.refs_2_ = bf16[4,608,128]{2,1,0:T(8,128)(2,1)} collective-permute-done((bf16[4,608,128]{2,1,0:T(8,128)(2,1)}, bf16[4,608,128]{2,1,0:T(8,128)(2,1)}, u32[]{:S(2)}, u32[]{:S(2)}) %collective-permute-start.18) | collective-permute-done | bytes 622624 | tf_op jit(solution)/shard_map/ppermute | solution.py:265
  266.7 6.5 %collective-permute-done.20.refs_2_ = bf16[4,608,128]{2,1,0:T(8,128)(2,1)} collective-permute-done((bf16[4,608,128]{2,1,0:T(8,128)(2,1)}, bf16[4,608,128]{2,1,0:T(8,128)(2,1)}, u32[]{:S(2)}, u32[]{:S(2)}) %collective-permute-start.20) | collective-permute-done | bytes 622624 | tf_op jit(solution)/shard_map/ppermute | solution.py:271
  276.9 42.5 %collective-permute-start.21 = (bf16[4,608,128]{2,1,0:T(8,128)(2,1)}, bf16[4,608,128]{2,1,0:T(8,128)(2,1)}, u32[]{:S(2)}, u32[]{:S(2)}) collective-permute-start(bf16[4,608,128]{2,1,0:T(8,128)(2,1)} %merge.13), channel_id=1, source_target_pairs={{0,4},{1,5},{2,6},{3,7},{4,8},{5,9},{6,10},{7,11},{16,20},{17,21},... | collective-permute-start | bytes 1867784 | tf_op jit(solution)/shard_map/ppermute | solution.py:271
  322.6 16.9 %collective-permute-done.24.refs_2_ = bf16[4,608,128]{2,1,0:T(8,128)(2,1)} collective-permute-done((bf16[4,608,128]{2,1,0:T(8,128)(2,1)}, bf16[4,608,128]{2,1,0:T(8,128)(2,1)}, u32[]{:S(2)}, u32[]{:S(2)}) %collective-permute-start.24) | collective-permute-done | bytes 622624 | tf_op jit(solution)/shard_map/ppermute | solution.py:271
  348.8 11.3 %collective-permute-start.22 = (bf16[4,608,128]{2,1,0:T(8,128)(2,1)}, bf16[4,608,128]{2,1,0:T(8,128)(2,1)}, u32[]{:S(2)}, u32[]{:S(2)}) collective-permute-start(bf16[4,608,128]{2,1,0:T(8,128)(2,1)} %merge.14), channel_id=1, source_target_pairs={{0,4},{1,5},{2,6},{3,7},{4,8},{5,9},{6,10},{7,11},{8,12},{9,13},{1... | collective-permute-start | bytes 1867784 | tf_op jit(solution)/shard_map/ppermute | solution.py:271
  372.0 8.4 %fresh_attention.1.refs_4_ = bf16[4,608,128]{2,1,0:T(8,128)(2,1)S(1)} custom-call(bf16[4,576,128]{2,1,0:T(8,128)(2,1)S(1)} %copy-done.6, bf16[4,1152,128]{2,1,0:T(8,128)(2,1)S(1)} %bitcast.58, bf16[4,1152,128]{2,1,0:T(8,128)(2,1)S(1)} %bitcast.59, s32[2,576]{1,0:T(2,128)S(1)} %pad_add_fusion.refs_3_, s32[1152,1]{1,0:T(8,128)S(1)} %copy-done.7), custom_call_target="tpu_custom_call" | custom-call | tf_op jit(solution)/shard_map/fresh_attention/pallas_call | solution.py:358
  381.2 4.6 %merge.17 = bf16[4,608,128]{2,1,0:T(8,128)(2,1)} custom-call(s32[4]{0:T(128)} %pad_add_fusion.5.refs_0_, bf16[4,608,128]{2,1,0:T(8,128)(2,1)} %merge.9.refs_1_, bf16[4,608,128]{2,1,0:T(8,128)(2,1)} %collective-permute-done.22.refs_2_, bf16[4,608,128]{2,1,0:T(8,128)(2,1)} %collective-permute-done.25.refs_3_, bf16[4,608,128]{2,1,0:T(8,128)(2,1)} %copy-done.4), custom_call_target="tpu_custom_call" | custom-call | tf_op jit(solution)/shard_map/merge/pallas_call | solution.py:218
  391.5 8.4 %write_pages.1 = (bf16[12,128,8,128]{3,2,1,0:T(8,128)(2,1)}, bf16[12,128,8,128]{3,2,1,0:T(8,128)(2,1)}) custom-call(s32[12]{0:T(128)S(1)} %convert_element_type.45.fresh_ref, s32[12]{0:T(128)S(1)} %fusion.2.index_ref, bf16[12,128,8,128]{3,2,1,0:T(8,128)(2,1)S(1)} %copy-done.2, bf16[12,128,8,128]{3,2,1,0:T(8,128)(2,1)S(1)} %copy-done.1, ...), custom_call_target="tpu_custom_call" | custom-call | tf_op jit(solution)/shard_map/write_pages/pallas_call | solution.py:249
  410.8 5.7 %project.1 = bf16[288,2048]{1,0:T(8,128)(2,1)} custom-call(s32[2]{0:T(128)S(1)} %pad_add_fusion.4.refs_0_, bf16[4,288,128]{2,1,0:T(8,128)(2,1)S(1)} %get-tuple-element.64.refs_1_, bf16[4,288,128]{2,1,0:T(8,128)(2,1)S(1)} %copy-done.9, bf16[4,288,128]{2,1,0:T(8,128)(2,1)S(1)} %copy-done.13, bf16[4,288,128]{2,1,0:T(8,128)(2,1)S(1)} %copy-done.11, ...), custom_call_target="tpu_custom_call" | custom-call | tf_op jit(solution)/shard_map/project/pallas_call | solution.py:409
  (192 shorter events, 116.8 us)
Async XLA Ops:
  7.2 358.1 %all-gather.5.cloned.1.call-start = ((), (), s32[]{:S(2)}) async-start(), calls=%async_computation | async-start | bytes 10027008 | tf_op jit(solution)/shard_map/all_gather | solution.py:498
  13.8 354.6 %all-gather.7.cloned.1.call-start = ((), (), s32[]{:S(2)}) async-start(), calls=%async_computation.1 | async-start | bytes 10027008 | tf_op jit(solution)/shard_map/all_gather | solution.py:499
  14.5 389.9 %all-gather.9.cloned.1.call-start = ((), (), s32[]{:S(2)}) async-start(), calls=%async_computation.2 | async-start | bytes 8912896 | tf_op jit(solution)/shard_map/all_gather | solution.py:502
  21.9 33.9 %collective-permute-start.2 = (bf16[4,576,128]{2,1,0:T(8,128)(2,1)S(1)}, bf16[4,576,128]{2,1,0:T(8,128)(2,1)S(1)}, u32[]{:S(2)}, u32[]{:S(2)}) collective-permute-start(bf16[4,576,128]{2,1,0:T(8,128)(2,1)S(1)} %maximum_select_fusion.refs_5_.refs_0_), channel_id=1, source_target_pairs={{0,4},{1,5},{2,6},{3,7},{4,8},{5,9},{6,10},{7,11},{8,12},{9,13},{1... | collective-permute-start | bytes 1769480 | tf_op jit(solution)/shard_map/ppermute | solution.py:271
  25.4 34.8 %collective-permute-start.4 = (bf16[4,576,128]{2,1,0:T(8,128)(2,1)S(1)}, bf16[4,576,128]{2,1,0:T(8,128)(2,1)S(1)}, u32[]{:S(2)}, u32[]{:S(2)}) collective-permute-start(bf16[4,576,128]{2,1,0:T(8,128)(2,1)S(1)} %maximum_select_fusion.refs_5_.refs_0_), channel_id=1, source_target_pairs={{4,0},{5,1},{6,2},{7,3},{8,4},{9,5},{10,6},{11,7},{12,8},{13,9},{1... | collective-permute-start | bytes 1769480 | tf_op jit(solution)/shard_map/ppermute | solution.py:271
  55.8 38.2 %collective-permute-start.6 = (bf16[4,576,128]{2,1,0:T(8,128)(2,1)S(1)}, bf16[4,576,128]{2,1,0:T(8,128)(2,1)S(1)}, u32[]{:S(2)}, u32[]{:S(2)}) collective-permute-start(bf16[4,576,128]{2,1,0:T(8,128)(2,1)S(1)} %collective-permute-done.2.refs_7_), channel_id=1, source_target_pairs={{4,8},{5,9},{6,10},{7,11},{8,12},{9,13},{10,14},{11,15},{20,24},{2... | collective-permute-start | bytes 1769480 | tf_op jit(solution)/shard_map/ppermute | solution.py:271
  60.2 38.9 %collective-permute-start.8 = (bf16[4,576,128]{2,1,0:T(8,128)(2,1)S(1)}, bf16[4,576,128]{2,1,0:T(8,128)(2,1)S(1)}, u32[]{:S(2)}, u32[]{:S(2)}) collective-permute-start(bf16[4,576,128]{2,1,0:T(8,128)(2,1)S(1)} %collective-permute-done.4.refs_9_), channel_id=1, source_target_pairs={{4,0},{5,1},{6,2},{7,3},{8,4},{9,5},{10,6},{11,7},{20,16},{21,17},... | collective-permute-start | bytes 1769480 | tf_op jit(solution)/shard_map/ppermute | solution.py:271
  62.2 40.6 %collective-permute-start.1 = (bf16[4,576,128]{2,1,0:T(8,128)(2,1)S(1)}, bf16[4,576,128]{2,1,0:T(8,128)(2,1)S(1)}, u32[]{:S(2)}, u32[]{:S(2)}) collective-permute-start(bf16[4,576,128]{2,1,0:T(8,128)(2,1)S(1)} %maximum_select_fusion.refs_5_.refs_0_), channel_id=1, source_target_pairs={{0,2},{1,3},{2,0},{3,1},{4,6},{5,7},{6,4},{7,5},{8,10},{9,11},{10,... | collective-permute-start | bytes 1769480 | tf_op jit(solution)/shard_map/ppermute | solution.py:265
  62.6 52.9 %collective-permute-start.3 = (bf16[4,576,128]{2,1,0:T(8,128)(2,1)S(1)}, bf16[4,576,128]{2,1,0:T(8,128)(2,1)S(1)}, u32[]{:S(2)}, u32[]{:S(2)}) collective-permute-start(bf16[4,576,128]{2,1,0:T(8,128)(2,1)S(1)} %collective-permute-done.2.refs_7_), channel_id=1, source_target_pairs={{4,6},{5,7},{6,4},{7,5},{8,10},{9,11},{10,8},{11,9},{12,14},{13,15... | collective-permute-start | bytes 1769480 | tf_op jit(solution)/shard_map/ppermute | solution.py:291
  94.0 24.6 %collective-permute-start.10 = (bf16[4,576,128]{2,1,0:T(8,128)(2,1)S(1)}, bf16[4,576,128]{2,1,0:T(8,128)(2,1)S(1)}, u32[]{:S(2)}, u32[]{:S(2)}) collective-permute-start(bf16[4,576,128]{2,1,0:T(8,128)(2,1)S(1)} %collective-permute-done.6.refs_11_), channel_id=1, source_target_pairs={{8,12},{9,13},{10,14},{11,15},{24,28},{25,29},{26,30},{27,31}} | collective-permute-start | bytes 1769480 | tf_op jit(solution)/shard_map/ppermute | solution.py:271
  100.5 27.7 %collective-permute-start.5 = (bf16[4,576,128]{2,1,0:T(8,128)(2,1)S(1)}, bf16[4,576,128]{2,1,0:T(8,128)(2,1)S(1)}, u32[]{:S(2)}, u32[]{:S(2)}) collective-permute-start(bf16[4,576,128]{2,1,0:T(8,128)(2,1)S(1)} %collective-permute-done.4.refs_9_), channel_id=1, source_target_pairs={{0,2},{1,3},{2,0},{3,1},{4,6},{5,7},{6,4},{7,5},{8,10},{9,11},{10,... | collective-permute-start | bytes 1769480 | tf_op jit(solution)/shard_map/ppermute | solution.py:293
  102.8 25.3 %collective-permute-start.7 = (bf16[4,576,128]{2,1,0:T(8,128)(2,1)S(1)}, bf16[4,576,128]{2,1,0:T(8,128)(2,1)S(1)}, u32[]{:S(2)}, u32[]{:S(2)}) collective-permute-start(bf16[4,576,128]{2,1,0:T(8,128)(2,1)S(1)} %collective-permute-done.6.refs_11_), channel_id=1, source_target_pairs={{8,10},{9,11},{10,8},{11,9},{12,14},{13,15},{14,12},{15,13},{24,26... | collective-permute-start | bytes 1769480 | tf_op jit(solution)/shard_map/ppermute | solution.py:291
  115.5 24.8 %collective-permute-start.9 = (bf16[4,576,128]{2,1,0:T(8,128)(2,1)S(1)}, bf16[4,576,128]{2,1,0:T(8,128)(2,1)S(1)}, u32[]{:S(2)}, u32[]{:S(2)}) collective-permute-start(bf16[4,576,128]{2,1,0:T(8,128)(2,1)S(1)} %collective-permute-done.8.refs_13_), channel_id=1, source_target_pairs={{0,2},{1,3},{2,0},{3,1},{4,6},{5,7},{6,4},{7,5},{16,18},{17,19},{1... | collective-permute-start | bytes 1769480 | tf_op jit(solution)/shard_map/ppermute | solution.py:293
  118.6 21.7 %collective-permute-start.11 = (bf16[4,576,128]{2,1,0:T(8,128)(2,1)S(1)}, bf16[4,576,128]{2,1,0:T(8,128)(2,1)S(1)}, u32[]{:S(2)}, u32[]{:S(2)}) collective-permute-start(bf16[4,576,128]{2,1,0:T(8,128)(2,1)S(1)} %collective-permute-done.10.refs_15_), channel_id=1, source_target_pairs={{12,14},{13,15},{14,12},{15,13},{28,30},{29,31},{30,28},{31,29}} | collective-permute-start | bytes 1769480 | tf_op jit(solution)/shard_map/ppermute | solution.py:291
  203.4 27.9 %collective-permute-start.17 = (bf16[4,608,128]{2,1,0:T(8,128)(2,1)}, bf16[4,608,128]{2,1,0:T(8,128)(2,1)}, u32[]{:S(2)}, u32[]{:S(2)}) collective-permute-start(bf16[4,608,128]{2,1,0:T(8,128)(2,1)} %get-tuple-element.45), channel_id=1, source_target_pairs={{0,2},{1,3},{2,0},{3,1},{4,6},{5,7},{6,4},{7,5},{8,10},{9,11},{10,... | collective-permute-start | bytes 1867784 | tf_op jit(solution)/shard_map/ppermute | solution.py:265
  212.1 32.6 %collective-permute-start.19 = (bf16[4,608,128]{2,1,0:T(8,128)(2,1)}, bf16[4,608,128]{2,1,0:T(8,128)(2,1)}, u32[]{:S(2)}, u32[]{:S(2)}) collective-permute-start(bf16[4,608,128]{2,1,0:T(8,128)(2,1)} %get-tuple-element.49), channel_id=1, source_target_pairs={{0,2},{1,3},{2,0},{3,1},{4,6},{5,7},{6,4},{7,5},{8,10},{9,11},{10,... | collective-permute-start | bytes 1867784 | tf_op jit(solution)/shard_map/ppermute | solution.py:265
  212.2 45.6 %collective-permute-start.18 = (bf16[4,608,128]{2,1,0:T(8,128)(2,1)}, bf16[4,608,128]{2,1,0:T(8,128)(2,1)}, u32[]{:S(2)}, u32[]{:S(2)}) collective-permute-start(bf16[4,608,128]{2,1,0:T(8,128)(2,1)} %get-tuple-element.47), channel_id=1, source_target_pairs={{0,2},{1,3},{2,0},{3,1},{4,6},{5,7},{6,4},{7,5},{8,10},{9,11},{10,... | collective-permute-start | bytes 1867784 | tf_op jit(solution)/shard_map/ppermute | solution.py:265
  235.0 26.5 %collective-permute-start.23 = (bf16[4,608,128]{2,1,0:T(8,128)(2,1)}, bf16[4,608,128]{2,1,0:T(8,128)(2,1)}, u32[]{:S(2)}, u32[]{:S(2)}) collective-permute-start(bf16[4,608,128]{2,1,0:T(8,128)(2,1)} %merge.10.refs_1_), channel_id=1, source_target_pairs={{12,8},{13,9},{14,10},{15,11},{28,24},{29,25},{30,26},{31,27}} | collective-permute-start | bytes 1867784 | tf_op jit(solution)/shard_map/ppermute | solution.py:271
  248.4 24.8 %collective-permute-start.20 = (bf16[4,608,128]{2,1,0:T(8,128)(2,1)}, bf16[4,608,128]{2,1,0:T(8,128)(2,1)}, u32[]{:S(2)}, u32[]{:S(2)}) collective-permute-start(bf16[4,608,128]{2,1,0:T(8,128)(2,1)} %merge.12.refs_1_), channel_id=1, source_target_pairs={{0,4},{1,5},{2,6},{3,7},{16,20},{17,21},{18,22},{19,23}} | collective-permute-start | bytes 1867784 | tf_op jit(solution)/shard_map/ppermute | solution.py:271
  265.2 74.2 %collective-permute-start.24 = (bf16[4,608,128]{2,1,0:T(8,128)(2,1)}, bf16[4,608,128]{2,1,0:T(8,128)(2,1)}, u32[]{:S(2)}, u32[]{:S(2)}) collective-permute-start(bf16[4,608,128]{2,1,0:T(8,128)(2,1)} %merge.15), channel_id=1, source_target_pairs={{8,4},{9,5},{10,6},{11,7},{12,8},{13,9},{14,10},{15,11},{24,20},{2... | collective-permute-start | bytes 1867784 | tf_op jit(solution)/shard_map/ppermute | solution.py:271
  276.9 68.2 %collective-permute-start.21 = (bf16[4,608,128]{2,1,0:T(8,128)(2,1)}, bf16[4,608,128]{2,1,0:T(8,128)(2,1)}, u32[]{:S(2)}, u32[]{:S(2)}) collective-permute-start(bf16[4,608,128]{2,1,0:T(8,128)(2,1)} %merge.13), channel_id=1, source_target_pairs={{0,4},{1,5},{2,6},{3,7},{4,8},{5,9},{6,10},{7,11},{16,20},{17,21},... | collective-permute-start | bytes 1867784 | tf_op jit(solution)/shard_map/ppermute | solution.py:271
  319.4 42.2 %collective-permute-start.16 = (bf16[4,608,128]{2,1,0:T(8,128)(2,1)}, bf16[4,608,128]{2,1,0:T(8,128)(2,1)}, u32[]{:S(2)}, u32[]{:S(2)}) collective-permute-start(bf16[4,608,128]{2,1,0:T(8,128)(2,1)} %get-tuple-element.43), channel_id=1, source_target_pairs={{0,2},{1,3},{2,0},{3,1},{4,6},{5,7},{6,4},{7,5},{8,10},{9,11},{10,... | collective-permute-start | bytes 1867784 | tf_op jit(solution)/shard_map/ppermute | solution.py:265
  343.1 38.1 %collective-permute-start.25 = (bf16[4,608,128]{2,1,0:T(8,128)(2,1)}, bf16[4,608,128]{2,1,0:T(8,128)(2,1)}, u32[]{:S(2)}, u32[]{:S(2)}) collective-permute-start(bf16[4,608,128]{2,1,0:T(8,128)(2,1)} %merge.16), channel_id=1, source_target_pairs={{4,0},{5,1},{6,2},{7,3},{8,4},{9,5},{10,6},{11,7},{12,8},{13,9},{1... | collective-permute-start | bytes 1867784 | tf_op jit(solution)/shard_map/ppermute | solution.py:271
  348.8 32.5 %collective-permute-start.22 = (bf16[4,608,128]{2,1,0:T(8,128)(2,1)}, bf16[4,608,128]{2,1,0:T(8,128)(2,1)}, u32[]{:S(2)}, u32[]{:S(2)}) collective-permute-start(bf16[4,608,128]{2,1,0:T(8,128)(2,1)} %merge.14), channel_id=1, source_target_pairs={{0,4},{1,5},{2,6},{3,7},{4,8},{5,9},{6,10},{7,11},{8,12},{9,13},{1... | collective-permute-start | bytes 1867784 | tf_op jit(solution)/shard_map/ppermute | solution.py:271
  (47 other events, 819.5 us)
Sparse Core Ops, SparseCore 0:
  13.9 118.7 all-gather.4
  135.0 101.5 all-gather.6
  238.8 109.5 all-gather.8

commit v2 on v1

--- a/solution.py
+++ b/solution.py
@@ -484,16 +484,23 @@
     groups = lax.axis_size("heads")
     group_at = lax.axis_index("heads")
     share = page_devs // groups
-    moves = [
-        (i * page_devs + h * share + j, h * page_devs + i * share + j)
-        for i in range(groups)
-        for h in range(groups)
-        for j in range(share)
-    ]
-    q_blocks, out_weight = lax.optimization_barrier(
-        ([q for q, _, _, _ in q_places], out_weight)
-    )
-    weight_block = lax.ppermute(out_weight, ("heads", "pages"), moves)
+    q_list = [q for q, _, _, _ in q_places]
+    own_share = device_at // share
+
+    def to_owner(block):
+        found = block
+        for s in range(1, groups):
+            moved = lax.ppermute(block, "heads", [(i, (i + s) % groups) for i in range(groups)])
+            moved, _ = lax.optimization_barrier((moved, q_list))
+            moved = lax.ppermute(
+                moved,
+                "pages",
+                [(p, (p - s * share) % page_devs) for p in range(page_devs)],
+            )
+            found = jnp.where(own_share == (group_at - s) % groups, moved, found)
+        return found
+
+    weight_block = to_owner(out_weight)
     natural = Layout((0, 1, 2))
     all_k = lax.all_gather(rotated_k, "pages", axis=0, tiled=True)
     all_v = lax.all_gather(values, "pages", axis=0, tiled=True)
@@ -531,11 +538,12 @@
     k_heads = jnp.concatenate([k_mine, swap(k_other, 1)], axis=1)
     v_heads = jnp.concatenate([v_mine, swap(v_other, 1)], axis=1)
 
+    q_list, k_heads, v_heads = lax.optimization_barrier((q_list, k_heads, v_heads))
     unit = math.gcd(span_len, tok_dev)
     line = page_devs // 4
     line_at, across = device_at // 4, (device_at // 2) % 2
     outs = cached_attention(
-        q_blocks,
+        q_list,
         [jnp.clip(at, 0, line - 1) * 2 + side for _, at, side, _ in q_places],
         [ok for _, _, _, ok in q_places],
         [((line_at + k) % line) * 2 + (across ^ d) for k in range(line) for d in range(2)],

time: 430 us -> 432 us (level); the launches traced: 423 us -> 429 us
  waiting for transfers between devices: 153 us -> 195 us
  starting transfers between devices: 103 us -> 64 us
    ppermute x1 -> x2, waiting for transfers between devices: 0.01 us -> 50.9 us  [the longest x1 40.2 us: to_owner(): lax.ppermute(moved, 'pages', [(p, (p - s * share) % page_devs) for p in r...]
    ppermute x12, starting transfers between devices: 74.1 us -> 34.4 us  [shift(): return lax.ppermute(x, 'pages', moves)]
    ppermute x8, waiting for transfers between devices: 34.2 us -> 51.7 us  [swap(): return lax.ppermute(x, 'pages', [(p, p ^ bit) for p in range(devs)])]
    ppermute x12, waiting for transfers between devices: 83.6 us -> 71.1 us  [shift(): return lax.ppermute(x, 'pages', moves)]
    ppermute x3, waiting for transfers between devices: 11.9 us -> 0.01 us  [gather_lines(): lax.ppermute(up, 'pages', cross_up)]
    unnamed x81 -> x87, local copies, waits for them, and re-layouts: 27.1 us -> 30.8 us
  transfers between devices with their start and end apart: 33 -> 34, of which waited for: 13 -> 13; matrix products, arithmetic and copies ran while one was open for 10% -> 10% of each run, Pallas kernels for 19% -> 19%
where the time goes in v2:
time: 432 us; the launch traced here: 429 us
  waiting for transfers between devices  195 us (45%)
  Pallas kernels  87.5 us (20%)
  starting transfers between devices  64 us (15%)
  local copies, waits for them, and re-layouts  47.8 us (11%)
  other arithmetic  20.5 us (5%)
  between operations  14.4 us (3%)
    ppermute x12, waiting for transfers between devices, shift(): return lax.ppermute(x, 'pages', moves)  71.1 us
    ppermute x8, waiting for transfers between devices, swap(): return lax.ppermute(x, 'pages', [(p, p ^ bit) for p in range(devs)])  51.7 us
    ppermute x1, waiting for transfers between devices, to_owner(): lax.ppermute(moved, 'pages', [(p, (p - s * share) % page_devs) for p in r...  40.2 us
    ppermute x12, starting transfers between devices, shift(): return lax.ppermute(x, 'pages', moves)  34.4 us
    pallas_call x9, Pallas kernels, merge(): pl.pallas_call(lambda *refs: merge_kernel(unit, part_len, scale2, *refs),...  34.2 us
    unnamed x87, local copies, waits for them, and re-layouts  30.8 us
    pallas_call x1, Pallas kernels, cached_attention(): pl.pallas_call(lambda *refs: cached_kernel(unit, stat_unit, span, scale2,...  30.1 us
    ppermute x3, waiting for transfers between devices, gather_lines(): lax.ppermute(down, 'pages', cross_down)  19.3 us
  transfers between devices with their start and end apart: 34, of which 13 were waited for; matrix products, arithmetic and copies ran while one was open for 10% of the time, Pallas kernels for 19%

profile of v2, /device:TPU:12, one launch (start us, length us, event | category | flops | bytes accessed | tf_op | source)
XLA Modules:
  0.0 429.4 jit_solution(14708096952016872978)
XLA Ops:
  27.4 29.4 %collective-permute-done.2.refs_7_ = bf16[4,576,128]{2,1,0:T(8,128)(2,1)S(1)} collective-permute-done((bf16[4,576,128]{2,1,0:T(8,128)(2,1)S(1)}, bf16[4,576,128]{2,1,0:T(8,128)(2,1)S(1)}, u32[]{:S(2)}, u32[]{:S(2)}) %collective-permute-start.2) | collective-permute-done | bytes 589856 | tf_op jit(solution)/shard_map/ppermute | solution.py:271
  56.8 4.4 %collective-permute-start.6 = (bf16[4,576,128]{2,1,0:T(8,128)(2,1)S(1)}, bf16[4,576,128]{2,1,0:T(8,128)(2,1)S(1)}, u32[]{:S(2)}, u32[]{:S(2)}) collective-permute-start(bf16[4,576,128]{2,1,0:T(8,128)(2,1)S(1)} %collective-permute-done.2.refs_7_), channel_id=1, source_target_pairs={{4,8},{5,9},{6,10},{7,11},{8,12},{9,13},{10,14},{11,15},{20,24},{2... | collective-permute-start | bytes 1769480 | tf_op jit(solution)/shard_map/ppermute | solution.py:271
  67.2 27.8 %collective-permute-done.6.refs_11_ = bf16[4,576,128]{2,1,0:T(8,128)(2,1)S(1)} collective-permute-done((bf16[4,576,128]{2,1,0:T(8,128)(2,1)S(1)}, bf16[4,576,128]{2,1,0:T(8,128)(2,1)S(1)}, u32[]{:S(2)}, u32[]{:S(2)}) %collective-permute-start.6) | collective-permute-done | bytes 589856 | tf_op jit(solution)/shard_map/ppermute | solution.py:271
  95.7 4.5 %collective-permute-done.8.refs_13_ = bf16[4,576,128]{2,1,0:T(8,128)(2,1)S(1)} collective-permute-done((bf16[4,576,128]{2,1,0:T(8,128)(2,1)S(1)}, bf16[4,576,128]{2,1,0:T(8,128)(2,1)S(1)}, u32[]{:S(2)}, u32[]{:S(2)}) %collective-permute-start.8) | collective-permute-done | bytes 589856 | tf_op jit(solution)/shard_map/ppermute | solution.py:271
  103.1 10.7 %collective-permute-done.29 = bf16[1024,256]{1,0:T(8,128)(2,1)} collective-permute-done((bf16[1024,256]{1,0:T(8,128)(2,1)}, bf16[1024,256]{1,0:T(8,128)(2,1)}, u32[]{:S(2)}, u32[]{:S(2)}) %collective-permute-start.29) | collective-permute-done | bytes 524320 | tf_op jit(solution)/shard_map/ppermute | solution.py:493
  122.0 9.9 %collective-permute-done.5.refs_10_ = bf16[4,576,128]{2,1,0:T(8,128)(2,1)S(1)} collective-permute-done((bf16[4,576,128]{2,1,0:T(8,128)(2,1)S(1)}, bf16[4,576,128]{2,1,0:T(8,128)(2,1)S(1)}, u32[]{:S(2)}, u32[]{:S(2)}) %collective-permute-start.5) | collective-permute-done | bytes 589856 | tf_op jit(solution)/shard_map/ppermute | solution.py:293
  132.0 9.4 %collective-permute-done.9.refs_14_ = bf16[4,576,128]{2,1,0:T(8,128)(2,1)S(1)} collective-permute-done((bf16[4,576,128]{2,1,0:T(8,128)(2,1)S(1)}, bf16[4,576,128]{2,1,0:T(8,128)(2,1)S(1)}, u32[]{:S(2)}, u32[]{:S(2)}) %collective-permute-start.9) | collective-permute-done | bytes 589856 | tf_op jit(solution)/shard_map/ppermute | solution.py:293
  143.3 40.2 %collective-permute-done.30 = bf16[1024,256]{1,0:T(8,128)(2,1)} collective-permute-done((bf16[1024,256]{1,0:T(8,128)(2,1)}, bf16[1024,256]{1,0:T(8,128)(2,1)}, u32[]{:S(2)}, u32[]{:S(2)}) %collective-permute-start.30) | collective-permute-done | bytes 524320 | tf_op jit(solution)/shard_map/ppermute | solution.py:495
  185.4 7.3 %constant_dynamic-slice_fusion.5 = (bf16[12,128,4,128]{3,2,1,0:T(4,128)(2,1)}, bf16[12,128,4,128]{3,2,1,0:T(4,128)(2,1)}, bf16[12,128,4,128]{3,2,1,0:T(4,128)(2,1)S(1)}, bf16[12,128,4,128]{3,2,1,0:T(4,128)(2,1)}) fusion(bf16[12,128,8,128]{3,2,1,0:T(8,128)(2,1)S(1)} %copy-done.1, s32[]{:T(128)S(6)} %select_n.175, s32[]{:T(128)S(6)} %select_n.176, ...), kind=kLoop, calls=%fused_computation.47 | loop fusion | bytes 12582920 | tf_op jit(solution)/shard_map/dynamic-slice.4
  194.2 3.8 copy.62
  208.6 3.9 pad_maximum_fusion.refs_19_
  215.9 30.1 %cached_attention.1 = (bf16[4,608,128]{2,1,0:T(8,128)(2,1)}, bf16[4,608,128]{2,1,0:T(8,128)(2,1)}, bf16[4,608,128]{2,1,0:T(8,128)(2,1)}, bf16[4,608,128]{2,1,0:T...) custom-call(s32[22]{0:T(128)} %stack.197.refs_0_, ...), custom_call_target="tpu_custom_call" | custom-call | flops 40000000000 | bytes 20971520 | tf_op jit(solution)/shard_map/cached_attention/pallas_call | solution.py:155
  246.0 9.5 %collective-permute-start.19 = (bf16[4,608,128]{2,1,0:T(8,128)(2,1)}, bf16[4,608,128]{2,1,0:T(8,128)(2,1)}, u32[]{:S(2)}, u32[]{:S(2)}) collective-permute-start(bf16[4,608,128]{2,1,0:T(8,128)(2,1)} %get-tuple-element.53), channel_id=1, source_target_pairs={{0,2},{1,3},{2,0},{3,1},{4,6},{5,7},{6,4},{7,5},{8,10},{9,11},{10,... | collective-permute-start | bytes 1867784 | tf_op jit(solution)/shard_map/ppermute | solution.py:265
  257.5 13.1 %collective-permute-done.19.refs_2_ = bf16[4,608,128]{2,1,0:T(8,128)(2,1)} collective-permute-done((bf16[4,608,128]{2,1,0:T(8,128)(2,1)}, bf16[4,608,128]{2,1,0:T(8,128)(2,1)}, u32[]{:S(2)}, u32[]{:S(2)}) %collective-permute-start.19) | collective-permute-done | bytes 622624 | tf_op jit(solution)/shard_map/ppermute | solution.py:265
  275.6 21.0 %collective-permute-done.17.refs_2_ = bf16[4,608,128]{2,1,0:T(8,128)(2,1)} collective-permute-done((bf16[4,608,128]{2,1,0:T(8,128)(2,1)}, bf16[4,608,128]{2,1,0:T(8,128)(2,1)}, u32[]{:S(2)}, u32[]{:S(2)}) %collective-permute-start.17) | collective-permute-done | bytes 622624 | tf_op jit(solution)/shard_map/ppermute | solution.py:265
  303.1 16.0 %collective-permute-done.18.refs_2_ = bf16[4,608,128]{2,1,0:T(8,128)(2,1)} collective-permute-done((bf16[4,608,128]{2,1,0:T(8,128)(2,1)}, bf16[4,608,128]{2,1,0:T(8,128)(2,1)}, u32[]{:S(2)}, u32[]{:S(2)}) %collective-permute-start.18) | collective-permute-done | bytes 622624 | tf_op jit(solution)/shard_map/ppermute | solution.py:265
  322.8 3.8 merge.13
  326.6 9.1 %collective-permute-start.21 = (bf16[4,608,128]{2,1,0:T(8,128)(2,1)}, bf16[4,608,128]{2,1,0:T(8,128)(2,1)}, u32[]{:S(2)}, u32[]{:S(2)}) collective-permute-start(bf16[4,608,128]{2,1,0:T(8,128)(2,1)} %merge.13), channel_id=1, source_target_pairs={{0,4},{1,5},{2,6},{3,7},{4,8},{5,9},{6,10},{7,11},{16,20},{17,21},... | collective-permute-start | bytes 1867784 | tf_op jit(solution)/shard_map/ppermute | solution.py:271
  343.2 9.3 %collective-permute-done.21.refs_2_ = bf16[4,608,128]{2,1,0:T(8,128)(2,1)} collective-permute-done((bf16[4,608,128]{2,1,0:T(8,128)(2,1)}, bf16[4,608,128]{2,1,0:T(8,128)(2,1)}, u32[]{:S(2)}, u32[]{:S(2)}) %collective-permute-start.21) | collective-permute-done | bytes 622624 | tf_op jit(solution)/shard_map/ppermute | solution.py:271
  361.8 5.0 %collective-permute-start.25 = (bf16[4,608,128]{2,1,0:T(8,128)(2,1)}, bf16[4,608,128]{2,1,0:T(8,128)(2,1)}, u32[]{:S(2)}, u32[]{:S(2)}) collective-permute-start(bf16[4,608,128]{2,1,0:T(8,128)(2,1)} %merge.16), channel_id=1, source_target_pairs={{4,0},{5,1},{6,2},{7,3},{8,4},{9,5},{10,6},{11,7},{12,8},{13,9},{1... | collective-permute-start | bytes 1867784 | tf_op jit(solution)/shard_map/ppermute | solution.py:271
  378.7 8.4 %fresh_attention.1.refs_4_ = bf16[4,608,128]{2,1,0:T(8,128)(2,1)S(1)} custom-call(bf16[4,576,128]{2,1,0:T(8,128)(2,1)S(1)} %copy-done.6, bf16[4,1152,128]{2,1,0:T(8,128)(2,1)S(1)} %bitcast.58, bf16[4,1152,128]{2,1,0:T(8,128)(2,1)S(1)} %bitcast.59, s32[2,576]{1,0:T(2,128)S(1)} %pad_add_fusion.refs_3_, s32[1152,1]{1,0:T(8,128)S(1)} %copy-done.7), custom_call_target="tpu_custom_call" | custom-call | tf_op jit(solution)/shard_map/fresh_attention/pallas_call | solution.py:358
  387.9 4.6 %merge.17 = bf16[4,608,128]{2,1,0:T(8,128)(2,1)} custom-call(s32[4]{0:T(128)} %pad_add_fusion.5.refs_0_, bf16[4,608,128]{2,1,0:T(8,128)(2,1)} %merge.9.refs_1_, bf16[4,608,128]{2,1,0:T(8,128)(2,1)} %collective-permute-done.22.refs_2_, bf16[4,608,128]{2,1,0:T(8,128)(2,1)} %collective-permute-done.25.refs_3_, bf16[4,608,128]{2,1,0:T(8,128)(2,1)} %copy-done.4), custom_call_target="tpu_custom_call" | custom-call | tf_op jit(solution)/shard_map/merge/pallas_call | solution.py:218
  398.2 9.1 %write_pages.1 = (bf16[12,128,8,128]{3,2,1,0:T(8,128)(2,1)}, bf16[12,128,8,128]{3,2,1,0:T(8,128)(2,1)}) custom-call(s32[12]{0:T(128)S(1)} %convert_element_type.45.fresh_ref, s32[12]{0:T(128)S(1)} %fusion.2.index_ref, bf16[12,128,8,128]{3,2,1,0:T(8,128)(2,1)S(1)} %copy-done.2, bf16[12,128,8,128]{3,2,1,0:T(8,128)(2,1)S(1)} %copy-done.1, ...), custom_call_target="tpu_custom_call" | custom-call | tf_op jit(solution)/shard_map/write_pages/pallas_call | solution.py:249
  417.2 5.7 %project.1 = bf16[288,2048]{1,0:T(8,128)(2,1)} custom-call(s32[2]{0:T(128)S(1)} %pad_add_fusion.4.refs_0_, bf16[4,288,128]{2,1,0:T(8,128)(2,1)S(1)} %get-tuple-element.68.refs_1_, bf16[4,288,128]{2,1,0:T(8,128)(2,1)S(1)} %copy-done.9, bf16[4,288,128]{2,1,0:T(8,128)(2,1)S(1)} %copy-done.13, bf16[4,288,128]{2,1,0:T(8,128)(2,1)S(1)} %copy-done.11, ...), custom_call_target="tpu_custom_call" | custom-call | tf_op jit(solution)/shard_map/project/pallas_call | solution.py:409
  (201 shorter events, 118.7 us)
Async XLA Ops:
  7.2 364.8 %all-gather.5.cloned.1.call-start = ((), (), s32[]{:S(2)}) async-start(), calls=%async_computation | async-start | bytes 10027008 | tf_op jit(solution)/shard_map/all_gather | solution.py:505
  14.8 360.3 %all-gather.7.cloned.1.call-start = ((), (), s32[]{:S(2)}) async-start(), calls=%async_computation.1 | async-start | bytes 10027008 | tf_op jit(solution)/shard_map/all_gather | solution.py:506
  15.6 395.3 %all-gather.9.cloned.1.call-start = ((), (), s32[]{:S(2)}) async-start(), calls=%async_computation.2 | async-start | bytes 8912896 | tf_op jit(solution)/shard_map/all_gather | solution.py:509
  21.5 35.3 %collective-permute-start.2 = (bf16[4,576,128]{2,1,0:T(8,128)(2,1)S(1)}, bf16[4,576,128]{2,1,0:T(8,128)(2,1)S(1)}, u32[]{:S(2)}, u32[]{:S(2)}) collective-permute-start(bf16[4,576,128]{2,1,0:T(8,128)(2,1)S(1)} %maximum_select_fusion.refs_5_.refs_0_), channel_id=1, source_target_pairs={{0,4},{1,5},{2,6},{3,7},{4,8},{5,9},{6,10},{7,11},{8,12},{9,13},{1... | collective-permute-start | bytes 1769480 | tf_op jit(solution)/shard_map/ppermute | solution.py:271
  25.0 36.2 %collective-permute-start.4 = (bf16[4,576,128]{2,1,0:T(8,128)(2,1)S(1)}, bf16[4,576,128]{2,1,0:T(8,128)(2,1)S(1)}, u32[]{:S(2)}, u32[]{:S(2)}) collective-permute-start(bf16[4,576,128]{2,1,0:T(8,128)(2,1)S(1)} %maximum_select_fusion.refs_5_.refs_0_), channel_id=1, source_target_pairs={{4,0},{5,1},{6,2},{7,3},{8,4},{9,5},{10,6},{11,7},{12,8},{13,9},{1... | collective-permute-start | bytes 1769480 | tf_op jit(solution)/shard_map/ppermute | solution.py:271
  56.8 38.2 %collective-permute-start.6 = (bf16[4,576,128]{2,1,0:T(8,128)(2,1)S(1)}, bf16[4,576,128]{2,1,0:T(8,128)(2,1)S(1)}, u32[]{:S(2)}, u32[]{:S(2)}) collective-permute-start(bf16[4,576,128]{2,1,0:T(8,128)(2,1)S(1)} %collective-permute-done.2.refs_7_), channel_id=1, source_target_pairs={{4,8},{5,9},{6,10},{7,11},{8,12},{9,13},{10,14},{11,15},{20,24},{2... | collective-permute-start | bytes 1769480 | tf_op jit(solution)/shard_map/ppermute | solution.py:271
  61.2 39.0 %collective-permute-start.8 = (bf16[4,576,128]{2,1,0:T(8,128)(2,1)S(1)}, bf16[4,576,128]{2,1,0:T(8,128)(2,1)S(1)}, u32[]{:S(2)}, u32[]{:S(2)}) collective-permute-start(bf16[4,576,128]{2,1,0:T(8,128)(2,1)S(1)} %collective-permute-done.4.refs_9_), channel_id=1, source_target_pairs={{4,0},{5,1},{6,2},{7,3},{8,4},{9,5},{10,6},{11,7},{20,16},{21,17},... | collective-permute-start | bytes 1769480 | tf_op jit(solution)/shard_map/ppermute | solution.py:271
  63.2 52.8 %collective-permute-start.1 = (bf16[4,576,128]{2,1,0:T(8,128)(2,1)S(1)}, bf16[4,576,128]{2,1,0:T(8,128)(2,1)S(1)}, u32[]{:S(2)}, u32[]{:S(2)}) collective-permute-start(bf16[4,576,128]{2,1,0:T(8,128)(2,1)S(1)} %maximum_select_fusion.refs_5_.refs_0_), channel_id=1, source_target_pairs={{0,2},{1,3},{2,0},{3,1},{4,6},{5,7},{6,4},{7,5},{8,10},{9,11},{10,... | collective-permute-start | bytes 1769480 | tf_op jit(solution)/shard_map/ppermute | solution.py:265
  63.7 53.0 %collective-permute-start.3 = (bf16[4,576,128]{2,1,0:T(8,128)(2,1)S(1)}, bf16[4,576,128]{2,1,0:T(8,128)(2,1)S(1)}, u32[]{:S(2)}, u32[]{:S(2)}) collective-permute-start(bf16[4,576,128]{2,1,0:T(8,128)(2,1)S(1)} %collective-permute-done.2.refs_7_), channel_id=1, source_target_pairs={{4,6},{5,7},{6,4},{7,5},{8,10},{9,11},{10,8},{11,9},{12,14},{13,15... | collective-permute-start | bytes 1769480 | tf_op jit(solution)/shard_map/ppermute | solution.py:291
  95.0 25.4 %collective-permute-start.10 = (bf16[4,576,128]{2,1,0:T(8,128)(2,1)S(1)}, bf16[4,576,128]{2,1,0:T(8,128)(2,1)S(1)}, u32[]{:S(2)}, u32[]{:S(2)}) collective-permute-start(bf16[4,576,128]{2,1,0:T(8,128)(2,1)S(1)} %collective-permute-done.6.refs_11_), channel_id=1, source_target_pairs={{8,12},{9,13},{10,14},{11,15},{24,28},{25,29},{26,30},{27,31}} | collective-permute-start | bytes 1769480 | tf_op jit(solution)/shard_map/ppermute | solution.py:271
  100.2 20.9 %collective-permute-start.12 = (bf16[4,576,128]{2,1,0:T(8,128)(2,1)S(1)}, bf16[4,576,128]{2,1,0:T(8,128)(2,1)S(1)}, u32[]{:S(2)}, u32[]{:S(2)}) collective-permute-start(bf16[4,576,128]{2,1,0:T(8,128)(2,1)S(1)} %collective-permute-done.8.refs_13_), channel_id=1, source_target_pairs={{4,0},{5,1},{6,2},{7,3},{20,16},{21,17},{22,18},{23,19}} | collective-permute-start | bytes 1769480 | tf_op jit(solution)/shard_map/ppermute | solution.py:271
  116.7 24.7 %collective-permute-start.9 = (bf16[4,576,128]{2,1,0:T(8,128)(2,1)S(1)}, bf16[4,576,128]{2,1,0:T(8,128)(2,1)S(1)}, u32[]{:S(2)}, u32[]{:S(2)}) collective-permute-start(bf16[4,576,128]{2,1,0:T(8,128)(2,1)S(1)} %collective-permute-done.8.refs_13_), channel_id=1, source_target_pairs={{0,2},{1,3},{2,0},{3,1},{4,6},{5,7},{6,4},{7,5},{16,18},{17,19},{1... | collective-permute-start | bytes 1769480 | tf_op jit(solution)/shard_map/ppermute | solution.py:293
  120.4 21.0 %collective-permute-start.11 = (bf16[4,576,128]{2,1,0:T(8,128)(2,1)S(1)}, bf16[4,576,128]{2,1,0:T(8,128)(2,1)S(1)}, u32[]{:S(2)}, u32[]{:S(2)}) collective-permute-start(bf16[4,576,128]{2,1,0:T(8,128)(2,1)S(1)} %collective-permute-done.10.refs_15_), channel_id=1, source_target_pairs={{12,14},{13,15},{14,12},{15,13},{28,30},{29,31},{30,28},{31,29}} | collective-permute-start | bytes 1769480 | tf_op jit(solution)/shard_map/ppermute | solution.py:291
  121.2 20.3 %collective-permute-start.13 = (bf16[4,576,128]{2,1,0:T(8,128)(2,1)S(1)}, bf16[4,576,128]{2,1,0:T(8,128)(2,1)S(1)}, u32[]{:S(2)}, u32[]{:S(2)}) collective-permute-start(bf16[4,576,128]{2,1,0:T(8,128)(2,1)S(1)} %collective-permute-done.12.refs_17_), channel_id=1, source_target_pairs={{0,2},{1,3},{2,0},{3,1},{16,18},{17,19},{18,16},{19,17}} | collective-permute-start | bytes 1769480 | tf_op jit(solution)/shard_map/ppermute | solution.py:293
  143.3 40.2 %collective-permute-start.30 = (bf16[1024,256]{1,0:T(8,128)(2,1)}, bf16[1024,256]{1,0:T(8,128)(2,1)}, u32[]{:S(2)}, u32[]{:S(2)}) collective-permute-start(bf16[1024,256]{1,0:T(8,128)(2,1)} %collective-permute-done.29), channel_id=1, source_target_pairs={{0,8},{1,9},{2,10},{3,11},{4,12},{5,13},{6,14},{7,15},{8,0},{9,1},... | collective-permute-start | bytes 1572872 | tf_op jit(solution)/shard_map/ppermute | solution.py:495
  246.0 24.7 %collective-permute-start.19 = (bf16[4,608,128]{2,1,0:T(8,128)(2,1)}, bf16[4,608,128]{2,1,0:T(8,128)(2,1)}, u32[]{:S(2)}, u32[]{:S(2)}) collective-permute-start(bf16[4,608,128]{2,1,0:T(8,128)(2,1)} %get-tuple-element.53), channel_id=1, source_target_pairs={{0,2},{1,3},{2,0},{3,1},{4,6},{5,7},{6,4},{7,5},{8,10},{9,11},{10,... | collective-permute-start | bytes 1867784 | tf_op jit(solution)/shard_map/ppermute | solution.py:265
  255.5 41.1 %collective-permute-start.17 = (bf16[4,608,128]{2,1,0:T(8,128)(2,1)}, bf16[4,608,128]{2,1,0:T(8,128)(2,1)}, u32[]{:S(2)}, u32[]{:S(2)}) collective-permute-start(bf16[4,608,128]{2,1,0:T(8,128)(2,1)} %get-tuple-element.49), channel_id=1, source_target_pairs={{0,2},{1,3},{2,0},{3,1},{4,6},{5,7},{6,4},{7,5},{8,10},{9,11},{10,... | collective-permute-start | bytes 1867784 | tf_op jit(solution)/shard_map/ppermute | solution.py:265
  255.6 63.5 %collective-permute-start.18 = (bf16[4,608,128]{2,1,0:T(8,128)(2,1)}, bf16[4,608,128]{2,1,0:T(8,128)(2,1)}, u32[]{:S(2)}, u32[]{:S(2)}) collective-permute-start(bf16[4,608,128]{2,1,0:T(8,128)(2,1)} %get-tuple-element.51), channel_id=1, source_target_pairs={{0,2},{1,3},{2,0},{3,1},{4,6},{5,7},{6,4},{7,5},{8,10},{9,11},{10,... | collective-permute-start | bytes 1867784 | tf_op jit(solution)/shard_map/ppermute | solution.py:265
  274.3 48.5 %collective-permute-start.20 = (bf16[4,608,128]{2,1,0:T(8,128)(2,1)}, bf16[4,608,128]{2,1,0:T(8,128)(2,1)}, u32[]{:S(2)}, u32[]{:S(2)}) collective-permute-start(bf16[4,608,128]{2,1,0:T(8,128)(2,1)} %merge.12.refs_1_), channel_id=1, source_target_pairs={{0,4},{1,5},{2,6},{3,7},{16,20},{17,21},{18,22},{19,23}} | collective-permute-start | bytes 1867784 | tf_op jit(solution)/shard_map/ppermute | solution.py:271
  300.3 35.4 %collective-permute-start.23 = (bf16[4,608,128]{2,1,0:T(8,128)(2,1)}, bf16[4,608,128]{2,1,0:T(8,128)(2,1)}, u32[]{:S(2)}, u32[]{:S(2)}) collective-permute-start(bf16[4,608,128]{2,1,0:T(8,128)(2,1)} %merge.10.refs_1_), channel_id=1, source_target_pairs={{12,8},{13,9},{14,10},{15,11},{28,24},{29,25},{30,26},{31,27}} | collective-permute-start | bytes 1867784 | tf_op jit(solution)/shard_map/ppermute | solution.py:271
  326.6 25.8 %collective-permute-start.21 = (bf16[4,608,128]{2,1,0:T(8,128)(2,1)}, bf16[4,608,128]{2,1,0:T(8,128)(2,1)}, u32[]{:S(2)}, u32[]{:S(2)}) collective-permute-start(bf16[4,608,128]{2,1,0:T(8,128)(2,1)} %merge.13), channel_id=1, source_target_pairs={{0,4},{1,5},{2,6},{3,7},{4,8},{5,9},{6,10},{7,11},{16,20},{17,21},... | collective-permute-start | bytes 1867784 | tf_op jit(solution)/shard_map/ppermute | solution.py:271
  340.8 27.5 %collective-permute-start.16 = (bf16[4,608,128]{2,1,0:T(8,128)(2,1)}, bf16[4,608,128]{2,1,0:T(8,128)(2,1)}, u32[]{:S(2)}, u32[]{:S(2)}) collective-permute-start(bf16[4,608,128]{2,1,0:T(8,128)(2,1)} %get-tuple-element.47), channel_id=1, source_target_pairs={{0,2},{1,3},{2,0},{3,1},{4,6},{5,7},{6,4},{7,5},{8,10},{9,11},{10,... | collective-permute-start | bytes 1867784 | tf_op jit(solution)/shard_map/ppermute | solution.py:265
  356.2 31.7 %collective-permute-start.22 = (bf16[4,608,128]{2,1,0:T(8,128)(2,1)}, bf16[4,608,128]{2,1,0:T(8,128)(2,1)}, u32[]{:S(2)}, u32[]{:S(2)}) collective-permute-start(bf16[4,608,128]{2,1,0:T(8,128)(2,1)} %merge.14), channel_id=1, source_target_pairs={{0,4},{1,5},{2,6},{3,7},{4,8},{5,9},{6,10},{7,11},{8,12},{9,13},{1... | collective-permute-start | bytes 1867784 | tf_op jit(solution)/shard_map/ppermute | solution.py:271
  361.8 26.1 %collective-permute-start.25 = (bf16[4,608,128]{2,1,0:T(8,128)(2,1)}, bf16[4,608,128]{2,1,0:T(8,128)(2,1)}, u32[]{:S(2)}, u32[]{:S(2)}) collective-permute-start(bf16[4,608,128]{2,1,0:T(8,128)(2,1)} %merge.16), channel_id=1, source_target_pairs={{4,0},{5,1},{6,2},{7,3},{8,4},{9,5},{10,6},{11,7},{12,8},{13,9},{1... | collective-permute-start | bytes 1867784 | tf_op jit(solution)/shard_map/ppermute | solution.py:271
  (51 other events, 714.2 us)
Sparse Core Ops, SparseCore 0:
  15.0 118.6 all-gather.4
  136.0 98.3 all-gather.6
  236.6 102.5 all-gather.8

commit v3 on v2

--- a/solution.py
+++ b/solution.py
@@ -491,7 +491,6 @@
         found = block
         for s in range(1, groups):
             moved = lax.ppermute(block, "heads", [(i, (i + s) % groups) for i in range(groups)])
-            moved, _ = lax.optimization_barrier((moved, q_list))
             moved = lax.ppermute(
                 moved,
                 "pages",
@@ -538,7 +537,6 @@
     k_heads = jnp.concatenate([k_mine, swap(k_other, 1)], axis=1)
     v_heads = jnp.concatenate([v_mine, swap(v_other, 1)], axis=1)
 
-    q_list, k_heads, v_heads = lax.optimization_barrier((q_list, k_heads, v_heads))
     unit = math.gcd(span_len, tok_dev)
     line = page_devs // 4
     line_at, across = device_at // 4, (device_at // 2) % 2

time: 432 us -> 413 us (0.956)
  waiting for transfers between devices: 195 us -> 173 us
  local copies, waits for them, and re-layouts: 47.8 us -> 39.5 us
  Pallas kernels: 87.5 us -> 93.1 us
    ppermute x8, waiting for transfers between devices: 51.7 us -> 18.3 us  [swap(): return lax.ppermute(x, 'pages', [(p, p ^ bit) for p in range(devs)])]
    ppermute x12, waiting for transfers between devices: 71.1 us -> 87 us  [shift(): return lax.ppermute(x, 'pages', moves)]
    unnamed x87 -> x39, local copies, waits for them, and re-layouts: 30.8 us -> 21.8 us
    ppermute x8, starting transfers between devices: 14.3 us -> 5.61 us  [swap(): return lax.ppermute(x, 'pages', [(p, p ^ bit) for p in range(devs)])]
    ppermute x12, starting transfers between devices: 34.4 us -> 42.7 us  [shift(): return lax.ppermute(x, 'pages', moves)]
    ppermute x1, waiting for transfers between devices: 40.2 us -> 34.6 us  [to_owner(): lax.ppermute(moved, 'pages', [(p, (p - s * share) % page_devs) for p in r...]
  transfers between devices with their start and end apart: 34 -> 34, of which waited for: 13 -> 14; matrix products, arithmetic and copies ran while one was open for 10% -> 11% of each run, Pallas kernels for 19% -> 21%
where the time goes in v3:
time: 413 us; the launch traced here: 409 us
  waiting for transfers between devices  173 us (42%)
  Pallas kernels  93.1 us (23%)
  starting transfers between devices  67.3 us (16%)
  local copies, waits for them, and re-layouts  39.5 us (10%)
  other arithmetic  22.5 us (5%)
  between operations  14.2 us (3%)
    ppermute x12, waiting for transfers between devices, shift(): return lax.ppermute(x, 'pages', moves)  87 us
    ppermute x12, starting transfers between devices, shift(): return lax.ppermute(x, 'pages', moves)  42.7 us
    ppermute x1, waiting for transfers between devices, to_owner(): lax.ppermute(moved, 'pages', [(p, (p - s * share) % page_devs) for p in r...  34.6 us
    pallas_call x9, Pallas kernels, merge(): pl.pallas_call(lambda *refs: merge_kernel(unit, part_len, scale2, *refs),...  34.2 us
    pallas_call x1, Pallas kernels, cached_attention(): pl.pallas_call(lambda *refs: cached_kernel(unit, stat_unit, span, scale2,...  33.8 us
    unnamed x39, local copies, waits for them, and re-layouts  21.8 us
    ppermute x8, waiting for transfers between devices, swap(): return lax.ppermute(x, 'pages', [(p, p ^ bit) for p in range(devs)])  18.3 us
    ppermute x3, waiting for transfers between devices, gather_lines(): lax.ppermute(down, 'pages', cross_down)  17.3 us
  transfers between devices with their start and end apart: 34, of which 14 were waited for; matrix products, arithmetic and copies ran while one was open for 11% of the time, Pallas kernels for 21%

profile of v3, /device:TPU:12, one launch (start us, length us, event | category | flops | bytes accessed | tf_op | source)
XLA Modules:
  0.0 409.1 jit_solution(17014429842818624267)
XLA Ops:
  16.3 12.2 %collective-permute-done.29 = bf16[1024,256]{1,0:T(8,128)(2,1)S(1)} collective-permute-done((bf16[1024,256]{1,0:T(8,128)(2,1)S(1)}, bf16[1024,256]{1,0:T(8,128)(2,1)S(1)}, u32[]{:S(2)}, u32[]{:S(2)}) %collective-permute-start.29) | collective-permute-done | bytes 524320 | tf_op jit(solution)/shard_map/ppermute | solution.py:493
  31.0 34.6 %collective-permute-done.30 = bf16[1024,256]{1,0:T(8,128)(2,1)S(1)} collective-permute-done((bf16[1024,256]{1,0:T(8,128)(2,1)S(1)}, bf16[1024,256]{1,0:T(8,128)(2,1)S(1)}, u32[]{:S(2)}, u32[]{:S(2)}) %collective-permute-start.30) | collective-permute-done | bytes 524320 | tf_op jit(solution)/shard_map/ppermute | solution.py:494
  74.7 3.8 collective-permute-start.2
  82.2 7.2 %constant_dynamic-slice_fusion.5 = (bf16[12,128,4,128]{3,2,1,0:T(4,128)(2,1)}, bf16[12,128,4,128]{3,2,1,0:T(4,128)(2,1)}, bf16[12,128,4,128]{3,2,1,0:T(4,128)(2,1)S(1)}, bf16[12,128,4,128]{3,2,1,0:T(4,128)(2,1)}) fusion(bf16[12,128,8,128]{3,2,1,0:T(8,128)(2,1)S(1)} %copy-done.1, s32[]{:T(128)S(6)} %select_n.175, s32[]{:T(128)S(6)} %select_n.176, ...), kind=kLoop, calls=%fused_computation.47 | loop fusion | bytes 12582920 | tf_op jit(solution)/shard_map/dynamic-slice.4
  91.0 3.7 copy.62
  95.8 20.7 %collective-permute-done.2.refs_7_ = bf16[4,576,128]{2,1,0:T(8,128)(2,1)} collective-permute-done((bf16[4,576,128]{2,1,0:T(8,128)(2,1)}, bf16[4,576,128]{2,1,0:T(8,128)(2,1)}, u32[]{:S(2)}, u32[]{:S(2)}) %collective-permute-start.2) | collective-permute-done | bytes 589856 | tf_op jit(solution)/shard_map/ppermute | solution.py:271
  116.5 5.9 %collective-permute-start.6 = (bf16[4,576,128]{2,1,0:T(8,128)(2,1)}, bf16[4,576,128]{2,1,0:T(8,128)(2,1)}, u32[]{:S(2)}, u32[]{:S(2)}) collective-permute-start(bf16[4,576,128]{2,1,0:T(8,128)(2,1)} %collective-permute-done.2.refs_7_), channel_id=1, source_target_pairs={{4,8},{5,9},{6,10},{7,11},{8,12},{9,13},{10,14},{11,15},{20,24},{2... | collective-permute-start | bytes 1769480 | tf_op jit(solution)/shard_map/ppermute | solution.py:271
  127.0 7.1 %collective-permute-done.6.refs_11_ = bf16[4,576,128]{2,1,0:T(8,128)(2,1)} collective-permute-done((bf16[4,576,128]{2,1,0:T(8,128)(2,1)}, bf16[4,576,128]{2,1,0:T(8,128)(2,1)}, u32[]{:S(2)}, u32[]{:S(2)}) %collective-permute-start.6) | collective-permute-done | bytes 589856 | tf_op jit(solution)/shard_map/ppermute | solution.py:271
  135.5 11.4 %collective-permute-done.8.refs_13_ = bf16[4,576,128]{2,1,0:T(8,128)(2,1)} collective-permute-done((bf16[4,576,128]{2,1,0:T(8,128)(2,1)}, bf16[4,576,128]{2,1,0:T(8,128)(2,1)}, u32[]{:S(2)}, u32[]{:S(2)}) %collective-permute-start.8) | collective-permute-done | bytes 589856 | tf_op jit(solution)/shard_map/ppermute | solution.py:271
  152.1 3.7 copy.61
  171.3 3.9 pad_maximum_fusion.refs_19_
  178.5 17.3 %collective-permute-done.9.refs_14_ = bf16[4,576,128]{2,1,0:T(8,128)(2,1)} collective-permute-done((bf16[4,576,128]{2,1,0:T(8,128)(2,1)}, bf16[4,576,128]{2,1,0:T(8,128)(2,1)}, u32[]{:S(2)}, u32[]{:S(2)}) %collective-permute-start.9) | collective-permute-done | bytes 589856 | tf_op jit(solution)/shard_map/ppermute | solution.py:293
  195.9 33.8 %cached_attention.1 = (bf16[4,608,128]{2,1,0:T(8,128)(2,1)}, bf16[4,608,128]{2,1,0:T(8,128)(2,1)}, bf16[4,608,128]{2,1,0:T(8,128)(2,1)}, bf16[4,608,128]{2,1,0:T...) custom-call(s32[22]{0:T(128)} %stack.197.refs_0_, ...), custom_call_target="tpu_custom_call" | custom-call | flops 40000000000 | bytes 20971520 | tf_op jit(solution)/shard_map/cached_attention/pallas_call | solution.py:155
  231.9 9.0 %collective-permute-done.17.refs_2_ = bf16[4,608,128]{2,1,0:T(8,128)(2,1)} collective-permute-done((bf16[4,608,128]{2,1,0:T(8,128)(2,1)}, bf16[4,608,128]{2,1,0:T(8,128)(2,1)}, u32[]{:S(2)}, u32[]{:S(2)}) %collective-permute-start.17) | collective-permute-done | bytes 622624 | tf_op jit(solution)/shard_map/ppermute | solution.py:265
  240.9 3.7 merge.10.refs_1_
  246.2 6.9 %collective-permute-done.19.refs_2_ = bf16[4,608,128]{2,1,0:T(8,128)(2,1)} collective-permute-done((bf16[4,608,128]{2,1,0:T(8,128)(2,1)}, bf16[4,608,128]{2,1,0:T(8,128)(2,1)}, u32[]{:S(2)}, u32[]{:S(2)}) %collective-permute-start.19) | collective-permute-done | bytes 622624 | tf_op jit(solution)/shard_map/ppermute | solution.py:265
  253.2 3.7 merge.12.refs_1_
  263.5 3.7 merge.15
  268.6 43.8 %collective-permute-done.20.refs_2_ = bf16[4,608,128]{2,1,0:T(8,128)(2,1)} collective-permute-done((bf16[4,608,128]{2,1,0:T(8,128)(2,1)}, bf16[4,608,128]{2,1,0:T(8,128)(2,1)}, u32[]{:S(2)}, u32[]{:S(2)}) %collective-permute-start.20) | collective-permute-done | bytes 622624 | tf_op jit(solution)/shard_map/ppermute | solution.py:271
  324.8 15.6 %collective-permute-start.25 = (bf16[4,608,128]{2,1,0:T(8,128)(2,1)}, bf16[4,608,128]{2,1,0:T(8,128)(2,1)}, u32[]{:S(2)}, u32[]{:S(2)}) collective-permute-start(bf16[4,608,128]{2,1,0:T(8,128)(2,1)} %merge.16), channel_id=1, source_target_pairs={{4,0},{5,1},{6,2},{7,3},{8,4},{9,5},{10,6},{11,7},{12,8},{13,9},{1... | collective-permute-start | bytes 1867784 | tf_op jit(solution)/shard_map/ppermute | solution.py:271
  359.7 9.4 %fresh_attention.1.refs_4_ = bf16[4,608,128]{2,1,0:T(8,128)(2,1)S(1)} custom-call(bf16[4,576,128]{2,1,0:T(8,128)(2,1)} %maximum_select_fusion.refs_5_.refs_0_, bf16[4,1152,128]{2,1,0:T(8,128)(2,1)S(1)} %bitcast.58, bf16[4,1152,128]{2,1,0:T(8,128)(2,1)S(1)} %bitcast.59, s32[2,576]{1,0:T(2,128)S(1)} %pad_add_fusion.refs_3_, s32[1152,1]{1,0:T(8,128)S(1)} %copy-done.5), custom_call_target="tpu_custom_call" | custom-call | tf_op jit(solution)/shard_map/fresh_attention/pallas_call | solution.py:358
  370.0 4.6 %merge.17 = bf16[4,608,128]{2,1,0:T(8,128)(2,1)} custom-call(s32[4]{0:T(128)} %pad_add_fusion.5.refs_0_, bf16[4,608,128]{2,1,0:T(8,128)(2,1)} %merge.9.refs_1_, bf16[4,608,128]{2,1,0:T(8,128)(2,1)} %collective-permute-done.22.refs_2_, bf16[4,608,128]{2,1,0:T(8,128)(2,1)} %collective-permute-done.25.refs_3_, bf16[4,608,128]{2,1,0:T(8,128)(2,1)} %copy-done.4), custom_call_target="tpu_custom_call" | custom-call | tf_op jit(solution)/shard_map/merge/pallas_call | solution.py:218
  380.9 8.9 %write_pages.1 = (bf16[12,128,8,128]{3,2,1,0:T(8,128)(2,1)}, bf16[12,128,8,128]{3,2,1,0:T(8,128)(2,1)}) custom-call(s32[12]{0:T(128)S(1)} %convert_element_type.45.fresh_ref, s32[12]{0:T(128)S(1)} %fusion.2.index_ref, bf16[12,128,8,128]{3,2,1,0:T(8,128)(2,1)S(1)} %copy-done.2, bf16[12,128,8,128]{3,2,1,0:T(8,128)(2,1)S(1)} %copy-done.1, ...), custom_call_target="tpu_custom_call" | custom-call | tf_op jit(solution)/shard_map/write_pages/pallas_call | solution.py:249
  395.8 6.8 %project.1 = bf16[288,2048]{1,0:T(8,128)(2,1)} custom-call(s32[2]{0:T(128)S(1)} %pad_add_fusion.4.refs_0_, bf16[4,288,128]{2,1,0:T(8,128)(2,1)S(1)} %get-tuple-element.34.refs_1_, bf16[4,288,128]{2,1,0:T(8,128)(2,1)} %collective-permute-done.26.refs_2_, bf16[4,288,128]{2,1,0:T(8,128)(2,1)} %collective-permute-done.27.refs_3_, ...), custom_call_target="tpu_custom_call" | custom-call | tf_op jit(solution)/shard_map/project/pallas_call | solution.py:409
  (153 shorter events, 113.3 us)
Async XLA Ops:
  7.2 346.1 %all-gather.5.cloned.1.call-start = ((), (), s32[]{:S(2)}) async-start(), calls=%async_computation | async-start | bytes 10027008 | tf_op jit(solution)/shard_map/all_gather | solution.py:504
  13.8 342.6 %all-gather.7.cloned.1.call-start = ((), (), s32[]{:S(2)}) async-start(), calls=%async_computation.1 | async-start | bytes 10027008 | tf_op jit(solution)/shard_map/all_gather | solution.py:505
  14.5 375.3 %all-gather.9.cloned.1.call-start = ((), (), s32[]{:S(2)}) async-start(), calls=%async_computation.2 | async-start | bytes 8912896 | tf_op jit(solution)/shard_map/all_gather | solution.py:508
  28.4 37.2 %collective-permute-start.30 = (bf16[1024,256]{1,0:T(8,128)(2,1)S(1)}, bf16[1024,256]{1,0:T(8,128)(2,1)S(1)}, u32[]{:S(2)}, u32[]{:S(2)}) collective-permute-start(bf16[1024,256]{1,0:T(8,128)(2,1)S(1)} %collective-permute-done.29), channel_id=1, source_target_pairs={{0,8},{1,9},{2,10},{3,11},{4,12},{5,13},{6,14},{7,15},{8,0},{9,1},... | collective-permute-start | bytes 1572872 | tf_op jit(solution)/shard_map/ppermute | solution.py:494
  74.7 41.8 %collective-permute-start.2 = (bf16[4,576,128]{2,1,0:T(8,128)(2,1)}, bf16[4,576,128]{2,1,0:T(8,128)(2,1)}, u32[]{:S(2)}, u32[]{:S(2)}) collective-permute-start(bf16[4,576,128]{2,1,0:T(8,128)(2,1)} %maximum_select_fusion.refs_5_.refs_0_), channel_id=1, source_target_pairs={{0,4},{1,5},{2,6},{3,7},{4,8},{5,9},{6,10},{7,11},{8,12},{9,13},{1... | collective-permute-start | bytes 1769480 | tf_op jit(solution)/shard_map/ppermute | solution.py:271
  78.5 43.9 %collective-permute-start.4 = (bf16[4,576,128]{2,1,0:T(8,128)(2,1)}, bf16[4,576,128]{2,1,0:T(8,128)(2,1)}, u32[]{:S(2)}, u32[]{:S(2)}) collective-permute-start(bf16[4,576,128]{2,1,0:T(8,128)(2,1)} %maximum_select_fusion.refs_5_.refs_0_), channel_id=1, source_target_pairs={{4,0},{5,1},{6,2},{7,3},{8,4},{9,5},{10,6},{11,7},{12,8},{13,9},{1... | collective-permute-start | bytes 1769480 | tf_op jit(solution)/shard_map/ppermute | solution.py:271
  91.0 69.4 %collective-permute-start.14 = (bf16[4,12,128,128]{3,2,1,0:T(8,128)(2,1)}, bf16[4,12,128,128]{3,2,1,0:T(8,128)(2,1)}, u32[]{:S(2)}, u32[]{:S(2)}) collective-permute-start(bf16[4,12,128,128]{3,2,1,0:T(8,128)(2,1)} %bitcast.52), channel_id=1, source_target_pairs={{0,1},{1,0},{2,3},{3,2},{4,5},{5,4},{6,7},{7,6},{8,9},{9,8},{10,11... | collective-permute-start | bytes 4718600 | tf_op jit(solution)/shard_map/ppermute | solution.py:265
  94.8 67.2 %collective-permute-start.15 = (bf16[4,12,128,128]{3,2,1,0:T(8,128)(2,1)}, bf16[4,12,128,128]{3,2,1,0:T(8,128)(2,1)}, u32[]{:S(2)}, u32[]{:S(2)}) collective-permute-start(bf16[4,12,128,128]{3,2,1,0:T(8,128)(2,1)} %bitcast.65), channel_id=1, source_target_pairs={{0,1},{1,0},{2,3},{3,2},{4,5},{5,4},{6,7},{7,6},{8,9},{9,8},{10,11... | collective-permute-start | bytes 4718600 | tf_op jit(solution)/shard_map/ppermute | solution.py:265
  95.3 29.3 %collective-permute-start.1 = (bf16[4,576,128]{2,1,0:T(8,128)(2,1)}, bf16[4,576,128]{2,1,0:T(8,128)(2,1)}, u32[]{:S(2)}, u32[]{:S(2)}) collective-permute-start(bf16[4,576,128]{2,1,0:T(8,128)(2,1)} %maximum_select_fusion.refs_5_.refs_0_), channel_id=1, source_target_pairs={{0,2},{1,3},{2,0},{3,1},{4,6},{5,7},{6,4},{7,5},{8,10},{9,11},{10,... | collective-permute-start | bytes 1769480 | tf_op jit(solution)/shard_map/ppermute | solution.py:265
  122.4 24.5 %collective-permute-start.8 = (bf16[4,576,128]{2,1,0:T(8,128)(2,1)}, bf16[4,576,128]{2,1,0:T(8,128)(2,1)}, u32[]{:S(2)}, u32[]{:S(2)}) collective-permute-start(bf16[4,576,128]{2,1,0:T(8,128)(2,1)} %collective-permute-done.4.refs_9_), channel_id=1, source_target_pairs={{4,0},{5,1},{6,2},{7,3},{8,4},{9,5},{10,6},{11,7},{20,16},{21,17},... | collective-permute-start | bytes 1769480 | tf_op jit(solution)/shard_map/ppermute | solution.py:271
  124.6 33.1 %collective-permute-start.3 = (bf16[4,576,128]{2,1,0:T(8,128)(2,1)}, bf16[4,576,128]{2,1,0:T(8,128)(2,1)}, u32[]{:S(2)}, u32[]{:S(2)}) collective-permute-start(bf16[4,576,128]{2,1,0:T(8,128)(2,1)} %collective-permute-done.2.refs_7_), channel_id=1, source_target_pairs={{4,6},{5,7},{6,4},{7,5},{8,10},{9,11},{10,8},{11,9},{12,14},{13,15... | collective-permute-start | bytes 1769480 | tf_op jit(solution)/shard_map/ppermute | solution.py:291
  134.0 31.0 %collective-permute-start.10 = (bf16[4,576,128]{2,1,0:T(8,128)(2,1)}, bf16[4,576,128]{2,1,0:T(8,128)(2,1)}, u32[]{:S(2)}, u32[]{:S(2)}) collective-permute-start(bf16[4,576,128]{2,1,0:T(8,128)(2,1)} %collective-permute-done.6.refs_11_), channel_id=1, source_target_pairs={{8,12},{9,13},{10,14},{11,15},{24,28},{25,29},{26,30},{27,31}} | collective-permute-start | bytes 1769480 | tf_op jit(solution)/shard_map/ppermute | solution.py:271
  146.9 21.5 %collective-permute-start.12 = (bf16[4,576,128]{2,1,0:T(8,128)(2,1)}, bf16[4,576,128]{2,1,0:T(8,128)(2,1)}, u32[]{:S(2)}, u32[]{:S(2)}) collective-permute-start(bf16[4,576,128]{2,1,0:T(8,128)(2,1)} %collective-permute-done.8.refs_13_), channel_id=1, source_target_pairs={{4,0},{5,1},{6,2},{7,3},{20,16},{21,17},{22,18},{23,19}} | collective-permute-start | bytes 1769480 | tf_op jit(solution)/shard_map/ppermute | solution.py:271
  161.9 33.9 %collective-permute-start.9 = (bf16[4,576,128]{2,1,0:T(8,128)(2,1)}, bf16[4,576,128]{2,1,0:T(8,128)(2,1)}, u32[]{:S(2)}, u32[]{:S(2)}) collective-permute-start(bf16[4,576,128]{2,1,0:T(8,128)(2,1)} %collective-permute-done.8.refs_13_), channel_id=1, source_target_pairs={{0,2},{1,3},{2,0},{3,1},{4,6},{5,7},{6,4},{7,5},{16,18},{17,19},{1... | collective-permute-start | bytes 1769480 | tf_op jit(solution)/shard_map/ppermute | solution.py:293
  165.0 30.8 %collective-permute-start.11 = (bf16[4,576,128]{2,1,0:T(8,128)(2,1)}, bf16[4,576,128]{2,1,0:T(8,128)(2,1)}, u32[]{:S(2)}, u32[]{:S(2)}) collective-permute-start(bf16[4,576,128]{2,1,0:T(8,128)(2,1)} %collective-permute-done.10.refs_15_), channel_id=1, source_target_pairs={{12,14},{13,15},{14,12},{15,13},{28,30},{29,31},{30,28},{31,29}} | collective-permute-start | bytes 1769480 | tf_op jit(solution)/shard_map/ppermute | solution.py:291
  168.4 27.4 %collective-permute-start.13 = (bf16[4,576,128]{2,1,0:T(8,128)(2,1)}, bf16[4,576,128]{2,1,0:T(8,128)(2,1)}, u32[]{:S(2)}, u32[]{:S(2)}) collective-permute-start(bf16[4,576,128]{2,1,0:T(8,128)(2,1)} %collective-permute-done.12.refs_17_), channel_id=1, source_target_pairs={{0,2},{1,3},{2,0},{3,1},{16,18},{17,19},{18,16},{19,17}} | collective-permute-start | bytes 1769480 | tf_op jit(solution)/shard_map/ppermute | solution.py:293
  229.8 23.4 %collective-permute-start.19 = (bf16[4,608,128]{2,1,0:T(8,128)(2,1)}, bf16[4,608,128]{2,1,0:T(8,128)(2,1)}, u32[]{:S(2)}, u32[]{:S(2)}) collective-permute-start(bf16[4,608,128]{2,1,0:T(8,128)(2,1)} %get-tuple-element.20), channel_id=1, source_target_pairs={{0,2},{1,3},{2,0},{3,1},{4,6},{5,7},{6,4},{7,5},{8,10},{9,11},{10,... | collective-permute-start | bytes 1867784 | tf_op jit(solution)/shard_map/ppermute | solution.py:265
  231.8 28.0 %collective-permute-start.18 = (bf16[4,608,128]{2,1,0:T(8,128)(2,1)}, bf16[4,608,128]{2,1,0:T(8,128)(2,1)}, u32[]{:S(2)}, u32[]{:S(2)}) collective-permute-start(bf16[4,608,128]{2,1,0:T(8,128)(2,1)} %get-tuple-element.18), channel_id=1, source_target_pairs={{0,2},{1,3},{2,0},{3,1},{4,6},{5,7},{6,4},{7,5},{8,10},{9,11},{10,... | collective-permute-start | bytes 1867784 | tf_op jit(solution)/shard_map/ppermute | solution.py:265
  256.9 55.5 %collective-permute-start.20 = (bf16[4,608,128]{2,1,0:T(8,128)(2,1)}, bf16[4,608,128]{2,1,0:T(8,128)(2,1)}, u32[]{:S(2)}, u32[]{:S(2)}) collective-permute-start(bf16[4,608,128]{2,1,0:T(8,128)(2,1)} %merge.12.refs_1_), channel_id=1, source_target_pairs={{0,4},{1,5},{2,6},{3,7},{16,20},{17,21},{18,22},{19,23}} | collective-permute-start | bytes 1867784 | tf_op jit(solution)/shard_map/ppermute | solution.py:271
  267.2 53.9 %collective-permute-start.24 = (bf16[4,608,128]{2,1,0:T(8,128)(2,1)}, bf16[4,608,128]{2,1,0:T(8,128)(2,1)}, u32[]{:S(2)}, u32[]{:S(2)}) collective-permute-start(bf16[4,608,128]{2,1,0:T(8,128)(2,1)} %merge.15), channel_id=1, source_target_pairs={{8,4},{9,5},{10,6},{11,7},{12,8},{13,9},{14,10},{15,11},{24,20},{2... | collective-permute-start | bytes 1867784 | tf_op jit(solution)/shard_map/ppermute | solution.py:271
  316.1 26.4 %collective-permute-start.21 = (bf16[4,608,128]{2,1,0:T(8,128)(2,1)}, bf16[4,608,128]{2,1,0:T(8,128)(2,1)}, u32[]{:S(2)}, u32[]{:S(2)}) collective-permute-start(bf16[4,608,128]{2,1,0:T(8,128)(2,1)} %merge.13), channel_id=1, source_target_pairs={{0,4},{1,5},{2,6},{3,7},{4,8},{5,9},{6,10},{7,11},{16,20},{17,21},... | collective-permute-start | bytes 1867784 | tf_op jit(solution)/shard_map/ppermute | solution.py:271
  318.0 31.5 %collective-permute-start.16 = (bf16[4,608,128]{2,1,0:T(8,128)(2,1)}, bf16[4,608,128]{2,1,0:T(8,128)(2,1)}, u32[]{:S(2)}, u32[]{:S(2)}) collective-permute-start(bf16[4,608,128]{2,1,0:T(8,128)(2,1)} %get-tuple-element.14), channel_id=1, source_target_pairs={{0,2},{1,3},{2,0},{3,1},{4,6},{5,7},{6,4},{7,5},{8,10},{9,11},{10,... | collective-permute-start | bytes 1867784 | tf_op jit(solution)/shard_map/ppermute | solution.py:265
  324.8 45.1 %collective-permute-start.25 = (bf16[4,608,128]{2,1,0:T(8,128)(2,1)}, bf16[4,608,128]{2,1,0:T(8,128)(2,1)}, u32[]{:S(2)}, u32[]{:S(2)}) collective-permute-start(bf16[4,608,128]{2,1,0:T(8,128)(2,1)} %merge.16), channel_id=1, source_target_pairs={{4,0},{5,1},{6,2},{7,3},{8,4},{9,5},{10,6},{11,7},{12,8},{13,9},{1... | collective-permute-start | bytes 1867784 | tf_op jit(solution)/shard_map/ppermute | solution.py:271
  346.2 23.8 %collective-permute-start.22 = (bf16[4,608,128]{2,1,0:T(8,128)(2,1)}, bf16[4,608,128]{2,1,0:T(8,128)(2,1)}, u32[]{:S(2)}, u32[]{:S(2)}) collective-permute-start(bf16[4,608,128]{2,1,0:T(8,128)(2,1)} %merge.14), channel_id=1, source_target_pairs={{0,4},{1,5},{2,6},{3,7},{4,8},{5,9},{6,10},{7,11},{8,12},{9,13},{1... | collective-permute-start | bytes 1867784 | tf_op jit(solution)/shard_map/ppermute | solution.py:271
  (27 other events, 353.1 us)
Sparse Core Ops, SparseCore 0:
  13.9 109.3 all-gather.4
  125.5 105.3 all-gather.6
  233.1 94.6 all-gather.8

commit v4 on v3

--- a/solution.py
+++ b/solution.py
@@ -366,66 +366,53 @@
     )(q_chip, k_window, v_window, token_rows, key_cols)
 
 
-def project_kernel(groups, at_ref, *refs):
-    att_refs, w_refs = refs[: 2 * groups], refs[2 * groups : -3]
-    bias_ref, out_ref, rows_ref = refs[-3:]
+def project_kernel(at_ref, mine_ref, other_ref, w_ref, out_ref, rows_ref):
     core = at_ref[0]
     wide = rows_ref.shape[2]
 
     @pl.when(pl.program_id(0) == 0)
     def _():
-        for index, ref in enumerate(att_refs):
+        for index, ref in enumerate((mine_ref, other_ref)):
             rows_ref[index] = jnp.concatenate([ref[h] for h in range(ref.shape[0])], axis=1)
 
-    total = bias_ref[...].reshape(1, -1)
-    for s in range(groups):
-        for d in range(2):
-            feats = pl.ds(pl.multiple_of((core ^ d) * wide, wide), wide)
-            total = total + jnp.dot(
-                rows_ref[2 * s + d], w_refs[s][0, feats, :], preferred_element_type=jnp.float32
-            )
-    out_ref[...] = total.astype(jnp.bfloat16).reshape(out_ref.shape)
-
-
-def project(pieces, weights, bias, core, group_at):
-    groups = len(pieces) // 2
-    half, tok_dev, head_dim = pieces[0].shape
+    total = 0.0
+    for d in range(2):
+        feats = pl.ds(pl.multiple_of((core ^ d) * wide, wide), wide)
+        total = total + jnp.dot(
+            rows_ref[d], w_ref[0, feats, :], preferred_element_type=jnp.float32
+        )
+    out_ref[...] = total.astype(out_ref.dtype).reshape(out_ref.shape)
+
+
+def project(mine, other, weights, core, owner, groups, dtype):
+    half, tok_dev, head_dim = mine.shape
     blocks, feats, cols = weights.shape
     blocks //= groups
     wide = cols % 128 == 0
-
-    def weight_spec(s):
-        return pl.BlockSpec(
-            (1, feats, cols),
-            lambda j, at: (lax.rem(at[1] + groups - s, groups) * blocks + j, 0, 0),
-        )
-
     if wide:
         out_spec = pl.BlockSpec((tok_dev, cols), lambda j, at: (0, j))
         out_shape = (tok_dev, blocks * cols)
     else:
         out_spec = pl.BlockSpec((1, tok_dev, cols), lambda j, at: (j, 0, 0))
         out_shape = (blocks, tok_dev, cols)
+    rows_spec = pl.BlockSpec(mine.shape, lambda j, at: (0, 0, 0))
     out = pl.pallas_call(
-        lambda *refs: project_kernel(groups, *refs),
+        project_kernel,
         grid_spec=pltpu.PrefetchScalarGridSpec(
             num_scalar_prefetch=1,
             grid=(blocks,),
-            in_specs=[pl.BlockSpec(x.shape, lambda j, at: (0, 0, 0)) for x in pieces]
-            + [weight_spec(s) for s in range(groups)]
-            + [pl.BlockSpec((1, 1, cols), lambda j, at: (j, 0, 0))],
+            in_specs=[
+                rows_spec,
+                rows_spec,
+                pl.BlockSpec((1, feats, cols), lambda j, at: (at[1] * blocks + j, 0, 0)),
+            ],
             out_specs=out_spec,
-            scratch_shapes=[pltpu.VMEM((2 * groups, tok_dev, half * head_dim), jnp.bfloat16)],
+            scratch_shapes=[pltpu.VMEM((2, tok_dev, half * head_dim), jnp.bfloat16)],
         ),
-        out_shape=jax.ShapeDtypeStruct(out_shape, jnp.bfloat16),
+        out_shape=jax.ShapeDtypeStruct(out_shape, dtype),
         compiler_params=pltpu.CompilerParams(vmem_limit_bytes=40 * 2**20),
         name="project",
-    )(
-        jnp.stack([core, group_at]),
-        *pieces,
-        *[weights] * groups,
-        bias.reshape(blocks, 1, cols),
-    )
+    )(jnp.stack([core, owner]), mine, other, weights)
     return out if wide else jnp.transpose(out, (1, 0, 2)).reshape(tok_dev, blocks * cols)
 
 
@@ -483,29 +470,13 @@
     q_places = gather_lines(q_chip)
     groups = lax.axis_size("heads")
     group_at = lax.axis_index("heads")
-    share = page_devs // groups
     q_list = [q for q, _, _, _ in q_places]
-    own_share = device_at // share
-
-    def to_owner(block):
-        found = block
-        for s in range(1, groups):
-            moved = lax.ppermute(block, "heads", [(i, (i + s) % groups) for i in range(groups)])
-            moved = lax.ppermute(
-                moved,
-                "pages",
-                [(p, (p - s * share) % page_devs) for p in range(page_devs)],
-            )
-            found = jnp.where(own_share == (group_at - s) % groups, moved, found)
-        return found
-
-    weight_block = to_owner(out_weight)
     natural = Layout((0, 1, 2))
     all_k = lax.all_gather(rotated_k, "pages", axis=0, tiled=True)
     all_v = lax.all_gather(values, "pages", axis=0, tiled=True)
     all_k = with_layout_constraint(all_k, natural)
     all_v = with_layout_constraint(all_v, natural)
-    weights = lax.all_gather(weight_block, "pages", axis=0, tiled=False)
+    weights = lax.all_gather(out_weight, "pages", axis=0, tiled=False)
 
     my_slots = device_at * slot_count + jnp.arange(slot_count, dtype=jnp.int32)
     chip_slots = jnp.concatenate(
@@ -579,22 +550,17 @@
         [outs[2 * k : 2 * k + 2] for k in range(line)], merged, fresh_part
     )
     rows_of = lambda c: lax.dynamic_slice_in_dim(chip_part[:, :chip_len], c * tok_dev, tok_dev, 1)
-    own_rows, other_rows = rows_of(core), rows_of(1 - core)
-    pieces = []
-    for s in range(groups):
-        for d, rows in ((0, own_rows), (1, other_rows)):
-            if s or d:
-                rows = lax.ppermute(
-                    rows,
-                    ("heads", "pages"),
-                    [
-                        (h * page_devs + p, (h + s) % groups * page_devs + (p ^ d))
-                        for h in range(groups)
-                        for p in range(page_devs)
-                    ],
-                )
-            pieces.append(rows)
-    hidden = project(pieces, weights, out_bias, core, group_at)
+    own_rows, got_rows = rows_of(core), swap(rows_of(1 - core), 1)
+    total = out_bias[None, :]
+    for s in range(groups - 1, -1, -1):
+        owner = (group_at + s) % groups
+        part = project(
+            own_rows, got_rows, weights, core, owner, groups, jnp.bfloat16 if s else jnp.float32
+        )
+        if s:
+            part = lax.ppermute(part, "heads", [(h, (h + s) % groups) for h in range(groups)])
+        total = total + part.astype(jnp.float32)
+    hidden = total.astype(jnp.bfloat16)
     page_shape = (requests * new_pages, PAGE, head_count, head_dim)
     key_out, value_out = write_pages(
         key_cache,

time: 413 us -> 383 us (0.927)
  waiting for transfers between devices: 173 us -> 151 us
  starting transfers between devices: 67.3 us -> 50.7 us
  Pallas kernels: 93.1 us -> 99.8 us
    ppermute x5 -> x1, waiting for transfers between devices: 49.3 us -> 13.2 us  [per_device(): lax.ppermute(part, 'heads', [(h, (h + s) % groups) for h in range(groups)])]
    ppermute x8 -> x9, waiting for transfers between devices: 18.3 us -> 36 us  [swap(): return lax.ppermute(x, 'pages', [(p, p ^ bit) for p in range(devs)])]
    ppermute x12, starting transfers between devices: 42.7 us -> 31.8 us  [shift(): return lax.ppermute(x, 'pages', moves)]
    ppermute x3, waiting for transfers between devices: 17.3 us -> 9.85 us  [gather_lines(): lax.ppermute(down, 'pages', cross_down)]
    pallas_call x1, Pallas kernels: 33.8 us -> 39.3 us  [cached_attention(): pl.pallas_call(lambda *refs: cached_kernel(unit, stat_unit, span, scale2,...]
    ppermute x5 -> x1, starting transfers between devices: 6.22 us -> 1.47 us  [per_device(): lax.ppermute(part, 'heads', [(h, (h + s) % groups) for h in range(groups)])]
    pallas_call x1 -> x2, Pallas kernels: 6.84 us -> 10.1 us  [project(): pl.pallas_call(project_kernel, grid_spec=pltpu.PrefetchScalarGridSpec(num...]
  transfers between devices with their start and end apart: 34 -> 31, of which waited for: 14 -> 14; matrix products, arithmetic and copies ran while one was open for 11% -> 12% of each run, Pallas kernels for 21% -> 25%
where the time goes in v4:
time: 383 us; the launch traced here: 379 us
  waiting for transfers between devices  151 us (39%)
  Pallas kernels  99.8 us (26%)
  starting transfers between devices  50.7 us (13%)
  local copies, waits for them, and re-layouts  39.4 us (10%)
  other arithmetic  24.3 us (6%)
  between operations  14.2 us (4%)
    ppermute x12, waiting for transfers between devices, shift(): return lax.ppermute(x, 'pages', moves)  90.4 us
    pallas_call x1, Pallas kernels, cached_attention(): pl.pallas_call(lambda *refs: cached_kernel(unit, stat_unit, span, scale2,...  39.3 us
    ppermute x9, waiting for transfers between devices, swap(): return lax.ppermute(x, 'pages', [(p, p ^ bit) for p in range(devs)])  36 us
    pallas_call x9, Pallas kernels, merge(): pl.pallas_call(lambda *refs: merge_kernel(unit, part_len, scale2, *refs),...  34.2 us
    ppermute x12, starting transfers between devices, shift(): return lax.ppermute(x, 'pages', moves)  31.8 us
    unnamed x39, local copies, waits for them, and re-layouts  21.7 us
    ppermute x1, waiting for transfers between devices, per_device(): lax.ppermute(part, 'heads', [(h, (h + s) % groups) for h in range(groups)])  13.2 us
    pallas_call x2, Pallas kernels, project(): pl.pallas_call(project_kernel, grid_spec=pltpu.PrefetchScalarGridSpec(num...  10.1 us
  transfers between devices with their start and end apart: 31, of which 14 were waited for; matrix products, arithmetic and copies ran while one was open for 12% of the time, Pallas kernels for 25%

profile of v4, /device:TPU:12, one launch (start us, length us, event | category | flops | bytes accessed | tf_op | source)
XLA Modules:
  0.0 379.3 jit_solution(6878805010382642447)
XLA Ops:
  29.9 7.3 %constant_dynamic-slice_fusion.5 = (bf16[12,128,4,128]{3,2,1,0:T(4,128)(2,1)}, bf16[12,128,4,128]{3,2,1,0:T(4,128)(2,1)}, bf16[12,128,4,128]{3,2,1,0:T(4,128)(2,1)S(1)}, bf16[12,128,4,128]{3,2,1,0:T(4,128)(2,1)}) fusion(bf16[12,128,8,128]{3,2,1,0:T(8,128)(2,1)S(1)} %copy-done.2, s32[]{:T(128)S(6)} %select_n.169, s32[]{:T(128)S(6)} %select_n.170, ...), kind=kLoop, calls=%fused_computation.47 | loop fusion | bytes 12582920 | tf_op jit(solution)/shard_map/dynamic-slice.4
  38.8 3.8 copy.62
  43.6 12.4 %collective-permute-done.2.refs_7_ = bf16[4,576,128]{2,1,0:T(8,128)(2,1)} collective-permute-done((bf16[4,576,128]{2,1,0:T(8,128)(2,1)}, bf16[4,576,128]{2,1,0:T(8,128)(2,1)}, u32[]{:S(2)}, u32[]{:S(2)}) %collective-permute-start.2) | collective-permute-done | bytes 589856 | tf_op jit(solution)/shard_map/ppermute | solution.py:271
  55.9 5.2 %collective-permute-start.6 = (bf16[4,576,128]{2,1,0:T(8,128)(2,1)}, bf16[4,576,128]{2,1,0:T(8,128)(2,1)}, u32[]{:S(2)}, u32[]{:S(2)}) collective-permute-start(bf16[4,576,128]{2,1,0:T(8,128)(2,1)} %collective-permute-done.2.refs_7_), channel_id=1, source_target_pairs={{4,8},{5,9},{6,10},{7,11},{8,12},{9,13},{10,14},{11,15},{20,24},{2... | collective-permute-start | bytes 1769480 | tf_op jit(solution)/shard_map/ppermute | solution.py:271
  65.5 35.3 %collective-permute-done.6.refs_11_ = bf16[4,576,128]{2,1,0:T(8,128)(2,1)} collective-permute-done((bf16[4,576,128]{2,1,0:T(8,128)(2,1)}, bf16[4,576,128]{2,1,0:T(8,128)(2,1)}, u32[]{:S(2)}, u32[]{:S(2)}) %collective-permute-start.6) | collective-permute-done | bytes 589856 | tf_op jit(solution)/shard_map/ppermute | solution.py:271
  108.4 3.8 copy.61
  117.4 3.9 %collective-permute-start.9 = (bf16[4,576,128]{2,1,0:T(8,128)(2,1)}, bf16[4,576,128]{2,1,0:T(8,128)(2,1)}, u32[]{:S(2)}, u32[]{:S(2)}) collective-permute-start(bf16[4,576,128]{2,1,0:T(8,128)(2,1)} %collective-permute-done.8.refs_13_), channel_id=1, source_target_pairs={{0,2},{1,3},{2,0},{3,1},{4,6},{5,7},{6,4},{7,5},{16,18},{17,19},{1... | collective-permute-start | bytes 1769480 | tf_op jit(solution)/shard_map/ppermute | solution.py:293
  122.8 5.9 %collective-permute-done.12.refs_17_ = bf16[4,576,128]{2,1,0:T(8,128)(2,1)} collective-permute-done((bf16[4,576,128]{2,1,0:T(8,128)(2,1)}, bf16[4,576,128]{2,1,0:T(8,128)(2,1)}, u32[]{:S(2)}, u32[]{:S(2)}) %collective-permute-start.12) | collective-permute-done | bytes 589856 | tf_op jit(solution)/shard_map/ppermute | solution.py:271
  131.5 3.9 %pad_maximum_fusion.refs_19_ = bf16[4,24,128,128]{3,2,1,0:T(8,128)(2,1)} fusion(bf16[4,12,128,128]{3,2,1,0:T(8,128)(2,1)} %collective-permute-done.14, bf16[4,12,128,128]{3,2,1,0:T(8,128)(2,1)} %bitcast.62), kind=kLoop, calls=%fused_computation | loop fusion | flops 1572864 | bytes 6291456 | tf_op jit(solution)/shard_map/concatenate | solution.py:508
  138.8 9.8 %collective-permute-done.9.refs_14_ = bf16[4,576,128]{2,1,0:T(8,128)(2,1)} collective-permute-done((bf16[4,576,128]{2,1,0:T(8,128)(2,1)}, bf16[4,576,128]{2,1,0:T(8,128)(2,1)}, u32[]{:S(2)}, u32[]{:S(2)}) %collective-permute-start.9) | collective-permute-done | bytes 589856 | tf_op jit(solution)/shard_map/ppermute | solution.py:293
  148.7 39.3 %cached_attention.1 = (bf16[4,608,128]{2,1,0:T(8,128)(2,1)}, bf16[4,608,128]{2,1,0:T(8,128)(2,1)}, bf16[4,608,128]{2,1,0:T(8,128)(2,1)}, bf16[4,608,128]{2,1,0:T...) custom-call(s32[22]{0:T(128)} %stack.204.refs_0_, ...), custom_call_target="tpu_custom_call" | custom-call | flops 40000000000 | bytes 20971520 | tf_op jit(solution)/shard_map/cached_attention/pallas_call | solution.py:155
  190.1 19.2 %collective-permute-done.17.refs_2_ = bf16[4,608,128]{2,1,0:T(8,128)(2,1)} collective-permute-done((bf16[4,608,128]{2,1,0:T(8,128)(2,1)}, bf16[4,608,128]{2,1,0:T(8,128)(2,1)}, u32[]{:S(2)}, u32[]{:S(2)}) %collective-permute-start.17) | collective-permute-done | bytes 622624 | tf_op jit(solution)/shard_map/ppermute | solution.py:265
  214.6 8.1 %collective-permute-done.19.refs_2_ = bf16[4,608,128]{2,1,0:T(8,128)(2,1)} collective-permute-done((bf16[4,608,128]{2,1,0:T(8,128)(2,1)}, bf16[4,608,128]{2,1,0:T(8,128)(2,1)}, u32[]{:S(2)}, u32[]{:S(2)}) %collective-permute-start.19) | collective-permute-done | bytes 622624 | tf_op jit(solution)/shard_map/ppermute | solution.py:265
  228.8 4.9 %collective-permute-done.18.refs_2_ = bf16[4,608,128]{2,1,0:T(8,128)(2,1)} collective-permute-done((bf16[4,608,128]{2,1,0:T(8,128)(2,1)}, bf16[4,608,128]{2,1,0:T(8,128)(2,1)}, u32[]{:S(2)}, u32[]{:S(2)}) %collective-permute-start.18) | collective-permute-done | bytes 622624 | tf_op jit(solution)/shard_map/ppermute | solution.py:265
  246.2 4.5 %collective-permute-start.21 = (bf16[4,608,128]{2,1,0:T(8,128)(2,1)}, bf16[4,608,128]{2,1,0:T(8,128)(2,1)}, u32[]{:S(2)}, u32[]{:S(2)}) collective-permute-start(bf16[4,608,128]{2,1,0:T(8,128)(2,1)} %merge.13), channel_id=1, source_target_pairs={{0,4},{1,5},{2,6},{3,7},{4,8},{5,9},{6,10},{7,11},{16,20},{17,21},... | collective-permute-start | bytes 1867784 | tf_op jit(solution)/shard_map/ppermute | solution.py:271
  253.0 18.8 %collective-permute-done.24.refs_2_ = bf16[4,608,128]{2,1,0:T(8,128)(2,1)} collective-permute-done((bf16[4,608,128]{2,1,0:T(8,128)(2,1)}, bf16[4,608,128]{2,1,0:T(8,128)(2,1)}, u32[]{:S(2)}, u32[]{:S(2)}) %collective-permute-start.24) | collective-permute-done | bytes 622624 | tf_op jit(solution)/shard_map/ppermute | solution.py:271
  281.2 3.9 %collective-permute-start.22 = (bf16[4,608,128]{2,1,0:T(8,128)(2,1)}, bf16[4,608,128]{2,1,0:T(8,128)(2,1)}, u32[]{:S(2)}, u32[]{:S(2)}) collective-permute-start(bf16[4,608,128]{2,1,0:T(8,128)(2,1)} %merge.14), channel_id=1, source_target_pairs={{0,4},{1,5},{2,6},{3,7},{4,8},{5,9},{6,10},{7,11},{8,12},{9,13},{1... | collective-permute-start | bytes 1867784 | tf_op jit(solution)/shard_map/ppermute | solution.py:271
  296.9 9.4 %fresh_attention.1.refs_4_ = bf16[4,608,128]{2,1,0:T(8,128)(2,1)S(1)} custom-call(bf16[4,576,128]{2,1,0:T(8,128)(2,1)} %maximum_select_fusion.refs_5_.refs_0_, bf16[4,1152,128]{2,1,0:T(8,128)(2,1)S(1)} %bitcast.58, bf16[4,1152,128]{2,1,0:T(8,128)(2,1)S(1)} %bitcast.59, s32[2,576]{1,0:T(2,128)S(1)} %pad_add_fusion.refs_3_, s32[1152,1]{1,0:T(8,128)S(1)} %copy-done.6), custom_call_target="tpu_custom_call" | custom-call | tf_op jit(solution)/shard_map/fresh_attention/pallas_call | solution.py:358
  307.1 13.7 %collective-permute-done.25.refs_3_ = bf16[4,608,128]{2,1,0:T(8,128)(2,1)} collective-permute-done((bf16[4,608,128]{2,1,0:T(8,128)(2,1)}, bf16[4,608,128]{2,1,0:T(8,128)(2,1)}, u32[]{:S(2)}, u32[]{:S(2)}) %collective-permute-start.25) | collective-permute-done | bytes 622624 | tf_op jit(solution)/shard_map/ppermute | solution.py:271
  324.1 4.6 %merge.17 = bf16[4,608,128]{2,1,0:T(8,128)(2,1)} custom-call(s32[4]{0:T(128)} %pad_add_fusion.5.refs_0_, bf16[4,608,128]{2,1,0:T(8,128)(2,1)} %merge.9.refs_1_, bf16[4,608,128]{2,1,0:T(8,128)(2,1)} %collective-permute-done.22.refs_2_, bf16[4,608,128]{2,1,0:T(8,128)(2,1)} %collective-permute-done.25.refs_3_, bf16[4,608,128]{2,1,0:T(8,128)(2,1)} %copy-done.5), custom_call_target="tpu_custom_call" | custom-call | tf_op jit(solution)/shard_map/merge/pallas_call | solution.py:218
  335.9 5.8 %project.2 = bf16[288,2048]{1,0:T(8,128)(2,1)} custom-call(s32[2]{0:T(128)S(1)} %pad_add_fusion.4.at_ref, bf16[4,288,128]{2,1,0:T(8,128)(2,1)S(1)} %get-tuple-element.34.mine_ref, bf16[4,288,128]{2,1,0:T(8,128)(2,1)} %collective-permute-done.26.other_ref, bf16[16,1024,256]{2,1,0:T(8,128)(2,1)S(1)} %bitcast.56), custom_call_target="tpu_custom_call" | custom-call | tf_op jit(solution)/shard_map/project/pallas_call | solution.py:399
  345.6 6.9 %write_pages.1 = (bf16[12,128,8,128]{3,2,1,0:T(8,128)(2,1)}, bf16[12,128,8,128]{3,2,1,0:T(8,128)(2,1)}) custom-call(s32[12]{0:T(128)S(1)} %convert_element_type.53.fresh_ref, s32[12]{0:T(128)S(1)} %fusion.2.index_ref, bf16[12,128,8,128]{3,2,1,0:T(8,128)(2,1)S(1)} %copy-done.3, bf16[12,128,8,128]{3,2,1,0:T(8,128)(2,1)S(1)} %copy-done.2, ...), custom_call_target="tpu_custom_call" | custom-call | tf_op jit(solution)/shard_map/write_pages/pallas_call | solution.py:249
  352.6 4.3 %project.3 = f32[288,2048]{1,0:T(8,128)S(1)} custom-call(s32[2]{0:T(128)S(1)} %pad_add_fusion.7.at_ref, bf16[4,288,128]{2,1,0:T(8,128)(2,1)S(1)} %get-tuple-element.34.mine_ref, bf16[4,288,128]{2,1,0:T(8,128)(2,1)} %collective-permute-done.26.other_ref, bf16[16,1024,256]{2,1,0:T(8,128)(2,1)S(1)} %bitcast.57), custom_call_target="tpu_custom_call" | custom-call | tf_op jit(solution)/shard_map/project/pallas_call | solution.py:399
  356.9 13.2 %collective-permute-done.27 = bf16[288,2048]{1,0:T(8,128)(2,1)} collective-permute-done((bf16[288,2048]{1,0:T(8,128)(2,1)}, bf16[288,2048]{1,0:T(8,128)(2,1)}, u32[]{:S(2)}, u32[]{:S(2)}) %collective-permute-start.27) | collective-permute-done | bytes 1179680 | tf_op jit(solution)/shard_map/ppermute | solution.py:561
  (149 shorter events, 117.1 us)
Async XLA Ops:
  7.2 283.1 %all-gather.5.cloned.1.call-start = ((), (), s32[]{:S(2)}) async-start(), calls=%async_computation | async-start | bytes 10027008 | tf_op jit(solution)/shard_map/all_gather | solution.py:475
  13.8 279.7 %all-gather.7.cloned.1.call-start = ((), (), s32[]{:S(2)}) async-start(), calls=%async_computation.1 | async-start | bytes 10027008 | tf_op jit(solution)/shard_map/all_gather | solution.py:476
  14.5 316.1 %all-gather.9.cloned.1.call-start = ((), (), s32[]{:S(2)}) async-start(), calls=%async_computation.2 | async-start | bytes 8912896 | tf_op jit(solution)/shard_map/all_gather | solution.py:479
  23.2 32.7 %collective-permute-start.2 = (bf16[4,576,128]{2,1,0:T(8,128)(2,1)}, bf16[4,576,128]{2,1,0:T(8,128)(2,1)}, u32[]{:S(2)}, u32[]{:S(2)}) collective-permute-start(bf16[4,576,128]{2,1,0:T(8,128)(2,1)} %maximum_select_fusion.refs_5_.refs_0_), channel_id=1, source_target_pairs={{0,4},{1,5},{2,6},{3,7},{4,8},{5,9},{6,10},{7,11},{8,12},{9,13},{1... | collective-permute-start | bytes 1769480 | tf_op jit(solution)/shard_map/ppermute | solution.py:271
  26.7 34.4 %collective-permute-start.4 = (bf16[4,576,128]{2,1,0:T(8,128)(2,1)}, bf16[4,576,128]{2,1,0:T(8,128)(2,1)}, u32[]{:S(2)}, u32[]{:S(2)}) collective-permute-start(bf16[4,576,128]{2,1,0:T(8,128)(2,1)} %maximum_select_fusion.refs_5_.refs_0_), channel_id=1, source_target_pairs={{4,0},{5,1},{6,2},{7,3},{8,4},{9,5},{10,6},{11,7},{12,8},{13,9},{1... | collective-permute-start | bytes 1769480 | tf_op jit(solution)/shard_map/ppermute | solution.py:271
  38.8 77.0 %collective-permute-start.14 = (bf16[4,12,128,128]{3,2,1,0:T(8,128)(2,1)}, bf16[4,12,128,128]{3,2,1,0:T(8,128)(2,1)}, u32[]{:S(2)}, u32[]{:S(2)}) collective-permute-start(bf16[4,12,128,128]{3,2,1,0:T(8,128)(2,1)} %bitcast.52), channel_id=1, source_target_pairs={{0,1},{1,0},{2,3},{3,2},{4,5},{5,4},{6,7},{7,6},{8,9},{9,8},{10,11... | collective-permute-start | bytes 4718600 | tf_op jit(solution)/shard_map/ppermute | solution.py:265
  42.6 74.8 %collective-permute-start.15 = (bf16[4,12,128,128]{3,2,1,0:T(8,128)(2,1)}, bf16[4,12,128,128]{3,2,1,0:T(8,128)(2,1)}, u32[]{:S(2)}, u32[]{:S(2)}) collective-permute-start(bf16[4,12,128,128]{3,2,1,0:T(8,128)(2,1)} %bitcast.64), channel_id=1, source_target_pairs={{0,1},{1,0},{2,3},{3,2},{4,5},{5,4},{6,7},{7,6},{8,9},{9,8},{10,11... | collective-permute-start | bytes 4718600 | tf_op jit(solution)/shard_map/ppermute | solution.py:265
  55.9 44.8 %collective-permute-start.6 = (bf16[4,576,128]{2,1,0:T(8,128)(2,1)}, bf16[4,576,128]{2,1,0:T(8,128)(2,1)}, u32[]{:S(2)}, u32[]{:S(2)}) collective-permute-start(bf16[4,576,128]{2,1,0:T(8,128)(2,1)} %collective-permute-done.2.refs_7_), channel_id=1, source_target_pairs={{4,8},{5,9},{6,10},{7,11},{8,12},{9,13},{10,14},{11,15},{20,24},{2... | collective-permute-start | bytes 1769480 | tf_op jit(solution)/shard_map/ppermute | solution.py:271
  61.1 42.1 %collective-permute-start.8 = (bf16[4,576,128]{2,1,0:T(8,128)(2,1)}, bf16[4,576,128]{2,1,0:T(8,128)(2,1)}, u32[]{:S(2)}, u32[]{:S(2)}) collective-permute-start(bf16[4,576,128]{2,1,0:T(8,128)(2,1)} %collective-permute-done.4.refs_9_), channel_id=1, source_target_pairs={{4,0},{5,1},{6,2},{7,3},{8,4},{9,5},{10,6},{11,7},{20,16},{21,17},... | collective-permute-start | bytes 1769480 | tf_op jit(solution)/shard_map/ppermute | solution.py:271
  63.2 50.7 %collective-permute-start.3 = (bf16[4,576,128]{2,1,0:T(8,128)(2,1)}, bf16[4,576,128]{2,1,0:T(8,128)(2,1)}, u32[]{:S(2)}, u32[]{:S(2)}) collective-permute-start(bf16[4,576,128]{2,1,0:T(8,128)(2,1)} %collective-permute-done.2.refs_7_), channel_id=1, source_target_pairs={{4,6},{5,7},{6,4},{7,5},{8,10},{9,11},{10,8},{11,9},{12,14},{13,15... | collective-permute-start | bytes 1769480 | tf_op jit(solution)/shard_map/ppermute | solution.py:291
  103.2 25.4 %collective-permute-start.12 = (bf16[4,576,128]{2,1,0:T(8,128)(2,1)}, bf16[4,576,128]{2,1,0:T(8,128)(2,1)}, u32[]{:S(2)}, u32[]{:S(2)}) collective-permute-start(bf16[4,576,128]{2,1,0:T(8,128)(2,1)} %collective-permute-done.8.refs_13_), channel_id=1, source_target_pairs={{4,0},{5,1},{6,2},{7,3},{20,16},{21,17},{22,18},{23,19}} | collective-permute-start | bytes 1769480 | tf_op jit(solution)/shard_map/ppermute | solution.py:271
  113.9 24.9 %collective-permute-start.5 = (bf16[4,576,128]{2,1,0:T(8,128)(2,1)}, bf16[4,576,128]{2,1,0:T(8,128)(2,1)}, u32[]{:S(2)}, u32[]{:S(2)}) collective-permute-start(bf16[4,576,128]{2,1,0:T(8,128)(2,1)} %collective-permute-done.4.refs_9_), channel_id=1, source_target_pairs={{0,2},{1,3},{2,0},{3,1},{4,6},{5,7},{6,4},{7,5},{8,10},{9,11},{10,... | collective-permute-start | bytes 1769480 | tf_op jit(solution)/shard_map/ppermute | solution.py:293
  115.8 23.0 %collective-permute-start.7 = (bf16[4,576,128]{2,1,0:T(8,128)(2,1)}, bf16[4,576,128]{2,1,0:T(8,128)(2,1)}, u32[]{:S(2)}, u32[]{:S(2)}) collective-permute-start(bf16[4,576,128]{2,1,0:T(8,128)(2,1)} %collective-permute-done.6.refs_11_), channel_id=1, source_target_pairs={{8,10},{9,11},{10,8},{11,9},{12,14},{13,15},{14,12},{15,13},{24,26... | collective-permute-start | bytes 1769480 | tf_op jit(solution)/shard_map/ppermute | solution.py:291
  117.4 31.3 %collective-permute-start.9 = (bf16[4,576,128]{2,1,0:T(8,128)(2,1)}, bf16[4,576,128]{2,1,0:T(8,128)(2,1)}, u32[]{:S(2)}, u32[]{:S(2)}) collective-permute-start(bf16[4,576,128]{2,1,0:T(8,128)(2,1)} %collective-permute-done.8.refs_13_), channel_id=1, source_target_pairs={{0,2},{1,3},{2,0},{3,1},{4,6},{5,7},{6,4},{7,5},{16,18},{17,19},{1... | collective-permute-start | bytes 1769480 | tf_op jit(solution)/shard_map/ppermute | solution.py:293
  121.3 27.4 %collective-permute-start.11 = (bf16[4,576,128]{2,1,0:T(8,128)(2,1)}, bf16[4,576,128]{2,1,0:T(8,128)(2,1)}, u32[]{:S(2)}, u32[]{:S(2)}) collective-permute-start(bf16[4,576,128]{2,1,0:T(8,128)(2,1)} %collective-permute-done.10.refs_15_), channel_id=1, source_target_pairs={{12,14},{13,15},{14,12},{15,13},{28,30},{29,31},{30,28},{31,29}} | collective-permute-start | bytes 1769480 | tf_op jit(solution)/shard_map/ppermute | solution.py:291
  188.0 34.7 %collective-permute-start.19 = (bf16[4,608,128]{2,1,0:T(8,128)(2,1)}, bf16[4,608,128]{2,1,0:T(8,128)(2,1)}, u32[]{:S(2)}, u32[]{:S(2)}) collective-permute-start(bf16[4,608,128]{2,1,0:T(8,128)(2,1)} %get-tuple-element.20), channel_id=1, source_target_pairs={{0,2},{1,3},{2,0},{3,1},{4,6},{5,7},{6,4},{7,5},{8,10},{9,11},{10,... | collective-permute-start | bytes 1867784 | tf_op jit(solution)/shard_map/ppermute | solution.py:265
  190.0 43.7 %collective-permute-start.18 = (bf16[4,608,128]{2,1,0:T(8,128)(2,1)}, bf16[4,608,128]{2,1,0:T(8,128)(2,1)}, u32[]{:S(2)}, u32[]{:S(2)}) collective-permute-start(bf16[4,608,128]{2,1,0:T(8,128)(2,1)} %get-tuple-element.18), channel_id=1, source_target_pairs={{0,2},{1,3},{2,0},{3,1},{4,6},{5,7},{6,4},{7,5},{8,10},{9,11},{10,... | collective-permute-start | bytes 1867784 | tf_op jit(solution)/shard_map/ppermute | solution.py:265
  213.0 24.4 %collective-permute-start.23 = (bf16[4,608,128]{2,1,0:T(8,128)(2,1)}, bf16[4,608,128]{2,1,0:T(8,128)(2,1)}, u32[]{:S(2)}, u32[]{:S(2)}) collective-permute-start(bf16[4,608,128]{2,1,0:T(8,128)(2,1)} %merge.10.refs_1_), channel_id=1, source_target_pairs={{12,8},{13,9},{14,10},{15,11},{28,24},{29,25},{30,26},{31,27}} | collective-permute-start | bytes 1867784 | tf_op jit(solution)/shard_map/ppermute | solution.py:271
  241.2 30.6 %collective-permute-start.24 = (bf16[4,608,128]{2,1,0:T(8,128)(2,1)}, bf16[4,608,128]{2,1,0:T(8,128)(2,1)}, u32[]{:S(2)}, u32[]{:S(2)}) collective-permute-start(bf16[4,608,128]{2,1,0:T(8,128)(2,1)} %merge.15), channel_id=1, source_target_pairs={{8,4},{9,5},{10,6},{11,7},{12,8},{13,9},{14,10},{15,11},{24,20},{2... | collective-permute-start | bytes 1867784 | tf_op jit(solution)/shard_map/ppermute | solution.py:271
  246.2 31.3 %collective-permute-start.21 = (bf16[4,608,128]{2,1,0:T(8,128)(2,1)}, bf16[4,608,128]{2,1,0:T(8,128)(2,1)}, u32[]{:S(2)}, u32[]{:S(2)}) collective-permute-start(bf16[4,608,128]{2,1,0:T(8,128)(2,1)} %merge.13), channel_id=1, source_target_pairs={{0,4},{1,5},{2,6},{3,7},{4,8},{5,9},{6,10},{7,11},{16,20},{17,21},... | collective-permute-start | bytes 1867784 | tf_op jit(solution)/shard_map/ppermute | solution.py:271
  250.8 35.8 %collective-permute-start.16 = (bf16[4,608,128]{2,1,0:T(8,128)(2,1)}, bf16[4,608,128]{2,1,0:T(8,128)(2,1)}, u32[]{:S(2)}, u32[]{:S(2)}) collective-permute-start(bf16[4,608,128]{2,1,0:T(8,128)(2,1)} %get-tuple-element.14), channel_id=1, source_target_pairs={{0,2},{1,3},{2,0},{3,1},{4,6},{5,7},{6,4},{7,5},{8,10},{9,11},{10,... | collective-permute-start | bytes 1867784 | tf_op jit(solution)/shard_map/ppermute | solution.py:265
  275.5 45.2 %collective-permute-start.25 = (bf16[4,608,128]{2,1,0:T(8,128)(2,1)}, bf16[4,608,128]{2,1,0:T(8,128)(2,1)}, u32[]{:S(2)}, u32[]{:S(2)}) collective-permute-start(bf16[4,608,128]{2,1,0:T(8,128)(2,1)} %merge.16), channel_id=1, source_target_pairs={{4,0},{5,1},{6,2},{7,3},{8,4},{9,5},{10,6},{11,7},{12,8},{13,9},{1... | collective-permute-start | bytes 1867784 | tf_op jit(solution)/shard_map/ppermute | solution.py:271
  281.2 43.0 %collective-permute-start.22 = (bf16[4,608,128]{2,1,0:T(8,128)(2,1)}, bf16[4,608,128]{2,1,0:T(8,128)(2,1)}, u32[]{:S(2)}, u32[]{:S(2)}) collective-permute-start(bf16[4,608,128]{2,1,0:T(8,128)(2,1)} %merge.14), channel_id=1, source_target_pairs={{0,4},{1,5},{2,6},{3,7},{4,8},{5,9},{6,10},{7,11},{8,12},{9,13},{1... | collective-permute-start | bytes 1867784 | tf_op jit(solution)/shard_map/ppermute | solution.py:271
  341.7 28.3 %collective-permute-start.27 = (bf16[288,2048]{1,0:T(8,128)(2,1)}, bf16[288,2048]{1,0:T(8,128)(2,1)}, u32[]{:S(2)}, u32[]{:S(2)}) collective-permute-start(bf16[288,2048]{1,0:T(8,128)(2,1)} %project.2), channel_id=1, source_target_pairs={{0,16},{16,0},{1,17},{17,1},{2,18},{18,2},{3,19},{19,3},{4,20},{20... | collective-permute-start | bytes 3538952 | tf_op jit(solution)/shard_map/ppermute | solution.py:561
  (24 other events, 218.0 us)
Sparse Core Ops, SparseCore 0:
  13.9 108.2 all-gather.4
  124.4 101.9 all-gather.6
  228.5 99.3 all-gather.8

commit v5 on v4

--- a/solution.py
+++ b/solution.py
@@ -271,6 +271,14 @@
     return lax.ppermute(x, "pages", moves)
 
 
+def cross_arrivals(up, down, t):
+    devs = lax.axis_size("pages")
+    line = devs // 4
+    cross_up = [(p, p ^ 2) for p in range(devs) if p // 4 >= t]
+    cross_down = [(p, p ^ 2) for p in range(devs) if p // 4 + t < line]
+    return lax.ppermute(up, "pages", cross_up), lax.ppermute(down, "pages", cross_down)
+
+
 def gather_lines(x):
     line = lax.axis_size("pages") // 4
     device_at = lax.axis_index("pages")
@@ -283,19 +291,17 @@
         down = shift(down, -1, range(1, line - t + 1))
         has_up = (at >= t).astype(jnp.int32)
         has_down = (at + t < line).astype(jnp.int32)
-        devs = lax.axis_size("pages")
-        cross_up = [(p, p ^ 2) for p in range(devs) if p // 4 >= t]
-        cross_down = [(p, p ^ 2) for p in range(devs) if p // 4 + t < line]
+        crossed_up, crossed_down = cross_arrivals(up, down, t)
         held += [
             (up, at - t, across, has_up),
-            (lax.ppermute(up, "pages", cross_up), at - t, 1 - across, has_up),
+            (crossed_up, at - t, 1 - across, has_up),
             (down, at + t, across, has_down),
-            (lax.ppermute(down, "pages", cross_down), at + t, 1 - across, has_down),
+            (crossed_down, at + t, 1 - across, has_down),
         ]
     return held
 
 
-def merge_lines(parts, merged, last):
+def merge_lines(parts, merged, beside, last):
     line = lax.axis_size("pages") // 4
     at = lax.axis_index("pages") // 4
     turns = []
@@ -316,6 +322,7 @@
         if up is not None:
             up_out = merged([up_out, up], [yes, (at >= 1) & (at <= t - 1)])
             down_out = merged([down_out, down], [yes, (at <= line - 2) & (at >= line - t)])
+        up_out, down_out = beside(t, (up_out, down_out))
         up = shift(up_out, 1, range(0, t))
         down = shift(down_out, -1, range(line - t, line))
     return merged([share(0), up, down, last()], [yes, at >= 1, at <= line - 2, yes])
@@ -366,7 +373,7 @@
     )(q_chip, k_window, v_window, token_rows, key_cols)
 
 
-def project_kernel(at_ref, mine_ref, other_ref, w_ref, out_ref, rows_ref):
+def project_kernel(at_ref, mine_ref, other_ref, w_mine_ref, w_other_ref, out_ref, rows_ref):
     core = at_ref[0]
     wide = rows_ref.shape[2]
 
@@ -375,45 +382,45 @@
         for index, ref in enumerate((mine_ref, other_ref)):
             rows_ref[index] = jnp.concatenate([ref[h] for h in range(ref.shape[0])], axis=1)
 
-    total = 0.0
-    for d in range(2):
-        feats = pl.ds(pl.multiple_of((core ^ d) * wide, wide), wide)
-        total = total + jnp.dot(
-            rows_ref[d], w_ref[0, feats, :], preferred_element_type=jnp.float32
-        )
-    out_ref[...] = total.astype(out_ref.dtype).reshape(out_ref.shape)
-
-
-def project(mine, other, weights, core, owner, groups, dtype):
+    parts = []
+    for w_ref in (w_mine_ref, w_other_ref):
+        total = 0.0
+        for d in range(2):
+            feats = pl.ds(pl.multiple_of((core ^ d) * wide, wide), wide)
+            total = total + jnp.dot(
+                rows_ref[d], w_ref[0, feats, :], preferred_element_type=jnp.float32
+            )
+        parts.append(total)
+    out = jnp.where(
+        core == 0, jnp.concatenate(parts, axis=1), jnp.concatenate(parts[::-1], axis=1)
+    )
+    out_ref[...] = out.astype(out_ref.dtype)
+
+
+def project(mine, other, weights, core, line_at, across, owner, groups, dtype):
     half, tok_dev, head_dim = mine.shape
-    blocks, feats, cols = weights.shape
-    blocks //= groups
-    wide = cols % 128 == 0
-    if wide:
-        out_spec = pl.BlockSpec((tok_dev, cols), lambda j, at: (0, j))
-        out_shape = (tok_dev, blocks * cols)
-    else:
-        out_spec = pl.BlockSpec((1, tok_dev, cols), lambda j, at: (j, 0, 0))
-        out_shape = (blocks, tok_dev, cols)
+    chips, feats, cols = weights[0].shape
+    line = chips // 2
+    blocks = chips // groups
+
+    def place(j, at):
+        there = at[3] * (line // groups) + j // 2
+        return (2 * lax.rem(at[1] + line - there, line) + ((j % 2) ^ at[2]), 0, 0)
+
     rows_spec = pl.BlockSpec(mine.shape, lambda j, at: (0, 0, 0))
-    out = pl.pallas_call(
+    return pl.pallas_call(
         project_kernel,
         grid_spec=pltpu.PrefetchScalarGridSpec(
             num_scalar_prefetch=1,
             grid=(blocks,),
-            in_specs=[
-                rows_spec,
-                rows_spec,
-                pl.BlockSpec((1, feats, cols), lambda j, at: (at[1] * blocks + j, 0, 0)),
-            ],
-            out_specs=out_spec,
+            in_specs=[rows_spec, rows_spec] + [pl.BlockSpec((1, feats, cols), place)] * 2,
+            out_specs=pl.BlockSpec((tok_dev, 2 * cols), lambda j, at: (0, j)),
             scratch_shapes=[pltpu.VMEM((2, tok_dev, half * head_dim), jnp.bfloat16)],
         ),
-        out_shape=jax.ShapeDtypeStruct(out_shape, dtype),
-        compiler_params=pltpu.CompilerParams(vmem_limit_bytes=40 * 2**20),
+        out_shape=jax.ShapeDtypeStruct((tok_dev, blocks * 2 * cols), dtype),
+        compiler_params=pltpu.CompilerParams(vmem_limit_bytes=60 * 2**20),
         name="project",
-    )(jnp.stack([core, owner]), mine, other, weights)
-    return out if wide else jnp.transpose(out, (1, 0, 2)).reshape(tok_dev, blocks * cols)
+    )(jnp.stack([core, line_at, across, owner]), mine, other, *weights)
 
 
 def per_device(
@@ -476,7 +483,11 @@
     all_v = lax.all_gather(values, "pages", axis=0, tiled=True)
     all_k = with_layout_constraint(all_k, natural)
     all_v = with_layout_constraint(all_v, natural)
-    weights = lax.all_gather(out_weight, "pages", axis=0, tiled=False)
+    barrier = lax.optimization_barrier
+    line = page_devs // 4
+    q_list, w_own = barrier((q_list, out_weight))
+    w_up, w_down = {1: shift(w_own, 1, range(line - 1))}, {1: shift(w_own, -1, range(1, line))}
+    w_cross = {0: swap(w_own, 2)}
 
     my_slots = device_at * slot_count + jnp.arange(slot_count, dtype=jnp.int32)
     chip_slots = jnp.concatenate(
@@ -509,7 +520,6 @@
     v_heads = jnp.concatenate([v_mine, swap(v_other, 1)], axis=1)
 
     unit = math.gcd(span_len, tok_dev)
-    line = page_devs // 4
     line_at, across = device_at // 4, (device_at // 2) % 2
     outs = cached_attention(
         q_list,
@@ -525,7 +535,18 @@
         unit,
         scale2,
     )
+    outs, w_up[1], w_down[1], w_cross[0] = barrier((outs, w_up[1], w_down[1], w_cross[0]))
     merged = lambda parts, ok: merge(parts, ok, chip_len, unit, scale2)
+
+    def beside(t, sent):
+        if t + 1 < line:
+            up = shift(w_up[t], 1, range(t, line - 1))
+            down = shift(w_down[t], -1, range(1, line - t))
+            sent, w_up[t + 1], w_down[t + 1] = barrier((sent, up, down))
+        if t > 1:
+            sent, w_cross[t - 1] = barrier((sent, w_cross[t - 1]))
+        w_cross[t] = cross_arrivals(w_up[t], w_down[t], t)
+        return sent
 
     def fresh_part():
         chip_at = device_at // 2
@@ -547,15 +568,29 @@
         )
 
     chip_part = merge_lines(
-        [outs[2 * k : 2 * k + 2] for k in range(line)], merged, fresh_part
+        [outs[2 * k : 2 * k + 2] for k in range(line)], merged, beside, fresh_part
     )
     rows_of = lambda c: lax.dynamic_slice_in_dim(chip_part[:, :chip_len], c * tok_dev, tok_dev, 1)
     own_rows, got_rows = rows_of(core), swap(rows_of(1 - core), 1)
+    found = [w_own, w_cross[0]]
+    for k in range(1, line):
+        for pick in (lambda t: (w_up[t], w_down[t]), lambda t: w_cross[t]):
+            found.append(jnp.where(line_at >= k, pick(k)[0], pick(line - k)[1]))
+    w_mine = jnp.stack(found)
+    weights = [w_mine, swap(w_mine, 1)]
     total = out_bias[None, :]
     for s in range(groups - 1, -1, -1):
         owner = (group_at + s) % groups
         part = project(
-            own_rows, got_rows, weights, core, owner, groups, jnp.bfloat16 if s else jnp.float32
+            own_rows,
+            got_rows,
+            weights,
+            core,
+            line_at,
+            across,
+            owner,
+            groups,
+            jnp.bfloat16 if s else jnp.float32,
         )
         if s:
             part = lax.ppermute(part, "heads", [(h, (h + s) % groups) for h in range(groups)])

time: 383 us -> 391 us (1.021)
  the two profiles are of different devices: /device:TPU:12 before, /device:TPU:18 now
where the time goes in v5:
time: 391 us; the launch traced here: 386 us
  starting transfers between devices  114 us (29%)
  waiting for transfers between devices  98.7 us (25%)
  Pallas kernels  80.4 us (21%)
  local copies, waits for them, and re-layouts  40.5 us (10%)
  other arithmetic  37.3 us (10%)
  between operations  14.7 us (4%)
    ppermute x18, starting transfers between devices, shift(): return lax.ppermute(x, 'pages', moves)  60.8 us
    ppermute x18, waiting for transfers between devices, shift(): return lax.ppermute(x, 'pages', moves)  51.2 us
    pallas_call x9, Pallas kernels, merge(): pl.pallas_call(lambda *refs: merge_kernel(unit, part_len, scale2, *refs),...  34.1 us
    ppermute x11, starting transfers between devices, swap(): return lax.ppermute(x, 'pages', [(p, p ^ bit) for p in range(devs)])  27.6 us
    ppermute x11, waiting for transfers between devices, swap(): return lax.ppermute(x, 'pages', [(p, p ^ bit) for p in range(devs)])  27 us
    unnamed x53, local copies, waits for them, and re-layouts  22.8 us
    ppermute x6, starting transfers between devices, cross_arrivals(): lax.ppermute(up, 'pages', cross_up)  16 us
    pallas_call x1, Pallas kernels, cached_attention(): pl.pallas_call(lambda *refs: cached_kernel(unit, stat_unit, span, scale2,...  15.9 us
  transfers between devices with their start and end apart: 44, of which 11 were waited for; matrix products, arithmetic and copies ran while one was open for 18% of the time, Pallas kernels for 19%

profile of v5, /device:TPU:18, one launch (start us, length us, event | category | flops | bytes accessed | tf_op | source)
XLA Modules:
  0.0 385.6 jit_solution(11373856753279260250)
XLA Ops:
  24.9 4.3 %collective-permute-start.2 = (bf16[4,576,128]{2,1,0:T(8,128)(2,1)}, bf16[4,576,128]{2,1,0:T(8,128)(2,1)}, u32[]{:S(2)}, u32[]{:S(2)}) collective-permute-start(bf16[4,576,128]{2,1,0:T(8,128)(2,1)} %maximum_select_fusion.refs_5_.refs_0_), channel_id=1, source_target_pairs={{0,4},{1,5},{2,6},{3,7},{4,8},{5,9},{6,10},{7,11},{8,12},{9,13},{1... | collective-permute-start | bytes 1769480 | tf_op jit(solution)/shard_map/ppermute | solution.py:271
  29.2 7.3 %constant_dynamic-slice_fusion.5 = (bf16[12,128,4,128]{3,2,1,0:T(4,128)(2,1)}, bf16[12,128,4,128]{3,2,1,0:T(4,128)(2,1)}, bf16[12,128,4,128]{3,2,1,0:T(4,128)(2,1)S(1)}, bf16[12,128,4,128]{3,2,1,0:T(4,128)(2,1)}) fusion(bf16[12,128,8,128]{3,2,1,0:T(8,128)(2,1)S(1)} %copy-done, s32[]{:T(128)S(6)} %select_n.201, s32[]{:T(128)S(6)} %select_n.202, ...), kind=kLoop, calls=%fused_computation.55 | loop fusion | bytes 12582920 | tf_op jit(solution)/shard_map/dynamic-slice.4
  43.8 9.4 %collective-permute-done.4.refs_9_ = bf16[4,576,128]{2,1,0:T(8,128)(2,1)} collective-permute-done((bf16[4,576,128]{2,1,0:T(8,128)(2,1)}, bf16[4,576,128]{2,1,0:T(8,128)(2,1)}, u32[]{:S(2)}, u32[]{:S(2)}) %collective-permute-start.4) | collective-permute-done | bytes 589856 | tf_op jit(solution)/shard_map/ppermute | solution.py:271
  53.2 4.2 %collective-permute-start.8 = (bf16[4,576,128]{2,1,0:T(8,128)(2,1)}, bf16[4,576,128]{2,1,0:T(8,128)(2,1)}, u32[]{:S(2)}, u32[]{:S(2)}) collective-permute-start(bf16[4,576,128]{2,1,0:T(8,128)(2,1)} %collective-permute-done.4.refs_9_), channel_id=1, source_target_pairs={{4,0},{5,1},{6,2},{7,3},{8,4},{9,5},{10,6},{11,7},{20,16},{21,17},... | collective-permute-start | bytes 1769480 | tf_op jit(solution)/shard_map/ppermute | solution.py:271
  63.0 32.5 %collective-permute-done.8.refs_13_ = bf16[4,576,128]{2,1,0:T(8,128)(2,1)} collective-permute-done((bf16[4,576,128]{2,1,0:T(8,128)(2,1)}, bf16[4,576,128]{2,1,0:T(8,128)(2,1)}, u32[]{:S(2)}, u32[]{:S(2)}) %collective-permute-start.8) | collective-permute-done | bytes 589856 | tf_op jit(solution)/shard_map/ppermute | solution.py:271
  108.7 4.2 %collective-permute-start.3 = (bf16[4,576,128]{2,1,0:T(8,128)(2,1)}, bf16[4,576,128]{2,1,0:T(8,128)(2,1)S(1)}, u32[]{:S(2)}, u32[]{:S(2)}) collective-permute-start(bf16[4,576,128]{2,1,0:T(8,128)(2,1)} %collective-permute-done.2.refs_7_), channel_id=1, source_target_pairs={{4,6},{5,7},{6,4},{7,5},{8,10},{9,11},{10,8},{11,9},{12,14},{13,15... | collective-permute-start | bytes 1769480 | tf_op jit(solution)/shard_map/ppermute | solution.py:279
  116.2 8.3 %collective-permute-done.10.refs_15_ = bf16[4,576,128]{2,1,0:T(8,128)(2,1)} collective-permute-done((bf16[4,576,128]{2,1,0:T(8,128)(2,1)}, bf16[4,576,128]{2,1,0:T(8,128)(2,1)}, u32[]{:S(2)}, u32[]{:S(2)}) %collective-permute-start.10) | collective-permute-done | bytes 589856 | tf_op jit(solution)/shard_map/ppermute | solution.py:271
  134.0 10.0 %collective-permute-done.7.refs_12_ = bf16[4,576,128]{2,1,0:T(8,128)(2,1)S(1)} collective-permute-done((bf16[4,576,128]{2,1,0:T(8,128)(2,1)}, bf16[4,576,128]{2,1,0:T(8,128)(2,1)S(1)}, u32[]{:S(2)}, u32[]{:S(2)}) %collective-permute-start.7) | collective-permute-done | bytes 589856 | tf_op jit(solution)/shard_map/ppermute | solution.py:279
  148.4 11.9 %collective-permute-start.16 = (bf16[1024,256]{1,0:T(8,128)(2,1)S(1)}, bf16[1024,256]{1,0:T(8,128)(2,1)}, u32[]{:S(2)}, u32[]{:S(2)}) collective-permute-start(bf16[1024,256]{1,0:T(8,128)(2,1)S(1)} %copy-done.11), channel_id=1, source_target_pairs={{0,4},{1,5},{2,6},{3,7},{4,8},{5,9},{6,10},{7,11},{8,12},{9,13},{1... | collective-permute-start | bytes 1572872 | tf_op jit(solution)/shard_map/ppermute | solution.py:271
  160.4 15.9 %cached_attention.1 = (bf16[4,608,128]{2,1,0:T(8,128)(2,1)}, bf16[4,608,128]{2,1,0:T(8,128)(2,1)}, bf16[4,608,128]{2,1,0:T(8,128)(2,1)}, bf16[4,608,128]{2,1,0:T...) custom-call(s32[22]{0:T(128)} %stack.241.refs_0_, ...), custom_call_target="tpu_custom_call" | custom-call | flops 40000000000 | bytes 20971520 | tf_op jit(solution)/shard_map/cached_attention/pallas_call | solution.py:155
  176.3 21.1 %collective-permute-start.20 = (bf16[4,608,128]{2,1,0:T(8,128)(2,1)}, bf16[4,608,128]{2,1,0:T(8,128)(2,1)}, u32[]{:S(2)}, u32[]{:S(2)}) collective-permute-start(bf16[4,608,128]{2,1,0:T(8,128)(2,1)} %get-tuple-element.81), channel_id=1, source_target_pairs={{0,2},{1,3},{2,0},{3,1},{4,6},{5,7},{6,4},{7,5},{8,10},{9,11},{10,... | collective-permute-start | bytes 1867784 | tf_op jit(solution)/shard_map/ppermute | solution.py:265
  199.4 5.5 %collective-permute-start.24 = (bf16[1024,256]{1,0:T(8,128)(2,1)}, bf16[1024,256]{1,0:T(8,128)(2,1)}, u32[]{:S(2)}, u32[]{:S(2)}) collective-permute-start(bf16[1024,256]{1,0:T(8,128)(2,1)} %collective-permute-done.17), channel_id=1, source_target_pairs={{4,0},{5,1},{6,2},{7,3},{8,4},{9,5},{10,6},{11,7},{20,16},{21,17},... | collective-permute-start | bytes 1572872 | tf_op jit(solution)/shard_map/ppermute | solution.py:271
  206.9 5.8 %collective-permute-done.20.refs_2_ = bf16[4,608,128]{2,1,0:T(8,128)(2,1)} collective-permute-done((bf16[4,608,128]{2,1,0:T(8,128)(2,1)}, bf16[4,608,128]{2,1,0:T(8,128)(2,1)}, u32[]{:S(2)}, u32[]{:S(2)}) %collective-permute-start.20) | collective-permute-done | bytes 622624 | tf_op jit(solution)/shard_map/ppermute | solution.py:265
  216.4 9.6 %collective-permute-done.22.refs_2_ = bf16[4,608,128]{2,1,0:T(8,128)(2,1)} collective-permute-done((bf16[4,608,128]{2,1,0:T(8,128)(2,1)}, bf16[4,608,128]{2,1,0:T(8,128)(2,1)}, u32[]{:S(2)}, u32[]{:S(2)}) %collective-permute-start.22) | collective-permute-done | bytes 622624 | tf_op jit(solution)/shard_map/ppermute | solution.py:265
  232.5 6.2 %collective-permute-start.27 = (bf16[1024,256]{1,0:T(8,128)(2,1)}, bf16[1024,256]{1,0:T(8,128)(2,1)}, u32[]{:S(2)}, u32[]{:S(2)}) collective-permute-start(bf16[1024,256]{1,0:T(8,128)(2,1)} %collective-permute-done.23), channel_id=1, source_target_pairs={{8,12},{9,13},{10,14},{11,15},{24,28},{25,29},{26,30},{27,31}} | collective-permute-start | bytes 1572872 | tf_op jit(solution)/shard_map/ppermute | solution.py:271
  269.7 4.6 %collective-permute-start.32 = (bf16[4,608,128]{2,1,0:T(8,128)(2,1)}, bf16[4,608,128]{2,1,0:T(8,128)(2,1)}, u32[]{:S(2)}, u32[]{:S(2)}) collective-permute-start(bf16[4,608,128]{2,1,0:T(8,128)(2,1)} %merge.14), channel_id=1, source_target_pairs={{8,4},{9,5},{10,6},{11,7},{12,8},{13,9},{14,10},{15,11},{24,20},{2... | collective-permute-start | bytes 1867784 | tf_op jit(solution)/shard_map/ppermute | solution.py:271
  295.0 4.6 %collective-permute-start.35 = (bf16[4,608,128]{2,1,0:T(8,128)(2,1)}, bf16[4,608,128]{2,1,0:T(8,128)(2,1)}, u32[]{:S(2)}, u32[]{:S(2)}) collective-permute-start(bf16[4,608,128]{2,1,0:T(8,128)(2,1)} %merge.15), channel_id=1, source_target_pairs={{0,4},{1,5},{2,6},{3,7},{4,8},{5,9},{6,10},{7,11},{8,12},{9,13},{1... | collective-permute-start | bytes 1867784 | tf_op jit(solution)/shard_map/ppermute | solution.py:271
  303.2 8.4 %collective-permute-done.19.refs_2_ = bf16[4,608,128]{2,1,0:T(8,128)(2,1)} collective-permute-done((bf16[4,608,128]{2,1,0:T(8,128)(2,1)}, bf16[4,608,128]{2,1,0:T(8,128)(2,1)}, u32[]{:S(2)}, u32[]{:S(2)}) %collective-permute-start.19) | collective-permute-done | bytes 622624 | tf_op jit(solution)/shard_map/ppermute | solution.py:265
  321.9 9.4 %fresh_attention.1.refs_4_ = bf16[4,608,128]{2,1,0:T(8,128)(2,1)S(1)} custom-call(bf16[4,576,128]{2,1,0:T(8,128)(2,1)} %maximum_select_fusion.refs_5_.refs_0_, bf16[4,1152,128]{2,1,0:T(8,128)(2,1)S(1)} %bitcast.74, bf16[4,1152,128]{2,1,0:T(8,128)(2,1)S(1)} %bitcast.73, s32[2,576]{1,0:T(2,128)S(1)} %pad_add_fusion.refs_3_, s32[1152,1]{1,0:T(8,128)S(1)} %copy-done.4), custom_call_target="tpu_custom_call" | custom-call | tf_op jit(solution)/shard_map/fresh_attention/pallas_call | solution.py:365
  332.1 4.6 %merge.17 = bf16[4,608,128]{2,1,0:T(8,128)(2,1)} custom-call(s32[4]{0:T(128)} %pad_add_fusion.6.refs_0_, bf16[4,608,128]{2,1,0:T(8,128)(2,1)} %merge.9.refs_1_, bf16[4,608,128]{2,1,0:T(8,128)(2,1)} %collective-permute-done.35.refs_2_, bf16[4,608,128]{2,1,0:T(8,128)(2,1)} %collective-permute-done.36.refs_3_, bf16[4,608,128]{2,1,0:T(8,128)(2,1)} %copy-done.3), custom_call_target="tpu_custom_call" | custom-call | tf_op jit(solution)/shard_map/merge/pallas_call | solution.py:218
  341.2 5.9 %project.2 = bf16[288,2048]{1,0:T(8,128)(2,1)} custom-call(s32[4]{0:T(128)} %get-tuple-element.109.at_ref, bf16[4,288,128]{2,1,0:T(8,128)(2,1)} %get-tuple-element.120.mine_ref, bf16[4,288,128]{2,1,0:T(8,128)(2,1)} %copy-done.9, bf16[8,1024,256]{2,1,0:T(8,128)(2,1)} %bitcast_dynamic-update-slice_fusion.w_mine_ref, ...), custom_call_target="tpu_custom_call" | custom-call | tf_op jit(solution)/shard_map/project/pallas_call | solution.py:411
  350.5 9.0 %write_pages.1 = (bf16[12,128,8,128]{3,2,1,0:T(8,128)(2,1)}, bf16[12,128,8,128]{3,2,1,0:T(8,128)(2,1)}) custom-call(s32[12]{0:T(128)S(1)} %convert_element_type.53.fresh_ref, s32[12]{0:T(128)S(1)} %fusion.2.index_ref, bf16[12,128,8,128]{3,2,1,0:T(8,128)(2,1)S(1)} %copy-done.1, bf16[12,128,8,128]{3,2,1,0:T(8,128)(2,1)S(1)} %copy-done, ...), custom_call_target="tpu_custom_call" | custom-call | tf_op jit(solution)/shard_map/write_pages/pallas_call | solution.py:249
  359.5 6.2 %project.3 = f32[288,2048]{1,0:T(8,128)} custom-call(s32[4]{0:T(128)} %pad_add_fusion.8.at_ref, bf16[4,288,128]{2,1,0:T(8,128)(2,1)} %get-tuple-element.120.mine_ref, bf16[4,288,128]{2,1,0:T(8,128)(2,1)} %copy-done.9, bf16[8,1024,256]{2,1,0:T(8,128)(2,1)} %bitcast_dynamic-update-slice_fusion.w_mine_ref, bf16[8,1024,256]{2,1,0:T(8,128)(2,1)} %collective-permute-done.40.w_other_ref), custom_call_target="tpu_custom_call" | custom-call | tf_op jit(solution)/shard_map/project/pallas_call | solution.py:411
  365.6 9.7 %collective-permute-done.41 = bf16[288,2048]{1,0:T(8,128)(2,1)} collective-permute-done((bf16[288,2048]{1,0:T(8,128)(2,1)}, bf16[288,2048]{1,0:T(8,128)(2,1)}, u32[]{:S(2)}, u32[]{:S(2)}) %collective-permute-start.41) | collective-permute-done | bytes 1179680 | tf_op jit(solution)/shard_map/ppermute | solution.py:596
  (193 shorter events, 152.3 us)
Async XLA Ops:
  7.2 308.2 %all-gather.5.cloned.1.call-start = ((), (), s32[]{:S(2)}) async-start(), calls=%async_computation.1 | async-start | bytes 10027008 | tf_op jit(solution)/shard_map/all_gather | solution.py:483
  7.9 310.6 %all-gather.3.cloned.1.call-start = ((), (), s32[]{:S(2)}) async-start(), calls=%async_computation | async-start | bytes 10027008 | tf_op jit(solution)/shard_map/all_gather | solution.py:482
  22.5 30.7 %collective-permute-start.4 = (bf16[4,576,128]{2,1,0:T(8,128)(2,1)}, bf16[4,576,128]{2,1,0:T(8,128)(2,1)}, u32[]{:S(2)}, u32[]{:S(2)}) collective-permute-start(bf16[4,576,128]{2,1,0:T(8,128)(2,1)} %maximum_select_fusion.refs_5_.refs_0_), channel_id=1, source_target_pairs={{4,0},{5,1},{6,2},{7,3},{8,4},{9,5},{10,6},{11,7},{12,8},{13,9},{1... | collective-permute-start | bytes 1769480 | tf_op jit(solution)/shard_map/ppermute | solution.py:271
  24.9 32.6 %collective-permute-start.2 = (bf16[4,576,128]{2,1,0:T(8,128)(2,1)}, bf16[4,576,128]{2,1,0:T(8,128)(2,1)}, u32[]{:S(2)}, u32[]{:S(2)}) collective-permute-start(bf16[4,576,128]{2,1,0:T(8,128)(2,1)} %maximum_select_fusion.refs_5_.refs_0_), channel_id=1, source_target_pairs={{0,4},{1,5},{2,6},{3,7},{4,8},{5,9},{6,10},{7,11},{8,12},{9,13},{1... | collective-permute-start | bytes 1769480 | tf_op jit(solution)/shard_map/ppermute | solution.py:271
  38.0 74.8 %collective-permute-start.14 = (bf16[4,12,128,128]{3,2,1,0:T(8,128)(2,1)}, bf16[4,12,128,128]{3,2,1,0:T(8,128)(2,1)}, u32[]{:S(2)}, u32[]{:S(2)}) collective-permute-start(bf16[4,12,128,128]{3,2,1,0:T(8,128)(2,1)} %bitcast.69), channel_id=1, source_target_pairs={{0,1},{1,0},{2,3},{3,2},{4,5},{5,4},{6,7},{7,6},{8,9},{9,8},{10,11... | collective-permute-start | bytes 4718600 | tf_op jit(solution)/shard_map/ppermute | solution.py:265
  41.8 71.8 %collective-permute-start.15 = (bf16[4,12,128,128]{3,2,1,0:T(8,128)(2,1)}, bf16[4,12,128,128]{3,2,1,0:T(8,128)(2,1)}, u32[]{:S(2)}, u32[]{:S(2)}) collective-permute-start(bf16[4,12,128,128]{3,2,1,0:T(8,128)(2,1)} %bitcast.79), channel_id=1, source_target_pairs={{0,1},{1,0},{2,3},{3,2},{4,5},{5,4},{6,7},{7,6},{8,9},{9,8},{10,11... | collective-permute-start | bytes 4718600 | tf_op jit(solution)/shard_map/ppermute | solution.py:265
  53.2 42.2 %collective-permute-start.8 = (bf16[4,576,128]{2,1,0:T(8,128)(2,1)}, bf16[4,576,128]{2,1,0:T(8,128)(2,1)}, u32[]{:S(2)}, u32[]{:S(2)}) collective-permute-start(bf16[4,576,128]{2,1,0:T(8,128)(2,1)} %collective-permute-done.4.refs_9_), channel_id=1, source_target_pairs={{4,0},{5,1},{6,2},{7,3},{8,4},{9,5},{10,6},{11,7},{20,16},{21,17},... | collective-permute-start | bytes 1769480 | tf_op jit(solution)/shard_map/ppermute | solution.py:271
  57.5 40.4 %collective-permute-start.6 = (bf16[4,576,128]{2,1,0:T(8,128)(2,1)}, bf16[4,576,128]{2,1,0:T(8,128)(2,1)}, u32[]{:S(2)}, u32[]{:S(2)}) collective-permute-start(bf16[4,576,128]{2,1,0:T(8,128)(2,1)} %collective-permute-done.2.refs_7_), channel_id=1, source_target_pairs={{4,8},{5,9},{6,10},{7,11},{8,12},{9,13},{10,14},{11,15},{20,24},{2... | collective-permute-start | bytes 1769480 | tf_op jit(solution)/shard_map/ppermute | solution.py:271
  59.6 49.1 %collective-permute-start.5 = (bf16[4,576,128]{2,1,0:T(8,128)(2,1)}, bf16[4,576,128]{2,1,0:T(8,128)(2,1)}, u32[]{:S(2)}, u32[]{:S(2)}) collective-permute-start(bf16[4,576,128]{2,1,0:T(8,128)(2,1)} %collective-permute-done.4.refs_9_), channel_id=1, source_target_pairs={{0,2},{1,3},{2,0},{3,1},{4,6},{5,7},{6,4},{7,5},{8,10},{9,11},{10,... | collective-permute-start | bytes 1769480 | tf_op jit(solution)/shard_map/ppermute | solution.py:279
  113.6 30.4 %collective-permute-start.7 = (bf16[4,576,128]{2,1,0:T(8,128)(2,1)}, bf16[4,576,128]{2,1,0:T(8,128)(2,1)S(1)}, u32[]{:S(2)}, u32[]{:S(2)}) collective-permute-start(bf16[4,576,128]{2,1,0:T(8,128)(2,1)} %collective-permute-done.6.refs_11_), channel_id=1, source_target_pairs={{8,10},{9,11},{10,8},{11,9},{12,14},{13,15},{14,12},{15,13},{24,26... | collective-permute-start | bytes 1769480 | tf_op jit(solution)/shard_map/ppermute | solution.py:279
  115.5 28.5 %collective-permute-start.13 = (bf16[4,576,128]{2,1,0:T(8,128)(2,1)}, bf16[4,576,128]{2,1,0:T(8,128)(2,1)S(1)}, u32[]{:S(2)}, u32[]{:S(2)}) collective-permute-start(bf16[4,576,128]{2,1,0:T(8,128)(2,1)} %collective-permute-done.12.refs_17_), channel_id=1, source_target_pairs={{0,2},{1,3},{2,0},{3,1},{16,18},{17,19},{18,16},{19,17}} | collective-permute-start | bytes 1769480 | tf_op jit(solution)/shard_map/ppermute | solution.py:279
  144.0 32.3 %collective-permute-start.18 = (bf16[1024,256]{1,0:T(8,128)(2,1)S(1)}, bf16[1024,256]{1,0:T(8,128)(2,1)}, u32[]{:S(2)}, u32[]{:S(2)}) collective-permute-start(bf16[1024,256]{1,0:T(8,128)(2,1)S(1)} %copy-done.11), channel_id=1, source_target_pairs={{0,2},{1,3},{2,0},{3,1},{4,6},{5,7},{6,4},{7,5},{8,10},{9,11},{10,... | collective-permute-start | bytes 1572872 | tf_op jit(solution)/shard_map/ppermute | solution.py:265
  146.5 29.8 %collective-permute-start.17 = (bf16[1024,256]{1,0:T(8,128)(2,1)S(1)}, bf16[1024,256]{1,0:T(8,128)(2,1)}, u32[]{:S(2)}, u32[]{:S(2)}) collective-permute-start(bf16[1024,256]{1,0:T(8,128)(2,1)S(1)} %copy-done.11), channel_id=1, source_target_pairs={{4,0},{5,1},{6,2},{7,3},{8,4},{9,5},{10,6},{11,7},{12,8},{13,9},{1... | collective-permute-start | bytes 1572872 | tf_op jit(solution)/shard_map/ppermute | solution.py:271
  148.4 27.9 %collective-permute-start.16 = (bf16[1024,256]{1,0:T(8,128)(2,1)S(1)}, bf16[1024,256]{1,0:T(8,128)(2,1)}, u32[]{:S(2)}, u32[]{:S(2)}) collective-permute-start(bf16[1024,256]{1,0:T(8,128)(2,1)S(1)} %copy-done.11), channel_id=1, source_target_pairs={{0,4},{1,5},{2,6},{3,7},{4,8},{5,9},{6,10},{7,11},{8,12},{9,13},{1... | collective-permute-start | bytes 1572872 | tf_op jit(solution)/shard_map/ppermute | solution.py:271
  176.3 36.4 %collective-permute-start.20 = (bf16[4,608,128]{2,1,0:T(8,128)(2,1)}, bf16[4,608,128]{2,1,0:T(8,128)(2,1)}, u32[]{:S(2)}, u32[]{:S(2)}) collective-permute-start(bf16[4,608,128]{2,1,0:T(8,128)(2,1)} %get-tuple-element.81), channel_id=1, source_target_pairs={{0,2},{1,3},{2,0},{3,1},{4,6},{5,7},{6,4},{7,5},{8,10},{9,11},{10,... | collective-permute-start | bytes 1867784 | tf_op jit(solution)/shard_map/ppermute | solution.py:265
  197.4 28.6 %collective-permute-start.22 = (bf16[4,608,128]{2,1,0:T(8,128)(2,1)}, bf16[4,608,128]{2,1,0:T(8,128)(2,1)}, u32[]{:S(2)}, u32[]{:S(2)}) collective-permute-start(bf16[4,608,128]{2,1,0:T(8,128)(2,1)} %get-tuple-element.85), channel_id=1, source_target_pairs={{0,2},{1,3},{2,0},{3,1},{4,6},{5,7},{6,4},{7,5},{8,10},{9,11},{10,... | collective-permute-start | bytes 1867784 | tf_op jit(solution)/shard_map/ppermute | solution.py:265
  197.5 32.2 %collective-permute-start.23 = (bf16[1024,256]{1,0:T(8,128)(2,1)}, bf16[1024,256]{1,0:T(8,128)(2,1)}, u32[]{:S(2)}, u32[]{:S(2)}) collective-permute-start(bf16[1024,256]{1,0:T(8,128)(2,1)} %collective-permute-done.16), channel_id=1, source_target_pairs={{4,8},{5,9},{6,10},{7,11},{8,12},{9,13},{10,14},{11,15},{20,24},{2... | collective-permute-start | bytes 1572872 | tf_op jit(solution)/shard_map/ppermute | solution.py:271
  199.4 30.3 %collective-permute-start.24 = (bf16[1024,256]{1,0:T(8,128)(2,1)}, bf16[1024,256]{1,0:T(8,128)(2,1)}, u32[]{:S(2)}, u32[]{:S(2)}) collective-permute-start(bf16[1024,256]{1,0:T(8,128)(2,1)} %collective-permute-done.17), channel_id=1, source_target_pairs={{4,0},{5,1},{6,2},{7,3},{8,4},{9,5},{10,6},{11,7},{20,16},{21,17},... | collective-permute-start | bytes 1572872 | tf_op jit(solution)/shard_map/ppermute | solution.py:271
  204.9 35.9 %collective-permute-start.21 = (bf16[4,608,128]{2,1,0:T(8,128)(2,1)}, bf16[4,608,128]{2,1,0:T(8,128)(2,1)}, u32[]{:S(2)}, u32[]{:S(2)}) collective-permute-start(bf16[4,608,128]{2,1,0:T(8,128)(2,1)} %get-tuple-element.83), channel_id=1, source_target_pairs={{0,2},{1,3},{2,0},{3,1},{4,6},{5,7},{6,4},{7,5},{8,10},{9,11},{10,... | collective-permute-start | bytes 1867784 | tf_op jit(solution)/shard_map/ppermute | solution.py:265
  240.8 27.5 %collective-permute-start.29 = (bf16[1024,256]{1,0:T(8,128)(2,1)}, bf16[1024,256]{1,0:T(8,128)(2,1)}, u32[]{:S(2)}, u32[]{:S(2)}) collective-permute-start(bf16[1024,256]{1,0:T(8,128)(2,1)} %collective-permute-done.16), channel_id=1, source_target_pairs={{4,6},{5,7},{6,4},{7,5},{8,10},{9,11},{10,8},{11,9},{12,14},{13,15... | collective-permute-start | bytes 1572872 | tf_op jit(solution)/shard_map/ppermute | solution.py:279
  294.9 44.3 %collective-permute-start.40 = (bf16[8,1024,256]{2,1,0:T(8,128)(2,1)}, bf16[8,1024,256]{2,1,0:T(8,128)(2,1)}, u32[]{:S(2)}, u32[]{:S(2)}) collective-permute-start(bf16[8,1024,256]{2,1,0:T(8,128)(2,1)} %bitcast_dynamic-update-slice_fusion.w_mine_ref), channel_id=1, source_target_pairs={{0,1},{1,0},{2,3},{3,2},{4,5},{5,4},{6,7},{7,6},{8,9},{9,8},{10,11... | collective-permute-start | bytes 12582920 | tf_op jit(solution)/shard_map/ppermute | solution.py:265
  295.0 37.1 %collective-permute-start.35 = (bf16[4,608,128]{2,1,0:T(8,128)(2,1)}, bf16[4,608,128]{2,1,0:T(8,128)(2,1)}, u32[]{:S(2)}, u32[]{:S(2)}) collective-permute-start(bf16[4,608,128]{2,1,0:T(8,128)(2,1)} %merge.15), channel_id=1, source_target_pairs={{0,4},{1,5},{2,6},{3,7},{4,8},{5,9},{6,10},{7,11},{8,12},{9,13},{1... | collective-permute-start | bytes 1867784 | tf_op jit(solution)/shard_map/ppermute | solution.py:271
  299.6 32.5 %collective-permute-start.36 = (bf16[4,608,128]{2,1,0:T(8,128)(2,1)}, bf16[4,608,128]{2,1,0:T(8,128)(2,1)}, u32[]{:S(2)}, u32[]{:S(2)}) collective-permute-start(bf16[4,608,128]{2,1,0:T(8,128)(2,1)} %merge.16), channel_id=1, source_target_pairs={{4,0},{5,1},{6,2},{7,3},{8,4},{9,5},{10,6},{11,7},{12,8},{13,9},{1... | collective-permute-start | bytes 1867784 | tf_op jit(solution)/shard_map/ppermute | solution.py:271
  347.1 28.3 %collective-permute-start.41 = (bf16[288,2048]{1,0:T(8,128)(2,1)}, bf16[288,2048]{1,0:T(8,128)(2,1)}, u32[]{:S(2)}, u32[]{:S(2)}) collective-permute-start(bf16[288,2048]{1,0:T(8,128)(2,1)} %project.2), channel_id=1, source_target_pairs={{0,16},{16,0},{1,17},{17,1},{2,18},{18,2},{3,19},{19,3},{4,20},{20... | collective-permute-start | bytes 3538952 | tf_op jit(solution)/shard_map/ppermute | solution.py:596
  (43 other events, 655.0 us)
Sparse Core Ops, SparseCore 0:
  10.3 109.4 all-gather.4
  122.0 100.0 all-gather.2

commit v6 on v4

--- a/solution.py
+++ b/solution.py
@@ -271,6 +271,12 @@
     return lax.ppermute(x, "pages", moves)
 
 
+def gather_line(x):
+    line = lax.axis_size("pages") // 4
+    groups = [[g + 4 * i for i in range(line)] for g in range(4)]
+    return lax.all_gather(x, "pages", axis=0, tiled=False, axis_index_groups=groups)
+
+
 def gather_lines(x):
     line = lax.axis_size("pages") // 4
     device_at = lax.axis_index("pages")
@@ -366,54 +372,61 @@
     )(q_chip, k_window, v_window, token_rows, key_cols)
 
 
-def project_kernel(at_ref, mine_ref, other_ref, w_ref, out_ref, rows_ref):
+def project_kernel(at_ref, mine_ref, other_ref, *refs):
+    w_refs, (out_ref, rows_ref) = refs[:4], refs[4:]
     core = at_ref[0]
     wide = rows_ref.shape[2]
 
-    @pl.when(pl.program_id(0) == 0)
+    @pl.when((pl.program_id(0) == 0) & (pl.program_id(1) == 0))
     def _():
         for index, ref in enumerate((mine_ref, other_ref)):
             rows_ref[index] = jnp.concatenate([ref[h] for h in range(ref.shape[0])], axis=1)
 
-    total = 0.0
-    for d in range(2):
-        feats = pl.ds(pl.multiple_of((core ^ d) * wide, wide), wide)
-        total = total + jnp.dot(
-            rows_ref[d], w_ref[0, feats, :], preferred_element_type=jnp.float32
-        )
-    out_ref[...] = total.astype(out_ref.dtype).reshape(out_ref.shape)
-
-
-def project(mine, other, weights, core, owner, groups, dtype):
+    for there in range(2):
+
+        @pl.when(pl.program_id(0) == there)
+        def _(there=there):
+            parts = []
+            for w_ref in w_refs[2 * there : 2 * there + 2]:
+                total = 0.0
+                for d in range(2):
+                    feats = pl.ds(pl.multiple_of((core ^ d) * wide, wide), wide)
+                    total = total + jnp.dot(
+                        rows_ref[d], w_ref[0, feats, :], preferred_element_type=jnp.float32
+                    )
+                parts.append(total)
+            out = jnp.where(
+                core == 0, jnp.concatenate(parts, axis=1), jnp.concatenate(parts[::-1], axis=1)
+            )
+            out_ref[...] = out.astype(out_ref.dtype)
+
+
+def project(mine, other, weights, core, across, owner, groups, dtype):
     half, tok_dev, head_dim = mine.shape
-    blocks, feats, cols = weights.shape
-    blocks //= groups
-    wide = cols % 128 == 0
-    if wide:
-        out_spec = pl.BlockSpec((tok_dev, cols), lambda j, at: (0, j))
-        out_shape = (tok_dev, blocks * cols)
-    else:
-        out_spec = pl.BlockSpec((1, tok_dev, cols), lambda j, at: (j, 0, 0))
-        out_shape = (blocks, tok_dev, cols)
-    rows_spec = pl.BlockSpec(mine.shape, lambda j, at: (0, 0, 0))
-    out = pl.pallas_call(
+    line, feats, cols = weights[0].shape
+    share = line // groups
+    rows_spec = pl.BlockSpec(mine.shape, lambda y, z, at: (0, 0, 0))
+
+    def weight_spec(there):
+        def place(y, z, at):
+            here = (y == there).astype(jnp.int32)
+            return (at[2] * share + here * z + (1 - here) * (1 - there) * (share - 1), 0, 0)
+
+        return pl.BlockSpec((1, feats, cols), place)
+
+    return pl.pallas_call(
         project_kernel,
         grid_spec=pltpu.PrefetchScalarGridSpec(
             num_scalar_prefetch=1,
-            grid=(blocks,),
-            in_specs=[
-                rows_spec,
-                rows_spec,
-                pl.BlockSpec((1, feats, cols), lambda j, at: (at[1] * blocks + j, 0, 0)),
-            ],
-            out_specs=out_spec,
+            grid=(2, share),
+            in_specs=[rows_spec, rows_spec] + [weight_spec(t) for t in (0, 0, 1, 1)],
+            out_specs=pl.BlockSpec((tok_dev, 2 * cols), lambda y, z, at: (0, 2 * z + (y ^ at[1]))),
             scratch_shapes=[pltpu.VMEM((2, tok_dev, half * head_dim), jnp.bfloat16)],
         ),
-        out_shape=jax.ShapeDtypeStruct(out_shape, dtype),
-        compiler_params=pltpu.CompilerParams(vmem_limit_bytes=40 * 2**20),
+        out_shape=jax.ShapeDtypeStruct((tok_dev, 4 * share * cols), dtype),
+        compiler_params=pltpu.CompilerParams(vmem_limit_bytes=60 * 2**20),
         name="project",
-    )(jnp.stack([core, owner]), mine, other, weights)
-    return out if wide else jnp.transpose(out, (1, 0, 2)).reshape(tok_dev, blocks * cols)
+    )(jnp.stack([core, across, owner]), mine, other, *weights)
 
 
 def per_device(
@@ -476,7 +489,9 @@
     all_v = lax.all_gather(values, "pages", axis=0, tiled=True)
     all_k = with_layout_constraint(all_k, natural)
     all_v = with_layout_constraint(all_v, natural)
-    weights = lax.all_gather(out_weight, "pages", axis=0, tiled=False)
+    barrier = lax.optimization_barrier
+    q_list, line_w = barrier((q_list, gather_line(out_weight)))
+    across_w = swap(line_w, 2)
 
     my_slots = device_at * slot_count + jnp.arange(slot_count, dtype=jnp.int32)
     chip_slots = jnp.concatenate(
@@ -525,6 +540,7 @@
         unit,
         scale2,
     )
+    outs, across_w = barrier((outs, across_w))
     merged = lambda parts, ok: merge(parts, ok, chip_len, unit, scale2)
 
     def fresh_part():
@@ -551,11 +567,19 @@
     )
     rows_of = lambda c: lax.dynamic_slice_in_dim(chip_part[:, :chip_len], c * tok_dev, tok_dev, 1)
     own_rows, got_rows = rows_of(core), swap(rows_of(1 - core), 1)
+    weights = [line_w, swap(line_w, 1), across_w, swap(across_w, 1)]
     total = out_bias[None, :]
     for s in range(groups - 1, -1, -1):
         owner = (group_at + s) % groups
         part = project(
-            own_rows, got_rows, weights, core, owner, groups, jnp.bfloat16 if s else jnp.float32
+            own_rows,
+            got_rows,
+            weights,
+            core,
+            across,
+            owner,
+            groups,
+            jnp.bfloat16 if s else jnp.float32,
         )
         if s:
             part = lax.ppermute(part, "heads", [(h, (h + s) % groups) for h in range(groups)])

time: 383 us -> 403 us (1.052)
  waiting for transfers between devices: 151 us -> 179 us
  Pallas kernels: 99.8 us -> 93.9 us
    ppermute x9 -> x12, waiting for transfers between devices: 36 us -> 70.2 us  [swap(): return lax.ppermute(x, 'pages', [(p, p ^ bit) for p in range(devs)])]
    ppermute x12, waiting for transfers between devices: 90.4 us -> 69.3 us  [shift(): return lax.ppermute(x, 'pages', moves)]
    ppermute x3, waiting for transfers between devices: 9.85 us -> 28.9 us  [gather_lines(): lax.ppermute(down, 'pages', cross_down)]
    pallas_call x1, Pallas kernels: 39.3 us -> 29.9 us  [cached_attention(): pl.pallas_call(lambda *refs: cached_kernel(unit, stat_unit, span, scale2,...]
    unnamed x39 -> x37, local copies, waits for them, and re-layouts: 21.7 us -> 20.1 us
  transfers between devices with their start and end apart: 31 -> 34, of which waited for: 14 -> 15; matrix products, arithmetic and copies ran while one was open for 12% -> 13% of each run, Pallas kernels for 25% -> 22%
where the time goes in v6:
time: 403 us; the launch traced here: 397 us
  waiting for transfers between devices  179 us (44%)
  Pallas kernels  93.9 us (23%)
  starting transfers between devices  47.4 us (12%)
  local copies, waits for them, and re-layouts  36.6 us (9%)
  other arithmetic  26 us (6%)
  between operations  14.1 us (3%)
    ppermute x12, waiting for transfers between devices, swap(): return lax.ppermute(x, 'pages', [(p, p ^ bit) for p in range(devs)])  70.2 us
    ppermute x12, waiting for transfers between devices, shift(): return lax.ppermute(x, 'pages', moves)  69.3 us
    pallas_call x9, Pallas kernels, merge(): pl.pallas_call(lambda *refs: merge_kernel(unit, part_len, scale2, *refs),...  34.2 us
    pallas_call x1, Pallas kernels, cached_attention(): pl.pallas_call(lambda *refs: cached_kernel(unit, stat_unit, span, scale2,...  29.9 us
    ppermute x3, waiting for transfers between devices, gather_lines(): lax.ppermute(down, 'pages', cross_down)  28.9 us
    ppermute x12, starting transfers between devices, shift(): return lax.ppermute(x, 'pages', moves)  28.2 us
    unnamed x37, local copies, waits for them, and re-layouts  20.1 us
    pallas_call x2, Pallas kernels, project(): pl.pallas_call(project_kernel, grid_spec=pltpu.PrefetchScalarGridSpec(num...  12.9 us
  transfers between devices with their start and end apart: 34, of which 15 were waited for; matrix products, arithmetic and copies ran while one was open for 13% of the time, Pallas kernels for 22%

profile of v6, /device:TPU:12, one launch (start us, length us, event | category | flops | bytes accessed | tf_op | source)
XLA Modules:
  0.0 397.4 jit_solution(1534098354313896389)
XLA Ops:
  30.0 7.3 %constant_dynamic-slice_fusion.5 = (bf16[12,128,4,128]{3,2,1,0:T(4,128)(2,1)}, bf16[12,128,4,128]{3,2,1,0:T(4,128)(2,1)}, bf16[12,128,4,128]{3,2,1,0:T(4,128)(2,1)S(1)}, bf16[12,128,4,128]{3,2,1,0:T(4,128)(2,1)}) fusion(bf16[12,128,8,128]{3,2,1,0:T(8,128)(2,1)S(1)} %copy-done, s32[]{:T(128)S(6)} %select_n.169, s32[]{:T(128)S(6)} %select_n.170, ...), kind=kLoop, calls=%fused_computation.47 | loop fusion | bytes 12582920 | tf_op jit(solution)/shard_map/dynamic-slice.4
  38.9 3.8 copy.62
  43.7 21.9 %collective-permute-done.2.refs_7_ = bf16[4,576,128]{2,1,0:T(8,128)(2,1)} collective-permute-done((bf16[4,576,128]{2,1,0:T(8,128)(2,1)}, bf16[4,576,128]{2,1,0:T(8,128)(2,1)}, u32[]{:S(2)}, u32[]{:S(2)}) %collective-permute-start.2) | collective-permute-done | bytes 589856 | tf_op jit(solution)/shard_map/ppermute | solution.py:271
  65.6 5.2 %collective-permute-start.6 = (bf16[4,576,128]{2,1,0:T(8,128)(2,1)}, bf16[4,576,128]{2,1,0:T(8,128)(2,1)}, u32[]{:S(2)}, u32[]{:S(2)}) collective-permute-start(bf16[4,576,128]{2,1,0:T(8,128)(2,1)} %collective-permute-done.2.refs_7_), channel_id=1, source_target_pairs={{4,8},{5,9},{6,10},{7,11},{8,12},{9,13},{10,14},{11,15},{20,24},{2... | collective-permute-start | bytes 1769480 | tf_op jit(solution)/shard_map/ppermute | solution.py:271
  75.3 16.6 %collective-permute-done.6.refs_11_ = bf16[4,576,128]{2,1,0:T(8,128)(2,1)} collective-permute-done((bf16[4,576,128]{2,1,0:T(8,128)(2,1)}, bf16[4,576,128]{2,1,0:T(8,128)(2,1)}, u32[]{:S(2)}, u32[]{:S(2)}) %collective-permute-start.6) | collective-permute-done | bytes 589856 | tf_op jit(solution)/shard_map/ppermute | solution.py:271
  93.5 10.1 %collective-permute-done.8.refs_13_ = bf16[4,576,128]{2,1,0:T(8,128)(2,1)} collective-permute-done((bf16[4,576,128]{2,1,0:T(8,128)(2,1)}, bf16[4,576,128]{2,1,0:T(8,128)(2,1)}, u32[]{:S(2)}, u32[]{:S(2)}) %collective-permute-start.8) | collective-permute-done | bytes 589856 | tf_op jit(solution)/shard_map/ppermute | solution.py:271
  108.7 3.8 copy.61
  123.0 4.2 %collective-permute-done.12.refs_17_ = bf16[4,576,128]{2,1,0:T(8,128)(2,1)} collective-permute-done((bf16[4,576,128]{2,1,0:T(8,128)(2,1)}, bf16[4,576,128]{2,1,0:T(8,128)(2,1)}, u32[]{:S(2)}, u32[]{:S(2)}) %collective-permute-start.12) | collective-permute-done | bytes 589856 | tf_op jit(solution)/shard_map/ppermute | solution.py:271
  130.1 3.9 pad_maximum_fusion.refs_19_
  137.4 7.6 %collective-permute-done.5.refs_10_ = bf16[4,576,128]{2,1,0:T(8,128)(2,1)} collective-permute-done((bf16[4,576,128]{2,1,0:T(8,128)(2,1)}, bf16[4,576,128]{2,1,0:T(8,128)(2,1)}, u32[]{:S(2)}, u32[]{:S(2)}) %collective-permute-start.5) | collective-permute-done | bytes 589856 | tf_op jit(solution)/shard_map/ppermute | solution.py:299
  145.0 21.2 %collective-permute-done.9.refs_14_ = bf16[4,576,128]{2,1,0:T(8,128)(2,1)} collective-permute-done((bf16[4,576,128]{2,1,0:T(8,128)(2,1)}, bf16[4,576,128]{2,1,0:T(8,128)(2,1)}, u32[]{:S(2)}, u32[]{:S(2)}) %collective-permute-start.9) | collective-permute-done | bytes 589856 | tf_op jit(solution)/shard_map/ppermute | solution.py:299
  166.6 29.9 %cached_attention.1 = (bf16[4,608,128]{2,1,0:T(8,128)(2,1)}, bf16[4,608,128]{2,1,0:T(8,128)(2,1)}, bf16[4,608,128]{2,1,0:T(8,128)(2,1)}, bf16[4,608,128]{2,1,0:T...) custom-call(s32[22]{0:T(128)} %stack.209.refs_0_, ...), custom_call_target="tpu_custom_call" | custom-call | flops 40000000000 | bytes 20971520 | tf_op jit(solution)/shard_map/cached_attention/pallas_call | solution.py:155
  196.4 24.1 %collective-permute-done.16.refs_2_ = bf16[4,1024,256]{2,1,0:T(8,128)(2,1)} collective-permute-done((bf16[4,1024,256]{2,1,0:T(8,128)(2,1)}, bf16[4,1024,256]{2,1,0:T(8,128)(2,1)}, u32[]{:S(2)}, u32[]{:S(2)}) %collective-permute-start.16) | collective-permute-done | bytes 2097184 | tf_op jit(solution)/shard_map/ppermute | solution.py:265
  222.6 28.3 %collective-permute-done.18.refs_2_ = bf16[4,608,128]{2,1,0:T(8,128)(2,1)} collective-permute-done((bf16[4,608,128]{2,1,0:T(8,128)(2,1)}, bf16[4,608,128]{2,1,0:T(8,128)(2,1)}, u32[]{:S(2)}, u32[]{:S(2)}) %collective-permute-start.18) | collective-permute-done | bytes 622624 | tf_op jit(solution)/shard_map/ppermute | solution.py:265
  256.0 14.6 %collective-permute-done.20.refs_2_ = bf16[4,608,128]{2,1,0:T(8,128)(2,1)} collective-permute-done((bf16[4,608,128]{2,1,0:T(8,128)(2,1)}, bf16[4,608,128]{2,1,0:T(8,128)(2,1)}, u32[]{:S(2)}, u32[]{:S(2)}) %collective-permute-start.20) | collective-permute-done | bytes 622624 | tf_op jit(solution)/shard_map/ppermute | solution.py:265
  277.4 3.7 merge.11.refs_1_
  286.1 7.8 %collective-permute-done.21.refs_2_ = bf16[4,608,128]{2,1,0:T(8,128)(2,1)} collective-permute-done((bf16[4,608,128]{2,1,0:T(8,128)(2,1)}, bf16[4,608,128]{2,1,0:T(8,128)(2,1)}, u32[]{:S(2)}, u32[]{:S(2)}) %collective-permute-start.21) | collective-permute-done | bytes 622624 | tf_op jit(solution)/shard_map/ppermute | solution.py:271
  309.7 6.6 %collective-permute-done.22.refs_2_ = bf16[4,608,128]{2,1,0:T(8,128)(2,1)} collective-permute-done((bf16[4,608,128]{2,1,0:T(8,128)(2,1)}, bf16[4,608,128]{2,1,0:T(8,128)(2,1)}, u32[]{:S(2)}, u32[]{:S(2)}) %collective-permute-start.22) | collective-permute-done | bytes 622624 | tf_op jit(solution)/shard_map/ppermute | solution.py:271
  333.6 9.4 %fresh_attention.1.refs_4_ = bf16[4,608,128]{2,1,0:T(8,128)(2,1)S(1)} custom-call(bf16[4,576,128]{2,1,0:T(8,128)(2,1)} %maximum_select_fusion.refs_5_.refs_0_, bf16[4,1152,128]{2,1,0:T(8,128)(2,1)S(1)} %bitcast.57, bf16[4,1152,128]{2,1,0:T(8,128)(2,1)S(1)} %bitcast.58, s32[2,576]{1,0:T(2,128)S(1)} %pad_add_fusion.refs_3_, s32[1152,1]{1,0:T(8,128)S(1)} %copy-done.4), custom_call_target="tpu_custom_call" | custom-call | tf_op jit(solution)/shard_map/fresh_attention/pallas_call | solution.py:364
  343.8 4.6 %merge.17 = bf16[4,608,128]{2,1,0:T(8,128)(2,1)} custom-call(s32[4]{0:T(128)} %pad_add_fusion.6.refs_0_, bf16[4,608,128]{2,1,0:T(8,128)(2,1)} %merge.9.refs_1_, bf16[4,608,128]{2,1,0:T(8,128)(2,1)} %collective-permute-done.23.refs_2_, bf16[4,608,128]{2,1,0:T(8,128)(2,1)} %collective-permute-done.26.refs_3_, bf16[4,608,128]{2,1,0:T(8,128)(2,1)} %copy-done.3), custom_call_target="tpu_custom_call" | custom-call | tf_op jit(solution)/shard_map/merge/pallas_call | solution.py:218
  352.9 6.3 %project.2 = bf16[288,2048]{1,0:T(8,128)(2,1)} custom-call(s32[3]{0:T(128)} %pad_add_fusion.4.at_ref, bf16[4,288,128]{2,1,0:T(8,128)(2,1)} %get-tuple-element.82.mine_ref, bf16[4,288,128]{2,1,0:T(8,128)(2,1)} %copy-done.9, bf16[4,1024,256]{2,1,0:T(8,128)(2,1)} %bitcast.63, bf16[4,1024,256]{2,1,0:T(8,128)(2,1)} %collective-permute-done.28.refs_1_, ...), custom_call_target="tpu_custom_call" | custom-call | tf_op jit(solution)/shard_map/project/pallas_call | solution.py:417
  363.7 7.6 %write_pages.1 = (bf16[12,128,8,128]{3,2,1,0:T(8,128)(2,1)}, bf16[12,128,8,128]{3,2,1,0:T(8,128)(2,1)}) custom-call(s32[12]{0:T(128)S(1)} %convert_element_type.53.fresh_ref, s32[12]{0:T(128)S(1)} %fusion.2.index_ref, bf16[12,128,8,128]{3,2,1,0:T(8,128)(2,1)S(1)} %copy-done.1, bf16[12,128,8,128]{3,2,1,0:T(8,128)(2,1)S(1)} %copy-done, ...), custom_call_target="tpu_custom_call" | custom-call | tf_op jit(solution)/shard_map/write_pages/pallas_call | solution.py:249
  371.3 6.6 %project.3 = f32[288,2048]{1,0:T(8,128)} custom-call(s32[3]{0:T(128)} %pad_add_fusion.8.at_ref, bf16[4,288,128]{2,1,0:T(8,128)(2,1)} %get-tuple-element.82.mine_ref, bf16[4,288,128]{2,1,0:T(8,128)(2,1)} %copy-done.9, bf16[4,1024,256]{2,1,0:T(8,128)(2,1)} %bitcast.64, bf16[4,1024,256]{2,1,0:T(8,128)(2,1)} %collective-permute-done.28.refs_1_, ...), custom_call_target="tpu_custom_call" | custom-call | tf_op jit(solution)/shard_map/project/pallas_call | solution.py:417
  377.9 9.6 %collective-permute-done.30 = bf16[288,2048]{1,0:T(8,128)(2,1)} collective-permute-done((bf16[288,2048]{1,0:T(8,128)(2,1)}, bf16[288,2048]{1,0:T(8,128)(2,1)}, u32[]{:S(2)}, u32[]{:S(2)}) %collective-permute-start.30) | collective-permute-done | bytes 1179680 | tf_op jit(solution)/shard_map/ppermute | solution.py:585
  (153 shorter events, 118.5 us)
Async XLA Ops:
  7.2 159.1 %all-gather.9.cloned.1.call-start = ((), (), s32[]{:S(2)}) async-start(), calls=%async_computation.2 | async-start | bytes 2621440 | tf_op jit(solution)/shard_map/all_gather | solution.py:277
  7.9 319.2 %all-gather.5.cloned.1.call-start = ((), (), s32[]{:S(2)}) async-start(), calls=%async_computation | async-start | bytes 10027008 | tf_op jit(solution)/shard_map/all_gather | solution.py:488
  14.2 316.1 %all-gather.7.cloned.1.call-start = ((), (), s32[]{:S(2)}) async-start(), calls=%async_computation.1 | async-start | bytes 10027008 | tf_op jit(solution)/shard_map/all_gather | solution.py:489
  23.3 42.4 %collective-permute-start.2 = (bf16[4,576,128]{2,1,0:T(8,128)(2,1)}, bf16[4,576,128]{2,1,0:T(8,128)(2,1)}, u32[]{:S(2)}, u32[]{:S(2)}) collective-permute-start(bf16[4,576,128]{2,1,0:T(8,128)(2,1)} %maximum_select_fusion.refs_5_.refs_0_), channel_id=1, source_target_pairs={{0,4},{1,5},{2,6},{3,7},{4,8},{5,9},{6,10},{7,11},{8,12},{9,13},{1... | collective-permute-start | bytes 1769480 | tf_op jit(solution)/shard_map/ppermute | solution.py:271
  26.7 44.1 %collective-permute-start.4 = (bf16[4,576,128]{2,1,0:T(8,128)(2,1)}, bf16[4,576,128]{2,1,0:T(8,128)(2,1)}, u32[]{:S(2)}, u32[]{:S(2)}) collective-permute-start(bf16[4,576,128]{2,1,0:T(8,128)(2,1)} %maximum_select_fusion.refs_5_.refs_0_), channel_id=1, source_target_pairs={{4,0},{5,1},{6,2},{7,3},{8,4},{9,5},{10,6},{11,7},{12,8},{13,9},{1... | collective-permute-start | bytes 1769480 | tf_op jit(solution)/shard_map/ppermute | solution.py:271
  38.9 78.4 %collective-permute-start.14 = (bf16[4,12,128,128]{3,2,1,0:T(8,128)(2,1)}, bf16[4,12,128,128]{3,2,1,0:T(8,128)(2,1)}, u32[]{:S(2)}, u32[]{:S(2)}) collective-permute-start(bf16[4,12,128,128]{3,2,1,0:T(8,128)(2,1)} %bitcast.53), channel_id=1, source_target_pairs={{0,1},{1,0},{2,3},{3,2},{4,5},{5,4},{6,7},{7,6},{8,9},{9,8},{10,11... | collective-permute-start | bytes 4718600 | tf_op jit(solution)/shard_map/ppermute | solution.py:265
  42.6 76.1 %collective-permute-start.15 = (bf16[4,12,128,128]{3,2,1,0:T(8,128)(2,1)}, bf16[4,12,128,128]{3,2,1,0:T(8,128)(2,1)}, u32[]{:S(2)}, u32[]{:S(2)}) collective-permute-start(bf16[4,12,128,128]{3,2,1,0:T(8,128)(2,1)} %bitcast.67), channel_id=1, source_target_pairs={{0,1},{1,0},{2,3},{3,2},{4,5},{5,4},{6,7},{7,6},{8,9},{9,8},{10,11... | collective-permute-start | bytes 4718600 | tf_op jit(solution)/shard_map/ppermute | solution.py:265
  43.2 29.8 %collective-permute-start.1 = (bf16[4,576,128]{2,1,0:T(8,128)(2,1)}, bf16[4,576,128]{2,1,0:T(8,128)(2,1)}, u32[]{:S(2)}, u32[]{:S(2)}) collective-permute-start(bf16[4,576,128]{2,1,0:T(8,128)(2,1)} %maximum_select_fusion.refs_5_.refs_0_), channel_id=1, source_target_pairs={{0,2},{1,3},{2,0},{3,1},{4,6},{5,7},{6,4},{7,5},{8,10},{9,11},{10,... | collective-permute-start | bytes 1769480 | tf_op jit(solution)/shard_map/ppermute | solution.py:265
  70.8 32.7 %collective-permute-start.8 = (bf16[4,576,128]{2,1,0:T(8,128)(2,1)}, bf16[4,576,128]{2,1,0:T(8,128)(2,1)}, u32[]{:S(2)}, u32[]{:S(2)}) collective-permute-start(bf16[4,576,128]{2,1,0:T(8,128)(2,1)} %collective-permute-done.4.refs_9_), channel_id=1, source_target_pairs={{4,0},{5,1},{6,2},{7,3},{8,4},{9,5},{10,6},{11,7},{20,16},{21,17},... | collective-permute-start | bytes 1769480 | tf_op jit(solution)/shard_map/ppermute | solution.py:271
  73.0 41.2 %collective-permute-start.3 = (bf16[4,576,128]{2,1,0:T(8,128)(2,1)}, bf16[4,576,128]{2,1,0:T(8,128)(2,1)}, u32[]{:S(2)}, u32[]{:S(2)}) collective-permute-start(bf16[4,576,128]{2,1,0:T(8,128)(2,1)} %collective-permute-done.2.refs_7_), channel_id=1, source_target_pairs={{4,6},{5,7},{6,4},{7,5},{8,10},{9,11},{10,8},{11,9},{12,14},{13,15... | collective-permute-start | bytes 1769480 | tf_op jit(solution)/shard_map/ppermute | solution.py:297
  92.0 29.6 %collective-permute-start.10 = (bf16[4,576,128]{2,1,0:T(8,128)(2,1)}, bf16[4,576,128]{2,1,0:T(8,128)(2,1)}, u32[]{:S(2)}, u32[]{:S(2)}) collective-permute-start(bf16[4,576,128]{2,1,0:T(8,128)(2,1)} %collective-permute-done.6.refs_11_), channel_id=1, source_target_pairs={{8,12},{9,13},{10,14},{11,15},{24,28},{25,29},{26,30},{27,31}} | collective-permute-start | bytes 1769480 | tf_op jit(solution)/shard_map/ppermute | solution.py:271
  114.2 30.8 %collective-permute-start.5 = (bf16[4,576,128]{2,1,0:T(8,128)(2,1)}, bf16[4,576,128]{2,1,0:T(8,128)(2,1)}, u32[]{:S(2)}, u32[]{:S(2)}) collective-permute-start(bf16[4,576,128]{2,1,0:T(8,128)(2,1)} %collective-permute-done.4.refs_9_), channel_id=1, source_target_pairs={{0,2},{1,3},{2,0},{3,1},{4,6},{5,7},{6,4},{7,5},{8,10},{9,11},{10,... | collective-permute-start | bytes 1769480 | tf_op jit(solution)/shard_map/ppermute | solution.py:299
  117.3 27.7 %collective-permute-start.7 = (bf16[4,576,128]{2,1,0:T(8,128)(2,1)}, bf16[4,576,128]{2,1,0:T(8,128)(2,1)}, u32[]{:S(2)}, u32[]{:S(2)}) collective-permute-start(bf16[4,576,128]{2,1,0:T(8,128)(2,1)} %collective-permute-done.6.refs_11_), channel_id=1, source_target_pairs={{8,10},{9,11},{10,8},{11,9},{12,14},{13,15},{14,12},{15,13},{24,26... | collective-permute-start | bytes 1769480 | tf_op jit(solution)/shard_map/ppermute | solution.py:297
  118.8 47.5 %collective-permute-start.9 = (bf16[4,576,128]{2,1,0:T(8,128)(2,1)}, bf16[4,576,128]{2,1,0:T(8,128)(2,1)}, u32[]{:S(2)}, u32[]{:S(2)}) collective-permute-start(bf16[4,576,128]{2,1,0:T(8,128)(2,1)} %collective-permute-done.8.refs_13_), channel_id=1, source_target_pairs={{0,2},{1,3},{2,0},{3,1},{4,6},{5,7},{6,4},{7,5},{16,18},{17,19},{1... | collective-permute-start | bytes 1769480 | tf_op jit(solution)/shard_map/ppermute | solution.py:299
  121.5 44.7 %collective-permute-start.11 = (bf16[4,576,128]{2,1,0:T(8,128)(2,1)}, bf16[4,576,128]{2,1,0:T(8,128)(2,1)}, u32[]{:S(2)}, u32[]{:S(2)}) collective-permute-start(bf16[4,576,128]{2,1,0:T(8,128)(2,1)} %collective-permute-done.10.refs_15_), channel_id=1, source_target_pairs={{12,14},{13,15},{14,12},{15,13},{28,30},{29,31},{30,28},{31,29}} | collective-permute-start | bytes 1769480 | tf_op jit(solution)/shard_map/ppermute | solution.py:297
  127.2 39.0 %collective-permute-start.13 = (bf16[4,576,128]{2,1,0:T(8,128)(2,1)}, bf16[4,576,128]{2,1,0:T(8,128)(2,1)}, u32[]{:S(2)}, u32[]{:S(2)}) collective-permute-start(bf16[4,576,128]{2,1,0:T(8,128)(2,1)} %collective-permute-done.12.refs_17_), channel_id=1, source_target_pairs={{0,2},{1,3},{2,0},{3,1},{16,18},{17,19},{18,16},{19,17}} | collective-permute-start | bytes 1769480 | tf_op jit(solution)/shard_map/ppermute | solution.py:299
  166.3 54.3 %collective-permute-start.16 = (bf16[4,1024,256]{2,1,0:T(8,128)(2,1)}, bf16[4,1024,256]{2,1,0:T(8,128)(2,1)}, u32[]{:S(2)}, u32[]{:S(2)}) collective-permute-start(bf16[4,1024,256]{2,1,0:T(8,128)(2,1)} %bitcast.61), channel_id=1, source_target_pairs={{0,2},{1,3},{2,0},{3,1},{4,6},{5,7},{6,4},{7,5},{8,10},{9,11},{10,... | collective-permute-start | bytes 6291464 | tf_op jit(solution)/shard_map/ppermute | solution.py:265
  220.5 30.3 %collective-permute-start.18 = (bf16[4,608,128]{2,1,0:T(8,128)(2,1)}, bf16[4,608,128]{2,1,0:T(8,128)(2,1)}, u32[]{:S(2)}, u32[]{:S(2)}) collective-permute-start(bf16[4,608,128]{2,1,0:T(8,128)(2,1)} %get-tuple-element.63), channel_id=1, source_target_pairs={{0,2},{1,3},{2,0},{3,1},{4,6},{5,7},{6,4},{7,5},{8,10},{9,11},{10,... | collective-permute-start | bytes 1867784 | tf_op jit(solution)/shard_map/ppermute | solution.py:265
  220.5 50.1 %collective-permute-start.20 = (bf16[4,608,128]{2,1,0:T(8,128)(2,1)}, bf16[4,608,128]{2,1,0:T(8,128)(2,1)}, u32[]{:S(2)}, u32[]{:S(2)}) collective-permute-start(bf16[4,608,128]{2,1,0:T(8,128)(2,1)} %get-tuple-element.67), channel_id=1, source_target_pairs={{0,2},{1,3},{2,0},{3,1},{4,6},{5,7},{6,4},{7,5},{8,10},{9,11},{10,... | collective-permute-start | bytes 1867784 | tf_op jit(solution)/shard_map/ppermute | solution.py:265
  222.6 54.9 %collective-permute-start.19 = (bf16[4,608,128]{2,1,0:T(8,128)(2,1)}, bf16[4,608,128]{2,1,0:T(8,128)(2,1)}, u32[]{:S(2)}, u32[]{:S(2)}) collective-permute-start(bf16[4,608,128]{2,1,0:T(8,128)(2,1)} %get-tuple-element.65), channel_id=1, source_target_pairs={{0,2},{1,3},{2,0},{3,1},{4,6},{5,7},{6,4},{7,5},{8,10},{9,11},{10,... | collective-permute-start | bytes 1867784 | tf_op jit(solution)/shard_map/ppermute | solution.py:265
  275.7 75.3 %collective-permute-start.28 = (bf16[4,1024,256]{2,1,0:T(8,128)(2,1)}, bf16[4,1024,256]{2,1,0:T(8,128)(2,1)}, u32[]{:S(2)}, u32[]{:S(2)}) collective-permute-start(bf16[4,1024,256]{2,1,0:T(8,128)(2,1)} %bitcast.62), channel_id=1, source_target_pairs={{0,1},{1,0},{2,3},{3,2},{4,5},{5,4},{6,7},{7,6},{8,9},{9,8},{10,11... | collective-permute-start | bytes 6291464 | tf_op jit(solution)/shard_map/ppermute | solution.py:265
  275.7 75.2 %collective-permute-start.29 = (bf16[4,1024,256]{2,1,0:T(8,128)(2,1)}, bf16[4,1024,256]{2,1,0:T(8,128)(2,1)}, u32[]{:S(2)}, u32[]{:S(2)}) collective-permute-start(bf16[4,1024,256]{2,1,0:T(8,128)(2,1)} %collective-permute-done.16.refs_2_), channel_id=1, source_target_pairs={{0,1},{1,0},{2,3},{3,2},{4,5},{5,4},{6,7},{7,6},{8,9},{9,8},{10,11... | collective-permute-start | bytes 6291464 | tf_op jit(solution)/shard_map/ppermute | solution.py:265
  306.7 37.1 %collective-permute-start.26 = (bf16[4,608,128]{2,1,0:T(8,128)(2,1)}, bf16[4,608,128]{2,1,0:T(8,128)(2,1)}, u32[]{:S(2)}, u32[]{:S(2)}) collective-permute-start(bf16[4,608,128]{2,1,0:T(8,128)(2,1)} %merge.16), channel_id=1, source_target_pairs={{4,0},{5,1},{6,2},{7,3},{8,4},{9,5},{10,6},{11,7},{12,8},{13,9},{1... | collective-permute-start | bytes 1867784 | tf_op jit(solution)/shard_map/ppermute | solution.py:271
  359.2 28.3 %collective-permute-start.30 = (bf16[288,2048]{1,0:T(8,128)(2,1)}, bf16[288,2048]{1,0:T(8,128)(2,1)}, u32[]{:S(2)}, u32[]{:S(2)}) collective-permute-start(bf16[288,2048]{1,0:T(8,128)(2,1)} %project.2), channel_id=1, source_target_pairs={{0,16},{16,0},{1,17},{17,1},{2,18},{18,2},{3,19},{19,3},{4,20},{20... | collective-permute-start | bytes 3538952 | tf_op jit(solution)/shard_map/ppermute | solution.py:585
  (26 other events, 296.6 us)
Sparse Core Ops, SparseCore 0:
  9.6 58.1 all-gather.8
  70.0 110.8 all-gather.4
  183.2 106.1 all-gather.6

commit v7 on v4

--- a/solution.py
+++ b/solution.py
@@ -103,16 +103,17 @@
                     v, weights.astype(jnp.bfloat16), preferred_element_type=jnp.float32
                 )
 
-        def pair(index, _):
-            at = first + 2 * index
-            pages([order_ref[at], order_ref[at + 1]])
+        def four(index, _):
+            pages([order_ref[first + 4 * index + i] for i in range(4)])
             return 0
 
-        lax.fori_loop(0, count // 2, pair, 0)
-
-        @pl.when(count % 2 == 1)
-        def _():
-            pages([order_ref[first + count - 1]])
+        lax.fori_loop(0, count // 4, four, 0)
+        for many in (2, 1):
+
+            @pl.when((count // many) % 2 == 1)
+            def _(many=many):
+                at = first + count // (2 * many) * (2 * many)
+                pages([order_ref[at + i] for i in range(many)])
 
         totals = l_scr[...]
         peaks = m_scr[...]
@@ -410,7 +411,7 @@
             scratch_shapes=[pltpu.VMEM((2, tok_dev, half * head_dim), jnp.bfloat16)],
         ),
         out_shape=jax.ShapeDtypeStruct(out_shape, dtype),
-        compiler_params=pltpu.CompilerParams(vmem_limit_bytes=40 * 2**20),
+        compiler_params=pltpu.CompilerParams(vmem_limit_bytes=60 * 2**20),
         name="project",
     )(jnp.stack([core, owner]), mine, other, weights)
     return out if wide else jnp.transpose(out, (1, 0, 2)).reshape(tok_dev, blocks * cols)
@@ -472,11 +473,22 @@
     group_at = lax.axis_index("heads")
     q_list = [q for q, _, _, _ in q_places]
     natural = Layout((0, 1, 2))
-    all_k = lax.all_gather(rotated_k, "pages", axis=0, tiled=True)
-    all_v = lax.all_gather(values, "pages", axis=0, tiled=True)
+    late_k, late_v, _ = lax.optimization_barrier((rotated_k, values, q_list[2]))
+    all_k = lax.all_gather(late_k, "pages", axis=0, tiled=True)
+    all_v = lax.all_gather(late_v, "pages", axis=0, tiled=True)
     all_k = with_layout_constraint(all_k, natural)
     all_v = with_layout_constraint(all_v, natural)
     weights = lax.all_gather(out_weight, "pages", axis=0, tiled=False)
+    own_kv = jnp.stack([jnp.transpose(rotated_k, (1, 0, 2)), jnp.transpose(values, (1, 0, 2))], 1)
+    kv_mine, kv_other = halves(own_kv)
+    kv_chip = in_order(kv_mine, swap(kv_other, 1), 2)
+    back = -(-(span_len - math.gcd(span_len, chip_len)) // chip_len)
+    barrier = lax.optimization_barrier
+    q_list, weights, kv_chip = barrier((q_list, weights, kv_chip))
+    kv_back = [
+        lax.ppermute(kv_chip, "pages", [(p, p + 2 * b) for p in range(page_devs - 2 * b)])
+        for b in range(back, 0, -1)
+    ]
 
     my_slots = device_at * slot_count + jnp.arange(slot_count, dtype=jnp.int32)
     chip_slots = jnp.concatenate(
@@ -525,25 +537,19 @@
         unit,
         scale2,
     )
+    outs, kv_back = barrier((outs, kv_back))
     merged = lambda parts, ok: merge(parts, ok, chip_len, unit, scale2)
 
     def fresh_part():
         chip_at = device_at // 2
-        back = -(-(span_len - math.gcd(span_len, chip_len)) // chip_len)
-        window = (back + 1) * chip_len
-        window_at = jnp.maximum(chip_at - back, 0) * chip_len
-
-        def by_head(rows):
-            rows = lax.dynamic_slice(
-                rows, (window_at, core * half, 0), (window, half, head_dim)
-            )
-            return jnp.transpose(rows, (1, 0, 2))
-
+        window = jnp.concatenate(kv_back + [kv_chip], axis=2)
         chip_tokens = chip_at * chip_len + jnp.arange(chip_len, dtype=jnp.int32)
         token_rows = jnp.stack([chip_tokens, chip_tokens // span_len * span_len])
-        key_cols = (window_at + jnp.arange(window, dtype=jnp.int32))[:, None]
+        keys_at = (chip_at - back) * chip_len
+        keys_at = keys_at + jnp.arange((back + 1) * chip_len, dtype=jnp.int32)
+        key_cols = jnp.where(keys_at < 0, tokens, keys_at)[:, None]
         return fresh_attention(
-            q_chip, by_head(all_k), by_head(all_v), token_rows, key_cols, unit, scale2
+            q_chip, window[:, 0], window[:, 1], token_rows, key_cols, unit, scale2
         )
 
     chip_part = merge_lines(

time: 383 us -> 419 us (1.094)
  starting transfers between devices: 50.7 us -> 71.1 us
  waiting for transfers between devices: 151 us -> 171 us
  Pallas kernels: 99.8 us -> 92.1 us
  other arithmetic: 24.3 us -> 29.3 us
    ppermute x9 -> x10, starting transfers between devices: 4.73 us -> 27.6 us  [swap(): return lax.ppermute(x, 'pages', [(p, p ^ bit) for p in range(devs)])]
    ppermute x0 -> x1, waiting for transfers between devices: none -> 16.7 us  [per_device(): lax.ppermute(kv_chip, 'pages', [(p, p + 2 * b) for p in range(page_devs -...]
    pallas_call x1, Pallas kernels: 39.3 us -> 23.6 us  [cached_attention(): pl.pallas_call(lambda *refs: cached_kernel(unit, stat_unit, span, scale2,...]
    ppermute x9 -> x10, waiting for transfers between devices: 36 us -> 45.2 us  [swap(): return lax.ppermute(x, 'pages', [(p, p ^ bit) for p in range(devs)])]
    pallas_call x2, Pallas kernels: 10.1 us -> 16.4 us  [project(): pl.pallas_call(project_kernel, grid_spec=pltpu.PrefetchScalarGridSpec(num...]
    ppermute x1, waiting for transfers between devices: 13.2 us -> 7.15 us  [per_device(): lax.ppermute(part, 'heads', [(h, (h + s) % groups) for h in range(groups)])]
    ppermute x12, waiting for transfers between devices: 90.4 us -> 95.3 us  [shift(): return lax.ppermute(x, 'pages', moves)]
    ppermute x12, starting transfers between devices: 31.8 us -> 27.4 us  [shift(): return lax.ppermute(x, 'pages', moves)]
  transfers between devices with their start and end apart: 31 -> 33, of which waited for: 14 -> 15; matrix products, arithmetic and copies ran while one was open for 12% -> 14% of each run, Pallas kernels for 25% -> 22%
where the time goes in v7:
time: 419 us; the launch traced here: 414 us
  waiting for transfers between devices  171 us (41%)
  Pallas kernels  92.1 us (22%)
  starting transfers between devices  71.1 us (17%)
  local copies, waits for them, and re-layouts  36.2 us (9%)
  other arithmetic  29.3 us (7%)
  between operations  14.3 us (3%)
    ppermute x12, waiting for transfers between devices, shift(): return lax.ppermute(x, 'pages', moves)  95.3 us
    ppermute x10, waiting for transfers between devices, swap(): return lax.ppermute(x, 'pages', [(p, p ^ bit) for p in range(devs)])  45.2 us
    pallas_call x9, Pallas kernels, merge(): pl.pallas_call(lambda *refs: merge_kernel(unit, part_len, scale2, *refs),...  34.3 us
    ppermute x10, starting transfers between devices, swap(): return lax.ppermute(x, 'pages', [(p, p ^ bit) for p in range(devs)])  27.6 us
    ppermute x12, starting transfers between devices, shift(): return lax.ppermute(x, 'pages', moves)  27.4 us
    pallas_call x1, Pallas kernels, cached_attention(): pl.pallas_call(lambda *refs: cached_kernel(unit, stat_unit, span, scale2,...  23.6 us
    unnamed x48, local copies, waits for them, and re-layouts  19.3 us
    ppermute x1, waiting for transfers between devices, per_device(): lax.ppermute(kv_chip, 'pages', [(p, p + 2 * b) for p in range(page_devs -...  16.7 us
  transfers between devices with their start and end apart: 33, of which 15 were waited for; matrix products, arithmetic and copies ran while one was open for 14% of the time, Pallas kernels for 22%

profile of v7, /device:TPU:12, one launch (start us, length us, event | category | flops | bytes accessed | tf_op | source)
XLA Modules:
  0.0 414.2 jit_solution(13549829230600359893)
XLA Ops:
  21.2 28.9 %collective-permute-done.2.refs_7_ = bf16[4,576,128]{2,1,0:T(8,128)(2,1)S(1)} collective-permute-done((bf16[4,576,128]{2,1,0:T(8,128)(2,1)}, bf16[4,576,128]{2,1,0:T(8,128)(2,1)S(1)}, u32[]{:S(2)}, u32[]{:S(2)}) %collective-permute-start.2) | collective-permute-done | bytes 589856 | tf_op jit(solution)/shard_map/ppermute | solution.py:272
  57.2 7.2 %constant_dynamic-slice_fusion.3 = (bf16[12,128,4,128]{3,2,1,0:T(4,128)(2,1)}, bf16[12,128,4,128]{3,2,1,0:T(4,128)(2,1)}, bf16[12,128,4,128]{3,2,1,0:T(4,128)(2,1)S(1)}, bf16[12,128,4,128]{3,2,1,0:T(4,128)(2,1)}) fusion(bf16[12,128,8,128]{3,2,1,0:T(8,128)(2,1)S(1)} %copy-done, s32[]{:T(128)S(6)} %select_n.184, s32[]{:T(128)S(6)} %select_n.185, ...), kind=kLoop, calls=%fused_computation.52 | loop fusion | bytes 12582920 | tf_op jit(solution)/shard_map/dynamic-slice.4
  66.4 3.8 copy.57
  70.6 5.2 %collective-permute-start.6 = (bf16[4,576,128]{2,1,0:T(8,128)(2,1)}, bf16[4,576,128]{2,1,0:T(8,128)(2,1)}, u32[]{:S(2)}, u32[]{:S(2)}) collective-permute-start(bf16[4,576,128]{2,1,0:T(8,128)(2,1)} %copy-done.19), channel_id=1, source_target_pairs={{4,8},{5,9},{6,10},{7,11},{8,12},{9,13},{10,14},{11,15},{20,24},{2... | collective-permute-start | bytes 1769480 | tf_op jit(solution)/shard_map/ppermute | solution.py:272
  75.8 23.3 %collective-permute-done.4.refs_9_ = bf16[4,576,128]{2,1,0:T(8,128)(2,1)} collective-permute-done((bf16[4,576,128]{2,1,0:T(8,128)(2,1)}, bf16[4,576,128]{2,1,0:T(8,128)(2,1)}, u32[]{:S(2)}, u32[]{:S(2)}) %collective-permute-start.4) | collective-permute-done | bytes 589856 | tf_op jit(solution)/shard_map/ppermute | solution.py:272
  104.7 12.5 %collective-permute-done.8.refs_13_ = bf16[4,576,128]{2,1,0:T(8,128)(2,1)} collective-permute-done((bf16[4,576,128]{2,1,0:T(8,128)(2,1)}, bf16[4,576,128]{2,1,0:T(8,128)(2,1)}, u32[]{:S(2)}, u32[]{:S(2)}) %collective-permute-start.8) | collective-permute-done | bytes 589856 | tf_op jit(solution)/shard_map/ppermute | solution.py:272
  138.6 11.3 %collective-permute-done.12.refs_17_ = bf16[4,576,128]{2,1,0:T(8,128)(2,1)} collective-permute-done((bf16[4,576,128]{2,1,0:T(8,128)(2,1)}, bf16[4,576,128]{2,1,0:T(8,128)(2,1)}, u32[]{:S(2)}, u32[]{:S(2)}) %collective-permute-start.12) | collective-permute-done | bytes 589856 | tf_op jit(solution)/shard_map/ppermute | solution.py:272
  162.1 5.5 %collective-permute-done.9.refs_14_ = bf16[4,576,128]{2,1,0:T(8,128)(2,1)} collective-permute-done((bf16[4,576,128]{2,1,0:T(8,128)(2,1)}, bf16[4,576,128]{2,1,0:T(8,128)(2,1)}, u32[]{:S(2)}, u32[]{:S(2)}) %collective-permute-start.9) | collective-permute-done | bytes 589856 | tf_op jit(solution)/shard_map/ppermute | solution.py:294
  169.7 23.6 %cached_attention.1 = (bf16[4,608,128]{2,1,0:T(8,128)(2,1)}, bf16[4,608,128]{2,1,0:T(8,128)(2,1)}, bf16[4,608,128]{2,1,0:T(8,128)(2,1)}, bf16[4,608,128]{2,1,0:T...) custom-call(s32[22]{0:T(128)} %stack.213.refs_0_, ...), custom_call_target="tpu_custom_call" | custom-call | flops 40000000000 | bytes 20971520 | tf_op jit(solution)/shard_map/cached_attention/pallas_call | solution.py:156
  193.4 16.7 %collective-permute-done.17 = bf16[4,2,576,128]{3,2,0,1:T(8,128)(2,1)} collective-permute-done((bf16[4,2,576,128]{3,2,0,1:T(8,128)(2,1)}, bf16[4,2,576,128]{3,2,0,1:T(8,128)(2,1)}, u32[]{:S(2)}, u32[]{:S(2)}) %collective-permute-start.17) | collective-permute-done | bytes 1179680 | tf_op jit(solution)/shard_map/ppermute | solution.py:489
  210.1 22.8 %collective-permute-start.19 = (bf16[4,608,128]{2,1,0:T(8,128)(2,1)}, bf16[4,608,128]{2,1,0:T(8,128)(2,1)}, u32[]{:S(2)}, u32[]{:S(2)}) collective-permute-start(bf16[4,608,128]{2,1,0:T(8,128)(2,1)} %get-tuple-element.66), channel_id=1, source_target_pairs={{0,2},{1,3},{2,0},{3,1},{4,6},{5,7},{6,4},{7,5},{8,10},{9,11},{10,... | collective-permute-start | bytes 1867784 | tf_op jit(solution)/shard_map/ppermute | solution.py:266
  235.0 19.6 %collective-permute-done.19.refs_2_ = bf16[4,608,128]{2,1,0:T(8,128)(2,1)} collective-permute-done((bf16[4,608,128]{2,1,0:T(8,128)(2,1)}, bf16[4,608,128]{2,1,0:T(8,128)(2,1)}, u32[]{:S(2)}, u32[]{:S(2)}) %collective-permute-start.19) | collective-permute-done | bytes 622624 | tf_op jit(solution)/shard_map/ppermute | solution.py:266
  259.7 8.2 %collective-permute-done.21.refs_2_ = bf16[4,608,128]{2,1,0:T(8,128)(2,1)} collective-permute-done((bf16[4,608,128]{2,1,0:T(8,128)(2,1)}, bf16[4,608,128]{2,1,0:T(8,128)(2,1)}, u32[]{:S(2)}, u32[]{:S(2)}) %collective-permute-start.21) | collective-permute-done | bytes 622624 | tf_op jit(solution)/shard_map/ppermute | solution.py:266
  267.9 3.9 merge.12.refs_1_
  274.9 14.7 %collective-permute-done.20.refs_2_ = bf16[4,608,128]{2,1,0:T(8,128)(2,1)} collective-permute-done((bf16[4,608,128]{2,1,0:T(8,128)(2,1)}, bf16[4,608,128]{2,1,0:T(8,128)(2,1)}, u32[]{:S(2)}, u32[]{:S(2)}) %collective-permute-start.20) | collective-permute-done | bytes 622624 | tf_op jit(solution)/shard_map/ppermute | solution.py:266
  298.3 3.8 collective-permute-done.22.refs_2_
  313.6 11.8 %collective-permute-done.26.refs_2_ = bf16[4,608,128]{2,1,0:T(8,128)(2,1)} collective-permute-done((bf16[4,608,128]{2,1,0:T(8,128)(2,1)}, bf16[4,608,128]{2,1,0:T(8,128)(2,1)}, u32[]{:S(2)}, u32[]{:S(2)}) %collective-permute-start.26) | collective-permute-done | bytes 622624 | tf_op jit(solution)/shard_map/ppermute | solution.py:272
  330.9 3.8 collective-permute-done.23.refs_2_
  344.9 9.4 %fresh_attention.1.refs_4_ = bf16[4,608,128]{2,1,0:T(8,128)(2,1)S(1)} custom-call(bf16[4,576,128]{2,1,0:T(8,128)(2,1)} %maximum_select_fusion.1.refs_5_.refs_0_, bf16[4,1152,128]{2,1,0:T(8,128)(2,1)S(1)} %get-tuple-element.84.refs_1_, bf16[4,1152,128]{2,1,0:T(8,128)(2,1)S(1)} %get-tuple-element.83.refs_2_, s32[2,576]{1,0:T(2,128)S(1)} %pad_add_fusion.refs_3_, ...), custom_call_target="tpu_custom_call" | custom-call | tf_op jit(solution)/shard_map/fresh_attention/pallas_call | solution.py:359
  358.8 4.6 %merge.17 = bf16[4,608,128]{2,1,0:T(8,128)(2,1)} custom-call(s32[4]{0:T(128)} %pad_add_fusion.5.refs_0_, bf16[4,608,128]{2,1,0:T(8,128)(2,1)} %merge.9.refs_1_, bf16[4,608,128]{2,1,0:T(8,128)(2,1)} %collective-permute-done.24.refs_2_, bf16[4,608,128]{2,1,0:T(8,128)(2,1)} %collective-permute-done.27.refs_3_, bf16[4,608,128]{2,1,0:T(8,128)(2,1)} %copy-done.2), custom_call_target="tpu_custom_call" | custom-call | tf_op jit(solution)/shard_map/merge/pallas_call | solution.py:219
  367.9 8.1 %project.2 = bf16[288,2048]{1,0:T(8,128)(2,1)} custom-call(s32[2]{0:T(128)} %pad_add_fusion.4.at_ref, bf16[4,288,128]{2,1,0:T(8,128)(2,1)} %get-tuple-element.92.mine_ref, bf16[4,288,128]{2,1,0:T(8,128)(2,1)} %copy-done.13, bf16[16,1024,256]{2,1,0:T(8,128)(2,1)} %bitcast.63), custom_call_target="tpu_custom_call" | custom-call | tf_op jit(solution)/shard_map/project/pallas_call | solution.py:400
  380.4 8.4 %write_pages.1 = (bf16[12,128,8,128]{3,2,1,0:T(8,128)(2,1)}, bf16[12,128,8,128]{3,2,1,0:T(8,128)(2,1)}) custom-call(s32[12]{0:T(128)S(1)} %convert_element_type.53.fresh_ref, s32[12]{0:T(128)S(1)} %fusion.4.index_ref, bf16[12,128,8,128]{3,2,1,0:T(8,128)(2,1)S(1)} %copy-done.1, bf16[12,128,8,128]{3,2,1,0:T(8,128)(2,1)S(1)} %copy-done, ...), custom_call_target="tpu_custom_call" | custom-call | tf_op jit(solution)/shard_map/write_pages/pallas_call | solution.py:250
  388.8 8.3 %project.3 = f32[288,2048]{1,0:T(8,128)} custom-call(s32[2]{0:T(128)} %pad_add_fusion.7.at_ref, bf16[4,288,128]{2,1,0:T(8,128)(2,1)} %get-tuple-element.92.mine_ref, bf16[4,288,128]{2,1,0:T(8,128)(2,1)} %copy-done.13, bf16[16,1024,256]{2,1,0:T(8,128)(2,1)} %bitcast.64), custom_call_target="tpu_custom_call" | custom-call | tf_op jit(solution)/shard_map/project/pallas_call | solution.py:400
  397.1 7.2 %collective-permute-done.29 = bf16[288,2048]{1,0:T(8,128)(2,1)} collective-permute-done((bf16[288,2048]{1,0:T(8,128)(2,1)}, bf16[288,2048]{1,0:T(8,128)(2,1)}, u32[]{:S(2)}, u32[]{:S(2)}) %collective-permute-start.29) | collective-permute-done | bytes 1179680 | tf_op jit(solution)/shard_map/ppermute | solution.py:567
  (164 shorter events, 127.6 us)
Async XLA Ops:
  7.2 160.5 %all-gather.9.cloned.1.call-start = ((), (), s32[]{:S(2)}) async-start(), calls=%async_computation.2 | async-start | bytes 8912896 | tf_op jit(solution)/shard_map/all_gather | solution.py:481
  7.9 370.6 %all-gather.5.cloned.1.call-start = ((), (), s32[]{:S(2)}) async-start(), calls=%async_computation | async-start | bytes 10027008 | tf_op jit(solution)/shard_map/all_gather | solution.py:477
  16.5 33.6 %collective-permute-start.2 = (bf16[4,576,128]{2,1,0:T(8,128)(2,1)}, bf16[4,576,128]{2,1,0:T(8,128)(2,1)S(1)}, u32[]{:S(2)}, u32[]{:S(2)}) collective-permute-start(bf16[4,576,128]{2,1,0:T(8,128)(2,1)} %maximum_select_fusion.1.refs_5_.refs_0_), channel_id=1, source_target_pairs={{0,4},{1,5},{2,6},{3,7},{4,8},{5,9},{6,10},{7,11},{8,12},{9,13},{1... | collective-permute-start | bytes 1769480 | tf_op jit(solution)/shard_map/ppermute | solution.py:272
  51.2 327.4 %all-gather.7.cloned.1.call-start = ((), (), s32[]{:S(2)}) async-start(), calls=%async_computation.1 | async-start | bytes 10027008 | tf_op jit(solution)/shard_map/all_gather | solution.py:478
  55.3 43.8 %collective-permute-start.4 = (bf16[4,576,128]{2,1,0:T(8,128)(2,1)}, bf16[4,576,128]{2,1,0:T(8,128)(2,1)}, u32[]{:S(2)}, u32[]{:S(2)}) collective-permute-start(bf16[4,576,128]{2,1,0:T(8,128)(2,1)} %maximum_select_fusion.1.refs_5_.refs_0_), channel_id=1, source_target_pairs={{4,0},{5,1},{6,2},{7,3},{8,4},{9,5},{10,6},{11,7},{12,8},{13,9},{1... | collective-permute-start | bytes 1769480 | tf_op jit(solution)/shard_map/ppermute | solution.py:272
  65.9 66.3 %collective-permute-start.15 = (bf16[4,12,128,128]{3,2,1,0:T(8,128)(2,1)}, bf16[4,12,128,128]{3,2,1,0:T(8,128)(2,1)}, u32[]{:S(2)}, u32[]{:S(2)}) collective-permute-start(bf16[4,12,128,128]{3,2,1,0:T(8,128)(2,1)} %bitcast.60), channel_id=1, source_target_pairs={{0,1},{1,0},{2,3},{3,2},{4,5},{5,4},{6,7},{7,6},{8,9},{9,8},{10,11... | collective-permute-start | bytes 4718600 | tf_op jit(solution)/shard_map/ppermute | solution.py:266
  70.2 63.6 %collective-permute-start.16 = (bf16[4,12,128,128]{3,2,1,0:T(8,128)(2,1)}, bf16[4,12,128,128]{3,2,1,0:T(8,128)(2,1)}, u32[]{:S(2)}, u32[]{:S(2)}) collective-permute-start(bf16[4,12,128,128]{3,2,1,0:T(8,128)(2,1)} %bitcast.70), channel_id=1, source_target_pairs={{0,1},{1,0},{2,3},{3,2},{4,5},{5,4},{6,7},{7,6},{8,9},{9,8},{10,11... | collective-permute-start | bytes 4718600 | tf_op jit(solution)/shard_map/ppermute | solution.py:266
  70.2 31.0 %collective-permute-start.1 = (bf16[4,576,128]{2,1,0:T(8,128)(2,1)}, bf16[4,576,128]{2,1,0:T(8,128)(2,1)}, u32[]{:S(2)}, u32[]{:S(2)}) collective-permute-start(bf16[4,576,128]{2,1,0:T(8,128)(2,1)} %maximum_select_fusion.1.refs_5_.refs_0_), channel_id=1, source_target_pairs={{0,2},{1,3},{2,0},{3,1},{4,6},{5,7},{6,4},{7,5},{8,10},{9,11},{10,... | collective-permute-start | bytes 1769480 | tf_op jit(solution)/shard_map/ppermute | solution.py:266
  70.6 32.6 %collective-permute-start.6 = (bf16[4,576,128]{2,1,0:T(8,128)(2,1)}, bf16[4,576,128]{2,1,0:T(8,128)(2,1)}, u32[]{:S(2)}, u32[]{:S(2)}) collective-permute-start(bf16[4,576,128]{2,1,0:T(8,128)(2,1)} %copy-done.19), channel_id=1, source_target_pairs={{4,8},{5,9},{6,10},{7,11},{8,12},{9,13},{10,14},{11,15},{20,24},{2... | collective-permute-start | bytes 1769480 | tf_op jit(solution)/shard_map/ppermute | solution.py:272
  103.2 33.9 %collective-permute-start.10 = (bf16[4,576,128]{2,1,0:T(8,128)(2,1)}, bf16[4,576,128]{2,1,0:T(8,128)(2,1)}, u32[]{:S(2)}, u32[]{:S(2)}) collective-permute-start(bf16[4,576,128]{2,1,0:T(8,128)(2,1)} %collective-permute-done.6.refs_11_), channel_id=1, source_target_pairs={{8,12},{9,13},{10,14},{11,15},{24,28},{25,29},{26,30},{27,31}} | collective-permute-start | bytes 1769480 | tf_op jit(solution)/shard_map/ppermute | solution.py:272
  117.3 32.6 %collective-permute-start.12 = (bf16[4,576,128]{2,1,0:T(8,128)(2,1)}, bf16[4,576,128]{2,1,0:T(8,128)(2,1)}, u32[]{:S(2)}, u32[]{:S(2)}) collective-permute-start(bf16[4,576,128]{2,1,0:T(8,128)(2,1)} %collective-permute-done.8.refs_13_), channel_id=1, source_target_pairs={{4,0},{5,1},{6,2},{7,3},{20,16},{21,17},{22,18},{23,19}} | collective-permute-start | bytes 1769480 | tf_op jit(solution)/shard_map/ppermute | solution.py:272
  129.8 32.3 %collective-permute-start.5 = (bf16[4,576,128]{2,1,0:T(8,128)(2,1)}, bf16[4,576,128]{2,1,0:T(8,128)(2,1)}, u32[]{:S(2)}, u32[]{:S(2)}) collective-permute-start(bf16[4,576,128]{2,1,0:T(8,128)(2,1)} %collective-permute-done.4.refs_9_), channel_id=1, source_target_pairs={{0,2},{1,3},{2,0},{3,1},{4,6},{5,7},{6,4},{7,5},{8,10},{9,11},{10,... | collective-permute-start | bytes 1769480 | tf_op jit(solution)/shard_map/ppermute | solution.py:294
  132.3 29.8 %collective-permute-start.7 = (bf16[4,576,128]{2,1,0:T(8,128)(2,1)}, bf16[4,576,128]{2,1,0:T(8,128)(2,1)}, u32[]{:S(2)}, u32[]{:S(2)}) collective-permute-start(bf16[4,576,128]{2,1,0:T(8,128)(2,1)} %collective-permute-done.6.refs_11_), channel_id=1, source_target_pairs={{8,10},{9,11},{10,8},{11,9},{12,14},{13,15},{14,12},{15,13},{24,26... | collective-permute-start | bytes 1769480 | tf_op jit(solution)/shard_map/ppermute | solution.py:292
  133.8 33.8 %collective-permute-start.9 = (bf16[4,576,128]{2,1,0:T(8,128)(2,1)}, bf16[4,576,128]{2,1,0:T(8,128)(2,1)}, u32[]{:S(2)}, u32[]{:S(2)}) collective-permute-start(bf16[4,576,128]{2,1,0:T(8,128)(2,1)} %collective-permute-done.8.refs_13_), channel_id=1, source_target_pairs={{0,2},{1,3},{2,0},{3,1},{4,6},{5,7},{6,4},{7,5},{16,18},{17,19},{1... | collective-permute-start | bytes 1769480 | tf_op jit(solution)/shard_map/ppermute | solution.py:294
  137.2 30.5 %collective-permute-start.11 = (bf16[4,576,128]{2,1,0:T(8,128)(2,1)}, bf16[4,576,128]{2,1,0:T(8,128)(2,1)}, u32[]{:S(2)}, u32[]{:S(2)}) collective-permute-start(bf16[4,576,128]{2,1,0:T(8,128)(2,1)} %collective-permute-done.10.refs_15_), channel_id=1, source_target_pairs={{12,14},{13,15},{14,12},{15,13},{28,30},{29,31},{30,28},{31,29}} | collective-permute-start | bytes 1769480 | tf_op jit(solution)/shard_map/ppermute | solution.py:292
  167.6 42.5 %collective-permute-start.17 = (bf16[4,2,576,128]{3,2,0,1:T(8,128)(2,1)}, bf16[4,2,576,128]{3,2,0,1:T(8,128)(2,1)}, u32[]{:S(2)}, u32[]{:S(2)}) collective-permute-start(bf16[4,2,576,128]{3,2,0,1:T(8,128)(2,1)} %maximum_select_fusion), channel_id=1, source_target_pairs={{0,2},{1,3},{2,4},{3,5},{4,6},{5,7},{6,8},{7,9},{8,10},{9,11},{10,... | collective-permute-start | bytes 3538952 | tf_op jit(solution)/shard_map/ppermute | solution.py:489
  210.1 44.4 %collective-permute-start.19 = (bf16[4,608,128]{2,1,0:T(8,128)(2,1)}, bf16[4,608,128]{2,1,0:T(8,128)(2,1)}, u32[]{:S(2)}, u32[]{:S(2)}) collective-permute-start(bf16[4,608,128]{2,1,0:T(8,128)(2,1)} %get-tuple-element.66), channel_id=1, source_target_pairs={{0,2},{1,3},{2,0},{3,1},{4,6},{5,7},{6,4},{7,5},{8,10},{9,11},{10,... | collective-permute-start | bytes 1867784 | tf_op jit(solution)/shard_map/ppermute | solution.py:266
  233.0 34.9 %collective-permute-start.21 = (bf16[4,608,128]{2,1,0:T(8,128)(2,1)}, bf16[4,608,128]{2,1,0:T(8,128)(2,1)}, u32[]{:S(2)}, u32[]{:S(2)}) collective-permute-start(bf16[4,608,128]{2,1,0:T(8,128)(2,1)} %get-tuple-element.70), channel_id=1, source_target_pairs={{0,2},{1,3},{2,0},{3,1},{4,6},{5,7},{6,4},{7,5},{8,10},{9,11},{10,... | collective-permute-start | bytes 1867784 | tf_op jit(solution)/shard_map/ppermute | solution.py:266
  233.0 56.6 %collective-permute-start.20 = (bf16[4,608,128]{2,1,0:T(8,128)(2,1)}, bf16[4,608,128]{2,1,0:T(8,128)(2,1)}, u32[]{:S(2)}, u32[]{:S(2)}) collective-permute-start(bf16[4,608,128]{2,1,0:T(8,128)(2,1)} %get-tuple-element.68), channel_id=1, source_target_pairs={{0,2},{1,3},{2,0},{3,1},{4,6},{5,7},{6,4},{7,5},{8,10},{9,11},{10,... | collective-permute-start | bytes 1867784 | tf_op jit(solution)/shard_map/ppermute | solution.py:266
  258.2 35.1 %collective-permute-start.25 = (bf16[4,608,128]{2,1,0:T(8,128)(2,1)}, bf16[4,608,128]{2,1,0:T(8,128)(2,1)}, u32[]{:S(2)}, u32[]{:S(2)}) collective-permute-start(bf16[4,608,128]{2,1,0:T(8,128)(2,1)} %merge.10.refs_1_), channel_id=1, source_target_pairs={{12,8},{13,9},{14,10},{15,11},{28,24},{29,25},{30,26},{31,27}} | collective-permute-start | bytes 1867784 | tf_op jit(solution)/shard_map/ppermute | solution.py:272
  271.8 30.3 %collective-permute-start.22 = (bf16[4,608,128]{2,1,0:T(8,128)(2,1)}, bf16[4,608,128]{2,1,0:T(8,128)(2,1)}, u32[]{:S(2)}, u32[]{:S(2)}) collective-permute-start(bf16[4,608,128]{2,1,0:T(8,128)(2,1)} %merge.12.refs_1_), channel_id=1, source_target_pairs={{0,4},{1,5},{2,6},{3,7},{16,20},{17,21},{18,22},{19,23}} | collective-permute-start | bytes 1867784 | tf_op jit(solution)/shard_map/ppermute | solution.py:272
  305.8 29.0 %collective-permute-start.23 = (bf16[4,608,128]{2,1,0:T(8,128)(2,1)}, bf16[4,608,128]{2,1,0:T(8,128)(2,1)}, u32[]{:S(2)}, u32[]{:S(2)}) collective-permute-start(bf16[4,608,128]{2,1,0:T(8,128)(2,1)} %merge.13), channel_id=1, source_target_pairs={{0,4},{1,5},{2,6},{3,7},{4,8},{5,9},{6,10},{7,11},{16,20},{17,21},... | collective-permute-start | bytes 1867784 | tf_op jit(solution)/shard_map/ppermute | solution.py:272
  309.3 45.9 %collective-permute-start.18 = (bf16[4,608,128]{2,1,0:T(8,128)(2,1)}, bf16[4,608,128]{2,1,0:T(8,128)(2,1)}, u32[]{:S(2)}, u32[]{:S(2)}) collective-permute-start(bf16[4,608,128]{2,1,0:T(8,128)(2,1)} %get-tuple-element.64), channel_id=1, source_target_pairs={{0,2},{1,3},{2,0},{3,1},{4,6},{5,7},{6,4},{7,5},{8,10},{9,11},{10,... | collective-permute-start | bytes 1867784 | tf_op jit(solution)/shard_map/ppermute | solution.py:266
  329.0 29.8 %collective-permute-start.27 = (bf16[4,608,128]{2,1,0:T(8,128)(2,1)}, bf16[4,608,128]{2,1,0:T(8,128)(2,1)}, u32[]{:S(2)}, u32[]{:S(2)}) collective-permute-start(bf16[4,608,128]{2,1,0:T(8,128)(2,1)} %merge.16), channel_id=1, source_target_pairs={{4,0},{5,1},{6,2},{7,3},{8,4},{9,5},{10,6},{11,7},{12,8},{13,9},{1... | collective-permute-start | bytes 1867784 | tf_op jit(solution)/shard_map/ppermute | solution.py:272
  (30 other events, 324.2 us)
Sparse Core Ops, SparseCore 0:
  10.2 96.3 all-gather.8
  108.8 119.3 all-gather.4
  230.5 105.7 all-gather.6

commit v8 on v4

--- a/solution.py
+++ b/solution.py
@@ -384,10 +384,9 @@
     out_ref[...] = total.astype(out_ref.dtype).reshape(out_ref.shape)
 
 
-def project(mine, other, weights, core, owner, groups, dtype):
+def project(mine, other, weights, core, first, blocks, dtype):
     half, tok_dev, head_dim = mine.shape
-    blocks, feats, cols = weights.shape
-    blocks //= groups
+    _, feats, cols = weights.shape
     wide = cols % 128 == 0
     if wide:
         out_spec = pl.BlockSpec((tok_dev, cols), lambda j, at: (0, j))
@@ -404,7 +403,7 @@
             in_specs=[
                 rows_spec,
                 rows_spec,
-                pl.BlockSpec((1, feats, cols), lambda j, at: (at[1] * blocks + j, 0, 0)),
+                pl.BlockSpec((1, feats, cols), lambda j, at: (at[1] + j, 0, 0)),
             ],
             out_specs=out_spec,
             scratch_shapes=[pltpu.VMEM((2, tok_dev, half * head_dim), jnp.bfloat16)],
@@ -412,7 +411,7 @@
         out_shape=jax.ShapeDtypeStruct(out_shape, dtype),
         compiler_params=pltpu.CompilerParams(vmem_limit_bytes=40 * 2**20),
         name="project",
-    )(jnp.stack([core, owner]), mine, other, weights)
+    )(jnp.stack([core, first]), mine, other, weights)
     return out if wide else jnp.transpose(out, (1, 0, 2)).reshape(tok_dev, blocks * cols)
 
 
@@ -446,7 +445,6 @@
     )
     positions = (starts + token_ids % span_len).astype(jnp.float32)
     rotated_q = rotate(queries.astype(jnp.float32), positions).astype(jnp.bfloat16)
-    rotated_k = rotate(keys.astype(jnp.float32), positions).astype(jnp.bfloat16)
     core = device_at % 2
     half = head_count // 2
     chip_len = 2 * tok_dev
@@ -467,16 +465,17 @@
     q_own = jnp.transpose(rotated_q, (1, 0, 2))
     q_mine, q_other = halves(q_own)
     q_chip = in_order(q_mine, swap(q_other, 1), 1)
-    q_places = gather_lines(q_chip)
     groups = lax.axis_size("heads")
     group_at = lax.axis_index("heads")
-    q_list = [q for q, _, _, _ in q_places]
     natural = Layout((0, 1, 2))
+    q_chip, late_k, late_weight = lax.optimization_barrier((q_chip, keys, out_weight))
+    q_places = gather_lines(q_chip)
+    rotated_k = rotate(late_k.astype(jnp.float32), positions).astype(jnp.bfloat16)
     all_k = lax.all_gather(rotated_k, "pages", axis=0, tiled=True)
     all_v = lax.all_gather(values, "pages", axis=0, tiled=True)
     all_k = with_layout_constraint(all_k, natural)
     all_v = with_layout_constraint(all_v, natural)
-    weights = lax.all_gather(out_weight, "pages", axis=0, tiled=False)
+    weights = lax.all_gather(late_weight, "pages", axis=0, tiled=False)
 
     my_slots = device_at * slot_count + jnp.arange(slot_count, dtype=jnp.int32)
     chip_slots = jnp.concatenate(
@@ -512,7 +511,7 @@
     line = page_devs // 4
     line_at, across = device_at // 4, (device_at // 2) % 2
     outs = cached_attention(
-        q_list,
+        [q for q, _, _, _ in q_places],
         [jnp.clip(at, 0, line - 1) * 2 + side for _, at, side, _ in q_places],
         [ok for _, _, _, ok in q_places],
         [((line_at + k) % line) * 2 + (across ^ d) for k in range(line) for d in range(2)],
@@ -551,15 +550,27 @@
     )
     rows_of = lambda c: lax.dynamic_slice_in_dim(chip_part[:, :chip_len], c * tok_dev, tok_dev, 1)
     own_rows, got_rows = rows_of(core), swap(rows_of(1 - core), 1)
-    total = out_bias[None, :]
-    for s in range(groups - 1, -1, -1):
-        owner = (group_at + s) % groups
-        part = project(
-            own_rows, got_rows, weights, core, owner, groups, jnp.bfloat16 if s else jnp.float32
-        )
-        if s:
-            part = lax.ppermute(part, "heads", [(h, (h + s) % groups) for h in range(groups)])
-        total = total + part.astype(jnp.float32)
+    blocks = page_devs // groups
+    pieces = 2
+    sent = []
+    for s in range(groups - 1, 0, -1):
+        for piece in range(pieces):
+            part = project(
+                own_rows,
+                got_rows,
+                weights,
+                core,
+                (group_at + s) % groups * blocks + piece * (blocks // pieces),
+                blocks // pieces,
+                jnp.bfloat16,
+            )
+            moves = [(h, (h + s) % groups) for h in range(groups)]
+            sent.append(lax.ppermute(part, "heads", moves))
+    total = project(
+        own_rows, got_rows, weights, core, group_at * blocks, blocks, jnp.float32
+    ) + out_bias[None, :]
+    for at in range(0, len(sent), pieces):
+        total = total + jnp.concatenate(sent[at : at + pieces], axis=1).astype(jnp.float32)
     hidden = total.astype(jnp.bfloat16)
     page_shape = (requests * new_pages, PAGE, head_count, head_dim)
     key_out, value_out = write_pages(

time: 383 us -> 381 us (level)
    ppermute x1 -> x2, waiting for transfers between devices: 13.2 us -> 4.04 us  [per_device(): sent.append(lax.ppermute(part, 'heads', moves))]
    ppermute x12, waiting for transfers between devices: 90.4 us -> 96.7 us  [shift(): return lax.ppermute(x, 'pages', moves)]
    pallas_call x2 -> x3, Pallas kernels: 10.1 us -> 12.1 us  [project(): pl.pallas_call(project_kernel, grid_spec=pltpu.PrefetchScalarGridSpec(num...]
  transfers between devices with their start and end apart: 31 -> 32, of which waited for: 14 -> 13; matrix products, arithmetic and copies ran while one was open for 12% -> 12% of each run, Pallas kernels for 25% -> 26%
where the time goes in v8:
time: 381 us; the launch traced here: 376 us
  waiting for transfers between devices  149 us (39%)
  Pallas kernels  101 us (27%)
  starting transfers between devices  51.5 us (14%)
  local copies, waits for them, and re-layouts  40.4 us (11%)
  other arithmetic  20.7 us (5%)
  between operations  14.2 us (4%)
    ppermute x12, waiting for transfers between devices, shift(): return lax.ppermute(x, 'pages', moves)  96.7 us
    pallas_call x1, Pallas kernels, cached_attention(): pl.pallas_call(lambda *refs: cached_kernel(unit, stat_unit, span, scale2,...  37.9 us
    ppermute x9, waiting for transfers between devices, swap(): return lax.ppermute(x, 'pages', [(p, p ^ bit) for p in range(devs)])  36.3 us
    pallas_call x9, Pallas kernels, merge(): pl.pallas_call(lambda *refs: merge_kernel(unit, part_len, scale2, *refs),...  34.1 us
    ppermute x12, starting transfers between devices, shift(): return lax.ppermute(x, 'pages', moves)  31.9 us
    unnamed x39, local copies, waits for them, and re-layouts  24.5 us
    pallas_call x3, Pallas kernels, project(): pl.pallas_call(project_kernel, grid_spec=pltpu.PrefetchScalarGridSpec(num...  12.1 us
    ppermute x3, waiting for transfers between devices, gather_lines(): lax.ppermute(down, 'pages', cross_down)  10.4 us
  transfers between devices with their start and end apart: 32, of which 13 were waited for; matrix products, arithmetic and copies ran while one was open for 12% of the time, Pallas kernels for 26%

profile of v8, /device:TPU:12, one launch (start us, length us, event | category | flops | bytes accessed | tf_op | source)
XLA Modules:
  0.0 376.4 jit_solution(427471883637672100)
XLA Ops:
  23.4 7.3 %constant_dynamic-slice_fusion.5 = (bf16[12,128,4,128]{3,2,1,0:T(4,128)(2,1)}, bf16[12,128,4,128]{3,2,1,0:T(4,128)(2,1)}, bf16[12,128,4,128]{3,2,1,0:T(4,128)(2,1)S(1)}, bf16[12,128,4,128]{3,2,1,0:T(4,128)(2,1)}) fusion(bf16[12,128,8,128]{3,2,1,0:T(8,128)(2,1)S(1)} %copy-done.2, s32[]{:T(128)S(6)} %select_n.166, s32[]{:T(128)S(6)} %select_n.167, ...), kind=kLoop, calls=%fused_computation.47 | loop fusion | bytes 12582920 | tf_op jit(solution)/shard_map/dynamic-slice.4
  32.3 3.8 copy.62
  37.0 15.3 %collective-permute-done.2.refs_7_ = bf16[4,576,128]{2,1,0:T(8,128)(2,1)} collective-permute-done((bf16[4,576,128]{2,1,0:T(8,128)(2,1)}, bf16[4,576,128]{2,1,0:T(8,128)(2,1)}, u32[]{:S(2)}, u32[]{:S(2)}) %collective-permute-start.2) | collective-permute-done | bytes 589856 | tf_op jit(solution)/shard_map/ppermute | solution.py:271
  52.3 5.2 %collective-permute-start.6 = (bf16[4,576,128]{2,1,0:T(8,128)(2,1)}, bf16[4,576,128]{2,1,0:T(8,128)(2,1)}, u32[]{:S(2)}, u32[]{:S(2)}) collective-permute-start(bf16[4,576,128]{2,1,0:T(8,128)(2,1)} %collective-permute-done.2.refs_7_), channel_id=1, source_target_pairs={{4,8},{5,9},{6,10},{7,11},{8,12},{9,13},{10,14},{11,15},{20,24},{2... | collective-permute-start | bytes 1769480 | tf_op jit(solution)/shard_map/ppermute | solution.py:271
  62.0 35.3 %collective-permute-done.6.refs_11_ = bf16[4,576,128]{2,1,0:T(8,128)(2,1)} collective-permute-done((bf16[4,576,128]{2,1,0:T(8,128)(2,1)}, bf16[4,576,128]{2,1,0:T(8,128)(2,1)}, u32[]{:S(2)}, u32[]{:S(2)}) %collective-permute-start.6) | collective-permute-done | bytes 589856 | tf_op jit(solution)/shard_map/ppermute | solution.py:271
  113.9 3.9 %collective-permute-start.9 = (bf16[4,576,128]{2,1,0:T(8,128)(2,1)}, bf16[4,576,128]{2,1,0:T(8,128)(2,1)}, u32[]{:S(2)}, u32[]{:S(2)}) collective-permute-start(bf16[4,576,128]{2,1,0:T(8,128)(2,1)} %collective-permute-done.8.refs_13_), channel_id=1, source_target_pairs={{0,2},{1,3},{2,0},{3,1},{4,6},{5,7},{6,4},{7,5},{16,18},{17,19},{1... | collective-permute-start | bytes 1769480 | tf_op jit(solution)/shard_map/ppermute | solution.py:293
  119.4 5.7 %collective-permute-done.12.refs_17_ = bf16[4,576,128]{2,1,0:T(8,128)(2,1)} collective-permute-done((bf16[4,576,128]{2,1,0:T(8,128)(2,1)}, bf16[4,576,128]{2,1,0:T(8,128)(2,1)}, u32[]{:S(2)}, u32[]{:S(2)}) %collective-permute-start.12) | collective-permute-done | bytes 589856 | tf_op jit(solution)/shard_map/ppermute | solution.py:271
  127.9 3.9 %pad_maximum_fusion.refs_19_ = bf16[4,24,128,128]{3,2,1,0:T(8,128)(2,1)} fusion(bf16[4,12,128,128]{3,2,1,0:T(8,128)(2,1)} %collective-permute-done.14, bf16[4,12,128,128]{3,2,1,0:T(8,128)(2,1)} %bitcast.64), kind=kLoop, calls=%fused_computation | loop fusion | flops 1572864 | bytes 6291456 | tf_op jit(solution)/shard_map/concatenate | solution.py:507
  135.2 10.3 %collective-permute-done.9.refs_14_ = bf16[4,576,128]{2,1,0:T(8,128)(2,1)} collective-permute-done((bf16[4,576,128]{2,1,0:T(8,128)(2,1)}, bf16[4,576,128]{2,1,0:T(8,128)(2,1)}, u32[]{:S(2)}, u32[]{:S(2)}) %collective-permute-start.9) | collective-permute-done | bytes 589856 | tf_op jit(solution)/shard_map/ppermute | solution.py:293
  145.6 37.9 %cached_attention.1 = (bf16[4,608,128]{2,1,0:T(8,128)(2,1)}, bf16[4,608,128]{2,1,0:T(8,128)(2,1)}, bf16[4,608,128]{2,1,0:T(8,128)(2,1)}, bf16[4,608,128]{2,1,0:T...) custom-call(s32[22]{0:T(128)} %stack.211.refs_0_, ...), custom_call_target="tpu_custom_call" | custom-call | flops 40000000000 | bytes 20971520 | tf_op jit(solution)/shard_map/cached_attention/pallas_call | solution.py:155
  185.7 19.8 %collective-permute-done.17.refs_2_ = bf16[4,608,128]{2,1,0:T(8,128)(2,1)} collective-permute-done((bf16[4,608,128]{2,1,0:T(8,128)(2,1)}, bf16[4,608,128]{2,1,0:T(8,128)(2,1)}, u32[]{:S(2)}, u32[]{:S(2)}) %collective-permute-start.17) | collective-permute-done | bytes 622624 | tf_op jit(solution)/shard_map/ppermute | solution.py:265
  210.7 8.1 %collective-permute-done.19.refs_2_ = bf16[4,608,128]{2,1,0:T(8,128)(2,1)} collective-permute-done((bf16[4,608,128]{2,1,0:T(8,128)(2,1)}, bf16[4,608,128]{2,1,0:T(8,128)(2,1)}, u32[]{:S(2)}, u32[]{:S(2)}) %collective-permute-start.19) | collective-permute-done | bytes 622624 | tf_op jit(solution)/shard_map/ppermute | solution.py:265
  225.0 5.1 %collective-permute-done.18.refs_2_ = bf16[4,608,128]{2,1,0:T(8,128)(2,1)} collective-permute-done((bf16[4,608,128]{2,1,0:T(8,128)(2,1)}, bf16[4,608,128]{2,1,0:T(8,128)(2,1)}, u32[]{:S(2)}, u32[]{:S(2)}) %collective-permute-start.18) | collective-permute-done | bytes 622624 | tf_op jit(solution)/shard_map/ppermute | solution.py:265
  242.5 4.6 %collective-permute-start.21 = (bf16[4,608,128]{2,1,0:T(8,128)(2,1)}, bf16[4,608,128]{2,1,0:T(8,128)(2,1)}, u32[]{:S(2)}, u32[]{:S(2)}) collective-permute-start(bf16[4,608,128]{2,1,0:T(8,128)(2,1)} %merge.13), channel_id=1, source_target_pairs={{0,4},{1,5},{2,6},{3,7},{4,8},{5,9},{6,10},{7,11},{16,20},{17,21},... | collective-permute-start | bytes 1867784 | tf_op jit(solution)/shard_map/ppermute | solution.py:271
  249.3 19.8 %collective-permute-done.24.refs_2_ = bf16[4,608,128]{2,1,0:T(8,128)(2,1)} collective-permute-done((bf16[4,608,128]{2,1,0:T(8,128)(2,1)}, bf16[4,608,128]{2,1,0:T(8,128)(2,1)}, u32[]{:S(2)}, u32[]{:S(2)}) %collective-permute-start.24) | collective-permute-done | bytes 622624 | tf_op jit(solution)/shard_map/ppermute | solution.py:271
  278.4 3.9 %collective-permute-start.22 = (bf16[4,608,128]{2,1,0:T(8,128)(2,1)}, bf16[4,608,128]{2,1,0:T(8,128)(2,1)}, u32[]{:S(2)}, u32[]{:S(2)}) collective-permute-start(bf16[4,608,128]{2,1,0:T(8,128)(2,1)} %merge.14), channel_id=1, source_target_pairs={{0,4},{1,5},{2,6},{3,7},{4,8},{5,9},{6,10},{7,11},{8,12},{9,13},{1... | collective-permute-start | bytes 1867784 | tf_op jit(solution)/shard_map/ppermute | solution.py:271
  294.3 8.4 %fresh_attention.1.refs_4_ = bf16[4,608,128]{2,1,0:T(8,128)(2,1)S(1)} custom-call(bf16[4,576,128]{2,1,0:T(8,128)(2,1)S(1)} %copy-done.6, bf16[4,1152,128]{2,1,0:T(8,128)(2,1)S(1)} %bitcast.61, bf16[4,1152,128]{2,1,0:T(8,128)(2,1)S(1)} %bitcast.60, s32[2,576]{1,0:T(2,128)S(1)} %pad_add_fusion.refs_3_, s32[1152,1]{1,0:T(8,128)S(1)} %copy-done.7), custom_call_target="tpu_custom_call" | custom-call | tf_op jit(solution)/shard_map/fresh_attention/pallas_call | solution.py:358
  303.6 19.7 %collective-permute-done.22.refs_2_ = bf16[4,608,128]{2,1,0:T(8,128)(2,1)} collective-permute-done((bf16[4,608,128]{2,1,0:T(8,128)(2,1)}, bf16[4,608,128]{2,1,0:T(8,128)(2,1)}, u32[]{:S(2)}, u32[]{:S(2)}) %collective-permute-start.22) | collective-permute-done | bytes 622624 | tf_op jit(solution)/shard_map/ppermute | solution.py:271
  323.3 4.6 %merge.17 = bf16[4,608,128]{2,1,0:T(8,128)(2,1)} custom-call(s32[4]{0:T(128)} %pad_add_fusion.5.refs_0_, bf16[4,608,128]{2,1,0:T(8,128)(2,1)} %merge.9.refs_1_, bf16[4,608,128]{2,1,0:T(8,128)(2,1)} %collective-permute-done.22.refs_2_, bf16[4,608,128]{2,1,0:T(8,128)(2,1)} %collective-permute-done.25.refs_3_, bf16[4,608,128]{2,1,0:T(8,128)(2,1)} %copy-done.5), custom_call_target="tpu_custom_call" | custom-call | tf_op jit(solution)/shard_map/merge/pallas_call | solution.py:218
  335.0 3.9 %project.4 = bf16[288,1024]{1,0:T(8,128)(2,1)} custom-call(s32[2]{0:T(128)S(1)} %pad_add_fusion.7.at_ref, bf16[4,288,128]{2,1,0:T(8,128)(2,1)S(1)} %get-tuple-element.40.mine_ref, bf16[4,288,128]{2,1,0:T(8,128)(2,1)} %collective-permute-done.26.other_ref, bf16[16,1024,256]{2,1,0:T(8,128)(2,1)S(1)} %bitcast.57), custom_call_target="tpu_custom_call" | custom-call | tf_op jit(solution)/shard_map/project/pallas_call | solution.py:398
  340.4 3.9 %project.5 = bf16[288,1024]{1,0:T(8,128)(2,1)} custom-call(s32[2]{0:T(128)S(1)} %pad_add_fusion.8.at_ref, bf16[4,288,128]{2,1,0:T(8,128)(2,1)S(1)} %get-tuple-element.40.mine_ref, bf16[4,288,128]{2,1,0:T(8,128)(2,1)} %collective-permute-done.26.other_ref, bf16[16,1024,256]{2,1,0:T(8,128)(2,1)S(1)} %bitcast.58), custom_call_target="tpu_custom_call" | custom-call | tf_op jit(solution)/shard_map/project/pallas_call | solution.py:398
  347.3 8.2 %write_pages.1 = (bf16[12,128,8,128]{3,2,1,0:T(8,128)(2,1)}, bf16[12,128,8,128]{3,2,1,0:T(8,128)(2,1)}) custom-call(s32[12]{0:T(128)S(1)} %convert_element_type.53.fresh_ref, s32[12]{0:T(128)S(1)} %fusion.2.index_ref, bf16[12,128,8,128]{3,2,1,0:T(8,128)(2,1)S(1)} %copy-done.3, bf16[12,128,8,128]{3,2,1,0:T(8,128)(2,1)S(1)} %copy-done.2, ...), custom_call_target="tpu_custom_call" | custom-call | tf_op jit(solution)/shard_map/write_pages/pallas_call | solution.py:249
  358.9 4.3 %project.3 = f32[288,2048]{1,0:T(8,128)S(1)} custom-call(s32[2]{0:T(128)S(1)} %pad_add_fusion.4.at_ref, bf16[4,288,128]{2,1,0:T(8,128)(2,1)S(1)} %get-tuple-element.40.mine_ref, bf16[4,288,128]{2,1,0:T(8,128)(2,1)} %collective-permute-done.26.other_ref, bf16[16,1024,256]{2,1,0:T(8,128)(2,1)S(1)} %bitcast.59), custom_call_target="tpu_custom_call" | custom-call | tf_op jit(solution)/shard_map/project/pallas_call | solution.py:398
  363.3 4.0 %collective-permute-done.28 = bf16[288,1024]{1,0:T(8,128)(2,1)} collective-permute-done((bf16[288,1024]{1,0:T(8,128)(2,1)}, bf16[288,1024]{1,0:T(8,128)(2,1)}, u32[]{:S(2)}, u32[]{:S(2)}) %collective-permute-start.28) | collective-permute-done | bytes 589856 | tf_op jit(solution)/shard_map/ppermute | solution.py:568
  (155 shorter events, 115.3 us)
Async XLA Ops:
  7.2 280.4 %all-gather.7.cloned.1.call-start = ((), (), s32[]{:S(2)}) async-start(), calls=%async_computation.1 | async-start | bytes 10027008 | tf_op jit(solution)/shard_map/all_gather | solution.py:475
  7.9 282.8 %all-gather.5.cloned.1.call-start = ((), (), s32[]{:S(2)}) async-start(), calls=%async_computation | async-start | bytes 10027008 | tf_op jit(solution)/shard_map/all_gather | solution.py:474
  15.9 313.9 %all-gather.9.cloned.1.call-start = ((), (), s32[]{:S(2)}) async-start(), calls=%async_computation.2 | async-start | bytes 8912896 | tf_op jit(solution)/shard_map/all_gather | solution.py:478
  16.7 35.6 %collective-permute-start.2 = (bf16[4,576,128]{2,1,0:T(8,128)(2,1)}, bf16[4,576,128]{2,1,0:T(8,128)(2,1)}, u32[]{:S(2)}, u32[]{:S(2)}) collective-permute-start(bf16[4,576,128]{2,1,0:T(8,128)(2,1)} %maximum_select_fusion.refs_5_.refs_0_), channel_id=1, source_target_pairs={{0,4},{1,5},{2,6},{3,7},{4,8},{5,9},{6,10},{7,11},{8,12},{9,13},{1... | collective-permute-start | bytes 1769480 | tf_op jit(solution)/shard_map/ppermute | solution.py:271
  20.2 37.4 %collective-permute-start.4 = (bf16[4,576,128]{2,1,0:T(8,128)(2,1)}, bf16[4,576,128]{2,1,0:T(8,128)(2,1)}, u32[]{:S(2)}, u32[]{:S(2)}) collective-permute-start(bf16[4,576,128]{2,1,0:T(8,128)(2,1)} %maximum_select_fusion.refs_5_.refs_0_), channel_id=1, source_target_pairs={{4,0},{5,1},{6,2},{7,3},{8,4},{9,5},{10,6},{11,7},{12,8},{13,9},{1... | collective-permute-start | bytes 1769480 | tf_op jit(solution)/shard_map/ppermute | solution.py:271
  32.2 80.1 %collective-permute-start.14 = (bf16[4,12,128,128]{3,2,1,0:T(8,128)(2,1)}, bf16[4,12,128,128]{3,2,1,0:T(8,128)(2,1)}, u32[]{:S(2)}, u32[]{:S(2)}) collective-permute-start(bf16[4,12,128,128]{3,2,1,0:T(8,128)(2,1)} %bitcast.53), channel_id=1, source_target_pairs={{0,1},{1,0},{2,3},{3,2},{4,5},{5,4},{6,7},{7,6},{8,9},{9,8},{10,11... | collective-permute-start | bytes 4718600 | tf_op jit(solution)/shard_map/ppermute | solution.py:265
  36.0 77.9 %collective-permute-start.15 = (bf16[4,12,128,128]{3,2,1,0:T(8,128)(2,1)}, bf16[4,12,128,128]{3,2,1,0:T(8,128)(2,1)}, u32[]{:S(2)}, u32[]{:S(2)}) collective-permute-start(bf16[4,12,128,128]{3,2,1,0:T(8,128)(2,1)} %bitcast.66), channel_id=1, source_target_pairs={{0,1},{1,0},{2,3},{3,2},{4,5},{5,4},{6,7},{7,6},{8,9},{9,8},{10,11... | collective-permute-start | bytes 4718600 | tf_op jit(solution)/shard_map/ppermute | solution.py:265
  36.5 23.1 %collective-permute-start.1 = (bf16[4,576,128]{2,1,0:T(8,128)(2,1)}, bf16[4,576,128]{2,1,0:T(8,128)(2,1)}, u32[]{:S(2)}, u32[]{:S(2)}) collective-permute-start(bf16[4,576,128]{2,1,0:T(8,128)(2,1)} %maximum_select_fusion.refs_5_.refs_0_), channel_id=1, source_target_pairs={{0,2},{1,3},{2,0},{3,1},{4,6},{5,7},{6,4},{7,5},{8,10},{9,11},{10,... | collective-permute-start | bytes 1769480 | tf_op jit(solution)/shard_map/ppermute | solution.py:265
  52.3 44.9 %collective-permute-start.6 = (bf16[4,576,128]{2,1,0:T(8,128)(2,1)}, bf16[4,576,128]{2,1,0:T(8,128)(2,1)}, u32[]{:S(2)}, u32[]{:S(2)}) collective-permute-start(bf16[4,576,128]{2,1,0:T(8,128)(2,1)} %collective-permute-done.2.refs_7_), channel_id=1, source_target_pairs={{4,8},{5,9},{6,10},{7,11},{8,12},{9,13},{10,14},{11,15},{20,24},{2... | collective-permute-start | bytes 1769480 | tf_op jit(solution)/shard_map/ppermute | solution.py:271
  57.5 42.2 %collective-permute-start.8 = (bf16[4,576,128]{2,1,0:T(8,128)(2,1)}, bf16[4,576,128]{2,1,0:T(8,128)(2,1)}, u32[]{:S(2)}, u32[]{:S(2)}) collective-permute-start(bf16[4,576,128]{2,1,0:T(8,128)(2,1)} %collective-permute-done.4.refs_9_), channel_id=1, source_target_pairs={{4,0},{5,1},{6,2},{7,3},{8,4},{9,5},{10,6},{11,7},{20,16},{21,17},... | collective-permute-start | bytes 1769480 | tf_op jit(solution)/shard_map/ppermute | solution.py:271
  59.7 50.8 %collective-permute-start.3 = (bf16[4,576,128]{2,1,0:T(8,128)(2,1)}, bf16[4,576,128]{2,1,0:T(8,128)(2,1)}, u32[]{:S(2)}, u32[]{:S(2)}) collective-permute-start(bf16[4,576,128]{2,1,0:T(8,128)(2,1)} %collective-permute-done.2.refs_7_), channel_id=1, source_target_pairs={{4,6},{5,7},{6,4},{7,5},{8,10},{9,11},{10,8},{11,9},{12,14},{13,15... | collective-permute-start | bytes 1769480 | tf_op jit(solution)/shard_map/ppermute | solution.py:291
  99.7 25.3 %collective-permute-start.12 = (bf16[4,576,128]{2,1,0:T(8,128)(2,1)}, bf16[4,576,128]{2,1,0:T(8,128)(2,1)}, u32[]{:S(2)}, u32[]{:S(2)}) collective-permute-start(bf16[4,576,128]{2,1,0:T(8,128)(2,1)} %collective-permute-done.8.refs_13_), channel_id=1, source_target_pairs={{4,0},{5,1},{6,2},{7,3},{20,16},{21,17},{22,18},{23,19}} | collective-permute-start | bytes 1769480 | tf_op jit(solution)/shard_map/ppermute | solution.py:271
  110.5 24.8 %collective-permute-start.5 = (bf16[4,576,128]{2,1,0:T(8,128)(2,1)}, bf16[4,576,128]{2,1,0:T(8,128)(2,1)}, u32[]{:S(2)}, u32[]{:S(2)}) collective-permute-start(bf16[4,576,128]{2,1,0:T(8,128)(2,1)} %collective-permute-done.4.refs_9_), channel_id=1, source_target_pairs={{0,2},{1,3},{2,0},{3,1},{4,6},{5,7},{6,4},{7,5},{8,10},{9,11},{10,... | collective-permute-start | bytes 1769480 | tf_op jit(solution)/shard_map/ppermute | solution.py:293
  113.9 31.7 %collective-permute-start.9 = (bf16[4,576,128]{2,1,0:T(8,128)(2,1)}, bf16[4,576,128]{2,1,0:T(8,128)(2,1)}, u32[]{:S(2)}, u32[]{:S(2)}) collective-permute-start(bf16[4,576,128]{2,1,0:T(8,128)(2,1)} %collective-permute-done.8.refs_13_), channel_id=1, source_target_pairs={{0,2},{1,3},{2,0},{3,1},{4,6},{5,7},{6,4},{7,5},{16,18},{17,19},{1... | collective-permute-start | bytes 1769480 | tf_op jit(solution)/shard_map/ppermute | solution.py:293
  117.9 27.7 %collective-permute-start.11 = (bf16[4,576,128]{2,1,0:T(8,128)(2,1)}, bf16[4,576,128]{2,1,0:T(8,128)(2,1)}, u32[]{:S(2)}, u32[]{:S(2)}) collective-permute-start(bf16[4,576,128]{2,1,0:T(8,128)(2,1)} %collective-permute-done.10.refs_15_), channel_id=1, source_target_pairs={{12,14},{13,15},{14,12},{15,13},{28,30},{29,31},{30,28},{31,29}} | collective-permute-start | bytes 1769480 | tf_op jit(solution)/shard_map/ppermute | solution.py:291
  183.6 35.2 %collective-permute-start.19 = (bf16[4,608,128]{2,1,0:T(8,128)(2,1)}, bf16[4,608,128]{2,1,0:T(8,128)(2,1)}, u32[]{:S(2)}, u32[]{:S(2)}) collective-permute-start(bf16[4,608,128]{2,1,0:T(8,128)(2,1)} %get-tuple-element.24), channel_id=1, source_target_pairs={{0,2},{1,3},{2,0},{3,1},{4,6},{5,7},{6,4},{7,5},{8,10},{9,11},{10,... | collective-permute-start | bytes 1867784 | tf_op jit(solution)/shard_map/ppermute | solution.py:265
  185.6 44.5 %collective-permute-start.18 = (bf16[4,608,128]{2,1,0:T(8,128)(2,1)}, bf16[4,608,128]{2,1,0:T(8,128)(2,1)}, u32[]{:S(2)}, u32[]{:S(2)}) collective-permute-start(bf16[4,608,128]{2,1,0:T(8,128)(2,1)} %get-tuple-element.22), channel_id=1, source_target_pairs={{0,2},{1,3},{2,0},{3,1},{4,6},{5,7},{6,4},{7,5},{8,10},{9,11},{10,... | collective-permute-start | bytes 1867784 | tf_op jit(solution)/shard_map/ppermute | solution.py:265
  209.1 24.7 %collective-permute-start.23 = (bf16[4,608,128]{2,1,0:T(8,128)(2,1)}, bf16[4,608,128]{2,1,0:T(8,128)(2,1)}, u32[]{:S(2)}, u32[]{:S(2)}) collective-permute-start(bf16[4,608,128]{2,1,0:T(8,128)(2,1)} %merge.10.refs_1_), channel_id=1, source_target_pairs={{12,8},{13,9},{14,10},{15,11},{28,24},{29,25},{30,26},{31,27}} | collective-permute-start | bytes 1867784 | tf_op jit(solution)/shard_map/ppermute | solution.py:271
  237.5 31.6 %collective-permute-start.24 = (bf16[4,608,128]{2,1,0:T(8,128)(2,1)}, bf16[4,608,128]{2,1,0:T(8,128)(2,1)}, u32[]{:S(2)}, u32[]{:S(2)}) collective-permute-start(bf16[4,608,128]{2,1,0:T(8,128)(2,1)} %merge.15), channel_id=1, source_target_pairs={{8,4},{9,5},{10,6},{11,7},{12,8},{13,9},{14,10},{15,11},{24,20},{2... | collective-permute-start | bytes 1867784 | tf_op jit(solution)/shard_map/ppermute | solution.py:271
  242.5 32.2 %collective-permute-start.21 = (bf16[4,608,128]{2,1,0:T(8,128)(2,1)}, bf16[4,608,128]{2,1,0:T(8,128)(2,1)}, u32[]{:S(2)}, u32[]{:S(2)}) collective-permute-start(bf16[4,608,128]{2,1,0:T(8,128)(2,1)} %merge.13), channel_id=1, source_target_pairs={{0,4},{1,5},{2,6},{3,7},{4,8},{5,9},{6,10},{7,11},{16,20},{17,21},... | collective-permute-start | bytes 1867784 | tf_op jit(solution)/shard_map/ppermute | solution.py:271
  247.1 36.8 %collective-permute-start.16 = (bf16[4,608,128]{2,1,0:T(8,128)(2,1)}, bf16[4,608,128]{2,1,0:T(8,128)(2,1)}, u32[]{:S(2)}, u32[]{:S(2)}) collective-permute-start(bf16[4,608,128]{2,1,0:T(8,128)(2,1)} %get-tuple-element.18), channel_id=1, source_target_pairs={{0,2},{1,3},{2,0},{3,1},{4,6},{5,7},{6,4},{7,5},{8,10},{9,11},{10,... | collective-permute-start | bytes 1867784 | tf_op jit(solution)/shard_map/ppermute | solution.py:265
  272.8 30.8 %collective-permute-start.25 = (bf16[4,608,128]{2,1,0:T(8,128)(2,1)}, bf16[4,608,128]{2,1,0:T(8,128)(2,1)}, u32[]{:S(2)}, u32[]{:S(2)}) collective-permute-start(bf16[4,608,128]{2,1,0:T(8,128)(2,1)} %merge.16), channel_id=1, source_target_pairs={{4,0},{5,1},{6,2},{7,3},{8,4},{9,5},{10,6},{11,7},{12,8},{13,9},{1... | collective-permute-start | bytes 1867784 | tf_op jit(solution)/shard_map/ppermute | solution.py:271
  278.4 44.9 %collective-permute-start.22 = (bf16[4,608,128]{2,1,0:T(8,128)(2,1)}, bf16[4,608,128]{2,1,0:T(8,128)(2,1)}, u32[]{:S(2)}, u32[]{:S(2)}) collective-permute-start(bf16[4,608,128]{2,1,0:T(8,128)(2,1)} %merge.14), channel_id=1, source_target_pairs={{0,4},{1,5},{2,6},{3,7},{4,8},{5,9},{6,10},{7,11},{8,12},{9,13},{1... | collective-permute-start | bytes 1867784 | tf_op jit(solution)/shard_map/ppermute | solution.py:271
  339.0 24.3 %collective-permute-start.27 = (bf16[288,1024]{1,0:T(8,128)(2,1)}, bf16[288,1024]{1,0:T(8,128)(2,1)}, u32[]{:S(2)}, u32[]{:S(2)}) collective-permute-start(bf16[288,1024]{1,0:T(8,128)(2,1)} %project.4), channel_id=1, source_target_pairs={{0,16},{16,0},{1,17},{17,1},{2,18},{18,2},{3,19},{19,3},{4,20},{20... | collective-permute-start | bytes 1769480 | tf_op jit(solution)/shard_map/ppermute | solution.py:568
  (25 other events, 229.6 us)
Sparse Core Ops, SparseCore 0:
  10.3 108.1 all-gather.6
  120.8 110.2 all-gather.4
  233.2 96.4 all-gather.8

commit v9 on v8

--- a/solution.py
+++ b/solution.py
@@ -141,17 +141,18 @@
         o_refs[index][0, part_len:, :] = s_all[part].astype(jnp.bfloat16)
 
 
-def cached_attention(q_places, at, ok, out_at, k_heads, v_heads, order, starts, counts, span,
-                     stat_unit, scale2):
+def cached_attention(first, heads, q_places, at, ok, out_at, k_heads, v_heads, order, starts,
+                     counts, span, stat_unit, scale2):
     places = len(q_places)
     chips = len(out_at)
-    heads, part_len, head_dim = q_places[0].shape
+    _, part_len, head_dim = q_places[0].shape
     slots = k_heads.shape[1]
     unit = math.gcd(span, part_len)
     _, _, pad_to = stat_rows_of(part_len, stat_unit)
     own_block = lambda *dims: pl.BlockSpec(
-        (1,) + dims, lambda h, *_: (h,) + (0,) * len(dims)
-    )
+        (1,) + dims, lambda h, *_: (first + h,) + (0,) * len(dims)
+    )
+    out_block = pl.BlockSpec((1, part_len + pad_to, head_dim), lambda h, *_: (h, 0, 0))
     return pl.pallas_call(
         lambda *refs: cached_kernel(unit, stat_unit, span, scale2, places, *refs),
         grid_spec=pltpu.PrefetchScalarGridSpec(
@@ -159,7 +160,7 @@
             grid=(heads,),
             in_specs=[own_block(part_len, head_dim)] * places
             + [own_block(slots, PAGE, head_dim), own_block(slots, head_dim, PAGE)],
-            out_specs=[own_block(part_len + pad_to, head_dim)] * chips,
+            out_specs=[out_block] * chips,
             scratch_shapes=[
                 pltpu.VMEM((chips, part_len, head_dim), jnp.bfloat16),
                 pltpu.VMEM((chips, part_len, head_dim), jnp.bfloat16),
@@ -175,7 +176,7 @@
         ] * chips,
         compiler_params=pltpu.CompilerParams(vmem_limit_bytes=60 * 2**20),
         cost_estimate=pl.CostEstimate(
-            flops=40 * 10**9, bytes_accessed=20 * 2**20, transcendentals=10**7
+            flops=20 * 10**9, bytes_accessed=10 * 2**20, transcendentals=10**7
         ),
         name="cached_attention",
     )(jnp.stack(at + out_at), jnp.stack(ok), order, starts, counts, *q_places, k_heads, v_heads)
@@ -228,6 +229,32 @@
     )(jnp.stack(ok).astype(jnp.int32), *parts)
 
 
+def merge_two(halves, part_len, unit, scale2):
+    heads, rows, width = halves[0][0].shape
+    whole = pl.BlockSpec((heads, rows, width), lambda h, *_: (0, 0, 0))
+
+    def kernel(ok_ref, *refs):
+        for half in range(2):
+
+            @pl.when(pl.program_id(0) == half)
+            def _(half=half):
+                merge_kernel(
+                    unit, part_len, scale2, ok_ref, refs[2 * half], refs[2 * half + 1], refs[4]
+                )
+
+    return pl.pallas_call(
+        kernel,
+        grid_spec=pltpu.PrefetchScalarGridSpec(
+            num_scalar_prefetch=1,
+            grid=(2,),
+            in_specs=[whole] * 4,
+            out_specs=pl.BlockSpec((heads, rows, width), lambda h, *_: (h, 0, 0)),
+        ),
+        out_shape=jax.ShapeDtypeStruct((2 * heads, rows, width), jnp.bfloat16),
+        name="merge_two",
+    )(jnp.ones((2,), jnp.int32), *halves[0], *halves[1])
+
+
 def page_kernel(fresh_ref, index_ref, kc_ref, vc_ref, kn_ref, vn_ref, ko_ref, vo_ref):
     fresh = fresh_ref[pl.program_id(0)] > 0
 
@@ -295,19 +322,19 @@
     return held
 
 
-def merge_lines(parts, merged, last):
+def merge_lines(parts, merged, merged_two, last):
     line = lax.axis_size("pages") // 4
     at = lax.axis_index("pages") // 4
     turns = []
     for t in range(1, line):
         turns += [k for k in (line - t, t) if k not in turns]
     yes = jnp.int32(1)
-    crossed = {k: swap(parts[k][1], 2) for k in turns + [0]}
+    crossed = {k: [swap(x, 2) for x in parts[k][1]] for k in turns + [0]}
     shares = {}
 
     def share(k):
         if k not in shares:
-            shares[k] = merged([parts[k][0], crossed[k]], [yes, yes])
+            shares[k] = merged_two(list(zip(parts[k][0], crossed[k])))
         return shares[k]
 
     up = down = None
@@ -318,7 +345,7 @@
             down_out = merged([down_out, down], [yes, (at <= line - 2) & (at >= line - t)])
         up = shift(up_out, 1, range(0, t))
         down = shift(down_out, -1, range(line - t, line))
-    return merged([share(0), up, down, last()], [yes, at >= 1, at <= line - 2, yes])
+    return merged([share(0), up, down, last([crossed[k] for k in turns])], [yes, at >= 1, at <= line - 2, yes])
 
 
 def fresh_kernel(unit, scale2, q_ref, k_ref, v_ref, tok_ref, key_ref, o_ref):
@@ -468,14 +495,14 @@
     groups = lax.axis_size("heads")
     group_at = lax.axis_index("heads")
     natural = Layout((0, 1, 2))
-    q_chip, late_k, late_weight = lax.optimization_barrier((q_chip, keys, out_weight))
+    q_chip, late_k, late_v = lax.optimization_barrier((q_chip, keys, values))
     q_places = gather_lines(q_chip)
     rotated_k = rotate(late_k.astype(jnp.float32), positions).astype(jnp.bfloat16)
     all_k = lax.all_gather(rotated_k, "pages", axis=0, tiled=True)
-    all_v = lax.all_gather(values, "pages", axis=0, tiled=True)
+    all_v = lax.all_gather(late_v, "pages", axis=0, tiled=True)
     all_k = with_layout_constraint(all_k, natural)
     all_v = with_layout_constraint(all_v, natural)
-    weights = lax.all_gather(late_weight, "pages", axis=0, tiled=False)
+    weights = lax.all_gather(out_weight, "pages", axis=0, tiled=False)
 
     my_slots = device_at * slot_count + jnp.arange(slot_count, dtype=jnp.int32)
     chip_slots = jnp.concatenate(
@@ -510,44 +537,54 @@
     unit = math.gcd(span_len, tok_dev)
     line = page_devs // 4
     line_at, across = device_at // 4, (device_at // 2) % 2
-    outs = cached_attention(
-        [q for q, _, _, _ in q_places],
-        [jnp.clip(at, 0, line - 1) * 2 + side for _, at, side, _ in q_places],
-        [ok for _, _, _, ok in q_places],
-        [((line_at + k) % line) * 2 + (across ^ d) for k in range(line) for d in range(2)],
-        k_heads,
-        v_heads,
-        order,
-        slot_starts,
-        slot_counts,
-        span_len,
-        unit,
-        scale2,
-    )
+    outs = [
+        cached_attention(
+            first,
+            half // 2,
+            [q for q, _, _, _ in q_places],
+            [jnp.clip(at, 0, line - 1) * 2 + side for _, at, side, _ in q_places],
+            [ok for _, _, _, ok in q_places],
+            [((line_at + k) % line) * 2 + (across ^ d) for k in range(line) for d in range(2)],
+            k_heads,
+            v_heads,
+            order,
+            slot_starts,
+            slot_counts,
+            span_len,
+            unit,
+            scale2,
+        )
+        for first in (0, half // 2)
+    ]
     merged = lambda parts, ok: merge(parts, ok, chip_len, unit, scale2)
 
-    def fresh_part():
+    merged_two = lambda halves: merge_two(halves, chip_len, unit, scale2)
+
+    def fresh_part(after):
+        back = -(-(span_len - math.gcd(span_len, chip_len)) // chip_len)
+        own_kv = jnp.stack(
+            [jnp.transpose(rotated_k, (1, 0, 2)), jnp.transpose(late_v, (1, 0, 2))], 1
+        )
+        kv_mine, kv_other = halves(own_kv)
+        kv_chip = in_order(kv_mine, swap(kv_other, 1), 2)
+        kv_chip, _ = lax.optimization_barrier((kv_chip, after))
+        kv_back = [
+            lax.ppermute(kv_chip, "pages", [(p, p + 2 * b) for p in range(page_devs - 2 * b)])
+            for b in range(back, 0, -1)
+        ]
         chip_at = device_at // 2
-        back = -(-(span_len - math.gcd(span_len, chip_len)) // chip_len)
-        window = (back + 1) * chip_len
-        window_at = jnp.maximum(chip_at - back, 0) * chip_len
-
-        def by_head(rows):
-            rows = lax.dynamic_slice(
-                rows, (window_at, core * half, 0), (window, half, head_dim)
-            )
-            return jnp.transpose(rows, (1, 0, 2))
-
+        window = jnp.concatenate(kv_back + [kv_chip], axis=2)
         chip_tokens = chip_at * chip_len + jnp.arange(chip_len, dtype=jnp.int32)
         token_rows = jnp.stack([chip_tokens, chip_tokens // span_len * span_len])
-        key_cols = (window_at + jnp.arange(window, dtype=jnp.int32))[:, None]
+        keys_at = (chip_at - back) * chip_len
+        keys_at = keys_at + jnp.arange((back + 1) * chip_len, dtype=jnp.int32)
+        key_cols = jnp.where(keys_at < 0, tokens, keys_at)[:, None]
         return fresh_attention(
-            q_chip, by_head(all_k), by_head(all_v), token_rows, key_cols, unit, scale2
+            q_chip, window[:, 0], window[:, 1], token_rows, key_cols, unit, scale2
         )
 
-    chip_part = merge_lines(
-        [outs[2 * k : 2 * k + 2] for k in range(line)], merged, fresh_part
-    )
+    parts = [[[out[2 * k + d] for out in outs] for d in range(2)] for k in range(line)]
+    chip_part = merge_lines(parts, merged, merged_two, fresh_part)
     rows_of = lambda c: lax.dynamic_slice_in_dim(chip_part[:, :chip_len], c * tok_dev, tok_dev, 1)
     own_rows, got_rows = rows_of(core), swap(rows_of(1 - core), 1)
     blocks = page_devs // groups

time: 381 us -> 401 us (1.052)
  waiting for transfers between devices: 149 us -> 154 us
  other arithmetic: 20.7 us -> 25.3 us
    ppermute x12, waiting for transfers between devices: 96.7 us -> 72.6 us  [shift(): return lax.ppermute(x, 'pages', moves)]
    ppermute x9 -> x14, waiting for transfers between devices: 36.3 us -> 52.4 us  [swap(): return lax.ppermute(x, 'pages', [(p, p ^ bit) for p in range(devs)])]
    pallas_call x0 -> x4, Pallas kernels: none -> 15.6 us  [merge_two(): pl.pallas_call(kernel, grid_spec=pltpu.PrefetchScalarGridSpec(num_scalar_...]
    pallas_call x9 -> x5, Pallas kernels: 34.1 us -> 19.7 us  [merge(): pl.pallas_call(lambda *refs: merge_kernel(unit, part_len, scale2, *refs),...]
    ppermute x2, waiting for transfers between devices: 4.04 us -> 14.1 us  [per_device(): sent.append(lax.ppermute(part, 'heads', moves))]
    ppermute x9 -> x14, starting transfers between devices: 4.81 us -> 8.55 us  [swap(): return lax.ppermute(x, 'pages', [(p, p ^ bit) for p in range(devs)])]
    unnamed x39 -> x56, local copies, waits for them, and re-layouts: 24.5 us -> 26.2 us
    pallas_call x1 -> x2, Pallas kernels: 37.9 us -> 37.7 us  [cached_attention(): pl.pallas_call(lambda *refs: cached_kernel(unit, stat_unit, span, scale2,...]
  transfers between devices with their start and end apart: 32 -> 38, of which waited for: 13 -> 17; matrix products, arithmetic and copies ran while one was open for 12% -> 14% of each run, Pallas kernels for 26% -> 24%
where the time goes in v9:
time: 401 us; the launch traced here: 395 us
  waiting for transfers between devices  154 us (38%)
  Pallas kernels  102 us (25%)
  starting transfers between devices  55.1 us (14%)
  local copies, waits for them, and re-layouts  44.1 us (11%)
  other arithmetic  25.3 us (6%)
  between operations  14.5 us (4%)
    ppermute x12, waiting for transfers between devices, shift(): return lax.ppermute(x, 'pages', moves)  72.6 us
    ppermute x14, waiting for transfers between devices, swap(): return lax.ppermute(x, 'pages', [(p, p ^ bit) for p in range(devs)])  52.4 us
    pallas_call x2, Pallas kernels, cached_attention(): pl.pallas_call(lambda *refs: cached_kernel(unit, stat_unit, span, scale2,...  37.7 us
    ppermute x12, starting transfers between devices, shift(): return lax.ppermute(x, 'pages', moves)  29.9 us
    unnamed x56, local copies, waits for them, and re-layouts  26.2 us
    pallas_call x5, Pallas kernels, merge(): pl.pallas_call(lambda *refs: merge_kernel(unit, part_len, scale2, *refs),...  19.7 us
    pallas_call x4, Pallas kernels, merge_two(): pl.pallas_call(kernel, grid_spec=pltpu.PrefetchScalarGridSpec(num_scalar_...  15.6 us
    ppermute x2, waiting for transfers between devices, per_device(): sent.append(lax.ppermute(part, 'heads', moves))  14.1 us
  transfers between devices with their start and end apart: 38, of which 17 were waited for; matrix products, arithmetic and copies ran while one was open for 14% of the time, Pallas kernels for 24%

profile of v9, /device:TPU:12, one launch (start us, length us, event | category | flops | bytes accessed | tf_op | source)
XLA Modules:
  0.0 394.7 jit_solution(16276444809605905433)
XLA Ops:
  23.7 7.2 %constant_dynamic-slice_fusion.3 = (bf16[12,128,4,128]{3,2,1,0:T(4,128)(2,1)}, bf16[12,128,4,128]{3,2,1,0:T(4,128)(2,1)}, bf16[12,128,4,128]{3,2,1,0:T(4,128)(2,1)S(1)}, bf16[12,128,4,128]{3,2,1,0:T(4,128)(2,1)}) fusion(bf16[12,128,8,128]{3,2,1,0:T(8,128)(2,1)S(1)} %copy-done.2, s32[]{:T(128)S(6)} %select_n.197, s32[]{:T(128)S(6)} %select_n.198, ...), kind=kLoop, calls=%fused_computation.52 | loop fusion | bytes 12582920 | tf_op jit(solution)/shard_map/dynamic-slice.4
  37.3 12.8 %collective-permute-done.2.refs_7_ = bf16[4,576,128]{2,1,0:T(8,128)(2,1)} collective-permute-done((bf16[4,576,128]{2,1,0:T(8,128)(2,1)}, bf16[4,576,128]{2,1,0:T(8,128)(2,1)}, u32[]{:S(2)}, u32[]{:S(2)}) %collective-permute-start.2) | collective-permute-done | bytes 589856 | tf_op jit(solution)/shard_map/ppermute | solution.py:298
  50.1 5.2 %collective-permute-start.6 = (bf16[4,576,128]{2,1,0:T(8,128)(2,1)}, bf16[4,576,128]{2,1,0:T(8,128)(2,1)}, u32[]{:S(2)}, u32[]{:S(2)}) collective-permute-start(bf16[4,576,128]{2,1,0:T(8,128)(2,1)} %collective-permute-done.2.refs_7_), channel_id=1, source_target_pairs={{4,8},{5,9},{6,10},{7,11},{8,12},{9,13},{10,14},{11,15},{20,24},{2... | collective-permute-start | bytes 1769480 | tf_op jit(solution)/shard_map/ppermute | solution.py:298
  59.8 33.6 %collective-permute-done.6.refs_11_ = bf16[4,576,128]{2,1,0:T(8,128)(2,1)} collective-permute-done((bf16[4,576,128]{2,1,0:T(8,128)(2,1)}, bf16[4,576,128]{2,1,0:T(8,128)(2,1)}, u32[]{:S(2)}, u32[]{:S(2)}) %collective-permute-start.6) | collective-permute-done | bytes 589856 | tf_op jit(solution)/shard_map/ppermute | solution.py:298
  130.4 13.4 %collective-permute-done.9.refs_14_ = bf16[4,576,128]{2,1,0:T(8,128)(2,1)} collective-permute-done((bf16[4,576,128]{2,1,0:T(8,128)(2,1)}, bf16[4,576,128]{2,1,0:T(8,128)(2,1)}, u32[]{:S(2)}, u32[]{:S(2)}) %collective-permute-start.9) | collective-permute-done | bytes 589856 | tf_op jit(solution)/shard_map/ppermute | solution.py:320
  143.8 18.9 %cached_attention.3 = (bf16[2,608,128]{2,1,0:T(8,128)(2,1)}, bf16[2,608,128]{2,1,0:T(8,128)(2,1)}, bf16[2,608,128]{2,1,0:T(8,128)(2,1)}, bf16[2,608,128]{2,1,0:T...) custom-call(s32[22]{0:T(128)} %stack.256.refs_0_, ...), custom_call_target="tpu_custom_call" | custom-call | flops 20000000000 | bytes 10485760 | tf_op jit(solution)/shard_map/cached_attention/pallas_call | solution.py:156
  162.8 18.8 %cached_attention.2 = (bf16[2,608,128]{2,1,0:T(8,128)(2,1)}, bf16[2,608,128]{2,1,0:T(8,128)(2,1)}, bf16[2,608,128]{2,1,0:T(8,128)(2,1)}, bf16[2,608,128]{2,1,0:T...) custom-call(s32[22]{0:T(128)} %stack.256.refs_0_, ...), custom_call_target="tpu_custom_call" | custom-call | flops 20000000000 | bytes 10485760 | tf_op jit(solution)/shard_map/cached_attention/pallas_call | solution.py:156
  186.5 11.2 %collective-permute-done.18.refs_1_ = bf16[2,608,128]{2,1,0:T(8,128)(2,1)} collective-permute-done((bf16[2,608,128]{2,1,0:T(8,128)(2,1)}, bf16[2,608,128]{2,1,0:T(8,128)(2,1)}, u32[]{:S(2)}, u32[]{:S(2)}) %collective-permute-start.18) | collective-permute-done | bytes 311328 | tf_op jit(solution)/shard_map/ppermute | solution.py:292
  198.8 3.9 merge_two.5.refs_1_
  205.8 5.2 %collective-permute-done.22.refs_1_ = bf16[2,608,128]{2,1,0:T(8,128)(2,1)} collective-permute-done((bf16[2,608,128]{2,1,0:T(8,128)(2,1)}, bf16[2,608,128]{2,1,0:T(8,128)(2,1)}, u32[]{:S(2)}, u32[]{:S(2)}) %collective-permute-start.22) | collective-permute-done | bytes 311328 | tf_op jit(solution)/shard_map/ppermute | solution.py:292
  211.0 3.9 merge_two.7.refs_1_
  219.2 4.4 %collective-permute-done.20.refs_1_ = bf16[2,608,128]{2,1,0:T(8,128)(2,1)} collective-permute-done((bf16[2,608,128]{2,1,0:T(8,128)(2,1)}, bf16[2,608,128]{2,1,0:T(8,128)(2,1)}, u32[]{:S(2)}, u32[]{:S(2)}) %collective-permute-start.20) | collective-permute-done | bytes 311328 | tf_op jit(solution)/shard_map/ppermute | solution.py:292
  226.8 3.9 merge_two.6.refs_1_
  239.5 4.5 %collective-permute-start.25 = (bf16[4,608,128]{2,1,0:T(8,128)(2,1)}, bf16[4,608,128]{2,1,0:T(8,128)(2,1)}, u32[]{:S(2)}, u32[]{:S(2)}) collective-permute-start(bf16[4,608,128]{2,1,0:T(8,128)(2,1)} %merge.5), channel_id=1, source_target_pairs={{0,4},{1,5},{2,6},{3,7},{4,8},{5,9},{6,10},{7,11},{16,20},{17,21},... | collective-permute-start | bytes 1867784 | tf_op jit(solution)/shard_map/ppermute | solution.py:298
  248.3 19.3 %collective-permute-done.17.refs_3_ = bf16[2,608,128]{2,1,0:T(8,128)(2,1)S(1)} collective-permute-done((bf16[2,608,128]{2,1,0:T(8,128)(2,1)}, bf16[2,608,128]{2,1,0:T(8,128)(2,1)S(1)}, u32[]{:S(2)}, u32[]{:S(2)}) %collective-permute-start.17) | collective-permute-done | bytes 311328 | tf_op jit(solution)/shard_map/ppermute | solution.py:292
  267.5 7.0 %collective-permute-done.16.refs_1_ = bf16[2,608,128]{2,1,0:T(8,128)(2,1)} collective-permute-done((bf16[2,608,128]{2,1,0:T(8,128)(2,1)}, bf16[2,608,128]{2,1,0:T(8,128)(2,1)}, u32[]{:S(2)}, u32[]{:S(2)}) %collective-permute-start.16) | collective-permute-done | bytes 311328 | tf_op jit(solution)/shard_map/ppermute | solution.py:292
  274.6 3.9 merge_two.4.refs_1_
  287.0 10.5 %collective-permute-done.25.refs_2_ = bf16[4,608,128]{2,1,0:T(8,128)(2,1)} collective-permute-done((bf16[4,608,128]{2,1,0:T(8,128)(2,1)}, bf16[4,608,128]{2,1,0:T(8,128)(2,1)}, u32[]{:S(2)}, u32[]{:S(2)}) %collective-permute-start.25) | collective-permute-done | bytes 622624 | tf_op jit(solution)/shard_map/ppermute | solution.py:298
  307.5 8.4 %fresh_attention.1.refs_4_ = bf16[4,608,128]{2,1,0:T(8,128)(2,1)S(1)} custom-call(bf16[4,576,128]{2,1,0:T(8,128)(2,1)S(1)} %copy-done.5, bf16[4,1152,128]{2,1,0:T(8,128)(2,1)S(1)} %get-tuple-element.54.refs_1_, bf16[4,1152,128]{2,1,0:T(8,128)(2,1)S(1)} %get-tuple-element.53.refs_2_, s32[2,576]{1,0:T(2,128)S(1)} %pad_add_fusion.refs_3_, s32[1152,1]{1,0:T(8,128)S(1)} %copy-done.6), custom_call_target="tpu_custom_call" | custom-call | tf_op jit(solution)/shard_map/fresh_attention/pallas_call | solution.py:385
  316.7 12.6 %collective-permute-done.29.refs_3_ = bf16[4,608,128]{2,1,0:T(8,128)(2,1)} collective-permute-done((bf16[4,608,128]{2,1,0:T(8,128)(2,1)}, bf16[4,608,128]{2,1,0:T(8,128)(2,1)}, u32[]{:S(2)}, u32[]{:S(2)}) %collective-permute-start.29) | collective-permute-done | bytes 622624 | tf_op jit(solution)/shard_map/ppermute | solution.py:298
  330.7 4.7 %merge.9 = bf16[4,608,128]{2,1,0:T(8,128)(2,1)} custom-call(s32[4]{0:T(128)} %pad_add_fusion.5.refs_0_, bf16[4,608,128]{2,1,0:T(8,128)(2,1)} %merge_two.4.refs_1_, bf16[4,608,128]{2,1,0:T(8,128)(2,1)} %collective-permute-done.26.refs_2_, bf16[4,608,128]{2,1,0:T(8,128)(2,1)} %collective-permute-done.29.refs_3_, bf16[4,608,128]{2,1,0:T(8,128)(2,1)} %copy-done.4), custom_call_target="tpu_custom_call" | custom-call | tf_op jit(solution)/shard_map/merge/pallas_call | solution.py:219
  356.8 4.3 %project.3 = f32[288,2048]{1,0:T(8,128)S(1)} custom-call(s32[2]{0:T(128)S(1)} %pad_add_fusion.4.at_ref, bf16[4,288,128]{2,1,0:T(8,128)(2,1)S(1)} %get-tuple-element.62.mine_ref, bf16[4,288,128]{2,1,0:T(8,128)(2,1)} %collective-permute-done.32.other_ref, bf16[16,1024,256]{2,1,0:T(8,128)(2,1)S(1)} %bitcast.66), custom_call_target="tpu_custom_call" | custom-call | tf_op jit(solution)/shard_map/project/pallas_call | solution.py:425
  363.4 11.8 %collective-permute-done.34 = bf16[288,1024]{1,0:T(8,128)(2,1)} collective-permute-done((bf16[288,1024]{1,0:T(8,128)(2,1)}, bf16[288,1024]{1,0:T(8,128)(2,1)}, u32[]{:S(2)}, u32[]{:S(2)}) %collective-permute-start.34) | collective-permute-done | bytes 589856 | tf_op jit(solution)/shard_map/ppermute | solution.py:605
  379.8 8.4 %write_pages.1 = (bf16[12,128,8,128]{3,2,1,0:T(8,128)(2,1)}, bf16[12,128,8,128]{3,2,1,0:T(8,128)(2,1)}) custom-call(s32[12]{0:T(128)S(1)} %convert_element_type.53.fresh_ref, s32[12]{0:T(128)S(1)} %fusion.4.index_ref, bf16[12,128,8,128]{3,2,1,0:T(8,128)(2,1)S(1)} %copy-done.3, bf16[12,128,8,128]{3,2,1,0:T(8,128)(2,1)S(1)} %copy-done.2, ...), custom_call_target="tpu_custom_call" | custom-call | tf_op jit(solution)/shard_map/write_pages/pallas_call | solution.py:276
  (188 shorter events, 142.5 us)
Async XLA Ops:
  7.2 332.4 %all-gather.9.cloned.1.call-start = ((), (), s32[]{:S(2)}) async-start(), calls=%async_computation.2 | async-start | bytes 8912896 | tf_op jit(solution)/shard_map/all_gather | solution.py:505
  7.9 370.0 %all-gather.5.cloned.1.call-start = ((), (), s32[]{:S(2)}) async-start(), calls=%async_computation | async-start | bytes 10027008 | tf_op jit(solution)/shard_map/all_gather | solution.py:501
  16.3 361.6 %all-gather.7.cloned.1.call-start = ((), (), s32[]{:S(2)}) async-start(), calls=%async_computation.1 | async-start | bytes 10027008 | tf_op jit(solution)/shard_map/all_gather | solution.py:502
  17.0 33.0 %collective-permute-start.2 = (bf16[4,576,128]{2,1,0:T(8,128)(2,1)}, bf16[4,576,128]{2,1,0:T(8,128)(2,1)}, u32[]{:S(2)}, u32[]{:S(2)}) collective-permute-start(bf16[4,576,128]{2,1,0:T(8,128)(2,1)} %maximum_select_fusion.1.refs_5_.refs_0_), channel_id=1, source_target_pairs={{0,4},{1,5},{2,6},{3,7},{4,8},{5,9},{6,10},{7,11},{8,12},{9,13},{1... | collective-permute-start | bytes 1769480 | tf_op jit(solution)/shard_map/ppermute | solution.py:298
  20.5 34.7 %collective-permute-start.4 = (bf16[4,576,128]{2,1,0:T(8,128)(2,1)}, bf16[4,576,128]{2,1,0:T(8,128)(2,1)}, u32[]{:S(2)}, u32[]{:S(2)}) collective-permute-start(bf16[4,576,128]{2,1,0:T(8,128)(2,1)} %maximum_select_fusion.1.refs_5_.refs_0_), channel_id=1, source_target_pairs={{4,0},{5,1},{6,2},{7,3},{8,4},{9,5},{10,6},{11,7},{12,8},{13,9},{1... | collective-permute-start | bytes 1769480 | tf_op jit(solution)/shard_map/ppermute | solution.py:298
  32.5 77.5 %collective-permute-start.14 = (bf16[4,12,128,128]{3,2,1,0:T(8,128)(2,1)}, bf16[4,12,128,128]{3,2,1,0:T(8,128)(2,1)}, u32[]{:S(2)}, u32[]{:S(2)}) collective-permute-start(bf16[4,12,128,128]{3,2,1,0:T(8,128)(2,1)} %bitcast.61), channel_id=1, source_target_pairs={{0,1},{1,0},{2,3},{3,2},{4,5},{5,4},{6,7},{7,6},{8,9},{9,8},{10,11... | collective-permute-start | bytes 4718600 | tf_op jit(solution)/shard_map/ppermute | solution.py:292
  36.3 75.3 %collective-permute-start.15 = (bf16[4,12,128,128]{3,2,1,0:T(8,128)(2,1)}, bf16[4,12,128,128]{3,2,1,0:T(8,128)(2,1)}, u32[]{:S(2)}, u32[]{:S(2)}) collective-permute-start(bf16[4,12,128,128]{3,2,1,0:T(8,128)(2,1)} %bitcast.72), channel_id=1, source_target_pairs={{0,1},{1,0},{2,3},{3,2},{4,5},{5,4},{6,7},{7,6},{8,9},{9,8},{10,11... | collective-permute-start | bytes 4718600 | tf_op jit(solution)/shard_map/ppermute | solution.py:292
  50.1 43.3 %collective-permute-start.6 = (bf16[4,576,128]{2,1,0:T(8,128)(2,1)}, bf16[4,576,128]{2,1,0:T(8,128)(2,1)}, u32[]{:S(2)}, u32[]{:S(2)}) collective-permute-start(bf16[4,576,128]{2,1,0:T(8,128)(2,1)} %collective-permute-done.2.refs_7_), channel_id=1, source_target_pairs={{4,8},{5,9},{6,10},{7,11},{8,12},{9,13},{10,14},{11,15},{20,24},{2... | collective-permute-start | bytes 1769480 | tf_op jit(solution)/shard_map/ppermute | solution.py:298
  55.2 39.6 %collective-permute-start.8 = (bf16[4,576,128]{2,1,0:T(8,128)(2,1)}, bf16[4,576,128]{2,1,0:T(8,128)(2,1)}, u32[]{:S(2)}, u32[]{:S(2)}) collective-permute-start(bf16[4,576,128]{2,1,0:T(8,128)(2,1)} %collective-permute-done.4.refs_9_), channel_id=1, source_target_pairs={{4,0},{5,1},{6,2},{7,3},{8,4},{9,5},{10,6},{11,7},{20,16},{21,17},... | collective-permute-start | bytes 1769480 | tf_op jit(solution)/shard_map/ppermute | solution.py:298
  57.5 50.4 %collective-permute-start.3 = (bf16[4,576,128]{2,1,0:T(8,128)(2,1)}, bf16[4,576,128]{2,1,0:T(8,128)(2,1)}, u32[]{:S(2)}, u32[]{:S(2)}) collective-permute-start(bf16[4,576,128]{2,1,0:T(8,128)(2,1)} %collective-permute-done.2.refs_7_), channel_id=1, source_target_pairs={{4,6},{5,7},{6,4},{7,5},{8,10},{9,11},{10,8},{11,9},{12,14},{13,15... | collective-permute-start | bytes 1769480 | tf_op jit(solution)/shard_map/ppermute | solution.py:318
  111.5 32.3 %collective-permute-start.9 = (bf16[4,576,128]{2,1,0:T(8,128)(2,1)}, bf16[4,576,128]{2,1,0:T(8,128)(2,1)}, u32[]{:S(2)}, u32[]{:S(2)}) collective-permute-start(bf16[4,576,128]{2,1,0:T(8,128)(2,1)} %collective-permute-done.8.refs_13_), channel_id=1, source_target_pairs={{0,2},{1,3},{2,0},{3,1},{4,6},{5,7},{6,4},{7,5},{16,18},{17,19},{1... | collective-permute-start | bytes 1769480 | tf_op jit(solution)/shard_map/ppermute | solution.py:320
  115.3 28.5 %collective-permute-start.11 = (bf16[4,576,128]{2,1,0:T(8,128)(2,1)}, bf16[4,576,128]{2,1,0:T(8,128)(2,1)}, u32[]{:S(2)}, u32[]{:S(2)}) collective-permute-start(bf16[4,576,128]{2,1,0:T(8,128)(2,1)} %collective-permute-done.10.refs_15_), channel_id=1, source_target_pairs={{12,14},{13,15},{14,12},{15,13},{28,30},{29,31},{30,28},{31,29}} | collective-permute-start | bytes 1769480 | tf_op jit(solution)/shard_map/ppermute | solution.py:318
  118.5 25.3 %collective-permute-start.13 = (bf16[4,576,128]{2,1,0:T(8,128)(2,1)}, bf16[4,576,128]{2,1,0:T(8,128)(2,1)}, u32[]{:S(2)}, u32[]{:S(2)}) collective-permute-start(bf16[4,576,128]{2,1,0:T(8,128)(2,1)} %collective-permute-done.12.refs_17_), channel_id=1, source_target_pairs={{0,2},{1,3},{2,0},{3,1},{16,18},{17,19},{18,16},{19,17}} | collective-permute-start | bytes 1769480 | tf_op jit(solution)/shard_map/ppermute | solution.py:320
  130.4 85.8 %collective-permute-start.30 = (bf16[4,2,288,128]{3,2,0,1:T(8,128)(2,1)}, bf16[4,2,288,128]{3,2,0,1:T(8,128)(2,1)}, u32[]{:S(2)}, u32[]{:S(2)}) collective-permute-start(bf16[4,2,288,128]{3,2,0,1:T(8,128)(2,1)} %get-tuple-element.60), channel_id=1, source_target_pairs={{0,1},{1,0},{2,3},{3,2},{4,5},{5,4},{6,7},{7,6},{8,9},{9,8},{10,11... | collective-permute-start | bytes 1769480 | tf_op jit(solution)/shard_map/ppermute | solution.py:292
  183.7 27.3 %collective-permute-start.22 = (bf16[2,608,128]{2,1,0:T(8,128)(2,1)}, bf16[2,608,128]{2,1,0:T(8,128)(2,1)}, u32[]{:S(2)}, u32[]{:S(2)}) collective-permute-start(bf16[2,608,128]{2,1,0:T(8,128)(2,1)} %get-tuple-element.39), channel_id=1, source_target_pairs={{0,2},{1,3},{2,0},{3,1},{4,6},{5,7},{6,4},{7,5},{8,10},{9,11},{10,... | collective-permute-start | bytes 933896 | tf_op jit(solution)/shard_map/ppermute | solution.py:292
  184.5 34.6 %collective-permute-start.21 = (bf16[2,608,128]{2,1,0:T(8,128)(2,1)}, bf16[2,608,128]{2,1,0:T(8,128)(2,1)S(1)}, u32[]{:S(2)}, u32[]{:S(2)}) collective-permute-start(bf16[2,608,128]{2,1,0:T(8,128)(2,1)} %get-tuple-element.37), channel_id=1, source_target_pairs={{0,2},{1,3},{2,0},{3,1},{4,6},{5,7},{6,4},{7,5},{8,10},{9,11},{10,... | collective-permute-start | bytes 933896 | tf_op jit(solution)/shard_map/ppermute | solution.py:292
  197.6 25.9 %collective-permute-start.20 = (bf16[2,608,128]{2,1,0:T(8,128)(2,1)}, bf16[2,608,128]{2,1,0:T(8,128)(2,1)}, u32[]{:S(2)}, u32[]{:S(2)}) collective-permute-start(bf16[2,608,128]{2,1,0:T(8,128)(2,1)} %get-tuple-element.35), channel_id=1, source_target_pairs={{0,2},{1,3},{2,0},{3,1},{4,6},{5,7},{6,4},{7,5},{8,10},{9,11},{10,... | collective-permute-start | bytes 933896 | tf_op jit(solution)/shard_map/ppermute | solution.py:292
  204.3 26.4 %collective-permute-start.27 = (bf16[4,608,128]{2,1,0:T(8,128)(2,1)}, bf16[4,608,128]{2,1,0:T(8,128)(2,1)}, u32[]{:S(2)}, u32[]{:S(2)}) collective-permute-start(bf16[4,608,128]{2,1,0:T(8,128)(2,1)} %merge_two.5.refs_1_), channel_id=1, source_target_pairs={{12,8},{13,9},{14,10},{15,11},{28,24},{29,25},{30,26},{31,27}} | collective-permute-start | bytes 1867784 | tf_op jit(solution)/shard_map/ppermute | solution.py:298
  223.5 54.9 %collective-permute-start.31 = (bf16[4,2,576,128]{3,2,0,1:T(8,128)(2,1)}, bf16[4,2,576,128]{3,2,0,1:T(8,128)(2,1)}, u32[]{:S(2)}, u32[]{:S(2)}) collective-permute-start(bf16[4,2,576,128]{3,2,0,1:T(8,128)(2,1)} %maximum_select_fusion), channel_id=1, source_target_pairs={{0,2},{1,3},{2,4},{3,5},{4,6},{5,7},{6,8},{7,9},{8,10},{9,11},{10,... | collective-permute-start | bytes 3538952 | tf_op jit(solution)/shard_map/ppermute | solution.py:572
  234.4 46.5 %collective-permute-start.28 = (bf16[4,608,128]{2,1,0:T(8,128)(2,1)}, bf16[4,608,128]{2,1,0:T(8,128)(2,1)}, u32[]{:S(2)}, u32[]{:S(2)}) collective-permute-start(bf16[4,608,128]{2,1,0:T(8,128)(2,1)} %merge.7), channel_id=1, source_target_pairs={{8,4},{9,5},{10,6},{11,7},{12,8},{13,9},{14,10},{15,11},{24,20},{2... | collective-permute-start | bytes 1867784 | tf_op jit(solution)/shard_map/ppermute | solution.py:298
  239.5 58.0 %collective-permute-start.25 = (bf16[4,608,128]{2,1,0:T(8,128)(2,1)}, bf16[4,608,128]{2,1,0:T(8,128)(2,1)}, u32[]{:S(2)}, u32[]{:S(2)}) collective-permute-start(bf16[4,608,128]{2,1,0:T(8,128)(2,1)} %merge.5), channel_id=1, source_target_pairs={{0,4},{1,5},{2,6},{3,7},{4,8},{5,9},{6,10},{7,11},{16,20},{17,21},... | collective-permute-start | bytes 1867784 | tf_op jit(solution)/shard_map/ppermute | solution.py:298
  246.7 27.9 %collective-permute-start.16 = (bf16[2,608,128]{2,1,0:T(8,128)(2,1)}, bf16[2,608,128]{2,1,0:T(8,128)(2,1)}, u32[]{:S(2)}, u32[]{:S(2)}) collective-permute-start(bf16[2,608,128]{2,1,0:T(8,128)(2,1)} %get-tuple-element.27), channel_id=1, source_target_pairs={{0,2},{1,3},{2,0},{3,1},{4,6},{5,7},{6,4},{7,5},{8,10},{9,11},{10,... | collective-permute-start | bytes 933896 | tf_op jit(solution)/shard_map/ppermute | solution.py:292
  284.8 44.5 %collective-permute-start.29 = (bf16[4,608,128]{2,1,0:T(8,128)(2,1)}, bf16[4,608,128]{2,1,0:T(8,128)(2,1)}, u32[]{:S(2)}, u32[]{:S(2)}) collective-permute-start(bf16[4,608,128]{2,1,0:T(8,128)(2,1)} %merge.8), channel_id=1, source_target_pairs={{4,0},{5,1},{6,2},{7,3},{8,4},{9,5},{10,6},{11,7},{12,8},{13,9},{1... | collective-permute-start | bytes 1867784 | tf_op jit(solution)/shard_map/ppermute | solution.py:298
  301.1 29.6 %collective-permute-start.26 = (bf16[4,608,128]{2,1,0:T(8,128)(2,1)}, bf16[4,608,128]{2,1,0:T(8,128)(2,1)}, u32[]{:S(2)}, u32[]{:S(2)}) collective-permute-start(bf16[4,608,128]{2,1,0:T(8,128)(2,1)} %merge.6), channel_id=1, source_target_pairs={{0,4},{1,5},{2,6},{3,7},{4,8},{5,9},{6,10},{7,11},{8,12},{9,13},{1... | collective-permute-start | bytes 1867784 | tf_op jit(solution)/shard_map/ppermute | solution.py:298
  (40 other events, 442.7 us)
Sparse Core Ops, SparseCore 0:
  10.2 100.7 all-gather.8
  113.3 111.8 all-gather.4
  227.5 114.8 all-gather.6

commit v10 on v9

--- a/solution.py
+++ b/solution.py
@@ -345,7 +345,7 @@
             down_out = merged([down_out, down], [yes, (at <= line - 2) & (at >= line - t)])
         up = shift(up_out, 1, range(0, t))
         down = shift(down_out, -1, range(line - t, line))
-    return merged([share(0), up, down, last([crossed[k] for k in turns])], [yes, at >= 1, at <= line - 2, yes])
+    return merged([share(0), up, down, last([crossed[k] for k in turns + [0]])], [yes, at >= 1, at <= line - 2, yes])
 
 
 def fresh_kernel(unit, scale2, q_ref, k_ref, v_ref, tok_ref, key_ref, o_ref):

time: 401 us -> 415 us (1.035)
  starting transfers between devices: 55.1 us -> 77.9 us
  Pallas kernels: 102 us -> 91.7 us
  waiting for transfers between devices: 154 us -> 159 us
    ppermute x1, waiting for transfers between devices: 0.01 us -> 20.5 us  [fresh_part(): lax.ppermute(kv_chip, 'pages', [(p, p + 2 * b) for p in range(page_devs -...]
    ppermute x14, waiting for transfers between devices: 52.4 us -> 38.4 us  [swap(): return lax.ppermute(x, 'pages', [(p, p ^ bit) for p in range(devs)])]
    ppermute x12, starting transfers between devices: 29.9 us -> 42.9 us  [shift(): return lax.ppermute(x, 'pages', moves)]
    ppermute x14, starting transfers between devices: 8.55 us -> 18.4 us  [swap(): return lax.ppermute(x, 'pages', [(p, p ^ bit) for p in range(devs)])]
    pallas_call x2, Pallas kernels: 37.7 us -> 28.6 us  [cached_attention(): pl.pallas_call(lambda *refs: cached_kernel(unit, stat_unit, span, scale2,...]
    unnamed x56 -> x54, local copies, waits for them, and re-layouts: 26.2 us -> 26.2 us
  transfers between devices with their start and end apart: 38 -> 38, of which waited for: 17 -> 15; matrix products, arithmetic and copies ran while one was open for 14% -> 14% of each run, Pallas kernels for 24% -> 20%
where the time goes in v10:
time: 415 us; the launch traced here: 413 us
  waiting for transfers between devices  159 us (38%)
  Pallas kernels  91.7 us (22%)
  starting transfers between devices  77.9 us (19%)
  local copies, waits for them, and re-layouts  44.1 us (11%)
  other arithmetic  25.3 us (6%)
  between operations  14.4 us (3%)
    ppermute x12, waiting for transfers between devices, shift(): return lax.ppermute(x, 'pages', moves)  71.3 us
    ppermute x12, starting transfers between devices, shift(): return lax.ppermute(x, 'pages', moves)  42.9 us
    ppermute x14, waiting for transfers between devices, swap(): return lax.ppermute(x, 'pages', [(p, p ^ bit) for p in range(devs)])  38.4 us
    pallas_call x2, Pallas kernels, cached_attention(): pl.pallas_call(lambda *refs: cached_kernel(unit, stat_unit, span, scale2,...  28.6 us
    unnamed x54, local copies, waits for them, and re-layouts  26.2 us
    ppermute x1, waiting for transfers between devices, fresh_part(): lax.ppermute(kv_chip, 'pages', [(p, p + 2 * b) for p in range(page_devs -...  20.5 us
    pallas_call x5, Pallas kernels, merge(): pl.pallas_call(lambda *refs: merge_kernel(unit, part_len, scale2, *refs),...  19.4 us
    ppermute x14, starting transfers between devices, swap(): return lax.ppermute(x, 'pages', [(p, p ^ bit) for p in range(devs)])  18.4 us
  transfers between devices with their start and end apart: 38, of which 15 were waited for; matrix products, arithmetic and copies ran while one was open for 14% of the time, Pallas kernels for 20%

profile of v10, /device:TPU:12, one launch (start us, length us, event | category | flops | bytes accessed | tf_op | source)
XLA Modules:
  0.0 412.6 jit_solution(2256745181900633426)
XLA Ops:
  23.7 7.2 %constant_dynamic-slice_fusion.3 = (bf16[12,128,4,128]{3,2,1,0:T(4,128)(2,1)}, bf16[12,128,4,128]{3,2,1,0:T(4,128)(2,1)}, bf16[12,128,4,128]{3,2,1,0:T(4,128)(2,1)S(1)}, bf16[12,128,4,128]{3,2,1,0:T(4,128)(2,1)}) fusion(bf16[12,128,8,128]{3,2,1,0:T(8,128)(2,1)S(1)} %copy-done.2, s32[]{:T(128)S(6)} %select_n.197, s32[]{:T(128)S(6)} %select_n.198, ...), kind=kLoop, calls=%fused_computation.52 | loop fusion | bytes 12582920 | tf_op jit(solution)/shard_map/dynamic-slice.4
  37.3 12.8 %collective-permute-done.2.refs_7_ = bf16[4,576,128]{2,1,0:T(8,128)(2,1)} collective-permute-done((bf16[4,576,128]{2,1,0:T(8,128)(2,1)}, bf16[4,576,128]{2,1,0:T(8,128)(2,1)}, u32[]{:S(2)}, u32[]{:S(2)}) %collective-permute-start.2) | collective-permute-done | bytes 589856 | tf_op jit(solution)/shard_map/ppermute | solution.py:298
  50.1 5.2 %collective-permute-start.6 = (bf16[4,576,128]{2,1,0:T(8,128)(2,1)}, bf16[4,576,128]{2,1,0:T(8,128)(2,1)}, u32[]{:S(2)}, u32[]{:S(2)}) collective-permute-start(bf16[4,576,128]{2,1,0:T(8,128)(2,1)} %collective-permute-done.2.refs_7_), channel_id=1, source_target_pairs={{4,8},{5,9},{6,10},{7,11},{8,12},{9,13},{10,14},{11,15},{20,24},{2... | collective-permute-start | bytes 1769480 | tf_op jit(solution)/shard_map/ppermute | solution.py:298
  59.8 33.6 %collective-permute-done.6.refs_11_ = bf16[4,576,128]{2,1,0:T(8,128)(2,1)} collective-permute-done((bf16[4,576,128]{2,1,0:T(8,128)(2,1)}, bf16[4,576,128]{2,1,0:T(8,128)(2,1)}, u32[]{:S(2)}, u32[]{:S(2)}) %collective-permute-start.6) | collective-permute-done | bytes 589856 | tf_op jit(solution)/shard_map/ppermute | solution.py:298
  130.4 13.5 %collective-permute-done.9.refs_14_ = bf16[4,576,128]{2,1,0:T(8,128)(2,1)} collective-permute-done((bf16[4,576,128]{2,1,0:T(8,128)(2,1)}, bf16[4,576,128]{2,1,0:T(8,128)(2,1)}, u32[]{:S(2)}, u32[]{:S(2)}) %collective-permute-start.9) | collective-permute-done | bytes 589856 | tf_op jit(solution)/shard_map/ppermute | solution.py:320
  143.9 14.3 %cached_attention.3 = (bf16[2,608,128]{2,1,0:T(8,128)(2,1)}, bf16[2,608,128]{2,1,0:T(8,128)(2,1)}, bf16[2,608,128]{2,1,0:T(8,128)(2,1)}, bf16[2,608,128]{2,1,0:T...) custom-call(s32[22]{0:T(128)} %stack.256.refs_0_, ...), custom_call_target="tpu_custom_call" | custom-call | flops 20000000000 | bytes 10485760 | tf_op jit(solution)/shard_map/cached_attention/pallas_call | solution.py:156
  158.3 4.3 %collective-permute-start.19 = (bf16[2,608,128]{2,1,0:T(8,128)(2,1)}, bf16[2,608,128]{2,1,0:T(8,128)(2,1)S(1)}, u32[]{:S(2)}, u32[]{:S(2)}) collective-permute-start(bf16[2,608,128]{2,1,0:T(8,128)(2,1)} %get-tuple-element.33), channel_id=1, source_target_pairs={{0,2},{1,3},{2,0},{3,1},{4,6},{5,7},{6,4},{7,5},{8,10},{9,11},{10,... | collective-permute-start | bytes 933896 | tf_op jit(solution)/shard_map/ppermute | solution.py:292
  162.6 14.3 %cached_attention.2 = (bf16[2,608,128]{2,1,0:T(8,128)(2,1)}, bf16[2,608,128]{2,1,0:T(8,128)(2,1)}, bf16[2,608,128]{2,1,0:T(8,128)(2,1)}, bf16[2,608,128]{2,1,0:T...) custom-call(s32[22]{0:T(128)} %stack.256.refs_0_, ...), custom_call_target="tpu_custom_call" | custom-call | flops 20000000000 | bytes 10485760 | tf_op jit(solution)/shard_map/cached_attention/pallas_call | solution.py:156
  177.0 6.0 %collective-permute-start.18 = (bf16[2,608,128]{2,1,0:T(8,128)(2,1)}, bf16[2,608,128]{2,1,0:T(8,128)(2,1)}, u32[]{:S(2)}, u32[]{:S(2)}) collective-permute-start(bf16[2,608,128]{2,1,0:T(8,128)(2,1)} %get-tuple-element.31), channel_id=1, source_target_pairs={{0,2},{1,3},{2,0},{3,1},{4,6},{5,7},{6,4},{7,5},{8,10},{9,11},{10,... | collective-permute-start | bytes 933896 | tf_op jit(solution)/shard_map/ppermute | solution.py:292
  185.7 5.3 %collective-permute-done.23.refs_3_ = bf16[2,608,128]{2,1,0:T(8,128)(2,1)} collective-permute-done((bf16[2,608,128]{2,1,0:T(8,128)(2,1)}, bf16[2,608,128]{2,1,0:T(8,128)(2,1)}, u32[]{:S(2)}, u32[]{:S(2)}) %collective-permute-start.23) | collective-permute-done | bytes 311328 | tf_op jit(solution)/shard_map/ppermute | solution.py:292
  193.1 11.2 %collective-permute-done.18.refs_1_ = bf16[2,608,128]{2,1,0:T(8,128)(2,1)} collective-permute-done((bf16[2,608,128]{2,1,0:T(8,128)(2,1)}, bf16[2,608,128]{2,1,0:T(8,128)(2,1)}, u32[]{:S(2)}, u32[]{:S(2)}) %collective-permute-start.18) | collective-permute-done | bytes 311328 | tf_op jit(solution)/shard_map/ppermute | solution.py:292
  205.7 5.2 %collective-permute-done.22.refs_1_ = bf16[2,608,128]{2,1,0:T(8,128)(2,1)} collective-permute-done((bf16[2,608,128]{2,1,0:T(8,128)(2,1)}, bf16[2,608,128]{2,1,0:T(8,128)(2,1)}, u32[]{:S(2)}, u32[]{:S(2)}) %collective-permute-start.22) | collective-permute-done | bytes 311328 | tf_op jit(solution)/shard_map/ppermute | solution.py:292
  225.9 5.0 %collective-permute-done.16.refs_1_ = bf16[2,608,128]{2,1,0:T(8,128)(2,1)} collective-permute-done((bf16[2,608,128]{2,1,0:T(8,128)(2,1)}, bf16[2,608,128]{2,1,0:T(8,128)(2,1)}, u32[]{:S(2)}, u32[]{:S(2)}) %collective-permute-start.16) | collective-permute-done | bytes 311328 | tf_op jit(solution)/shard_map/ppermute | solution.py:292
  231.0 8.2 %collective-permute-done.20.refs_1_ = bf16[2,608,128]{2,1,0:T(8,128)(2,1)} collective-permute-done((bf16[2,608,128]{2,1,0:T(8,128)(2,1)}, bf16[2,608,128]{2,1,0:T(8,128)(2,1)}, u32[]{:S(2)}, u32[]{:S(2)}) %collective-permute-start.20) | collective-permute-done | bytes 311328 | tf_op jit(solution)/shard_map/ppermute | solution.py:292
  255.6 7.0 %collective-permute-start.25 = (bf16[4,608,128]{2,1,0:T(8,128)(2,1)}, bf16[4,608,128]{2,1,0:T(8,128)(2,1)}, u32[]{:S(2)}, u32[]{:S(2)}) collective-permute-start(bf16[4,608,128]{2,1,0:T(8,128)(2,1)} %merge.5), channel_id=1, source_target_pairs={{0,4},{1,5},{2,6},{3,7},{4,8},{5,9},{6,10},{7,11},{16,20},{17,21},... | collective-permute-start | bytes 1867784 | tf_op jit(solution)/shard_map/ppermute | solution.py:298
  268.1 20.5 %collective-permute-done.31 = bf16[4,2,576,128]{3,2,0,1:T(8,128)(2,1)} collective-permute-done((bf16[4,2,576,128]{3,2,0,1:T(8,128)(2,1)}, bf16[4,2,576,128]{3,2,0,1:T(8,128)(2,1)}, u32[]{:S(2)}, u32[]{:S(2)}) %collective-permute-start.31) | collective-permute-done | bytes 1179680 | tf_op jit(solution)/shard_map/ppermute | solution.py:572
  294.8 8.6 %collective-permute-start.29 = (bf16[4,608,128]{2,1,0:T(8,128)(2,1)}, bf16[4,608,128]{2,1,0:T(8,128)(2,1)}, u32[]{:S(2)}, u32[]{:S(2)}) collective-permute-start(bf16[4,608,128]{2,1,0:T(8,128)(2,1)} %merge.8), channel_id=1, source_target_pairs={{4,0},{5,1},{6,2},{7,3},{8,4},{9,5},{10,6},{11,7},{12,8},{13,9},{1... | collective-permute-start | bytes 1867784 | tf_op jit(solution)/shard_map/ppermute | solution.py:298
  303.4 23.3 %collective-permute-done.25.refs_2_ = bf16[4,608,128]{2,1,0:T(8,128)(2,1)} collective-permute-done((bf16[4,608,128]{2,1,0:T(8,128)(2,1)}, bf16[4,608,128]{2,1,0:T(8,128)(2,1)}, u32[]{:S(2)}, u32[]{:S(2)}) %collective-permute-start.25) | collective-permute-done | bytes 622624 | tf_op jit(solution)/shard_map/ppermute | solution.py:298
  330.3 5.9 %collective-permute-start.26 = (bf16[4,608,128]{2,1,0:T(8,128)(2,1)}, bf16[4,608,128]{2,1,0:T(8,128)(2,1)}, u32[]{:S(2)}, u32[]{:S(2)}) collective-permute-start(bf16[4,608,128]{2,1,0:T(8,128)(2,1)} %merge.6), channel_id=1, source_target_pairs={{0,4},{1,5},{2,6},{3,7},{4,8},{5,9},{6,10},{7,11},{8,12},{9,13},{1... | collective-permute-start | bytes 1867784 | tf_op jit(solution)/shard_map/ppermute | solution.py:298
  340.7 8.4 %fresh_attention.1.refs_4_ = bf16[4,608,128]{2,1,0:T(8,128)(2,1)S(1)} custom-call(bf16[4,576,128]{2,1,0:T(8,128)(2,1)S(1)} %copy-done.5, bf16[4,1152,128]{2,1,0:T(8,128)(2,1)S(1)} %get-tuple-element.54.refs_1_, bf16[4,1152,128]{2,1,0:T(8,128)(2,1)S(1)} %get-tuple-element.53.refs_2_, s32[2,576]{1,0:T(2,128)S(1)} %pad_add_fusion.refs_3_, s32[1152,1]{1,0:T(8,128)S(1)} %copy-done.6), custom_call_target="tpu_custom_call" | custom-call | tf_op jit(solution)/shard_map/fresh_attention/pallas_call | solution.py:385
  350.0 4.6 %merge.9 = bf16[4,608,128]{2,1,0:T(8,128)(2,1)} custom-call(s32[4]{0:T(128)} %pad_add_fusion.5.refs_0_, bf16[4,608,128]{2,1,0:T(8,128)(2,1)} %merge_two.4.refs_1_, bf16[4,608,128]{2,1,0:T(8,128)(2,1)} %collective-permute-done.26.refs_2_, bf16[4,608,128]{2,1,0:T(8,128)(2,1)} %collective-permute-done.29.refs_3_, bf16[4,608,128]{2,1,0:T(8,128)(2,1)} %copy-done.4), custom_call_target="tpu_custom_call" | custom-call | tf_op jit(solution)/shard_map/merge/pallas_call | solution.py:219
  375.6 4.3 %project.3 = f32[288,2048]{1,0:T(8,128)S(1)} custom-call(s32[2]{0:T(128)S(1)} %pad_add_fusion.4.at_ref, bf16[4,288,128]{2,1,0:T(8,128)(2,1)S(1)} %get-tuple-element.62.mine_ref, bf16[4,288,128]{2,1,0:T(8,128)(2,1)} %collective-permute-done.32.other_ref, bf16[16,1024,256]{2,1,0:T(8,128)(2,1)S(1)} %bitcast.66), custom_call_target="tpu_custom_call" | custom-call | tf_op jit(solution)/shard_map/project/pallas_call | solution.py:425
  382.2 11.8 %collective-permute-done.34 = bf16[288,1024]{1,0:T(8,128)(2,1)} collective-permute-done((bf16[288,1024]{1,0:T(8,128)(2,1)}, bf16[288,1024]{1,0:T(8,128)(2,1)}, u32[]{:S(2)}, u32[]{:S(2)}) %collective-permute-start.34) | collective-permute-done | bytes 589856 | tf_op jit(solution)/shard_map/ppermute | solution.py:605
  398.5 7.6 %write_pages.1 = (bf16[12,128,8,128]{3,2,1,0:T(8,128)(2,1)}, bf16[12,128,8,128]{3,2,1,0:T(8,128)(2,1)}) custom-call(s32[12]{0:T(128)S(1)} %convert_element_type.53.fresh_ref, s32[12]{0:T(128)S(1)} %fusion.4.index_ref, bf16[12,128,8,128]{3,2,1,0:T(8,128)(2,1)S(1)} %copy-done.3, bf16[12,128,8,128]{3,2,1,0:T(8,128)(2,1)S(1)} %copy-done.2, ...), custom_call_target="tpu_custom_call" | custom-call | tf_op jit(solution)/shard_map/write_pages/pallas_call | solution.py:276
  (186 shorter events, 149.9 us)
Async XLA Ops:
  7.2 351.2 %all-gather.9.cloned.1.call-start = ((), (), s32[]{:S(2)}) async-start(), calls=%async_computation.2 | async-start | bytes 8912896 | tf_op jit(solution)/shard_map/all_gather | solution.py:505
  7.9 388.7 %all-gather.5.cloned.1.call-start = ((), (), s32[]{:S(2)}) async-start(), calls=%async_computation | async-start | bytes 10027008 | tf_op jit(solution)/shard_map/all_gather | solution.py:501
  16.3 380.4 %all-gather.7.cloned.1.call-start = ((), (), s32[]{:S(2)}) async-start(), calls=%async_computation.1 | async-start | bytes 10027008 | tf_op jit(solution)/shard_map/all_gather | solution.py:502
  17.0 33.1 %collective-permute-start.2 = (bf16[4,576,128]{2,1,0:T(8,128)(2,1)}, bf16[4,576,128]{2,1,0:T(8,128)(2,1)}, u32[]{:S(2)}, u32[]{:S(2)}) collective-permute-start(bf16[4,576,128]{2,1,0:T(8,128)(2,1)} %maximum_select_fusion.1.refs_5_.refs_0_), channel_id=1, source_target_pairs={{0,4},{1,5},{2,6},{3,7},{4,8},{5,9},{6,10},{7,11},{8,12},{9,13},{1... | collective-permute-start | bytes 1769480 | tf_op jit(solution)/shard_map/ppermute | solution.py:298
  20.5 34.7 %collective-permute-start.4 = (bf16[4,576,128]{2,1,0:T(8,128)(2,1)}, bf16[4,576,128]{2,1,0:T(8,128)(2,1)}, u32[]{:S(2)}, u32[]{:S(2)}) collective-permute-start(bf16[4,576,128]{2,1,0:T(8,128)(2,1)} %maximum_select_fusion.1.refs_5_.refs_0_), channel_id=1, source_target_pairs={{4,0},{5,1},{6,2},{7,3},{8,4},{9,5},{10,6},{11,7},{12,8},{13,9},{1... | collective-permute-start | bytes 1769480 | tf_op jit(solution)/shard_map/ppermute | solution.py:298
  32.5 77.6 %collective-permute-start.14 = (bf16[4,12,128,128]{3,2,1,0:T(8,128)(2,1)}, bf16[4,12,128,128]{3,2,1,0:T(8,128)(2,1)}, u32[]{:S(2)}, u32[]{:S(2)}) collective-permute-start(bf16[4,12,128,128]{3,2,1,0:T(8,128)(2,1)} %bitcast.61), channel_id=1, source_target_pairs={{0,1},{1,0},{2,3},{3,2},{4,5},{5,4},{6,7},{7,6},{8,9},{9,8},{10,11... | collective-permute-start | bytes 4718600 | tf_op jit(solution)/shard_map/ppermute | solution.py:292
  36.3 75.3 %collective-permute-start.15 = (bf16[4,12,128,128]{3,2,1,0:T(8,128)(2,1)}, bf16[4,12,128,128]{3,2,1,0:T(8,128)(2,1)}, u32[]{:S(2)}, u32[]{:S(2)}) collective-permute-start(bf16[4,12,128,128]{3,2,1,0:T(8,128)(2,1)} %bitcast.72), channel_id=1, source_target_pairs={{0,1},{1,0},{2,3},{3,2},{4,5},{5,4},{6,7},{7,6},{8,9},{9,8},{10,11... | collective-permute-start | bytes 4718600 | tf_op jit(solution)/shard_map/ppermute | solution.py:292
  50.1 43.3 %collective-permute-start.6 = (bf16[4,576,128]{2,1,0:T(8,128)(2,1)}, bf16[4,576,128]{2,1,0:T(8,128)(2,1)}, u32[]{:S(2)}, u32[]{:S(2)}) collective-permute-start(bf16[4,576,128]{2,1,0:T(8,128)(2,1)} %collective-permute-done.2.refs_7_), channel_id=1, source_target_pairs={{4,8},{5,9},{6,10},{7,11},{8,12},{9,13},{10,14},{11,15},{20,24},{2... | collective-permute-start | bytes 1769480 | tf_op jit(solution)/shard_map/ppermute | solution.py:298
  55.2 39.6 %collective-permute-start.8 = (bf16[4,576,128]{2,1,0:T(8,128)(2,1)}, bf16[4,576,128]{2,1,0:T(8,128)(2,1)}, u32[]{:S(2)}, u32[]{:S(2)}) collective-permute-start(bf16[4,576,128]{2,1,0:T(8,128)(2,1)} %collective-permute-done.4.refs_9_), channel_id=1, source_target_pairs={{4,0},{5,1},{6,2},{7,3},{8,4},{9,5},{10,6},{11,7},{20,16},{21,17},... | collective-permute-start | bytes 1769480 | tf_op jit(solution)/shard_map/ppermute | solution.py:298
  57.5 50.4 %collective-permute-start.3 = (bf16[4,576,128]{2,1,0:T(8,128)(2,1)}, bf16[4,576,128]{2,1,0:T(8,128)(2,1)}, u32[]{:S(2)}, u32[]{:S(2)}) collective-permute-start(bf16[4,576,128]{2,1,0:T(8,128)(2,1)} %collective-permute-done.2.refs_7_), channel_id=1, source_target_pairs={{4,6},{5,7},{6,4},{7,5},{8,10},{9,11},{10,8},{11,9},{12,14},{13,15... | collective-permute-start | bytes 1769480 | tf_op jit(solution)/shard_map/ppermute | solution.py:318
  111.6 32.3 %collective-permute-start.9 = (bf16[4,576,128]{2,1,0:T(8,128)(2,1)}, bf16[4,576,128]{2,1,0:T(8,128)(2,1)}, u32[]{:S(2)}, u32[]{:S(2)}) collective-permute-start(bf16[4,576,128]{2,1,0:T(8,128)(2,1)} %collective-permute-done.8.refs_13_), channel_id=1, source_target_pairs={{0,2},{1,3},{2,0},{3,1},{4,6},{5,7},{6,4},{7,5},{16,18},{17,19},{1... | collective-permute-start | bytes 1769480 | tf_op jit(solution)/shard_map/ppermute | solution.py:320
  115.3 28.6 %collective-permute-start.11 = (bf16[4,576,128]{2,1,0:T(8,128)(2,1)}, bf16[4,576,128]{2,1,0:T(8,128)(2,1)}, u32[]{:S(2)}, u32[]{:S(2)}) collective-permute-start(bf16[4,576,128]{2,1,0:T(8,128)(2,1)} %collective-permute-done.10.refs_15_), channel_id=1, source_target_pairs={{12,14},{13,15},{14,12},{15,13},{28,30},{29,31},{30,28},{31,29}} | collective-permute-start | bytes 1769480 | tf_op jit(solution)/shard_map/ppermute | solution.py:318
  130.4 89.8 %collective-permute-start.30 = (bf16[4,2,288,128]{3,2,0,1:T(8,128)(2,1)}, bf16[4,2,288,128]{3,2,0,1:T(8,128)(2,1)}, u32[]{:S(2)}, u32[]{:S(2)}) collective-permute-start(bf16[4,2,288,128]{3,2,0,1:T(8,128)(2,1)} %get-tuple-element.60), channel_id=1, source_target_pairs={{0,1},{1,0},{2,3},{3,2},{4,5},{5,4},{6,7},{7,6},{8,9},{9,8},{10,11... | collective-permute-start | bytes 1769480 | tf_op jit(solution)/shard_map/ppermute | solution.py:292
  162.6 28.5 %collective-permute-start.23 = (bf16[2,608,128]{2,1,0:T(8,128)(2,1)}, bf16[2,608,128]{2,1,0:T(8,128)(2,1)}, u32[]{:S(2)}, u32[]{:S(2)}) collective-permute-start(bf16[2,608,128]{2,1,0:T(8,128)(2,1)} %get-tuple-element.41), channel_id=1, source_target_pairs={{0,2},{1,3},{2,0},{3,1},{4,6},{5,7},{6,4},{7,5},{8,10},{9,11},{10,... | collective-permute-start | bytes 933896 | tf_op jit(solution)/shard_map/ppermute | solution.py:292
  177.0 27.3 %collective-permute-start.18 = (bf16[2,608,128]{2,1,0:T(8,128)(2,1)}, bf16[2,608,128]{2,1,0:T(8,128)(2,1)}, u32[]{:S(2)}, u32[]{:S(2)}) collective-permute-start(bf16[2,608,128]{2,1,0:T(8,128)(2,1)} %get-tuple-element.31), channel_id=1, source_target_pairs={{0,2},{1,3},{2,0},{3,1},{4,6},{5,7},{6,4},{7,5},{8,10},{9,11},{10,... | collective-permute-start | bytes 933896 | tf_op jit(solution)/shard_map/ppermute | solution.py:292
  183.0 28.0 %collective-permute-start.22 = (bf16[2,608,128]{2,1,0:T(8,128)(2,1)}, bf16[2,608,128]{2,1,0:T(8,128)(2,1)}, u32[]{:S(2)}, u32[]{:S(2)}) collective-permute-start(bf16[2,608,128]{2,1,0:T(8,128)(2,1)} %get-tuple-element.39), channel_id=1, source_target_pairs={{0,2},{1,3},{2,0},{3,1},{4,6},{5,7},{6,4},{7,5},{8,10},{9,11},{10,... | collective-permute-start | bytes 933896 | tf_op jit(solution)/shard_map/ppermute | solution.py:292
  183.8 37.9 %collective-permute-start.17 = (bf16[2,608,128]{2,1,0:T(8,128)(2,1)}, bf16[2,608,128]{2,1,0:T(8,128)(2,1)S(1)}, u32[]{:S(2)}, u32[]{:S(2)}) collective-permute-start(bf16[2,608,128]{2,1,0:T(8,128)(2,1)} %get-tuple-element.29), channel_id=1, source_target_pairs={{0,2},{1,3},{2,0},{3,1},{4,6},{5,7},{6,4},{7,5},{8,10},{9,11},{10,... | collective-permute-start | bytes 933896 | tf_op jit(solution)/shard_map/ppermute | solution.py:292
  191.1 34.8 %collective-permute-start.21 = (bf16[2,608,128]{2,1,0:T(8,128)(2,1)}, bf16[2,608,128]{2,1,0:T(8,128)(2,1)}, u32[]{:S(2)}, u32[]{:S(2)}) collective-permute-start(bf16[2,608,128]{2,1,0:T(8,128)(2,1)} %get-tuple-element.37), channel_id=1, source_target_pairs={{0,2},{1,3},{2,0},{3,1},{4,6},{5,7},{6,4},{7,5},{8,10},{9,11},{10,... | collective-permute-start | bytes 933896 | tf_op jit(solution)/shard_map/ppermute | solution.py:292
  210.9 28.2 %collective-permute-start.20 = (bf16[2,608,128]{2,1,0:T(8,128)(2,1)}, bf16[2,608,128]{2,1,0:T(8,128)(2,1)}, u32[]{:S(2)}, u32[]{:S(2)}) collective-permute-start(bf16[2,608,128]{2,1,0:T(8,128)(2,1)} %get-tuple-element.35), channel_id=1, source_target_pairs={{0,2},{1,3},{2,0},{3,1},{4,6},{5,7},{6,4},{7,5},{8,10},{9,11},{10,... | collective-permute-start | bytes 933896 | tf_op jit(solution)/shard_map/ppermute | solution.py:292
  221.7 30.2 %collective-permute-start.24 = (bf16[4,608,128]{2,1,0:T(8,128)(2,1)}, bf16[4,608,128]{2,1,0:T(8,128)(2,1)}, u32[]{:S(2)}, u32[]{:S(2)}) collective-permute-start(bf16[4,608,128]{2,1,0:T(8,128)(2,1)} %merge_two.7.refs_1_), channel_id=1, source_target_pairs={{0,4},{1,5},{2,6},{3,7},{16,20},{17,21},{18,22},{19,23}} | collective-permute-start | bytes 1867784 | tf_op jit(solution)/shard_map/ppermute | solution.py:298
  239.2 49.4 %collective-permute-start.31 = (bf16[4,2,576,128]{3,2,0,1:T(8,128)(2,1)}, bf16[4,2,576,128]{3,2,0,1:T(8,128)(2,1)}, u32[]{:S(2)}, u32[]{:S(2)}) collective-permute-start(bf16[4,2,576,128]{3,2,0,1:T(8,128)(2,1)} %maximum_select_fusion), channel_id=1, source_target_pairs={{0,2},{1,3},{2,4},{3,5},{4,6},{5,7},{6,8},{7,9},{8,10},{9,11},{10,... | collective-permute-start | bytes 3538952 | tf_op jit(solution)/shard_map/ppermute | solution.py:572
  250.6 40.5 %collective-permute-start.28 = (bf16[4,608,128]{2,1,0:T(8,128)(2,1)}, bf16[4,608,128]{2,1,0:T(8,128)(2,1)}, u32[]{:S(2)}, u32[]{:S(2)}) collective-permute-start(bf16[4,608,128]{2,1,0:T(8,128)(2,1)} %merge.7), channel_id=1, source_target_pairs={{8,4},{9,5},{10,6},{11,7},{12,8},{13,9},{14,10},{15,11},{24,20},{2... | collective-permute-start | bytes 1867784 | tf_op jit(solution)/shard_map/ppermute | solution.py:298
  255.6 71.0 %collective-permute-start.25 = (bf16[4,608,128]{2,1,0:T(8,128)(2,1)}, bf16[4,608,128]{2,1,0:T(8,128)(2,1)}, u32[]{:S(2)}, u32[]{:S(2)}) collective-permute-start(bf16[4,608,128]{2,1,0:T(8,128)(2,1)} %merge.5), channel_id=1, source_target_pairs={{0,4},{1,5},{2,6},{3,7},{4,8},{5,9},{6,10},{7,11},{16,20},{17,21},... | collective-permute-start | bytes 1867784 | tf_op jit(solution)/shard_map/ppermute | solution.py:298
  294.8 55.2 %collective-permute-start.29 = (bf16[4,608,128]{2,1,0:T(8,128)(2,1)}, bf16[4,608,128]{2,1,0:T(8,128)(2,1)}, u32[]{:S(2)}, u32[]{:S(2)}) collective-permute-start(bf16[4,608,128]{2,1,0:T(8,128)(2,1)} %merge.8), channel_id=1, source_target_pairs={{4,0},{5,1},{6,2},{7,3},{8,4},{9,5},{10,6},{11,7},{12,8},{13,9},{1... | collective-permute-start | bytes 1867784 | tf_op jit(solution)/shard_map/ppermute | solution.py:298
  (39 other events, 451.4 us)
Sparse Core Ops, SparseCore 0:
  10.2 100.7 all-gather.8
  113.2 110.2 all-gather.4
  225.8 110.7 all-gather.6
